TPU v7x, 32 devices: a whole 2x2x4 slice. The times are simulated.
32 devices in a mesh: wide: 8 (over z, x), narrow: 4 (over y, core).
Axes of the slice: x: 2, y: 2, z: 4, core: 2. Of those that a mesh axis runs over, the one named last changes fastest.
Arguments:
- tokens: bfloat16 [4, 2048, 2048], P('narrow', 'wide'), may hold values from -6 to 6
- starts: int32 [4, 4], P('narrow'), may hold values from 0 to 2044, as said below
- init_state: float32 [4, 4, 2560], P('narrow'), may hold values from -4 to 4
- init_conv: bfloat16 [4, 4, 3, 2560], P('narrow'), may hold values from -6 to 6
- w_y: bfloat16 [2048, 2560], P(('wide', 'narrow')), may hold values from -0.125 to 0.125
- w_x: bfloat16 [2048, 2560], P(('wide', 'narrow')), may hold values from -0.125 to 0.125
- gate_a: bfloat16 [2560, 160], P(('wide', 'narrow')), may hold values from -0.5 to 0.5
- gate_i: bfloat16 [2560, 160], P(('wide', 'narrow')), may hold values from -0.5 to 0.5
- w_out: bfloat16 [2560, 2048], P(('wide', 'narrow')), may hold values from -0.3125 to 0.3125
- norm1_gain: bfloat16 [2048], P(('wide', 'narrow')), may hold values from 0.5 to 1.5
- conv_kernel: bfloat16 [4, 2560], P(None, ('wide', 'narrow')), may hold values from -3 to 3
- conv_bias: bfloat16 [2560], P(('wide', 'narrow')), may hold values from -3 to 3
- bias_a: bfloat16 [2560], P(('wide', 'narrow')), may hold values from -4 to 4
- bias_i: bfloat16 [2560], P(('wide', 'narrow')), may hold values from -4 to 4
- decay_param: bfloat16 [2560], P(('wide', 'narrow')), may hold values from -14 to -2
- w_gate: bfloat16 [2048, 6144], P(('wide', 'narrow')), may hold values from -0.125 to 0.125
- w_up: bfloat16 [2048, 6144], P(('wide', 'narrow')), may hold values from -0.125 to 0.125
- w_down: bfloat16 [6144, 2048], P(('wide', 'narrow')), may hold values from -0.15625 to 0.15625
- norm2_gain: bfloat16 [2048], P(('wide', 'narrow')), may hold values from 0.5 to 1.5
- cotangent: bfloat16 [4, 2048, 2048], P('narrow', 'wide'), may hold values from -6 to 6
Outputs:
- mixed: bfloat16 [4, 2048, 2048], P('narrow', 'wide')
- input_grad: bfloat16 [4, 2048, 2048], P('narrow', 'wide')
- final_state: float32 [4, 4, 2560], P('narrow')
- final_conv: bfloat16 [4, 4, 3, 2560], P('narrow')
- grad_w_y: float32 [2048, 2560], P(('wide', 'narrow'))
- grad_w_x: float32 [2048, 2560], P(('wide', 'narrow'))
- grad_gate_a: float32 [2560, 160], P(('wide', 'narrow'))
- grad_gate_i: float32 [2560, 160], P(('wide', 'narrow'))
- grad_w_out: float32 [2560, 2048], P(('wide', 'narrow'))
- grad_norm1_gain: float32 [2048], P(('wide', 'narrow'))
- grad_conv_kernel: float32 [4, 2560], P(None, ('wide', 'narrow'))
- grad_conv_bias: float32 [2560], P(('wide', 'narrow'))
- grad_bias_a: float32 [2560], P(('wide', 'narrow'))
- grad_bias_i: float32 [2560], P(('wide', 'narrow'))
- grad_decay_param: float32 [2560], P(('wide', 'narrow'))
- grad_w_gate: float32 [2048, 6144], P(('wide', 'narrow'))
- grad_w_up: float32 [2048, 6144], P(('wide', 'narrow'))
- grad_w_down: float32 [6144, 2048], P(('wide', 'narrow'))
- grad_norm2_gain: float32 [2048], P(('wide', 'narrow'))
Inputs may be any that keep to these rules, and one draw needn't show every extreme that they name: `starts`: in each stream the 4 offsets increase, the first is 0, and every sequence holds 4 tokens or more of the 2048 tokens.
All inputs are finite; a program needn't handle non-finite values.
Results may differ from a plain program's by a relative error of at most 0.012.
Values may be sent and summed in bfloat16 or wider, within the bound.
A program may use at most 448 MiB of HBM per device.

v0:
```python
import jax
import jax.numpy as jnp
from jax import lax
from jax.sharding import PartitionSpec as P

EPS = 1e-06
FLOOR = 0.001
HIGH = lax.Precision.HIGHEST


def passed_along(value, axis, by):
    size = lax.axis_size(axis)
    pairs = [(i, i + by) for i in range(size) if 0 <= i + by < size]
    return lax.ppermute(value, axis, pairs)


def entering(value, axis, combine, identity, reverse):
    size, place = (lax.axis_size(axis), lax.axis_index(axis))
    everything = jax.tree.map(lambda part: lax.all_gather(part, axis), value)
    start = jax.tree.map(
        lambda part, zero: jnp.broadcast_to(jnp.asarray(zero, part.dtype), part.shape),
        value,
        identity,
    )

    def hop(k, before):
        at = size - 1 - k if reverse else k
        reached = at > place if reverse else at < place
        new = combine(before, jax.tree.map(lambda part: part[at], everything))
        return jax.tree.map(lambda a, b: jnp.where(reached, a, b), new, before)

    return lax.fori_loop(0, size, hop, start)


def merged_2(value, axis, combine):
    everything = jax.tree.map(
        lambda part, kind: lax.all_gather(part.astype(kind), axis),
        value,
        jax.tree.map(lambda a: jnp.bfloat16 if a.dtype == jnp.float32 else a.dtype, value),
    )

    def take(k):
        return jax.tree.map(lambda part, own: part[k].astype(own.dtype), everything, value)

    return lax.fori_loop(
        1, lax.axis_size(axis), lambda k, so_far: combine(so_far, take(k)), take(0)
    )


def link(earlier, later):
    return (earlier[0] * later[0], later[0] * earlier[1] + later[1])


def tdot(left, right):
    return lax.dot_general(
        left, right, (((0,), (0,)), ((), ())), preferred_element_type=jnp.float32
    )


def ndot(left, right):
    return lax.dot_general(
        left, right, (((1,), (1,)), ((), ())), preferred_element_type=jnp.float32
    )


def mdot(left, right):
    return jnp.dot(left, right, preferred_element_type=jnp.float32)


def norm_back(value, factor, gain, grad):
    weighted = grad * gain
    inner = jnp.mean(weighted * value, axis=-1, keepdims=True)
    return (
        factor * weighted - value * factor * factor * factor * inner,
        jnp.sum(grad * value * factor, axis=0),
    )


def later_one(first, second):
    pick = first[0] > second[0]
    return (
        jnp.where(pick, first[0], second[0]),
        jnp.where(pick[:, None], first[1], second[1]),
        jnp.where(pick[:, None, None], first[2], second[2]),
    )


def on_device(
    tokens,
    starts,
    init_state,
    init_conv,
    w_y,
    w_x,
    gate_a,
    gate_i,
    w_out,
    norm1_gain,
    conv_kernel,
    conv_bias,
    bias_a,
    bias_i,
    decay_param,
    w_gate,
    w_up,
    w_down,
    norm2_gain,
    cotangent,
):
    inputs = tokens[0].astype(jnp.float32)
    offsets = starts[0]
    nseqs = offsets.shape[0]
    rows_here = inputs.shape[0]
    width = w_y.shape[1]
    head_w = gate_a.shape[1]
    heads = width // head_w
    place = lax.axis_index("wide")
    mixer = (
        lax.all_gather(w_y, ("wide", "narrow"), axis=0, tiled=True),
        lax.all_gather(w_x, ("wide", "narrow"), axis=0, tiled=True),
        lax.all_gather(gate_a, ("wide", "narrow"), axis=0, tiled=True),
        lax.all_gather(gate_i, ("wide", "narrow"), axis=0, tiled=True),
        lax.all_gather(w_out, ("wide", "narrow"), axis=0, tiled=True),
        lax.all_gather(norm1_gain, ("wide", "narrow"), axis=0, tiled=True),
        lax.all_gather(conv_kernel, ("wide", "narrow"), axis=1, tiled=True),
        lax.all_gather(conv_bias, ("wide", "narrow"), axis=0, tiled=True),
        lax.all_gather(bias_a, ("wide", "narrow"), axis=0, tiled=True),
        lax.all_gather(bias_i, ("wide", "narrow"), axis=0, tiled=True),
        lax.all_gather(decay_param, ("wide", "narrow"), axis=0, tiled=True),
    )
    wy_full, wx_full, wa_full, wi_full, wo_full, gain_one, kernel, cbias, abias, ibias, decay = (
        mixer
    )
    gain_one = gain_one.astype(jnp.float32)
    kernel = kernel.astype(jnp.float32)
    taps = kernel.shape[0]
    back = taps - 1
    position = place * rows_here + jnp.arange(rows_here, dtype=jnp.int32)

    def segment_of(where_at):
        return jnp.sum((where_at[:, None] >= offsets[None, :]).astype(jnp.int32), axis=1) - 1

    segment = segment_of(position)
    member = segment[:, None] == jnp.arange(nseqs, dtype=jnp.int32)[None, :]
    begin = jnp.sum(jnp.where(member, offsets[None, :], 0), axis=1)
    opening = (position == begin)[:, None]
    scale_one = lax.rsqrt(jnp.mean(inputs * inputs, axis=-1, keepdims=True) + EPS)
    normed = (inputs * scale_one * gain_one).astype(jnp.bfloat16)
    gate_in = mdot(normed, wy_full)
    linear = mdot(normed, wx_full).astype(jnp.bfloat16)
    rim_rows = passed_along(linear[rows_here - back :], "wide", 1)
    extended = jnp.concatenate([rim_rows, linear], 0)
    stored = mdot(member.astype(jnp.bfloat16), init_conv[0].reshape(nseqs, back * width)).reshape(
        rows_here, back, width
    )
    inputs_by_tap = [linear.astype(jnp.float32)]
    for shift_by in range(1, taps):
        earlier = extended[back - shift_by : back - shift_by + rows_here].astype(jnp.float32)
        offset = position - shift_by - begin
        from_start = jnp.zeros((rows_here, width), jnp.float32)
        for slot in range(back):
            from_start = from_start + jnp.where(
                (offset + back == slot)[:, None], stored[:, slot], 0.0
            )
        inputs_by_tap.append(jnp.where((offset >= 0)[:, None], earlier, from_start))
    conv_sum = cbias.astype(jnp.float32)
    for shift_by in range(taps):
        conv_sum = conv_sum + kernel[shift_by] * inputs_by_tap[shift_by]
    conv_low = conv_sum.astype(jnp.bfloat16)
    conv_val = conv_low.astype(jnp.float32)
    blocks = conv_low.reshape(rows_here, heads, head_w)
    wa_heads = wa_full.reshape(heads, head_w, head_w)
    wi_heads = wi_full.reshape(heads, head_w, head_w)
    rate = jnp.einsum("thi,hij->thj", blocks, wa_heads, preferred_element_type=jnp.float32).reshape(
        rows_here, width
    ) + abias.astype(jnp.float32)
    inflow = jnp.einsum(
        "thi,hij->thj", blocks, wi_heads, preferred_element_type=jnp.float32
    ).reshape(rows_here, width) + ibias.astype(jnp.float32)
    retain = jax.nn.sigmoid(rate)
    admit = jax.nn.sigmoid(inflow)
    decay_f = decay.astype(jnp.float32)
    soft_decay = jax.nn.softplus(decay_f)
    log_a = -8.0 * retain * soft_decay
    decay_now = jnp.exp(log_a)
    spread = -jnp.expm1(2.0 * log_a)
    mult = jnp.sqrt(jnp.maximum(spread, FLOOR))
    drive = mult * admit * conv_val
    state_rows = jnp.dot(member.astype(jnp.float32), init_state[0], precision=HIGH)
    a_used = jnp.where(opening, 0.0, decay_now)
    b_used = jnp.where(opening, decay_now * state_rows + drive, drive)
    carry_mul, carry_add = lax.associative_scan(link, (a_used, b_used), axis=0)
    identity = (jnp.ones((width,), jnp.float32), jnp.zeros((width,), jnp.float32))
    state_in = entering(
        (carry_mul[rows_here - 1], carry_add[rows_here - 1]), "wide", link, identity, False
    )[1]
    hidden = carry_mul * state_in + carry_add
    gelu_y, gelu_y_back = jax.vjp(jax.nn.gelu, gate_in)
    mixed_in = (hidden * gelu_y).astype(jnp.bfloat16)
    resid = inputs + mdot(mixed_in, wo_full)
    wg_full, wu_full, wd_full, gain_two = (
        lax.all_gather(w_gate, ("wide", "narrow"), axis=0, tiled=True),
        lax.all_gather(w_up, ("wide", "narrow"), axis=0, tiled=True),
        lax.all_gather(w_down, ("wide", "narrow"), axis=0, tiled=True),
        lax.all_gather(norm2_gain, ("wide", "narrow"), axis=0, tiled=True),
    )
    gain_two = gain_two.astype(jnp.float32)
    scale_two = lax.rsqrt(jnp.mean(resid * resid, axis=-1, keepdims=True) + EPS)
    normed_two = (resid * scale_two * gain_two).astype(jnp.bfloat16)
    gate = mdot(normed_two, wg_full)
    upward = mdot(normed_two, wu_full)
    active, gate_back = jax.vjp(jax.nn.gelu, gate)
    inner = (active * upward).astype(jnp.bfloat16)
    result = (resid + mdot(inner, wd_full)).astype(jnp.bfloat16)
    local_rows = jnp.arange(rows_here, dtype=jnp.int32)
    last_row = jnp.max(jnp.where(member, local_rows[:, None], -1), axis=0)
    present = last_row >= 0
    safe_row = jnp.maximum(last_row, 0)
    marker = jnp.where(present, (place * rows_here + last_row).astype(jnp.float32), -1.0)
    state_last = jnp.where(present[:, None], hidden[safe_row], 0.0)
    conv_rows = extended[safe_row[:, None] + 1 + jnp.arange(back, dtype=jnp.int32)[None, :]].astype(
        jnp.float32
    )
    conv_last = jnp.where(present[:, None, None], conv_rows, 0.0)
    merged = merged_2((marker, state_last, conv_last), "wide", later_one)
    wg_back, wu_back, wd_back = (
        lax.all_gather(w_gate, ("wide", "narrow"), axis=0, tiled=True),
        lax.all_gather(w_up, ("wide", "narrow"), axis=0, tiled=True),
        lax.all_gather(w_down, ("wide", "narrow"), axis=0, tiled=True),
    )
    grad_low = cotangent[0]
    grad_out = grad_low.astype(jnp.float32)
    d_inner = ndot(grad_low, wd_back)
    grad_wd = tdot(inner, grad_low)
    d_gate = gate_back(d_inner * upward)[0].astype(jnp.bfloat16)
    d_up = (d_inner * active).astype(jnp.bfloat16)
    grad_wg = tdot(normed_two, d_gate)
    grad_wu = tdot(normed_two, d_up)
    d_normed_two = ndot(d_gate, wg_back) + ndot(d_up, wu_back)
    d_resid_norm, grad_gain_two = norm_back(resid, scale_two, gain_two, d_normed_two)
    d_resid = grad_out + d_resid_norm
    wy_back, wx_back, wa_back, wi_back, wo_back = (
        lax.all_gather(w_y, ("wide", "narrow"), axis=0, tiled=True),
        lax.all_gather(w_x, ("wide", "narrow"), axis=0, tiled=True),
        lax.all_gather(gate_a, ("wide", "narrow"), axis=0, tiled=True),
        lax.all_gather(gate_i, ("wide", "narrow"), axis=0, tiled=True),
        lax.all_gather(w_out, ("wide", "narrow"), axis=0, tiled=True),
    )
    d_resid_low = d_resid.astype(jnp.bfloat16)
    d_mixed = ndot(d_resid_low, wo_back)
    grad_wo = tdot(mixed_in, d_resid_low)
    d_hidden = d_mixed * gelu_y
    d_gate_in = gelu_y_back(d_mixed * hidden)[0].astype(jnp.bfloat16)
    forward_mul = jnp.concatenate([a_used[1:], jnp.ones((1, width), jnp.float32)], 0)
    back_mul, back_add = lax.associative_scan(link, (forward_mul, d_hidden), reverse=True, axis=0)
    head_map = (a_used[0] * back_mul[0], a_used[0] * back_add[0])
    grad_in = entering(head_map, "wide", link, identity, True)[1]
    total_grad = back_mul * grad_in + back_add
    previous = jnp.concatenate([state_in[None], hidden[:-1]], 0)
    previous = jnp.where(opening, state_rows, previous)
    d_decay = total_grad * previous
    d_mult = total_grad * admit * conv_val
    d_admit = total_grad * mult * conv_val
    d_conv = total_grad * mult * admit
    d_spread = jnp.where(spread > FLOOR, d_mult * 0.5 / mult, 0.0)
    d_log = d_decay * decay_now - 2.0 * decay_now * decay_now * d_spread
    d_retain = d_log * (-8.0 * soft_decay)
    grad_decay = jnp.sum(d_log * (-8.0 * retain), axis=0) * jax.nn.sigmoid(decay_f)
    d_rate = (d_retain * retain * (1.0 - retain)).astype(jnp.bfloat16)
    d_inflow = (d_admit * admit * (1.0 - admit)).astype(jnp.bfloat16)
    grad_abias = jnp.sum(d_rate.astype(jnp.float32), axis=0)
    grad_ibias = jnp.sum(d_inflow.astype(jnp.float32), axis=0)
    rate_heads = d_rate.reshape(rows_here, heads, head_w)
    inflow_heads = d_inflow.reshape(rows_here, heads, head_w)
    grad_wa = jnp.einsum(
        "thi,thj->hij", blocks, rate_heads, preferred_element_type=jnp.float32
    ).reshape(width, head_w)
    grad_wi = jnp.einsum(
        "thi,thj->hij", blocks, inflow_heads, preferred_element_type=jnp.float32
    ).reshape(width, head_w)
    d_conv = d_conv + jnp.einsum(
        "thj,hij->thi",
        rate_heads,
        wa_back.reshape(heads, head_w, head_w),
        preferred_element_type=jnp.float32,
    ).reshape(rows_here, width)
    d_conv = d_conv + jnp.einsum(
        "thj,hij->thi",
        inflow_heads,
        wi_back.reshape(heads, head_w, head_w),
        preferred_element_type=jnp.float32,
    ).reshape(rows_here, width)
    d_conv_low = d_conv.astype(jnp.bfloat16)
    d_conv_val = d_conv_low.astype(jnp.float32)
    rim_back = passed_along(d_conv_low[:back], "wide", -1)
    ahead = jnp.concatenate([d_conv_low, rim_back], 0)
    d_linear = kernel[0] * d_conv_val
    kernel_grads = [jnp.sum(d_conv_val * inputs_by_tap[0], axis=0)]
    for shift_by in range(1, taps):
        later_rows = ahead[shift_by : shift_by + rows_here].astype(jnp.float32)
        same = (segment_of(position + shift_by) == segment)[:, None]
        d_linear = d_linear + kernel[shift_by] * jnp.where(same, later_rows, 0.0)
        kernel_grads.append(jnp.sum(d_conv_val * inputs_by_tap[shift_by], axis=0))
    grad_kernel = jnp.stack(kernel_grads, 0)
    grad_cbias = jnp.sum(d_conv_val, axis=0)
    d_linear_low = d_linear.astype(jnp.bfloat16)
    d_normed = ndot(d_gate_in, wy_back) + ndot(d_linear_low, wx_back)
    grad_wy = tdot(normed, d_gate_in)
    grad_wx = tdot(normed, d_linear_low)
    d_input_norm, grad_gain_one = norm_back(inputs, scale_one, gain_one, d_normed)
    input_grad = (d_resid + d_input_norm).astype(jnp.bfloat16)
    every_sum = (
        lax.psum_scatter(grad_wy, ("wide", "narrow"), scatter_dimension=0, tiled=True),
        lax.psum_scatter(grad_wx, ("wide", "narrow"), scatter_dimension=0, tiled=True),
        lax.psum_scatter(grad_wa, ("wide", "narrow"), scatter_dimension=0, tiled=True),
        lax.psum_scatter(grad_wi, ("wide", "narrow"), scatter_dimension=0, tiled=True),
        lax.psum_scatter(grad_wo, ("wide", "narrow"), scatter_dimension=0, tiled=True),
        lax.psum_scatter(grad_gain_one, ("wide", "narrow"), scatter_dimension=0, tiled=True),
        lax.psum_scatter(grad_kernel, ("wide", "narrow"), scatter_dimension=1, tiled=True),
        lax.psum_scatter(grad_cbias, ("wide", "narrow"), scatter_dimension=0, tiled=True),
        lax.psum_scatter(grad_abias, ("wide", "narrow"), scatter_dimension=0, tiled=True),
        lax.psum_scatter(grad_ibias, ("wide", "narrow"), scatter_dimension=0, tiled=True),
        lax.psum_scatter(grad_decay, ("wide", "narrow"), scatter_dimension=0, tiled=True),
        lax.psum_scatter(grad_wg, ("wide", "narrow"), scatter_dimension=0, tiled=True),
        lax.psum_scatter(grad_wu, ("wide", "narrow"), scatter_dimension=0, tiled=True),
        lax.psum_scatter(grad_wd, ("wide", "narrow"), scatter_dimension=0, tiled=True),
        lax.psum_scatter(grad_gain_two, ("wide", "narrow"), scatter_dimension=0, tiled=True),
    )
    mixer_sums = every_sum[:11]
    mlp_sums = every_sum[11:]
    return (
        result[None],
        input_grad[None],
        merged[1][None],
        merged[2].astype(jnp.bfloat16)[None],
        mixer_sums[0],
        mixer_sums[1],
        mixer_sums[2],
        mixer_sums[3],
        mixer_sums[4],
        mixer_sums[5],
        mixer_sums[6],
        mixer_sums[7],
        mixer_sums[8],
        mixer_sums[9],
        mixer_sums[10],
        mlp_sums[0],
        mlp_sums[1],
        mlp_sums[2],
        mlp_sums[3],
    )


def solution(mesh):
    placed = (
        P("narrow", "wide", None),
        P("narrow", None),
        P("narrow", None, None),
        P("narrow", None, None, None),
        P(("wide", "narrow"), None),
        P(("wide", "narrow"), None),
        P(("wide", "narrow"), None),
        P(("wide", "narrow"), None),
        P(("wide", "narrow"), None),
        P(("wide", "narrow")),
        P(None, ("wide", "narrow")),
        P(("wide", "narrow")),
        P(("wide", "narrow")),
        P(("wide", "narrow")),
        P(("wide", "narrow")),
        P(("wide", "narrow"), None),
        P(("wide", "narrow"), None),
        P(("wide", "narrow"), None),
        P(("wide", "narrow")),
        P("narrow", "wide", None),
    )
    return jax.shard_map(
        on_device,
        mesh=mesh,
        in_specs=placed,
        out_specs=(
            P("narrow", "wide", None),
            P("narrow", "wide", None),
            P("narrow", None, None),
            P("narrow", None, None, None),
            P(("wide", "narrow"), None),
            P(("wide", "narrow"), None),
            P(("wide", "narrow"), None),
            P(("wide", "narrow"), None),
            P(("wide", "narrow"), None),
            P(("wide", "narrow")),
            P(None, ("wide", "narrow")),
            P(("wide", "narrow")),
            P(("wide", "narrow")),
            P(("wide", "narrow")),
            P(("wide", "narrow")),
            P(("wide", "narrow"), None),
            P(("wide", "narrow"), None),
            P(("wide", "narrow"), None),
            P(("wide", "narrow")),
        ),
        check_vma=False,
    )
```

profile of v0, /device:TPU:0, one launch (start us, length us, event | category | flops | bytes accessed | tf_op | source)
XLA Modules:
  0.0 3562.2 jit_solution(11703602564341241118)
XLA Ops:
  12.9 42.9 %all-reduce.80 = (bf16[2048]{0:T(1024)(128)(2,1)S(1)}, bf16[2560]{0:T(1024)(128)(2,1)S(1)}, bf16[2560]{0:T(1024)(128)(2,1)S(1)}, bf16[2560]{0:T(1024)(128)(2,1)S...) all-reduce(bf16[2048]{0:T(1024)(128)(2,1)S(1)} %dynamic-update-slic, ...), channel_id=1, replica_groups=mesh['wide'=8,'narrow'=4] {'wide','narrow'}, use_global_device_ids=true, to_apply=%add.67 | all-reduce | flops 14336 | bytes 57344
  55.8 41.1 %all-gather.1 = bf16[32,80,4]{1,2,0:T(4,128)(2,1)S(1)} all-gather(bf16[1,80,4]{1,2,0:T(4,128)(2,1)S(1)} %bitcast.239), channel_id=1, replica_groups=mesh['wide'=8,'narrow'=4] {'wide','narrow'}, dimensions={0}, use_global_device_ids=true | all-gather | bytes 21120 | tf_op jit(solution)/shard_map/all_gather | solution.py:125
  98.4 45.5 %all_gather.87 = bf16[2560,160]{1,0:T(8,128)(2,1)} all-gather(bf16[80,160]{1,0:T(8,128)(2,1)S(1)} %copy-done.111), channel_id=1, replica_groups=mesh['wide'=8,'narrow'=4] {'wide','narrow'}, dimensions={0}, use_global_device_ids=true | all-gather | bytes 844800 | tf_op jit(solution)/shard_map/all_gather | solution.py:122
  143.9 49.3 %all_gather.83 = bf16[2560,160]{1,0:T(8,128)(2,1)} all-gather(bf16[80,160]{1,0:T(8,128)(2,1)S(1)} %copy-done.112), channel_id=1, replica_groups=mesh['wide'=8,'narrow'=4] {'wide','narrow'}, dimensions={0}, use_global_device_ids=true | all-gather | bytes 844800 | tf_op jit(solution)/shard_map/all_gather | solution.py:121
  432.6 30.7 all-gather.3
  479.9 31.4 all-gather.2
  559.9 15.3 fusion.149
  575.1 27.8 all-gather.21.cloned.1.call-done
  603.0 14.2 fusion.150
  617.2 141.4 %all-gather.23.cloned.1.call-done = bf16[6144,2048]{1,0:T(8,128)(2,1)} async-done(((bf16[192,2048]{1,0:T(8,128)(2,1)}), bf16[6144,2048]{1,0:T(8,128)(2,1)}) %all-gather.23.cloned.1.call-update) | async-done | bytes 25165840 | tf_op jit(solution)/shard_map/all_gather | solution.py:204
  758.6 21.9 multiply_convert_fusion
  780.4 13.5 fusion.151
  793.9 15.1 multiply_reduce_fusion.1
  1004.8 30.5 all-gather.5
  1035.4 30.5 all-gather.4
  1066.9 13.2 rev.8
  1080.0 21.1 rev.9
  1189.1 21.4 fusion.155
  1210.7 21.4 fusion.156
  1233.4 21.4 fusion.66
  1256.9 17.7 all-reduce.72
  1281.1 31.4 all_gather.100
  1312.7 30.8 all_gather.99
  1352.3 13.0 fusion.44
  1375.0 38.1 %all-reduce.79 = (f32[2048]{0:T(1024)S(1)}, f32[2560]{0:T(1024)S(1)}, f32[2560]{0:T(1024)S(1)}, f32[2560]{0:T(1024)S(1)}, f32[2560]{0:T(1024)S(1)}, /*index=5*/f32[2048]{0:T(1024)S(1)}) all-reduce(f32[2048]{0:T(1024)S(1)} %get-tuple-element.478, ...), channel_id=8, replica_groups=mesh['wide'=8,'narrow'=4] {'wide','narrow'}, use_global_device_ids=true, to_apply=%region_22.23.clone | all-reduce | flops 14336 | bytes 114688
  1421.5 129.3 %reduce-scatter.18.cloned.1.call-done = f32[80,160]{1,0:T(8,128)} async-done(((f32[2560,160]{1,0:T(8,128)}), f32[80,160]{1,0:T(8,128)}) %reduce-scatter.18.cloned.1.call-update) | async-done | bytes 51216 | tf_op jit(solution)/shard_map/reduce_scatter | solution.py:316
  1550.8 223.8 %reduce-scatter.20.cloned.1.call-done = f32[80,2048]{1,0:T(8,128)} async-done(((f32[2560,2048]{1,0:T(8,128)}), f32[80,2048]{1,0:T(8,128)}) %reduce-scatter.20.cloned.1.call-update) | async-done | bytes 655376 | tf_op jit(solution)/shard_map/reduce_scatter | solution.py:317
  1774.6 230.7 %reduce-scatter.12.cloned.1.call-done = f32[64,2560]{1,0:T(8,128)} async-done(((f32[2048,2560]{1,0:T(8,128)}), f32[64,2560]{1,0:T(8,128)}) %reduce-scatter.12.cloned.1.call-update) | async-done | bytes 655376 | tf_op jit(solution)/shard_map/reduce_scatter | solution.py:313
  2005.3 230.7 %reduce-scatter.14.cloned.1.call-done = f32[64,2560]{1,0:T(8,128)} async-done(((f32[2048,2560]{1,0:T(8,128)}), f32[64,2560]{1,0:T(8,128)}) %reduce-scatter.14.cloned.1.call-update) | async-done | bytes 655376 | tf_op jit(solution)/shard_map/reduce_scatter | solution.py:314
  2236.0 442.2 %reduce-scatter.22.cloned.1.call-done = f32[64,6144]{1,0:T(8,128)} async-done(((f32[2048,6144]{1,0:T(8,128)}), f32[64,6144]{1,0:T(8,128)}) %reduce-scatter.22.cloned.1.call-update) | async-done | bytes 1572880 | tf_op jit(solution)/shard_map/reduce_scatter | solution.py:324
  2678.2 438.5 %reduce-scatter.24.cloned.1.call-done = f32[64,6144]{1,0:T(8,128)} async-done(((f32[2048,6144]{1,0:T(8,128)}), f32[64,6144]{1,0:T(8,128)}) %reduce-scatter.24.cloned.1.call-update) | async-done | bytes 1572880 | tf_op jit(solution)/shard_map/reduce_scatter | solution.py:325
  3116.7 438.5 %reduce-scatter.26.cloned.1.call-done = f32[192,2048]{1,0:T(8,128)} async-done(((f32[6144,2048]{1,0:T(8,128)}), f32[192,2048]{1,0:T(8,128)}) %reduce-scatter.26.cloned.1.call-update) | async-done | bytes 1572880 | tf_op jit(solution)/shard_map/reduce_scatter | solution.py:326
  (759 shorter events, 633.5 us)
Async XLA Ops:
  7.2 186.0 %copy-start = (bf16[1,4,3,2560]{3,1,2,0:T(4,128)(2,1)S(1)}, bf16[1,4,3,2560]{3,1,2,0:T(4,128)(2,1)}, u32[]{:S(2)}) copy-start(bf16[1,4,3,2560]{3,1,2,0:T(4,128)(2,1)} %param.29) | copy-start | bytes 184324
  7.3 89.9 %copy-start.130 = (s32[1,4]{1,0:T(1,128)S(1)}, s32[1,4]{1,0:T(1,128)}, u32[]{:S(2)}) copy-start(s32[1,4]{1,0:T(1,128)} %param.27) | copy-start | bytes 52
  7.3 90.7 %copy-start.2 = (bf16[1,256,2048]{2,1,0:T(8,128)(2,1)S(1)}, bf16[1,256,2048]{2,1,0:T(8,128)(2,1)}, u32[]{:S(2)}) copy-start(bf16[1,256,2048]{2,1,0:T(8,128)(2,1)} %param.26) | copy-start | bytes 3145732
  7.3 91.0 %copy-start.111 = (bf16[80,160]{1,0:T(8,128)(2,1)S(1)}, bf16[80,160]{1,0:T(8,128)(2,1)}, u32[]{:S(2)}) copy-start(bf16[80,160]{1,0:T(8,128)(2,1)} %param.33) | copy-start | bytes 76804
  7.3 190.2 %all-gather.13.cloned.1.call-start = ((), (), s32[]{:S(2)}) async-start(), calls=%async_computation.9 | async-start | bytes 10813440 | tf_op jit(solution)/shard_map/all_gather | solution.py:120
  8.0 532.9 %all-gather.15.cloned.1.call-start = ((), (), s32[]{:S(2)}) async-start(), calls=%async_computation.10 | async-start | bytes 10813440 | tf_op jit(solution)/shard_map/all_gather | solution.py:119
  8.8 544.6 %all-gather.17.cloned.1.call-start = ((), (), s32[]{:S(2)}) async-start(), calls=%async_computation.11 | async-start | bytes 10813440 | tf_op jit(solution)/shard_map/all_gather | solution.py:123
  9.5 134.3 %copy-start.112 = (bf16[80,160]{1,0:T(8,128)(2,1)S(1)}, bf16[80,160]{1,0:T(8,128)(2,1)}, u32[]{:S(2)}) copy-start(bf16[80,160]{1,0:T(8,128)(2,1)} %param.32) | copy-start | bytes 76804
  9.5 550.3 %all-gather.19.cloned.1.call-start = ((), (), s32[]{:S(2)}) async-start(), calls=%async_computation.12 | async-start | bytes 25952256 | tf_op jit(solution)/shard_map/all_gather | solution.py:202
  10.1 592.8 %all-gather.21.cloned.1.call-start = ((), (), s32[]{:S(2)}) async-start(), calls=%async_computation.13 | async-start | bytes 25952256 | tf_op jit(solution)/shard_map/all_gather | solution.py:203
  10.7 747.9 %all-gather.23.cloned.1.call-start = ((), (), s32[]{:S(2)}) async-start(), calls=%async_computation.14 | async-start | bytes 25952256 | tf_op jit(solution)/shard_map/all_gather | solution.py:204
  11.3 1408.7 %reduce-scatter.28.cloned.1.call-start = ((), (), s32[]{:S(2)}) async-start(), calls=%async_computation.23 | async-start | bytes 1351680
  55.8 141.7 %copy-start.120 = (bf16[2560]{0:T(1024)(128)(2,1)}, bf16[2560]{0:T(1024)(128)(2,1)S(1)}, u32[]{:S(2)}) copy-start(bf16[2560]{0:T(1024)(128)(2,1)S(1)} %get-tuple-element.536) | copy-start | bytes 15364
  55.8 485.1 %copy-start.52 = (f32[2048]{0:T(1024)}, f32[2048]{0:T(1024)S(1)}, u32[]{:S(2)}) copy-start(f32[2048]{0:T(1024)S(1)} %convert_element_type.247) | copy-start | bytes 24580
  97.2 100.2 %copy-start.122 = (s32[256]{0:T(256)}, s32[256]{0:T(256)S(1)}, u32[]{:S(2)}) copy-start(s32[256]{0:T(256)S(1)} %convert_reduce_fusion.6) | copy-start | bytes 3076
  98.3 442.7 %copy-start.65 = (f32[256]{0:T(256)}, f32[256]{0:T(256)S(1)}, u32[]{:S(2)}) copy-start(f32[256]{0:T(256)S(1)} %add_rsqrt_fusion.1) | copy-start | bytes 3076
  98.3 134.7 %copy-start.128 = (pred[256]{0:T(512)(128)(4,1)}, pred[256]{0:T(512)(128)(4,1)S(1)}, u32[]{:S(2)}) copy-start(pred[256]{0:T(512)(128)(4,1)S(1)} %get-tuple-element.641) | copy-start | bytes 772
  98.4 134.6 %copy-start.77 = (f32[2560]{0:T(1024)}, f32[2560]{0:T(1024)S(1)}, u32[]{:S(2)}) copy-start(f32[2560]{0:T(1024)S(1)} %fusion.101) | copy-start | bytes 30724
  204.6 2.8 collective-permute-start
  559.5 249.5 %copy-start.26 = (f32[256,2048]{1,0:T(8,128)}, f32[256,2048]{1,0:T(8,128)S(1)}, u32[]{:S(2)}) copy-start(f32[256,2048]{1,0:T(8,128)S(1)} %get-tuple-element.659) | copy-start | bytes 6291460
  1143.3 278.1 %reduce-scatter.16.cloned.1.call-start = ((), (), s32[]{:S(2)}) async-start(), calls=%async_computation.17 | async-start | bytes 2703360 | tf_op jit(solution)/shard_map/reduce_scatter | solution.py:315
  1145.9 404.8 %reduce-scatter.18.cloned.1.call-start = ((), (), s32[]{:S(2)}) async-start(), calls=%async_computation.18 | async-start | bytes 2703360 | tf_op jit(solution)/shard_map/reduce_scatter | solution.py:316
  1149.3 625.3 %reduce-scatter.20.cloned.1.call-start = ((), (), s32[]{:S(2)}) async-start(), calls=%async_computation.19 | async-start | bytes 21626880 | tf_op jit(solution)/shard_map/reduce_scatter | solution.py:317
  1160.9 844.5 %reduce-scatter.12.cloned.1.call-start = ((), (), s32[]{:S(2)}) async-start(), calls=%async_computation.15 | async-start | bytes 21626880 | tf_op jit(solution)/shard_map/reduce_scatter | solution.py:313
  1171.4 1064.6 %reduce-scatter.14.cloned.1.call-start = ((), (), s32[]{:S(2)}) async-start(), calls=%async_computation.16 | async-start | bytes 21626880 | tf_op jit(solution)/shard_map/reduce_scatter | solution.py:314
  1172.7 5.7 collective-permute-start.1
  1187.9 1490.3 %reduce-scatter.22.cloned.1.call-start = ((), (), s32[]{:S(2)}) async-start(), calls=%async_computation.20 | async-start | bytes 51904512 | tf_op jit(solution)/shard_map/reduce_scatter | solution.py:324
  1210.5 1906.2 %reduce-scatter.24.cloned.1.call-start = ((), (), s32[]{:S(2)}) async-start(), calls=%async_computation.21 | async-start | bytes 51904512 | tf_op jit(solution)/shard_map/reduce_scatter | solution.py:325
  1232.2 2323.0 %reduce-scatter.26.cloned.1.call-start = ((), (), s32[]{:S(2)}) async-start(), calls=%async_computation.22 | async-start | bytes 51904512 | tf_op jit(solution)/shard_map/reduce_scatter | solution.py:326
  1278.7 67.7 %copy-start.121 = (bf16[2560]{0:T(1024)(128)(2,1)S(1)}, bf16[2560]{0:T(1024)(128)(2,1)}, u32[]{:S(2)}) copy-start(bf16[2560]{0:T(1024)(128)(2,1)} %copy-done.120) | copy-start | bytes 15364
  1278.7 67.7 %copy-start.47 = (bf16[256,2560]{1,0:T(8,128)(2,1)S(1)}, bf16[256,2560]{1,0:T(8,128)(2,1)}, u32[]{:S(2)}) copy-start(bf16[256,2560]{1,0:T(8,128)(2,1)} %get-tuple-element.565) | copy-start | bytes 3932164
  1416.7 2138.5 %copy-start.1 = (bf16[1,4,3,2560]{3,1,2,0:T(4,128)(2,1)S(1)}, bf16[1,4,3,2560]{3,1,2,0:T(4,128)(2,1)}, u32[]{:S(2)}) copy-start(bf16[1,4,3,2560]{3,1,2,0:T(4,128)(2,1)} %param.29) | copy-start | bytes 184324
  (126 other events, 1271.2 us)
Sparse Core Ops, SparseCore 0:
  11.0 91.0 all-gather.12
  105.0 94.2 all-gather.14
  202.2 87.6 all-gather.16
  292.7 153.4 all-gather.18
  448.9 154.0 all-gather.20
  605.7 152.8 all-gather.22
  1143.5 133.6 reduce-scatter.27
  1280.1 134.0 reduce-scatter.15
  1417.1 133.6 reduce-scatter.17
  1553.6 220.9 reduce-scatter.19
  1777.6 227.7 reduce-scatter.11
  2008.2 227.7 reduce-scatter.13
  2244.1 434.0 reduce-scatter.21
  2686.2 430.4 reduce-scatter.23
  3124.6 430.4 reduce-scatter.25
where the time goes:
time: 3580 us; the launch traced here: 3560 us
  waiting for transfers between devices  2310 us (65%)
  local copies, waits for them, and re-layouts  427 us (12%)
  blocking collectives  420 us (12%)
  matrix products  268 us (7%)
  other arithmetic  113 us (3%)
    reduce_scatter x1, waiting for transfers between devices, on_device(): lax.psum_scatter(grad_wg, ('wide', 'narrow'), scatter_dimension=0, tiled=...  442 us
    reduce_scatter x1, waiting for transfers between devices, on_device(): lax.psum_scatter(grad_wd, ('wide', 'narrow'), scatter_dimension=0, tiled=...  439 us
    reduce_scatter x1, waiting for transfers between devices, on_device(): lax.psum_scatter(grad_wu, ('wide', 'narrow'), scatter_dimension=0, tiled=...  438 us
    reduce_scatter x1, waiting for transfers between devices, on_device(): lax.psum_scatter(grad_wy, ('wide', 'narrow'), scatter_dimension=0, tiled=...  231 us
    reduce_scatter x1, waiting for transfers between devices, on_device(): lax.psum_scatter(grad_wx, ('wide', 'narrow'), scatter_dimension=0, tiled=...  231 us
    reduce_scatter x1, waiting for transfers between devices, on_device(): lax.psum_scatter(grad_wo, ('wide', 'narrow'), scatter_dimension=0, tiled=...  224 us
    slice x57, local copies, waits for them, and re-layouts, on_device(): lax.associative_scan(link, (forward_mul, d_hidden), reverse=True, axis=0)  145 us
    all_gather x1, waiting for transfers between devices, on_device(): lax.all_gather(w_down, ('wide', 'narrow'), axis=0, tiled=True)  141 us
  transfers between devices with their start and end apart: 17, of which 11 were waited for; matrix products, arithmetic and copies ran while one was open for 13% of the time, Pallas kernels for 0%

commit v1 on v0

--- a/solution.py
+++ b/solution.py
@@ -1,10 +1,543 @@
+import functools
+
 import jax
 import jax.numpy as jnp
 from jax import lax
+from jax.experimental import pallas as pl
+from jax.experimental.pallas import tpu as pltpu
+from jax.sharding import Mesh
 from jax.sharding import PartitionSpec as P
 
 EPS = 1e-06
 FLOOR = 0.001
+BF = jnp.bfloat16
+F32 = jnp.float32
+
+
+def tdot(left, right):
+    return lax.dot_general(left, right, (((0,), (0,)), ((), ())), preferred_element_type=F32)
+
+
+def ndot(left, right):
+    return lax.dot_general(left, right, (((1,), (1,)), ((), ())), preferred_element_type=F32)
+
+
+def mdot(left, right):
+    return jnp.dot(left, right, preferred_element_type=F32)
+
+
+def pick(stacked, index, axis=0):
+    return lax.dynamic_index_in_dim(stacked, index, axis, keepdims=False)
+
+
+def swap_c(value):
+    return lax.ppermute(value, "c", [(0, 1), (1, 0)])
+
+
+def xor_u(value, k):
+    size = lax.axis_size("b") * lax.axis_size("n")
+    return lax.ppermute(value, ("b", "n"), [(i, i ^ k) for i in range(size)])
+
+
+def xor_stream(value, k):
+    size = lax.axis_size("n") * lax.axis_size("c")
+    return lax.ppermute(value, ("n", "c"), [(i, i ^ k) for i in range(size)])
+
+
+def shift_a(value, by):
+    size = lax.axis_size("a")
+    return lax.ppermute(value, "a", [(i, i + by) for i in range(size) if 0 <= i + by < size])
+
+
+def cycle_a(value, by):
+    size = lax.axis_size("a")
+    return lax.ppermute(value, "a", [(i, (i + by) % size) for i in range(size)])
+
+
+def chips():
+    return lax.axis_size("b") * lax.axis_size("n")
+
+
+def chip():
+    return lax.axis_index("b") * lax.axis_size("n") + lax.axis_index("n")
+
+
+def plane_gather(value):
+    mine = jnp.stack([value] + [xor_u(value, k) for k in range(1, chips())])
+    return jnp.concatenate([mine, swap_c(mine)])
+
+
+def plane_scatter(parts):
+    count = chips()
+    parts = parts.reshape((2, count, -1) + parts.shape[1:])
+    got = swap_c(parts[1].astype(BF))
+    summed = parts[0].astype(F32) + got.astype(F32)
+    low = summed.astype(BF)
+    total = summed[0]
+    for k in range(1, count):
+        total = total + xor_u(low[k], k).astype(F32)
+    return total
+
+
+def exchange(pieces):
+    c, u = lax.axis_index("c"), chip()
+    both = jnp.stack([pick(pieces, c), swap_c(pick(pieces, 1 - c))])
+    out = []
+    for k in range(chips()):
+        piece = pick(both, u ^ k, 1)
+        out.append(piece if k == 0 else xor_u(piece, k))
+    return jnp.stack(out, 1)
+
+
+def by_owner(rel):
+    c, u = lax.axis_index("c"), chip()
+    rel = jnp.stack([pick(rel, c), pick(rel, 1 - c)])
+    return jnp.stack([pick(rel, u ^ q, 1) for q in range(chips())], 1)
+
+
+def scan_kernel(reverse, a_ref, b_ref, p_ref, s_ref):
+    blocks, rows, width = a_ref.shape
+    groups = rows // 8
+    row = lax.broadcasted_iota(jnp.int32, (blocks, 8, width), 1)
+    if reverse:
+        row = 7 - row
+
+    def step(i, carry):
+        cp, cs = carry
+        g = groups - 1 - i if reverse else i
+        at = pl.ds(pl.multiple_of(g * 8, 8), 8)
+        a, b = a_ref[:, at, :], b_ref[:, at, :]
+        for d in (1, 2, 4):
+            by = 8 - d if reverse else d
+            inside = row >= d
+            a_far = jnp.where(inside, pltpu.roll(a, by, 1), 1.0)
+            b_far = jnp.where(inside, pltpu.roll(b, by, 1), 0.0)
+            b = a * b_far + b
+            a = a * a_far
+        b = a * cs + b
+        a = a * cp
+        p_ref[:, at, :] = a
+        s_ref[:, at, :] = b
+        last = 0 if reverse else 7
+        return a[:, last : last + 1], b[:, last : last + 1]
+
+    start = (jnp.ones((blocks, 1, width), F32), jnp.zeros((blocks, 1, width), F32))
+    lax.fori_loop(0, groups, step, start)
+
+
+def scan(a, b, reverse):
+    blocks, rows, width = a.shape
+    per = 4
+    spec = pl.BlockSpec((per, rows, width), lambda i: (i, 0, 0))
+    return pl.pallas_call(
+        functools.partial(scan_kernel, reverse),
+        grid=(blocks // per,),
+        in_specs=[spec, spec],
+        out_specs=[spec, spec],
+        out_shape=[jax.ShapeDtypeStruct(a.shape, F32)] * 2,
+        compiler_params=pltpu.CompilerParams(vmem_limit_bytes=48 * 1024 * 1024),
+        name="scan",
+    )(a, b)
+
+
+def on_device(
+    tokens,
+    starts,
+    init_state,
+    init_conv,
+    w_y,
+    w_x,
+    gate_a,
+    gate_i,
+    w_out,
+    norm1_gain,
+    conv_kernel,
+    conv_bias,
+    bias_a,
+    bias_i,
+    decay_param,
+    w_gate,
+    w_up,
+    w_down,
+    norm2_gain,
+    cotangent,
+):
+    planes, count = lax.axis_size("a"), chips()
+    a, b, n, c = (lax.axis_index(name) for name in ("a", "b", "n", "c"))
+    u = chip()
+    nn = count // 2
+    rows, d_model = tokens.shape[1], tokens.shape[2]
+    nseq = starts.shape[1]
+    width = w_y.shape[1]
+    head_w = gate_a.shape[1]
+    half = gate_a.shape[0]
+    taps = conv_kernel.shape[0]
+    back = taps - 1
+    heads_here = planes // 2
+    wide_here = heads_here * head_w
+    hid = w_down.shape[0]
+    drows = w_y.shape[0]
+    nblocks = 2 * count
+
+    def head_pieces(w):
+        w = w.reshape(w.shape[0], 2, heads_here, count, head_w)
+        return w.transpose(1, 3, 0, 2, 4).reshape(2, count, w.shape[0], wide_here)
+
+    def from_head_pieces(pieces):
+        r = pieces.shape[2]
+        pieces = pieces.reshape(2, count, r, heads_here, head_w)
+        return pieces.transpose(2, 0, 3, 1, 4).reshape(r, width)
+
+    def hidden_pieces(w):
+        w = w.reshape(w.shape[0], planes, count, 2, hid)
+        return w.transpose(3, 2, 0, 1, 4).reshape(2, count, w.shape[0], planes * hid)
+
+    def from_hidden_pieces(pieces):
+        r = pieces.shape[2]
+        pieces = pieces.reshape(2, count, r, planes, hid)
+        return pieces.transpose(2, 3, 1, 0, 4).reshape(r, planes * count * 2 * hid)
+
+    def row_blocks(owned):
+        return owned.swapaxes(0, 1).reshape((-1,) + owned.shape[3:])
+
+    def to_owner_rows(full):
+        return full.reshape((count, 2, -1) + full.shape[1:]).swapaxes(0, 1)
+
+    def gather_a(value):
+        return lax.all_gather(value, "a", axis=0, tiled=True)
+
+    def scatter_a(value):
+        return lax.psum_scatter(value, "a", scatter_dimension=0, tiled=True)
+
+    packed = jnp.concatenate([head_pieces(w_y), head_pieces(w_x)], -1)
+    w_yx = gather_a(row_blocks(by_owner(exchange(packed))))
+
+    def join_halves(mine_all):
+        away = swap_c(lax.dynamic_slice_in_dim(mine_all, (1 - c) * heads_here, heads_here, 0))
+        own = lax.dynamic_slice_in_dim(mine_all, c * heads_here, heads_here, 0)
+        first = jnp.where(c == 0, own, away)
+        second = jnp.where(c == 0, away, own)
+        return jnp.stack([first, second], 1).reshape((wide_here,) + mine_all.shape[2:])
+
+    def part_halves(full):
+        full = full.reshape((heads_here, 2, half) + full.shape[1:])
+        own, away = pick(full, c, 1), swap_c(pick(full, 1 - c, 1))
+        first = jnp.where(c == 0, own, away)
+        second = jnp.where(c == 0, away, own)
+        return jnp.concatenate([first, second], 0).reshape((planes * half,) + full.shape[3:])
+
+    mixer_rows = jnp.concatenate([w_out, gate_a, gate_i], 1)
+    mixer_rows = join_halves(gather_a(mixer_rows).reshape(planes, half, -1))
+    w_o = mixer_rows[:, :d_model]
+
+    def block_diagonal(m):
+        m = m.reshape(heads_here, head_w, head_w)
+        eye = jnp.eye(heads_here, dtype=m.dtype)
+        return (m[:, :, None, :] * eye[:, None, :, None]).reshape(wide_here, wide_here)
+
+    w_gates = jnp.concatenate(
+        [
+            block_diagonal(mixer_rows[:, d_model : d_model + head_w]),
+            block_diagonal(mixer_rows[:, d_model + head_w :]),
+        ],
+        1,
+    )
+
+    packed = jnp.concatenate([hidden_pieces(w_gate), hidden_pieces(w_up)], -1)
+    w_gu = gather_a(row_blocks(by_owner(exchange(packed))))
+    w_d = gather_a(w_down)
+    f_here = planes * hid
+
+    vectors = jnp.concatenate(
+        [conv_kernel, conv_bias[None], bias_a[None], bias_i[None], decay_param[None]], 0
+    ).reshape(-1)
+    small = jnp.concatenate([vectors, norm1_gain, norm2_gain])
+    small = jnp.stack([small] + [xor_u(small, k) for k in range(1, count)])
+    small = jnp.stack([small, swap_c(small)])
+    small = jnp.stack([small] + [cycle_a(small, d) for d in range(1, planes)])
+    small = small.reshape(planes * nblocks, -1)
+    rel = jnp.arange(planes * nblocks, dtype=jnp.int32)
+    r_a, r_c, r_u = rel // nblocks, (rel // count) % 2, rel % count
+    owner = ((a - r_a + planes) % planes) * nblocks + (u ^ r_u) * 2 + (c ^ r_c)
+    order = (rel[:, None] == owner[None, :]).astype(BF)
+    canon = mdot(order, small)
+    nvec = (taps + 4) * half
+    gain_one = canon[:, nvec : nvec + drows].reshape(-1)
+    gain_two = canon[:, nvec + drows :].reshape(-1)
+    mine = pick(canon[:, :nvec].reshape(2, heads_here, count, 2, taps + 4, half), c)
+    mine = pick(mine, u, 1).transpose(2, 0, 1, 3).reshape(taps + 4, wide_here)
+    kernel, cbias, abias, ibias, decay_f = (
+        mine[:taps], mine[taps], mine[taps + 1], mine[taps + 2], mine[taps + 3]
+    )
+    gate_bias = jnp.concatenate([abias, ibias])
+
+    def my_channels(v):
+        lead = v.shape[:-1]
+        v = v.reshape(lead + (2, heads_here, count, head_w))
+        v = pick(v, c, len(lead))
+        return pick(v, u, len(lead) + 1).reshape(lead + (wide_here,))
+
+    streams = 2 * nn
+    at_start = jnp.concatenate([init_state[0][:, None], init_conv[0].astype(F32)], 1)
+    at_start = jnp.concatenate([at_start.reshape(-1), starts[0].astype(F32)])
+    rel_streams = [at_start] + [xor_stream(at_start, k) for k in range(1, streams)]
+    at_start = jnp.stack([rel_streams[kn * 2 + kc] for kc in range(2) for kn in range(nn)])
+    offsets = at_start[:, -nseq:].astype(jnp.int32)
+    at_start = my_channels(at_start[:, :-nseq].reshape(streams, nseq, taps, width))
+    state_0 = at_start[:, :, 0]
+    conv_0 = at_start[:, :, 1:].reshape(streams, nseq * back, wide_here).astype(BF)
+
+    def per_block(v):
+        v = v.reshape((2, 1, nn) + v.shape[1:])
+        return jnp.broadcast_to(v, (2, 2, nn) + v.shape[3:]).reshape((nblocks,) + v.shape[3:])
+
+    block_b = (jnp.arange(nblocks, dtype=jnp.int32) // nn) % 2
+    first_row = (a * 2 + (b ^ block_b)) * rows
+    position = first_row[:, None] + jnp.arange(rows, dtype=jnp.int32)[None]
+    off_b = per_block(offsets)
+
+    def segment_of(where_at):
+        return jnp.sum((where_at[:, :, None] >= off_b[:, None, :]).astype(jnp.int32), 2) - 1
+
+    segment = segment_of(position)
+    member = segment[:, :, None] == jnp.arange(nseq, dtype=jnp.int32)
+    begin = jnp.sum(jnp.where(member, off_b[:, None, :], 0), 2)
+    opening = position == begin
+
+    def norm(value, gain):
+        factor = lax.rsqrt(jnp.mean(value * value, axis=-1, keepdims=True) + EPS)
+        return factor, (value * factor * gain).astype(BF)
+
+    inputs = tokens[0].astype(F32)
+    normed = norm(plane_gather(tokens[0]).reshape(nblocks * rows, d_model).astype(F32), gain_one)[1]
+    prod = mdot(normed, w_yx)
+    gate_in = prod[:, :wide_here].reshape(nblocks, rows, wide_here)
+    linear = prod[:, wide_here:].astype(BF).reshape(nblocks, rows, wide_here)
+
+    def two(v):
+        return v.reshape((2, 2, nn) + v.shape[1:])
+
+    def flip(v):
+        v = two(v)
+        return jnp.stack([v[:, 1], v[:, 0]], 1).reshape((nblocks,) + v.shape[3:])
+
+    def of_stream(v, which):
+        v = two(v)
+        return jnp.where(b == which, v[:, 0], v[:, 1]).reshape((streams,) + v.shape[3:])
+
+    def second_half(shape):
+        return ((b ^ block_b) == 1).reshape((nblocks,) + (1,) * (len(shape) - 1))
+
+    tail = linear[:, rows - back :]
+    rim = per_block(shift_a(of_stream(tail, 1), 1))
+    rim = jnp.where(second_half(rim.shape), flip(tail), rim)
+    extended = jnp.concatenate([rim, linear], 1)
+    conv_0b = per_block(conv_0)
+    slots = jnp.arange(back, dtype=jnp.int32)
+    by_tap = [linear.astype(F32)]
+    for k in range(1, taps):
+        offset = position - k - begin
+        hot = member[:, :, :, None] & ((offset + back)[:, :, None, None] == slots)
+        hot = hot.reshape(nblocks, rows, nseq * back).astype(BF)
+        stored = lax.dot_general(
+            hot, conv_0b, (((2,), (1,)), ((0,), (0,))), preferred_element_type=F32
+        )
+        earlier = extended[:, back - k : back - k + rows].astype(F32)
+        by_tap.append(jnp.where((offset >= 0)[:, :, None], earlier, stored))
+    conv_sum = cbias
+    for k in range(taps):
+        conv_sum = conv_sum + kernel[k] * by_tap[k]
+    conv_low = conv_sum.astype(BF)
+    conv_val = conv_low.astype(F32)
+    conv_flat = conv_low.reshape(-1, wide_here)
+    gates = jax.nn.sigmoid(mdot(conv_flat, w_gates) + gate_bias)
+    retain = gates[:, :wide_here].reshape(nblocks, rows, wide_here)
+    admit = gates[:, wide_here:].reshape(nblocks, rows, wide_here)
+    soft_decay = jax.nn.softplus(decay_f)
+    log_a = -8.0 * retain * soft_decay
+    decay_now = jnp.exp(log_a)
+    spread = -jnp.expm1(2.0 * log_a)
+    mult = jnp.sqrt(jnp.maximum(spread, FLOOR))
+    drive = mult * admit * conv_val
+    state_0b = per_block(state_0)
+    state_rows = jnp.zeros_like(drive)
+    for s in range(nseq):
+        state_rows = jnp.where(member[:, :, s, None], state_0b[:, s, None], state_rows)
+    open_3 = opening[:, :, None]
+    a_used = jnp.where(open_3, 0.0, decay_now)
+    b_used = jnp.where(open_3, decay_now * state_rows + drive, drive)
+    carry_mul, carry_add = scan(a_used, b_used, False)
+
+    def entering(mul, add, reverse):
+        pair = jnp.stack([mul, add])
+        near = of_stream(pair.swapaxes(0, 1), 1 if reverse else 0)
+        far = of_stream(pair.swapaxes(0, 1), 0 if reverse else 1)
+        whole = jnp.stack([near[:, 0] * far[:, 0], far[:, 0] * near[:, 1] + far[:, 1]])
+        came = [shift_a(whole, -d if reverse else d) for d in range(1, planes)]
+        value = came[-1][1]
+        for part in came[-2::-1]:
+            value = part[0] * value + part[1]
+        to_far = near[:, 0] * value + near[:, 1]
+        value, to_far = per_block(value), per_block(to_far)
+        is_far = second_half(value.shape)
+        return jnp.where(is_far != reverse, to_far, value)
+
+    state_in = entering(carry_mul[:, -1], carry_add[:, -1], False)[:, None]
+    hidden = carry_mul * state_in + carry_add
+    gelu_y, gelu_y_back = jax.vjp(jax.nn.gelu, gate_in)
+    mixed_in = (hidden * gelu_y).astype(BF).reshape(-1, wide_here)
+    resid = inputs + plane_scatter(mdot(mixed_in, w_o))
+    scale_two, normed_two = norm(resid, gain_two)
+    normed_two = plane_gather(normed_two).reshape(nblocks * rows, d_model)
+    grad_low = cotangent[0]
+    grads = plane_gather(grad_low).reshape(nblocks * rows, d_model)
+
+    pair = mdot(normed_two, w_gu)
+    gate, upward = pair[:, :f_here], pair[:, f_here:]
+    active, gate_back = jax.vjp(jax.nn.gelu, gate)
+    inner = (active * upward).astype(BF)
+    result = (resid + plane_scatter(mdot(inner, w_d))).astype(BF)
+    d_inner = ndot(grads, w_d)
+    grad_wd = scatter_a(tdot(inner, grads).astype(BF)).astype(F32)
+    d_gate = gate_back(d_inner * upward)[0].astype(BF)
+    d_up = (d_inner * active).astype(BF)
+    d_pair = jnp.concatenate([d_gate, d_up], 1)
+    d_normed_two = plane_scatter(ndot(d_pair, w_gu))
+    sums = scatter_a(tdot(normed_two, d_pair).astype(BF))
+    sums = by_owner(exchange(to_owner_rows(sums)))
+    grad_wg = from_hidden_pieces(sums[..., :f_here]).astype(F32)
+    grad_wu = from_hidden_pieces(sums[..., f_here:]).astype(F32)
+
+    def norm_back(value, factor, gain, grad):
+        weighted = grad * gain
+        inner = jnp.mean(weighted * value, axis=-1, keepdims=True)
+        return factor * weighted - value * factor * factor * factor * inner
+
+    d_resid = grad_low.astype(F32) + norm_back(resid, scale_two, gain_two, d_normed_two)
+    d_resid_low = plane_gather(d_resid.astype(BF)).reshape(nblocks * rows, d_model)
+
+    d_mixed = ndot(d_resid_low, w_o).reshape(nblocks, rows, wide_here)
+    sums_o = tdot(mixed_in, d_resid_low).astype(BF)
+    grad_wo = scatter_a(part_halves(sums_o)).astype(F32)
+    d_hidden = d_mixed * gelu_y
+    d_gate_in = gelu_y_back(d_mixed * hidden)[0].astype(BF).reshape(-1, wide_here)
+    forward_mul = jnp.concatenate([a_used[:, 1:], jnp.ones((nblocks, 1, wide_here), F32)], 1)
+    back_mul, back_add = scan(forward_mul, d_hidden, True)
+    grad_in = entering(a_used[:, 0] * back_mul[:, 0], a_used[:, 0] * back_add[:, 0], True)[:, None]
+    total_grad = back_mul * grad_in + back_add
+    previous = jnp.concatenate([state_in, hidden[:, :-1]], 1)
+    previous = jnp.where(open_3, state_rows, previous)
+    d_decay = total_grad * previous
+    d_mult = total_grad * admit * conv_val
+    d_admit = total_grad * mult * conv_val
+    d_conv = total_grad * mult * admit
+    d_spread = jnp.where(spread > FLOOR, d_mult * 0.5 / mult, 0.0)
+    d_log = d_decay * decay_now - 2.0 * decay_now * decay_now * d_spread
+    d_retain = d_log * (-8.0 * soft_decay)
+    grad_decay = jnp.sum(d_log * (-8.0 * retain), axis=(0, 1)) * jax.nn.sigmoid(decay_f)
+    d_rate = (d_retain * retain * (1.0 - retain)).astype(BF)
+    d_inflow = (d_admit * admit * (1.0 - admit)).astype(BF)
+    grad_abias = jnp.sum(d_rate.astype(F32), axis=(0, 1))
+    grad_ibias = jnp.sum(d_inflow.astype(F32), axis=(0, 1))
+    d_gates = jnp.concatenate([d_rate, d_inflow], 2).reshape(-1, 2 * wide_here)
+    d_conv = d_conv + ndot(d_gates, w_gates).reshape(d_conv.shape)
+    sums_gates = tdot(conv_flat, d_gates)
+
+    def diagonal(m):
+        m = m.reshape(heads_here, head_w, heads_here, head_w)
+        return jnp.concatenate([m[h, :, h] for h in range(heads_here)], 0)
+
+    grad_gates = jnp.concatenate(
+        [diagonal(sums_gates[:, :wide_here]), diagonal(sums_gates[:, wide_here:])], 1
+    )
+    d_conv_low = d_conv.astype(BF)
+    d_conv_val = d_conv_low.astype(F32)
+    head = d_conv_low[:, :back]
+    rim_back = per_block(shift_a(of_stream(head, 0), -1))
+    rim_back = jnp.where(second_half(head.shape), rim_back, flip(head))
+    ahead = jnp.concatenate([d_conv_low, rim_back], 1)
+    d_linear = kernel[0] * d_conv_val
+    kernel_grads = [jnp.sum(d_conv_val * by_tap[0], axis=(0, 1))]
+    for k in range(1, taps):
+        later_rows = ahead[:, k : k + rows].astype(F32)
+        same = (segment_of(position + k) == segment)[:, :, None]
+        d_linear = d_linear + kernel[k] * jnp.where(same, later_rows, 0.0)
+        kernel_grads.append(jnp.sum(d_conv_val * by_tap[k], axis=(0, 1)))
+    grad_cbias = jnp.sum(d_conv_val, axis=(0, 1))
+    vec_grads = jnp.stack(kernel_grads + [grad_cbias, grad_abias, grad_ibias, grad_decay], 1)
+    late = jnp.concatenate([grad_gates, vec_grads], 1).astype(BF)
+    late = scatter_a(part_halves(late)).astype(F32)
+    grad_wa, grad_wi = late[:, :head_w], late[:, head_w : 2 * head_w]
+    vec_grads = late[:, 2 * head_w :].T
+
+    d_linear_low = d_linear.astype(BF).reshape(-1, wide_here)
+    d_both = jnp.concatenate([d_gate_in, d_linear_low], 1)
+    d_normed = plane_scatter(ndot(d_both, w_yx))
+    sums = scatter_a(tdot(normed, d_both).astype(BF))
+    sums = by_owner(exchange(to_owner_rows(sums)))
+    grad_wy = from_head_pieces(sums[..., :wide_here]).astype(F32)
+    grad_wx = from_head_pieces(sums[..., wide_here:]).astype(F32)
+    scale_one = lax.rsqrt(jnp.mean(inputs * inputs, axis=-1, keepdims=True) + EPS)
+    input_grad = (d_resid + norm_back(inputs, scale_one, gain_one, d_normed)).astype(BF)
+
+    def gain_grad(gain, *pairs):
+        total = sum(jnp.sum(w.astype(F32) * g, axis=1) for w, g in pairs)
+        return total / gain.astype(F32)
+
+    grad_gain_one = gain_grad(norm1_gain, (w_y, grad_wy), (w_x, grad_wx))
+    grad_gain_two = gain_grad(norm2_gain, (w_gate, grad_wg), (w_up, grad_wu))
+
+    end = jnp.concatenate(
+        [offsets[:, 1:], jnp.full((streams, 1), planes * 2 * rows, jnp.int32)], 1
+    )
+    end_b = per_block(end) - 1
+    hot = (position[:, None, :] == end_b[:, :, None]).astype(BF)
+    lasts = lax.dot_general(
+        hot, hidden.astype(BF), (((2,), (1,)), ((0,), (0,))), preferred_element_type=F32
+    )
+    where_conv = (end_b[:, :, None] - back + 1 + slots).reshape(nblocks, nseq * back)
+    hot = (position[:, None, :] == where_conv[:, :, None]).astype(BF)
+    conv_lasts = lax.dot_general(
+        hot, linear, (((2,), (1,)), ((0,), (0,))), preferred_element_type=F32
+    )
+    lasts = two(jnp.concatenate([lasts, conv_lasts], 1))
+    lasts = (lasts[:, 0] + lasts[:, 1]).astype(BF)
+    came = [cycle_a(lasts, d) for d in range(1, planes)]
+    lasts = sum(part.astype(F32) for part in [lasts] + came).astype(BF)
+    both = jnp.stack([lasts[0], swap_c(lasts[1])])
+    found = jnp.stack(
+        [both[:, k % nn] if k == 0 else xor_u(both[:, k % nn], k) for k in range(count)], 1
+    )
+    found = by_owner(found).reshape(2, count, nseq * taps, heads_here, head_w)
+    found = found.transpose(2, 0, 3, 1, 4).reshape(nseq * taps, width)
+    final_state = found[:nseq].astype(F32)
+    final_conv = found[nseq:].reshape(nseq, back, width)
+
+    return (
+        result[None],
+        input_grad[None],
+        final_state[None],
+        final_conv[None],
+        grad_wy,
+        grad_wx,
+        grad_wa,
+        grad_wi,
+        grad_wo,
+        grad_gain_one,
+        vec_grads[:taps],
+        vec_grads[taps],
+        vec_grads[taps + 1],
+        vec_grads[taps + 2],
+        vec_grads[taps + 3],
+        grad_wg,
+        grad_wu,
+        grad_wd,
+        grad_gain_two,
+    )
+
+
+WIDE = ("a", "b")
+EVERY = ("a", "b", "n", "c")
 HIGH = lax.Precision.HIGHEST
 
 
@@ -51,22 +584,6 @@
     return (earlier[0] * later[0], later[0] * earlier[1] + later[1])
 
 
-def tdot(left, right):
-    return lax.dot_general(
-        left, right, (((0,), (0,)), ((), ())), preferred_element_type=jnp.float32
-    )
-
-
-def ndot(left, right):
-    return lax.dot_general(
-        left, right, (((1,), (1,)), ((), ())), preferred_element_type=jnp.float32
-    )
-
-
-def mdot(left, right):
-    return jnp.dot(left, right, preferred_element_type=jnp.float32)
-
-
 def norm_back(value, factor, gain, grad):
     weighted = grad * gain
     inner = jnp.mean(weighted * value, axis=-1, keepdims=True)
@@ -85,7 +602,7 @@
     )
 
 
-def on_device(
+def on_device_any(
     tokens,
     starts,
     init_state,
@@ -114,19 +631,19 @@
     width = w_y.shape[1]
     head_w = gate_a.shape[1]
     heads = width // head_w
-    place = lax.axis_index("wide")
+    place = lax.axis_index(WIDE)
     mixer = (
-        lax.all_gather(w_y, ("wide", "narrow"), axis=0, tiled=True),
-        lax.all_gather(w_x, ("wide", "narrow"), axis=0, tiled=True),
-        lax.all_gather(gate_a, ("wide", "narrow"), axis=0, tiled=True),
-        lax.all_gather(gate_i, ("wide", "narrow"), axis=0, tiled=True),
-        lax.all_gather(w_out, ("wide", "narrow"), axis=0, tiled=True),
-        lax.all_gather(norm1_gain, ("wide", "narrow"), axis=0, tiled=True),
-        lax.all_gather(conv_kernel, ("wide", "narrow"), axis=1, tiled=True),
-        lax.all_gather(conv_bias, ("wide", "narrow"), axis=0, tiled=True),
-        lax.all_gather(bias_a, ("wide", "narrow"), axis=0, tiled=True),
-        lax.all_gather(bias_i, ("wide", "narrow"), axis=0, tiled=True),
-        lax.all_gather(decay_param, ("wide", "narrow"), axis=0, tiled=True),
+        lax.all_gather(w_y, EVERY, axis=0, tiled=True),
+        lax.all_gather(w_x, EVERY, axis=0, tiled=True),
+        lax.all_gather(gate_a, EVERY, axis=0, tiled=True),
+        lax.all_gather(gate_i, EVERY, axis=0, tiled=True),
+        lax.all_gather(w_out, EVERY, axis=0, tiled=True),
+        lax.all_gather(norm1_gain, EVERY, axis=0, tiled=True),
+        lax.all_gather(conv_kernel, EVERY, axis=1, tiled=True),
+        lax.all_gather(conv_bias, EVERY, axis=0, tiled=True),
+        lax.all_gather(bias_a, EVERY, axis=0, tiled=True),
+        lax.all_gather(bias_i, EVERY, axis=0, tiled=True),
+        lax.all_gather(decay_param, EVERY, axis=0, tiled=True),
     )
     wy_full, wx_full, wa_full, wi_full, wo_full, gain_one, kernel, cbias, abias, ibias, decay = (
         mixer
@@ -148,7 +665,7 @@
     normed = (inputs * scale_one * gain_one).astype(jnp.bfloat16)
     gate_in = mdot(normed, wy_full)
     linear = mdot(normed, wx_full).astype(jnp.bfloat16)
-    rim_rows = passed_along(linear[rows_here - back :], "wide", 1)
+    rim_rows = passed_along(linear[rows_here - back :], WIDE, 1)
     extended = jnp.concatenate([rim_rows, linear], 0)
     stored = mdot(member.astype(jnp.bfloat16), init_conv[0].reshape(nseqs, back * width)).reshape(
         rows_here, back, width
@@ -192,17 +709,17 @@
     carry_mul, carry_add = lax.associative_scan(link, (a_used, b_used), axis=0)
     identity = (jnp.ones((width,), jnp.float32), jnp.zeros((width,), jnp.float32))
     state_in = entering(
-        (carry_mul[rows_here - 1], carry_add[rows_here - 1]), "wide", link, identity, False
+        (carry_mul[rows_here - 1], carry_add[rows_here - 1]), WIDE, link, identity, False
     )[1]
     hidden = carry_mul * state_in + carry_add
     gelu_y, gelu_y_back = jax.vjp(jax.nn.gelu, gate_in)
     mixed_in = (hidden * gelu_y).astype(jnp.bfloat16)
     resid = inputs + mdot(mixed_in, wo_full)
     wg_full, wu_full, wd_full, gain_two = (
-        lax.all_gather(w_gate, ("wide", "narrow"), axis=0, tiled=True),
-        lax.all_gather(w_up, ("wide", "narrow"), axis=0, tiled=True),
-        lax.all_gather(w_down, ("wide", "narrow"), axis=0, tiled=True),
-        lax.all_gather(norm2_gain, ("wide", "narrow"), axis=0, tiled=True),
+        lax.all_gather(w_gate, EVERY, axis=0, tiled=True),
+        lax.all_gather(w_up, EVERY, axis=0, tiled=True),
+        lax.all_gather(w_down, EVERY, axis=0, tiled=True),
+        lax.all_gather(norm2_gain, EVERY, axis=0, tiled=True),
     )
     gain_two = gain_two.astype(jnp.float32)
     scale_two = lax.rsqrt(jnp.mean(resid * resid, axis=-1, keepdims=True) + EPS)
@@ -222,11 +739,11 @@
         jnp.float32
     )
     conv_last = jnp.where(present[:, None, None], conv_rows, 0.0)
-    merged = merged_2((marker, state_last, conv_last), "wide", later_one)
+    merged = merged_2((marker, state_last, conv_last), WIDE, later_one)
     wg_back, wu_back, wd_back = (
-        lax.all_gather(w_gate, ("wide", "narrow"), axis=0, tiled=True),
-        lax.all_gather(w_up, ("wide", "narrow"), axis=0, tiled=True),
-        lax.all_gather(w_down, ("wide", "narrow"), axis=0, tiled=True),
+        lax.all_gather(w_gate, EVERY, axis=0, tiled=True),
+        lax.all_gather(w_up, EVERY, axis=0, tiled=True),
+        lax.all_gather(w_down, EVERY, axis=0, tiled=True),
     )
     grad_low = cotangent[0]
     grad_out = grad_low.astype(jnp.float32)
@@ -240,11 +757,11 @@
     d_resid_norm, grad_gain_two = norm_back(resid, scale_two, gain_two, d_normed_two)
     d_resid = grad_out + d_resid_norm
     wy_back, wx_back, wa_back, wi_back, wo_back = (
-        lax.all_gather(w_y, ("wide", "narrow"), axis=0, tiled=True),
-        lax.all_gather(w_x, ("wide", "narrow"), axis=0, tiled=True),
-        lax.all_gather(gate_a, ("wide", "narrow"), axis=0, tiled=True),
-        lax.all_gather(gate_i, ("wide", "narrow"), axis=0, tiled=True),
-        lax.all_gather(w_out, ("wide", "narrow"), axis=0, tiled=True),
+        lax.all_gather(w_y, EVERY, axis=0, tiled=True),
+        lax.all_gather(w_x, EVERY, axis=0, tiled=True),
+        lax.all_gather(gate_a, EVERY, axis=0, tiled=True),
+        lax.all_gather(gate_i, EVERY, axis=0, tiled=True),
+        lax.all_gather(w_out, EVERY, axis=0, tiled=True),
     )
     d_resid_low = d_resid.astype(jnp.bfloat16)
     d_mixed = ndot(d_resid_low, wo_back)
@@ -254,7 +771,7 @@
     forward_mul = jnp.concatenate([a_used[1:], jnp.ones((1, width), jnp.float32)], 0)
     back_mul, back_add = lax.associative_scan(link, (forward_mul, d_hidden), reverse=True, axis=0)
     head_map = (a_used[0] * back_mul[0], a_used[0] * back_add[0])
-    grad_in = entering(head_map, "wide", link, identity, True)[1]
+    grad_in = entering(head_map, WIDE, link, identity, True)[1]
     total_grad = back_mul * grad_in + back_add
     previous = jnp.concatenate([state_in[None], hidden[:-1]], 0)
     previous = jnp.where(opening, state_rows, previous)
@@ -292,7 +809,7 @@
     ).reshape(rows_here, width)
     d_conv_low = d_conv.astype(jnp.bfloat16)
     d_conv_val = d_conv_low.astype(jnp.float32)
-    rim_back = passed_along(d_conv_low[:back], "wide", -1)
+    rim_back = passed_along(d_conv_low[:back], WIDE, -1)
     ahead = jnp.concatenate([d_conv_low, rim_back], 0)
     d_linear = kernel[0] * d_conv_val
     kernel_grads = [jnp.sum(d_conv_val * inputs_by_tap[0], axis=0)]
@@ -310,21 +827,21 @@
     d_input_norm, grad_gain_one = norm_back(inputs, scale_one, gain_one, d_normed)
     input_grad = (d_resid + d_input_norm).astype(jnp.bfloat16)
     every_sum = (
-        lax.psum_scatter(grad_wy, ("wide", "narrow"), scatter_dimension=0, tiled=True),
-        lax.psum_scatter(grad_wx, ("wide", "narrow"), scatter_dimension=0, tiled=True),
-        lax.psum_scatter(grad_wa, ("wide", "narrow"), scatter_dimension=0, tiled=True),
-        lax.psum_scatter(grad_wi, ("wide", "narrow"), scatter_dimension=0, tiled=True),
-        lax.psum_scatter(grad_wo, ("wide", "narrow"), scatter_dimension=0, tiled=True),
-        lax.psum_scatter(grad_gain_one, ("wide", "narrow"), scatter_dimension=0, tiled=True),
-        lax.psum_scatter(grad_kernel, ("wide", "narrow"), scatter_dimension=1, tiled=True),
-        lax.psum_scatter(grad_cbias, ("wide", "narrow"), scatter_dimension=0, tiled=True),
-        lax.psum_scatter(grad_abias, ("wide", "narrow"), scatter_dimension=0, tiled=True),
-        lax.psum_scatter(grad_ibias, ("wide", "narrow"), scatter_dimension=0, tiled=True),
-        lax.psum_scatter(grad_decay, ("wide", "narrow"), scatter_dimension=0, tiled=True),
-        lax.psum_scatter(grad_wg, ("wide", "narrow"), scatter_dimension=0, tiled=True),
-        lax.psum_scatter(grad_wu, ("wide", "narrow"), scatter_dimension=0, tiled=True),
-        lax.psum_scatter(grad_wd, ("wide", "narrow"), scatter_dimension=0, tiled=True),
-        lax.psum_scatter(grad_gain_two, ("wide", "narrow"), scatter_dimension=0, tiled=True),
+        lax.psum_scatter(grad_wy, EVERY, scatter_dimension=0, tiled=True),
+        lax.psum_scatter(grad_wx, EVERY, scatter_dimension=0, tiled=True),
+        lax.psum_scatter(grad_wa, EVERY, scatter_dimension=0, tiled=True),
+        lax.psum_scatter(grad_wi, EVERY, scatter_dimension=0, tiled=True),
+        lax.psum_scatter(grad_wo, EVERY, scatter_dimension=0, tiled=True),
+        lax.psum_scatter(grad_gain_one, EVERY, scatter_dimension=0, tiled=True),
+        lax.psum_scatter(grad_kernel, EVERY, scatter_dimension=1, tiled=True),
+        lax.psum_scatter(grad_cbias, EVERY, scatter_dimension=0, tiled=True),
+        lax.psum_scatter(grad_abias, EVERY, scatter_dimension=0, tiled=True),
+        lax.psum_scatter(grad_ibias, EVERY, scatter_dimension=0, tiled=True),
+        lax.psum_scatter(grad_decay, EVERY, scatter_dimension=0, tiled=True),
+        lax.psum_scatter(grad_wg, EVERY, scatter_dimension=0, tiled=True),
+        lax.psum_scatter(grad_wu, EVERY, scatter_dimension=0, tiled=True),
+        lax.psum_scatter(grad_wd, EVERY, scatter_dimension=0, tiled=True),
+        lax.psum_scatter(grad_gain_two, EVERY, scatter_dimension=0, tiled=True),
     )
     mixer_sums = every_sum[:11]
     mlp_sums = every_sum[11:]
@@ -352,52 +869,42 @@
 
 
 def solution(mesh):
-    placed = (
-        P("narrow", "wide", None),
-        P("narrow", None),
-        P("narrow", None, None),
-        P("narrow", None, None, None),
-        P(("wide", "narrow"), None),
-        P(("wide", "narrow"), None),
-        P(("wide", "narrow"), None),
-        P(("wide", "narrow"), None),
-        P(("wide", "narrow"), None),
-        P(("wide", "narrow")),
-        P(None, ("wide", "narrow")),
-        P(("wide", "narrow")),
-        P(("wide", "narrow")),
-        P(("wide", "narrow")),
-        P(("wide", "narrow")),
-        P(("wide", "narrow"), None),
-        P(("wide", "narrow"), None),
-        P(("wide", "narrow"), None),
-        P(("wide", "narrow")),
-        P("narrow", "wide", None),
-    )
+    wide, narrow = mesh.shape["wide"], mesh.shape["narrow"]
+    def plan(*args):
+        fits = args[6].shape[0] * 2 == args[6].shape[1]
+        return (on_device if fits else on_device_any)(*args)
+
+    fine = Mesh(mesh.devices.reshape(wide // 2, 2, narrow // 2, 2), ("a", "b", "n", "c"))
+    w, s = ("a", "b"), ("n", "c")
+    everywhere = ("a", "b", "n", "c")
+    acts, rows, vec = P(s, w, None), P(everywhere, None), P(everywhere)
     return jax.shard_map(
-        on_device,
-        mesh=mesh,
-        in_specs=placed,
+        plan,
+        mesh=fine,
+        in_specs=(
+            acts,
+            P(s, None),
+            P(s, None, None),
+            P(s, None, None, None),
+            rows, rows, rows, rows, rows,
+            vec,
+            P(None, everywhere),
+            vec, vec, vec, vec,
+            rows, rows, rows,
+            vec,
+            acts,
+        ),
         out_specs=(
-            P("narrow", "wide", None),
-            P("narrow", "wide", None),
-            P("narrow", None, None),
-            P("narrow", None, None, None),
-            P(("wide", "narrow"), None),
-            P(("wide", "narrow"), None),
-            P(("wide", "narrow"), None),
-            P(("wide", "narrow"), None),
-            P(("wide", "narrow"), None),
-            P(("wide", "narrow")),
-            P(None, ("wide", "narrow")),
-            P(("wide", "narrow")),
-            P(("wide", "narrow")),
-            P(("wide", "narrow")),
-            P(("wide", "narrow")),
-            P(("wide", "narrow"), None),
-            P(("wide", "narrow"), None),
-            P(("wide", "narrow"), None),
-            P(("wide", "narrow")),
+            acts,
+            acts,
+            P(s, None, None),
+            P(s, None, None, None),
+            rows, rows, rows, rows, rows,
+            vec,
+            P(None, everywhere),
+            vec, vec, vec, vec,
+            rows, rows, rows,
+            vec,
         ),
         check_vma=False,
     )

time: 3580 us -> 1020 us (0.28)
  waiting for transfers between devices: 2310 us -> 318 us
  blocking collectives: 420 us -> 0 us
  local copies, waits for them, and re-layouts: 427 us -> 216 us
  matrix products: 268 us -> 174 us
  starting transfers between devices: 3.78 us -> 88.1 us
  other arithmetic: 113 us -> 180 us
    reduce_scatter x8 -> x5, waiting for transfers between devices: 2130 us -> 0.03 us  [scatter_a(): return lax.psum_scatter(value, 'a', scatter_dimension=0, tiled=True)]
    all_gather x9 -> x0, blocking collectives: 321 us -> none  [the longest x4 123 us: entering(): everything = jax.tree.map(lambda part: lax.all_gather(part, axis), value)]
    ppermute x2 -> x76, waiting for transfers between devices: 5.33 us -> 273 us  [the longest x42 264 us: xor_u(): return lax.ppermute(value, ('b', 'n'), [(i, i ^ k) for i in range(size)])]
    slice x113 -> x32, local copies, waits for them, and re-layouts: 243 us -> 65.5 us  [the longest x4 29.6 us: plane_scatter(): summed = parts[0].astype(F32) + got.astype(F32)]
    all_gather x6 -> x4, waiting for transfers between devices: 169 us -> 45 us  [gather_a(): return lax.all_gather(value, 'a', axis=0, tiled=True)]
    pad x56 -> x0, local copies, waits for them, and re-layouts: 99.8 us -> none  [the longest x28 54 us: on_device(): carry_mul, carry_add = lax.associative_scan(link, (a_used, b_used), axis=0)]
    unnamed x3 -> x0, blocking collectives: 98.8 us -> none
    ppermute x2 -> x76, starting transfers between devices: 2.8 us -> 86.2 us  [the longest x42 51.4 us: xor_u(): return lax.ppermute(value, ('b', 'n'), [(i, i ^ k) for i in range(size)])]
  transfers between devices with their start and end apart: 17 -> 85, of which waited for: 11 -> 31; matrix products, arithmetic and copies ran while one was open for 13% -> 47% of each run, Pallas kernels for 0% -> 1%
where the time goes in v1:
time: 1020 us; the launch traced here: 1010 us
  waiting for transfers between devices  318 us (31%)
  local copies, waits for them, and re-layouts  216 us (21%)
  other arithmetic  180 us (18%)
  matrix products  174 us (17%)
  starting transfers between devices  88.1 us (9%)
  between operations  17 us (2%)
  Pallas kernels  12.9 us (1%)
    ppermute x42, waiting for transfers between devices, xor_u(): return lax.ppermute(value, ('b', 'n'), [(i, i ^ k) for i in range(size)])  264 us
    dot_general x5, matrix products, ndot(): lax.dot_general(left, right, (((1,), (1,)), ((), ())), preferred_element_...  67.6 us
    ppermute x42, starting transfers between devices, xor_u(): return lax.ppermute(value, ('b', 'n'), [(i, i ^ k) for i in range(size)])  51.4 us
    dot_general x5, matrix products, tdot(): lax.dot_general(left, right, (((0,), (0,)), ((), ())), preferred_element_...  49.4 us
    unnamed x279, local copies, waits for them, and re-layouts  46.4 us
    all_gather x4, waiting for transfers between devices, gather_a(): return lax.all_gather(value, 'a', axis=0, tiled=True)  45 us
    dot_general x6, matrix products, mdot(): return jnp.dot(left, right, preferred_element_type=F32)  43.8 us
    convert_element_type x4, other arithmetic, plane_scatter(): low = summed.astype(BF)  42.7 us
  transfers between devices with their start and end apart: 85, of which 31 were waited for; matrix products, arithmetic and copies ran while one was open for 47% of the time, Pallas kernels for 1%

profile of v1, /device:TPU:0, one launch (start us, length us, event | category | flops | bytes accessed | tf_op | source)
XLA Modules:
  0.0 1006.2 jit_solution(10238490902969703746)
XLA Ops:
  85.0 18.7 %collective-permute-done.10 = bf16[256,2048]{1,0:T(8,128)(2,1)S(1)} collective-permute-done((bf16[256,2048]{1,0:T(8,128)(2,1)S(1)}, bf16[256,2048]{1,0:T(8,128)(2,1)S(1)}, u32[]{:S(2)}, u32[]{:S(2)}) %collective-permute-start.10) | collective-permute-done | bytes 1048608 | tf_op jit(solution)/shard_map/ppermute | solution.py:39
  137.3 8.7 fusion.1
  146.0 17.5 %all-gather.5.cloned.1.call-done = bf16[2048,640]{1,0:T(8,128)(2,1)} async-done(((bf16[512,640]{1,0:T(8,128)(2,1)}), bf16[2048,640]{1,0:T(8,128)(2,1)}) %all-gather.5.cloned.1.call-update) | async-done | bytes 2621456 | tf_op jit(solution)/shard_map/all_gather | solution.py:207
  163.5 8.9 fusion.213
  198.4 9.2 add_select_fusion
  257.8 8.8 slice.596
  266.6 10.3 %fusion.204 = (bf16[4,256,2048]{2,1,0:T(8,128)(2,1)S(1)}, f32[4,256,2048]{2,1,0:T(8,128)}) fusion(f32[4,256,2048]{2,1,0:T(8,128)} %bitcast.470, bf16[4,256,2048]{2,1,0:T(8,128)(2,1)} %collective-permute-done.23), kind=kLoop, calls=%fused_computation.580 | loop fusion | flops 6291456 | bytes 25165824 | tf_op jit(solution)/shard_map/convert_element_type | solution.py:75
  282.3 43.0 %collective-permute-done.39 = bf16[256,2048]{1,0:T(8,128)(2,1)} collective-permute-done((bf16[256,2048]{1,0:T(8,128)(2,1)S(1)}, bf16[256,2048]{1,0:T(8,128)(2,1)}, u32[]{:S(2)}, u32[]{:S(2)}) %collective-permute-start.39) | collective-permute-done | bytes 1048608 | tf_op jit(solution)/shard_map/ppermute | solution.py:39
  328.9 17.9 %collective-permute-done.24 = bf16[256,2048]{1,0:T(8,128)(2,1)} collective-permute-done((bf16[256,2048]{1,0:T(8,128)(2,1)}, bf16[256,2048]{1,0:T(8,128)(2,1)}, u32[]{:S(2)}, u32[]{:S(2)}) %collective-permute-start.24) | collective-permute-done | bytes 1048608 | tf_op jit(solution)/shard_map/ppermute | solution.py:39
  355.0 23.5 %collective-permute-done.29 = bf16[256,2048]{1,0:T(8,128)(2,1)S(1)} collective-permute-done((bf16[256,2048]{1,0:T(8,128)(2,1)S(1)}, bf16[256,2048]{1,0:T(8,128)(2,1)S(1)}, u32[]{:S(2)}, u32[]{:S(2)}) %collective-permute-start.29) | collective-permute-done | bytes 1048608 | tf_op jit(solution)/shard_map/ppermute | solution.py:39
  378.6 19.4 %collective-permute-done.28 = bf16[256,2048]{1,0:T(8,128)(2,1)S(1)} collective-permute-done((bf16[256,2048]{1,0:T(8,128)(2,1)S(1)}, bf16[256,2048]{1,0:T(8,128)(2,1)S(1)}, u32[]{:S(2)}, u32[]{:S(2)}) %collective-permute-start.28) | collective-permute-done | bytes 1048608 | tf_op jit(solution)/shard_map/ppermute | solution.py:39
  416.0 19.0 %fusion.214 = f32[2048,1536]{0,1:T(8,128)} fusion(bf16[2048,2048]{1,0:T(8,128)(2,1)} %bitcast.548, bf16[2048,1536]{1,0:T(8,128)(2,1)} %all-gather.9.cloned.1.call-done), kind=kOutput, calls=%fused_computation.590 | convolution fusion | flops 12884901888 | bytes 27262976 | tf_op jit(solution)/shard_map/dot_general | solution.py:26
  435.0 27.5 %all-gather.11.cloned.1.call-done = bf16[768,2048]{1,0:T(8,128)(2,1)} async-done(((bf16[192,2048]{1,0:T(8,128)(2,1)}), bf16[768,2048]{1,0:T(8,128)(2,1)}) %all-gather.11.cloned.1.call-update) | async-done | bytes 3145744 | tf_op jit(solution)/shard_map/all_gather | solution.py:207
  462.5 20.5 %fusion.8 = (bf16[2048,768]{0,1:T(8,128)(2,1)}, bf16[2048,768]{0,1:T(8,128)(2,1)}, bf16[2048,768]{0,1:T(8,128)(2,1)}) fusion(f32[2048,1536]{0,1:T(8,128)} %fusion.214, bf16[2048,2048]{1,0:T(8,128)(2,1)} %bitcast.550, bf16[768,2048]{1,0:T(8,128)(2,1)} %all-gather.11.cloned.1.call-done), kind=kOutput, calls=%fused_computation.21 | convolution fusion | flops 6483345408 | bytes 33554432 | tf_op jit(solution)/shard_map/dot_general | solution.py:22
  483.1 19.2 %fusion.9 = f32[2048,2048]{1,0:T(8,128)} fusion(bf16[2048,1536]{1,0:T(8,128)(2,1)S(1)} %copy-done.121, bf16[2048,768]{0,1:T(8,128)(2,1)} %get-tuple-element.165, bf16[2048,768]{0,1:T(8,128)(2,1)} %get-tuple-element.164), kind=kOutput, calls=%fused_computation.43 | convolution fusion | flops 12897484800 | bytes 29360128 | tf_op jit(solution)/shard_map/dot_general | solution.py:22
  508.4 8.9 fusion.215
  526.3 18.5 %convolution_convert_fusion = bf16[2048,1536]{1,0:T(8,128)(2,1)} fusion(bf16[2048,2048]{1,0:T(8,128)(2,1)} %bitcast.549, bf16[2048,768]{0,1:T(8,128)(2,1)} %get-tuple-element.165, bf16[2048,768]{0,1:T(8,128)(2,1)S(1)} %copy-done.125), kind=kOutput, calls=%fused_computation.14 | convolution fusion | flops 12900630528 | bytes 20971520 | tf_op jit(solution)/shard_map/dot_general | solution.py:18
  545.3 8.9 slice.611
  561.2 10.3 %fusion.202 = (bf16[4,256,2048]{2,1,0:T(8,128)(2,1)S(1)}, f32[4,256,2048]{2,1,0:T(8,128)}) fusion(f32[4,256,2048]{2,1,0:T(8,128)} %bitcast.469, bf16[4,256,2048]{2,1,0:T(8,128)(2,1)} %collective-permute-done.43), kind=kLoop, calls=%fused_computation.578 | loop fusion | flops 6291456 | bytes 25165824 | tf_op jit(solution)/shard_map/convert_element_type | solution.py:75
  576.8 11.8 %fusion.203 = (bf16[4,256,2048]{2,1,0:T(8,128)(2,1)}, f32[4,256,2048]{2,1,0:T(8,128)}) fusion(f32[4,256,2048]{2,1,0:T(8,128)} %bitcast.468, bf16[4,256,2048]{2,1,0:T(8,128)(2,1)} %collective-permute-done.35), kind=kLoop, calls=%fused_computation.579 | loop fusion | flops 6291456 | bytes 25165824 | tf_op jit(solution)/shard_map/convert_element_type | solution.py:75
  595.1 27.3 %collective-permute-done.44 = bf16[256,2048]{1,0:T(8,128)(2,1)S(1)} collective-permute-done((bf16[256,2048]{1,0:T(8,128)(2,1)}, bf16[256,2048]{1,0:T(8,128)(2,1)S(1)}, u32[]{:S(2)}, u32[]{:S(2)}) %collective-permute-start.44) | collective-permute-done | bytes 1048608 | tf_op jit(solution)/shard_map/ppermute | solution.py:39
  623.8 42.1 %collective-permute-done.36 = bf16[256,2048]{1,0:T(8,128)(2,1)} collective-permute-done((bf16[256,2048]{1,0:T(8,128)(2,1)}, bf16[256,2048]{1,0:T(8,128)(2,1)}, u32[]{:S(2)}, u32[]{:S(2)}) %collective-permute-start.36) | collective-permute-done | bytes 1048608 | tf_op jit(solution)/shard_map/ppermute | solution.py:39
  690.6 15.7 %collective-permute-done.49 = bf16[256,2048]{1,0:T(8,128)(2,1)} collective-permute-done((bf16[256,2048]{1,0:T(8,128)(2,1)}, bf16[256,2048]{1,0:T(8,128)(2,1)}, u32[]{:S(2)}, u32[]{:S(2)}) %collective-permute-start.49) | collective-permute-done | bytes 1048608 | tf_op jit(solution)/shard_map/ppermute | solution.py:39
  706.3 20.1 %collective-permute-done.48 = bf16[256,2048]{1,0:T(8,128)(2,1)} collective-permute-done((bf16[256,2048]{1,0:T(8,128)(2,1)}, bf16[256,2048]{1,0:T(8,128)(2,1)}, u32[]{:S(2)}, u32[]{:S(2)}) %collective-permute-start.48) | collective-permute-done | bytes 1048608 | tf_op jit(solution)/shard_map/ppermute | solution.py:39
  738.4 10.3 %convolution_convert_fusion.1 = bf16[768,2048]{1,0:T(8,128)(2,1)} fusion(bf16[2048,768]{0,1:T(8,128)(2,1)S(1)} %copy-done.124, bf16[2048,2048]{1,0:T(8,128)(2,1)} %bitcast.551), kind=kOutput, calls=%fused_computation.49 | convolution fusion | flops 6444023808 | bytes 14680064 | tf_op jit(solution)/shard_map/dot_general | solution.py:18
  767.4 12.6 %fusion.21 = (bf16[8,256,320]{2,1,0:T(8,128)(2,1)}, f32[8,256,320]{2,1,0:T(8,128)}) fusion(f32[8,256,320]{2,1,0:T(8,128)S(1)} %bitcast.477, f32[8,256,320]{2,1,0:T(8,128)S(1)} %copy-done.5, bf16[8,256,2048]{2,1,0:T(8,128)(2,1)} %constant_dynamic-update-slice_fusion.17, bf16[320,2368]{1,0:T(8,128)(2,1)S(1)} %bitcast.486), kind=kOutput, calls=%fused_computation.62 | convolution fusion | flops 2699427840 | bytes 19922944 | tf_op jit(solution)/shard_map/dot_general | solution.py:22
  797.7 11.5 %multiply_reduce_fusion.1 = (f32[320]{0:T(512)S(1)}, f32[8,256,320]{2,1,0:T(8,128)}) fusion(f32[2048,320]{1,0:T(8,128)} %copy.255, bf16[8,256,320]{2,1,0:T(8,128)(2,1)} %copy-done.9, f32[320]{0:T(512)S(1)} %copy-done.85, f32[8,255,320]{2,1,0:T(8,128)} %bitcast.471, f32[8,1,320]{2,1,0:T(1,128)S(1)} %broadcast_select_fusion, f32[8,320]{1,0:T(8,128)S(1)} %copy-done.71, ...), kind=kLoop, calls=%fused_computation.82 | loop fusion | flops 18349760 | bytes 17103360 | tf_op jit(solution)/shard_map/reduce_sum | solution.py:437
  809.4 8.4 fusion.200
  847.6 8.6 fusion.74
  864.9 10.8 %convolution_convert_fusion.2 = bf16[2048,640]{1,0:T(8,128)(2,1)} fusion(bf16[2048,2048]{1,0:T(8,128)(2,1)} %fusion.1, bf16[2048,320]{1,0:T(8,128)(2,1)S(1)} %bitcast.514, bf16[2048,320]{1,0:T(8,128)(2,1)S(1)} %bitcast.586), kind=kOutput, calls=%fused_computation.50 | convolution fusion | flops 5375262720 | bytes 13631488 | tf_op jit(solution)/shard_map/dot_general | solution.py:18
  919.0 10.3 %fusion.201 = (bf16[4,256,2048]{2,1,0:T(8,128)(2,1)S(1)}, f32[4,256,2048]{2,1,0:T(8,128)}) fusion(f32[4,256,2048]{2,1,0:T(8,128)} %bitcast.467, bf16[4,256,2048]{2,1,0:T(8,128)(2,1)} %collective-permute-done.55), kind=kLoop, calls=%fused_computation.577 | loop fusion | flops 6291456 | bytes 25165824 | tf_op jit(solution)/shard_map/convert_element_type | solution.py:75
  962.2 14.5 %collective-permute-done.56 = bf16[256,2048]{1,0:T(8,128)(2,1)} collective-permute-done((bf16[256,2048]{1,0:T(8,128)(2,1)}, bf16[256,2048]{1,0:T(8,128)(2,1)}, u32[]{:S(2)}, u32[]{:S(2)}) %collective-permute-start.56) | collective-permute-done | bytes 1048608 | tf_op jit(solution)/shard_map/ppermute | solution.py:39
  (739 shorter events, 466.5 us)
Async XLA Ops:
  7.2 111.2 %all-gather.7.cloned.1.call-start = ((), (), s32[]{:S(2)}) async-start(), calls=%async_computation.6 | async-start | bytes 1945600 | tf_op jit(solution)/shard_map/all_gather | solution.py:207
  20.5 143.0 %all-gather.5.cloned.1.call-start = ((), (), s32[]{:S(2)}) async-start(), calls=%async_computation.5 | async-start | bytes 3276800 | tf_op jit(solution)/shard_map/all_gather | solution.py:207
  51.7 52.1 %collective-permute-start.10 = (bf16[256,2048]{1,0:T(8,128)(2,1)S(1)}, bf16[256,2048]{1,0:T(8,128)(2,1)S(1)}, u32[]{:S(2)}, u32[]{:S(2)}) collective-permute-start(bf16[256,2048]{1,0:T(8,128)(2,1)S(1)} %bitcast.473), channel_id=1, source_target_pairs={{0,2},{2,0},{4,6},{6,4},{1,3},{3,1},{5,7},{7,5},{8,10},{10,8},{12,... | collective-permute-start | bytes 3145736 | tf_op jit(solution)/shard_map/ppermute | solution.py:39
  59.9 45.3 %collective-permute-start.12 = (bf16[256,2048]{1,0:T(8,128)(2,1)S(1)}, bf16[256,2048]{1,0:T(8,128)(2,1)}, u32[]{:S(2)}, u32[]{:S(2)}) collective-permute-start(bf16[256,2048]{1,0:T(8,128)(2,1)S(1)} %bitcast.474), channel_id=1, source_target_pairs={{0,6},{2,4},{4,2},{6,0},{1,7},{3,5},{5,3},{7,1},{8,14},{10,12},{12... | collective-permute-start | bytes 3145736 | tf_op jit(solution)/shard_map/ppermute | solution.py:39
  62.7 48.8 %collective-permute-start.31 = (bf16[4,64,1536]{2,1,0:T(8,128)(2,1)}, bf16[4,64,1536]{2,1,0:T(8,128)(2,1)}, u32[]{:S(2)}, u32[]{:S(2)}) collective-permute-start(bf16[4,64,1536]{2,1,0:T(8,128)(2,1)} %get-tuple-element.217), channel_id=1, source_target_pairs={{0,1},{1,0},{2,3},{3,2},{4,5},{5,4},{6,7},{7,6},{8,9},{9,8},{10,11... | collective-permute-start | bytes 2359304 | tf_op jit(solution)/shard_map/ppermute | solution.py:34
  111.3 304.8 %all-gather.9.cloned.1.call-start = ((), (), s32[]{:S(2)}) async-start(), calls=%async_computation.7 | async-start | bytes 7864320 | tf_op jit(solution)/shard_map/all_gather | solution.py:207
  113.9 109.9 %collective-permute-start.32 = (bf16[2,64,1536]{2,1,0:T(8,128)(2,1)}, bf16[2,64,1536]{2,1,0:T(8,128)(2,1)}, u32[]{:S(2)}, u32[]{:S(2)}) collective-permute-start(bf16[2,64,1536]{2,1,0:T(8,128)(2,1)} %get-tuple-element.214), channel_id=1, source_target_pairs={{0,2},{2,0},{4,6},{6,4},{1,3},{3,1},{5,7},{7,5},{8,10},{10,8},{12,... | collective-permute-start | bytes 1179656 | tf_op jit(solution)/shard_map/ppermute | solution.py:39
  113.9 112.5 %collective-permute-start.33 = (bf16[2,64,1536]{2,1,0:T(8,128)(2,1)}, bf16[2,64,1536]{2,1,0:T(8,128)(2,1)}, u32[]{:S(2)}, u32[]{:S(2)}) collective-permute-start(bf16[2,64,1536]{2,1,0:T(8,128)(2,1)} %get-tuple-element.215), channel_id=1, source_target_pairs={{0,4},{2,6},{4,0},{6,2},{1,5},{3,7},{5,1},{7,3},{8,12},{10,14},{12... | collective-permute-start | bytes 1179656 | tf_op jit(solution)/shard_map/ppermute | solution.py:39
  115.8 110.5 %collective-permute-start.34 = (bf16[2,64,1536]{2,1,0:T(8,128)(2,1)}, bf16[2,64,1536]{2,1,0:T(8,128)(2,1)}, u32[]{:S(2)}, u32[]{:S(2)}) collective-permute-start(bf16[2,64,1536]{2,1,0:T(8,128)(2,1)} %get-tuple-element.216), channel_id=1, source_target_pairs={{0,6},{2,4},{4,2},{6,0},{1,7},{3,5},{5,3},{7,1},{8,14},{10,12},{12... | collective-permute-start | bytes 1179656 | tf_op jit(solution)/shard_map/ppermute | solution.py:39
  254.0 208.5 %all-gather.11.cloned.1.call-start = ((), (), s32[]{:S(2)}) async-start(), calls=%async_computation.8 | async-start | bytes 3932160 | tf_op jit(solution)/shard_map/all_gather | solution.py:207
  256.1 69.2 %collective-permute-start.39 = (bf16[256,2048]{1,0:T(8,128)(2,1)S(1)}, bf16[256,2048]{1,0:T(8,128)(2,1)}, u32[]{:S(2)}, u32[]{:S(2)}) collective-permute-start(bf16[256,2048]{1,0:T(8,128)(2,1)S(1)} %bitcast.479), channel_id=1, source_target_pairs={{0,2},{2,0},{4,6},{6,4},{1,3},{3,1},{5,7},{7,5},{8,10},{10,8},{12,... | collective-permute-start | bytes 3145736 | tf_op jit(solution)/shard_map/ppermute | solution.py:39
  257.5 67.7 %collective-permute-start.41 = (bf16[256,2048]{1,0:T(8,128)(2,1)S(1)}, bf16[256,2048]{1,0:T(8,128)(2,1)}, u32[]{:S(2)}, u32[]{:S(2)}) collective-permute-start(bf16[256,2048]{1,0:T(8,128)(2,1)S(1)} %bitcast.480), channel_id=1, source_target_pairs={{0,6},{2,4},{4,2},{6,0},{1,7},{3,5},{5,3},{7,1},{8,14},{10,12},{12... | collective-permute-start | bytes 3145736 | tf_op jit(solution)/shard_map/ppermute | solution.py:39
  278.8 68.0 %collective-permute-start.24 = (bf16[256,2048]{1,0:T(8,128)(2,1)}, bf16[256,2048]{1,0:T(8,128)(2,1)}, u32[]{:S(2)}, u32[]{:S(2)}) collective-permute-start(bf16[256,2048]{1,0:T(8,128)(2,1)} %get-tuple-element.180), channel_id=1, source_target_pairs={{0,2},{2,0},{4,6},{6,4},{1,3},{3,1},{5,7},{7,5},{8,10},{10,8},{12,... | collective-permute-start | bytes 3145736 | tf_op jit(solution)/shard_map/ppermute | solution.py:39
  280.4 66.3 %collective-permute-start.26 = (bf16[256,2048]{1,0:T(8,128)(2,1)}, bf16[256,2048]{1,0:T(8,128)(2,1)}, u32[]{:S(2)}, u32[]{:S(2)}) collective-permute-start(bf16[256,2048]{1,0:T(8,128)(2,1)} %get-tuple-element.181), channel_id=1, source_target_pairs={{0,6},{2,4},{4,2},{6,0},{1,7},{3,5},{5,3},{7,1},{8,14},{10,12},{12... | collective-permute-start | bytes 3145736 | tf_op jit(solution)/shard_map/ppermute | solution.py:39
  281.9 64.8 %collective-permute-start.25 = (bf16[256,2048]{1,0:T(8,128)(2,1)}, bf16[256,2048]{1,0:T(8,128)(2,1)}, u32[]{:S(2)}, u32[]{:S(2)}) collective-permute-start(bf16[256,2048]{1,0:T(8,128)(2,1)} %get-tuple-element.182), channel_id=1, source_target_pairs={{0,4},{2,6},{4,0},{6,2},{1,5},{3,7},{5,1},{7,3},{8,12},{10,14},{12... | collective-permute-start | bytes 3145736 | tf_op jit(solution)/shard_map/ppermute | solution.py:39
  328.9 75.2 %collective-permute-start.42 = (bf16[4,256,2048]{2,1,0:T(8,128)(2,1)}, bf16[4,256,2048]{2,1,0:T(8,128)(2,1)}, u32[]{:S(2)}, u32[]{:S(2)}) collective-permute-start(bf16[4,256,2048]{2,1,0:T(8,128)(2,1)} %pad_maximum_fusion.3), channel_id=1, source_target_pairs={{0,1},{1,0},{2,3},{3,2},{4,5},{5,4},{6,7},{7,6},{8,9},{9,8},{10,11... | collective-permute-start | bytes 12582920 | tf_op jit(solution)/shard_map/ppermute | solution.py:34
  400.9 474.8 %reduce-scatter.12.cloned.1.call-start = ((), (), s32[]{:S(2)}) async-start(), calls=%async_computation.12 | async-start | bytes 7864320 | tf_op jit(solution)/shard_map/reduce_scatter | solution.py:210
  508.4 52.8 %collective-permute-start.43 = (bf16[4,256,2048]{2,1,0:T(8,128)(2,1)}, bf16[4,256,2048]{2,1,0:T(8,128)(2,1)}, u32[]{:S(2)}, u32[]{:S(2)}) collective-permute-start(bf16[4,256,2048]{2,1,0:T(8,128)(2,1)} %bitcast.110), channel_id=1, source_target_pairs={{0,1},{1,0},{2,3},{3,2},{4,5},{5,4},{6,7},{7,6},{8,9},{9,8},{10,11... | collective-permute-start | bytes 12582920 | tf_op jit(solution)/shard_map/ppermute | solution.py:34
  525.8 50.9 %collective-permute-start.35 = (bf16[4,256,2048]{2,1,0:T(8,128)(2,1)}, bf16[4,256,2048]{2,1,0:T(8,128)(2,1)}, u32[]{:S(2)}, u32[]{:S(2)}) collective-permute-start(bf16[4,256,2048]{2,1,0:T(8,128)(2,1)} %bitcast.98), channel_id=1, source_target_pairs={{0,1},{1,0},{2,3},{3,2},{4,5},{5,4},{6,7},{7,6},{8,9},{9,8},{10,11... | collective-permute-start | bytes 12582920 | tf_op jit(solution)/shard_map/ppermute | solution.py:34
  544.9 342.2 %reduce-scatter.14.cloned.1.call-start = ((), (), s32[]{:S(2)}) async-start(), calls=%async_computation.13 | async-start | bytes 3932160 | tf_op jit(solution)/shard_map/reduce_scatter | solution.py:210
  573.3 49.2 %collective-permute-start.44 = (bf16[256,2048]{1,0:T(8,128)(2,1)}, bf16[256,2048]{1,0:T(8,128)(2,1)S(1)}, u32[]{:S(2)}, u32[]{:S(2)}) collective-permute-start(bf16[256,2048]{1,0:T(8,128)(2,1)} %get-tuple-element.174), channel_id=1, source_target_pairs={{0,2},{2,0},{4,6},{6,4},{1,3},{3,1},{5,7},{7,5},{8,10},{10,8},{12,... | collective-permute-start | bytes 3145736 | tf_op jit(solution)/shard_map/ppermute | solution.py:39
  574.6 49.2 %collective-permute-start.46 = (bf16[256,2048]{1,0:T(8,128)(2,1)}, bf16[256,2048]{1,0:T(8,128)(2,1)}, u32[]{:S(2)}, u32[]{:S(2)}) collective-permute-start(bf16[256,2048]{1,0:T(8,128)(2,1)} %get-tuple-element.175), channel_id=1, source_target_pairs={{0,6},{2,4},{4,2},{6,0},{1,7},{3,5},{5,3},{7,1},{8,14},{10,12},{12... | collective-permute-start | bytes 3145736 | tf_op jit(solution)/shard_map/ppermute | solution.py:39
  576.0 47.8 %collective-permute-start.45 = (bf16[256,2048]{1,0:T(8,128)(2,1)}, bf16[256,2048]{1,0:T(8,128)(2,1)}, u32[]{:S(2)}, u32[]{:S(2)}) collective-permute-start(bf16[256,2048]{1,0:T(8,128)(2,1)} %get-tuple-element.176), channel_id=1, source_target_pairs={{0,4},{2,6},{4,0},{6,2},{1,5},{3,7},{5,1},{7,3},{8,12},{10,14},{12... | collective-permute-start | bytes 3145736 | tf_op jit(solution)/shard_map/ppermute | solution.py:39
  592.3 73.6 %collective-permute-start.36 = (bf16[256,2048]{1,0:T(8,128)(2,1)}, bf16[256,2048]{1,0:T(8,128)(2,1)}, u32[]{:S(2)}, u32[]{:S(2)}) collective-permute-start(bf16[256,2048]{1,0:T(8,128)(2,1)} %get-tuple-element.177), channel_id=1, source_target_pairs={{0,2},{2,0},{4,6},{6,4},{1,3},{3,1},{5,7},{7,5},{8,10},{10,8},{12,... | collective-permute-start | bytes 3145736 | tf_op jit(solution)/shard_map/ppermute | solution.py:39
  593.7 72.3 %collective-permute-start.38 = (bf16[256,2048]{1,0:T(8,128)(2,1)}, bf16[256,2048]{1,0:T(8,128)(2,1)}, u32[]{:S(2)}, u32[]{:S(2)}) collective-permute-start(bf16[256,2048]{1,0:T(8,128)(2,1)} %get-tuple-element.178), channel_id=1, source_target_pairs={{0,6},{2,4},{4,2},{6,0},{1,7},{3,5},{5,3},{7,1},{8,14},{10,12},{12... | collective-permute-start | bytes 3145736 | tf_op jit(solution)/shard_map/ppermute | solution.py:39
  738.3 139.1 %collective-permute-start.62 = (bf16[2,16,320]{2,1,0:T(8,128)(2,1)}, bf16[2,16,320]{2,1,0:T(8,128)(2,1)}, u32[]{:S(2)}, u32[]{:S(2)}) collective-permute-start(bf16[2,16,320]{2,1,0:T(8,128)(2,1)} %get-tuple-element.269), channel_id=1, source_target_pairs={{0,1},{1,0},{2,3},{3,2},{4,5},{5,4},{6,7},{7,6},{8,9},{9,8},{10,11... | collective-permute-start | bytes 61448 | tf_op jit(solution)/shard_map/ppermute | solution.py:34
  748.7 148.8 %reduce-scatter.8.cloned.1.call-start = ((), (), s32[]{:S(2)}) async-start(), calls=%async_computation.10 | async-start | bytes 307200 | tf_op jit(solution)/shard_map/reduce_scatter | solution.py:210
  792.6 51.8 %collective-permute-start.71 = (bf16[2,80,2048]{2,1,0:T(8,128)(2,1)}, bf16[2,80,2048]{2,1,0:T(8,128)(2,1)}, u32[]{:S(2)}, u32[]{:S(2)}) collective-permute-start(bf16[2,80,2048]{2,1,0:T(8,128)(2,1)} %dynamic-slice_bitcast_fusion.3), channel_id=1, source_target_pairs={{0,1},{1,0},{2,3},{3,2},{4,5},{5,4},{6,7},{7,6},{8,9},{9,8},{10,11... | collective-permute-start | bytes 1966088 | tf_op jit(solution)/shard_map/ppermute | solution.py:34
  844.3 114.8 %reduce-scatter.10.cloned.1.call-start = ((), (), s32[]{:S(2)}) async-start(), calls=%async_computation.11 | async-start | bytes 1638400 | tf_op jit(solution)/shard_map/reduce_scatter | solution.py:210
  847.1 113.9 %reduce-scatter.6.cloned.1.call-start = ((), (), s32[]{:S(2)}) async-start(), calls=%async_computation.9 | async-start | bytes 3276800 | tf_op jit(solution)/shard_map/reduce_scatter | solution.py:210
  864.5 54.4 %collective-permute-start.55 = (bf16[4,256,2048]{2,1,0:T(8,128)(2,1)}, bf16[4,256,2048]{2,1,0:T(8,128)(2,1)}, u32[]{:S(2)}, u32[]{:S(2)}) collective-permute-start(bf16[4,256,2048]{2,1,0:T(8,128)(2,1)} %bitcast.138), channel_id=1, source_target_pairs={{0,1},{1,0},{2,3},{3,2},{4,5},{5,4},{6,7},{7,6},{8,9},{9,8},{10,11... | collective-permute-start | bytes 12582920 | tf_op jit(solution)/shard_map/ppermute | solution.py:34
  931.0 45.7 %collective-permute-start.56 = (bf16[256,2048]{1,0:T(8,128)(2,1)}, bf16[256,2048]{1,0:T(8,128)(2,1)}, u32[]{:S(2)}, u32[]{:S(2)}) collective-permute-start(bf16[256,2048]{1,0:T(8,128)(2,1)} %get-tuple-element.171), channel_id=1, source_target_pairs={{0,2},{2,0},{4,6},{6,4},{1,3},{3,1},{5,7},{7,5},{8,10},{10,8},{12,... | collective-permute-start | bytes 3145736 | tf_op jit(solution)/shard_map/ppermute | solution.py:39
  (181 other events, 2602.4 us)
Sparse Core Ops, SparseCore 0:
  20.6 38.1 all-gather.6
  111.4 52.0 all-gather.4
  254.1 113.7 all-gather.8
  401.1 61.4 all-gather.10
  545.0 109.3 reduce-scatter.11
  748.8 62.3 reduce-scatter.13
  844.4 22.2 reduce-scatter.7
  869.2 29.4 reduce-scatter.9
  901.1 50.8 reduce-scatter.5

commit v2 on v1

--- a/solution.py
+++ b/solution.py
@@ -39,11 +39,6 @@
     return lax.ppermute(value, ("b", "n"), [(i, i ^ k) for i in range(size)])
 
 
-def xor_stream(value, k):
-    size = lax.axis_size("n") * lax.axis_size("c")
-    return lax.ppermute(value, ("n", "c"), [(i, i ^ k) for i in range(size)])
-
-
 def shift_a(value, by):
     size = lax.axis_size("a")
     return lax.ppermute(value, "a", [(i, i + by) for i in range(size) if 0 <= i + by < size])
@@ -65,18 +60,6 @@
 def plane_gather(value):
     mine = jnp.stack([value] + [xor_u(value, k) for k in range(1, chips())])
     return jnp.concatenate([mine, swap_c(mine)])
-
-
-def plane_scatter(parts):
-    count = chips()
-    parts = parts.reshape((2, count, -1) + parts.shape[1:])
-    got = swap_c(parts[1].astype(BF))
-    summed = parts[0].astype(F32) + got.astype(F32)
-    low = summed.astype(BF)
-    total = summed[0]
-    for k in range(1, count):
-        total = total + xor_u(low[k], k).astype(F32)
-    return total
 
 
 def exchange(pieces):
@@ -95,10 +78,491 @@
     return jnp.stack([pick(rel, u ^ q, 1) for q in range(chips())], 1)
 
 
-def scan_kernel(reverse, a_ref, b_ref, p_ref, s_ref):
-    blocks, rows, width = a_ref.shape
+MESH = pl.DeviceIdType.MESH
+VMEM_LIMIT = 60 * 1024 * 1024
+
+
+def places():
+    return tuple(lax.axis_index(name) for name in ("a", "b", "n", "c"))
+
+
+def neighbours():
+    a, b, n, c = places()
+    return (a, 1 - b, n, c), (a, b, 1 - n, c), (a, b, n, 1 - c)
+
+
+def greet(peers):
+    barrier = pltpu.get_barrier_semaphore()
+    for peer in peers:
+        pl.semaphore_signal(barrier, inc=1, device_id=peer, device_id_type=MESH)
+    pl.semaphore_wait(barrier, len(peers))
+
+
+class Mover:
+    def __init__(self, send, recv):
+        self.send, self.recv, self.made = send, recv, {}
+        self.names = []
+
+    def copy(self, name, src, dst, peer):
+        if name not in self.names:
+            self.names.append(name)
+        at = self.names.index(name)
+        made = pltpu.make_async_remote_copy(
+            src_ref=src,
+            dst_ref=dst,
+            send_sem=self.send.at[at],
+            recv_sem=self.recv.at[at],
+            device_id=peer,
+            device_id_type=MESH,
+        )
+        self.made[name] = made
+        return made
+
+    def start(self, name, src, dst, peer):
+        self.copy(name, src, dst, peer).start()
+
+    def arrived(self, name):
+        self.made[name].wait_recv()
+
+    def sent(self):
+        for made in self.made.values():
+            made.wait_send()
+
+
+def gather_plane_start(move, mine, everyone, h, half_rows):
+    x, y, z = neighbours()
+    at = pl.ds(h * half_rows, half_rows)
+    move.start(f"gx{h}", mine.at[at], everyone.at[2, at], x)
+    move.start(f"gy{h}", mine.at[at], everyone.at[1, at], y)
+    move.start(f"gc{h}", mine.at[at], everyone.at[4, at], z)
+
+
+def gather_plane_rest(move, everyone, half_rows, stage=None):
+    x, y, z = neighbours()
+    rows = [pl.ds(h * half_rows, half_rows) for h in range(2)]
+
+    def on(name, k, h):
+        move.start(name, everyone.at[k, rows[h]], everyone.at[4 + k, rows[h]], z)
+
+    if stage in (None, 0):
+        move.arrived("gx0")
+        move.start("fy", everyone.at[2, rows[0]], everyone.at[3, rows[0]], y)
+        on("cx0", 2, 0)
+        move.arrived("gy1")
+        move.start("fx", everyone.at[1, rows[1]], everyone.at[3, rows[1]], x)
+        on("cy1", 1, 1)
+    if stage in (None, 1):
+        move.arrived("gx1")
+        on("cx1", 2, 1)
+        move.arrived("gy0")
+        on("cy0", 1, 0)
+    if stage in (None, 2):
+        move.arrived("fy")
+        on("cd0", 3, 0)
+        move.arrived("fx")
+        on("cd1", 3, 1)
+        for name in ("gc0", "gc1", "cx0", "cx1", "cy0", "cy1", "cd0", "cd1"):
+            move.arrived(name)
+
+
+GATHER_COPIES = 14
+
+
+def reduce_kernel(nt, post, waits, x_hbm, w_hbm, *refs):
+    gain_ref, first_ref, second_ref = refs[:3]
+    out_ref, refs = refs[3 + waits], refs[4 + waits :]
+    if post == "last":
+        everyone = mine = None
+    else:
+        everyone, refs = refs[0], refs[1:]
+        mine, refs = refs[0], refs[1:]
+    x_v, w_v, away_s, away_r, acc, out_b, in_b, local, send, recv = refs
+    rows, d_model = acc.shape[1:]
+    half = rows // 2
+    tile = min(512, d_model)
+    px, py, pc = neighbours()
+    move = Mover(send, recv)
+
+    w_copy = pltpu.make_async_copy(w_hbm, w_v, local.at[8])
+    w_copy.start()
+    loads = {}
+    for i, (k, kc) in enumerate((k, kc) for k in (3, 2, 1, 0) for kc in (1, 0)):
+        loads[kc, k] = pltpu.make_async_copy(x_hbm.at[kc, k], x_v.at[kc, k], local.at[i])
+        loads[kc, k].start()
+    greet((px, py, pc))
+    w_copy.wait()
+
+    def product(kc, k, t):
+        at = pl.ds(pl.multiple_of(t * tile, tile), tile)
+        if nt:
+            return at, ndot(x_v[kc, k], w_v[at, :])
+        return at, mdot(x_v[kc, k], w_v[:, at])
+
+    step = min(32, half)
+
+    def by_rows(h, body):
+        @pl.loop(0, half // step)
+        def _(i):
+            body(pl.ds(pl.multiple_of(i * step, step), step),
+                 pl.ds(pl.multiple_of(h * half + i * step, step), step))
+
+    def hand_on(name, slot, k, h, peer, extra=None):
+        def body(inner, outer):
+            value = acc[k, outer, :]
+            if extra is not None:
+                value = value + in_b[extra, inner, :].astype(F32)
+            out_b[slot, inner, :] = value.astype(BF)
+
+        by_rows(h, body)
+        move.start(name, out_b.at[slot], in_b.at[slot], peer)
+
+    for k in (3, 2, 1, 0):
+        loads[1, k].wait()
+
+        @pl.loop(0, d_model // tile)
+        def _(t):
+            at, value = product(1, k, t)
+            away_s[k, :, at] = value.astype(BF)
+
+        move.start(f"away{k}", away_s.at[k], away_r.at[k], pc)
+        loads[0, k].wait()
+
+        @pl.loop(0, d_model // tile)
+        def _(t):
+            at, value = product(0, k, t)
+            acc[k, :, at] = value
+
+        move.arrived(f"away{k}")
+        for h in range(2):
+            def add(inner, outer):
+                acc[k, outer, :] += away_r[k, outer, :].astype(F32)
+
+            by_rows(h, add)
+        if k == 3:
+            hand_on("d0", 0, 3, 0, px)
+            hand_on("d1", 1, 3, 1, py)
+        elif k == 2:
+            hand_on("x0", 2, 2, 0, px)
+        elif k == 1:
+            hand_on("y1", 5, 1, 1, py)
+    move.arrived("d0")
+    hand_on("y0", 4, 1, 0, py, 0)
+    move.arrived("d1")
+    hand_on("x1", 3, 2, 1, px, 1)
+
+    for h in range(2):
+        move.arrived(f"x{h}")
+        move.arrived(f"y{h}")
+
+        def body(inner, outer):
+            total = acc[0, outer, :]
+            total = total + in_b[2 + h, inner, :].astype(F32)
+            total = total + in_b[4 + h, inner, :].astype(F32)
+            gain = gain_ref[...]
+            if post == "fwd":
+                value = first_ref[outer, :].astype(F32) + total
+                out_ref[outer, :] = value
+                factor = lax.rsqrt(jnp.mean(value * value, axis=-1, keepdims=True) + EPS)
+                mine[outer, :] = (value * factor * gain).astype(BF)
+                return
+            value = second_ref[outer, :] if post == "mid" else first_ref[outer, :].astype(F32)
+            base = first_ref[outer, :].astype(F32) if post == "mid" else second_ref[outer, :]
+            factor = lax.rsqrt(jnp.mean(value * value, axis=-1, keepdims=True) + EPS)
+            weighted = total * gain
+            inner_mean = jnp.mean(weighted * value, axis=-1, keepdims=True)
+            grad = base + factor * weighted - value * (factor * factor * factor * inner_mean)
+            if post == "mid":
+                out_ref[outer, :] = grad
+                mine[outer, :] = grad.astype(BF)
+            else:
+                out_ref[outer, :] = grad.astype(BF)
+
+        by_rows(h, body)
+        if everyone is not None:
+            gather_plane_start(move, mine, everyone, h, half)
+    if everyone is not None:
+        own = pltpu.make_async_copy(mine, everyone.at[0], local.at[9])
+        own.start()
+        gather_plane_rest(move, everyone, half)
+        own.wait()
+    move.sent()
+
+
+def plane_reduce(ident, post, nt, x, w, gain, first, second, done=()):
+    rows, d_model = first.shape
+    vmem = pl.BlockSpec(memory_space=pltpu.VMEM)
+    hbm = pl.BlockSpec(memory_space=pl.ANY)
+    out_type = BF if post == "last" else F32
+    out_shape = [jax.ShapeDtypeStruct((rows, d_model), out_type)]
+    out_specs = [vmem]
+    scratch = []
+    copies = 10
+    if post != "last":
+        out_shape.append(jax.ShapeDtypeStruct((8, rows, d_model), BF))
+        out_specs.append(hbm)
+        scratch.append(pltpu.VMEM((rows, d_model), BF))
+        copies += GATHER_COPIES
+    scratch += [
+        pltpu.VMEM(x.shape, BF),
+        pltpu.VMEM(w.shape, BF),
+        pltpu.VMEM((4, rows, d_model), BF),
+        pltpu.VMEM((4, rows, d_model), BF),
+        pltpu.VMEM((4, rows, d_model), F32),
+        pltpu.VMEM((6, rows // 2, d_model), BF),
+        pltpu.VMEM((6, rows // 2, d_model), BF),
+        pltpu.SemaphoreType.DMA((10,)),
+        pltpu.SemaphoreType.DMA((copies,)),
+        pltpu.SemaphoreType.DMA((copies,)),
+    ]
+    return pl.pallas_call(
+        functools.partial(reduce_kernel, nt, post, len(done)),
+        in_specs=[hbm, hbm, vmem, vmem, vmem] + [hbm] * len(done),
+        out_specs=out_specs,
+        out_shape=out_shape,
+        scratch_shapes=scratch,
+        compiler_params=pltpu.CompilerParams(
+            collective_id=ident, has_side_effects=True, vmem_limit_bytes=VMEM_LIMIT
+        ),
+        cost_estimate=pl.CostEstimate(
+            flops=2 * x.size * d_model, bytes_accessed=2 * (x.size + w.size), transcendentals=0
+        ),
+        name=f"plane_reduce_{post}",
+    )(x, w, gain.reshape(1, -1), first, second, *done)
+
+
+def start_kernel(
+    tokens_ref, yx_ref, gu_ref, rows_ref, vec_ref, stream_ref,
+    tok_out, yx_out, gu_out, rows_out, halves_out, vec_out, stream_out,
+    local, send, recv,
+):
+    a, b, n, c = places()
+    planes = yx_out.shape[0]
+    u = b * 2 + n
+    p = u * 2 + c
+    px, py, pc = neighbours()
+    plane_peers = {}
+    for kc in range(2):
+        for k in range(4):
+            if (kc, k) != (0, 0):
+                b2 = 1 - b if k & 2 else b
+                n2 = 1 - n if k & 1 else n
+                plane_peers[kc, k] = (a, b2, n2, 1 - c if kc else c)
+    up, down = (a + 1, b, n, c), (a - 1, b, n, c)
+
+    barrier = pltpu.get_barrier_semaphore()
+    for peer in plane_peers.values():
+        pl.semaphore_signal(barrier, inc=1, device_id=peer, device_id_type=MESH)
+
+    @pl.when(a < planes - 1)
+    def _():
+        pl.semaphore_signal(barrier, inc=1, device_id=up, device_id_type=MESH)
+
+    @pl.when(a > 0)
+    def _():
+        pl.semaphore_signal(barrier, inc=1, device_id=down, device_id_type=MESH)
+
+    others = len(plane_peers) + jnp.minimum(planes - 1 - a, 1) + jnp.minimum(a, 1)
+    pl.semaphore_wait(barrier, others)
+
+    move = Mover(send, recv)
+    half = tokens_ref.shape[0] // 2
+    locals_ = []
+
+    def keep(i, src, dst):
+        made = pltpu.make_async_copy(src, dst, local.at[i])
+        made.start()
+        return made
+
+    def to_owners(name, pieces, out):
+        for (kc, k), peer in plane_peers.items():
+            owner = (u ^ k) * 2 + (1 - c if kc else c)
+            move.start(f"{name}{kc}{k}", pieces.at[owner], out.at[a, p], peer)
+
+    chains = {}
+
+    def chain_step(name, out, s):
+        def up_copy(block):
+            return move.copy(f"{name}u{s}", out.at[block], out.at[block], up)
+
+        def down_copy(block):
+            return move.copy(f"{name}d{s}", out.at[block], out.at[block], down)
+
+        sends_up, sends_down = (a < planes - 1) & (a >= s), (a > 0) & (a + s < planes)
+
+        @pl.when(sends_up)
+        def _():
+            up_copy(a - s).start()
+
+        @pl.when(sends_down)
+        def _():
+            down_copy(a + s).start()
+
+        chains[name, s] = (up_copy, down_copy, sends_up, sends_down)
+
+    def chain_arrived(name, s):
+        up_copy, down_copy, _, _ = chains[name, s]
+
+        @pl.when(a - 1 >= s)
+        def _():
+            up_copy(a - 1 - s).wait_recv()
+
+        @pl.when(a + 1 + s < planes)
+        def _():
+            down_copy(a + 1 + s).wait_recv()
+
+    def chain_sent(name, s):
+        up_copy, down_copy, sends_up, sends_down = chains[name, s]
+
+        @pl.when(sends_up)
+        def _():
+            up_copy(a - s).wait_send()
+
+        @pl.when(sends_down)
+        def _():
+            down_copy(a + s).wait_send()
+
+    to_owners("yx", yx_ref, yx_out)
+    for (kc, k), peer in plane_peers.items():
+        move.start(f"vec{kc}{k}", vec_ref, vec_out.at[a, p], peer)
+    own_yx = keep(1, yx_ref.at[p], yx_out.at[a, p])
+    own_vec = keep(2, vec_ref, vec_out.at[a, p])
+    own_rows = keep(0, rows_ref, rows_out.at[a])
+    own_gu = keep(3, gu_ref.at[p], gu_out.at[p])
+    own_tok = keep(4, tokens_ref, tok_out.at[0])
+    own_stream = keep(5, stream_ref, stream_out.at[0, 0])
+    own_yx.wait()
+    own_vec.wait()
+    for kc, k in plane_peers:
+        move.arrived(f"yx{kc}{k}")
+        move.arrived(f"vec{kc}{k}")
+    own_rows.wait()
+    outs = (("yx", yx_out), ("vec", vec_out), ("rows", rows_out))
+    for name, out in outs:
+        chain_step(name, out, 0)
+    for h in range(2):
+        gather_plane_start(move, tokens_ref, tok_out, h, half)
+    gather_plane_rest(move, tok_out, half, 0)
+    for kc in range(2):
+        for kn in range(2):
+            if (kc, kn) != (0, 0):
+                move.start(f"st{kc}{kn}", stream_ref, stream_out.at[kc, kn], plane_peers[kc, kn])
+    for name, out in outs:
+        chain_arrived(name, 0)
+        chain_step(name, out, 1)
+    gather_plane_rest(move, tok_out, half, 1)
+    for (kc, k), peer in plane_peers.items():
+        owner = (u ^ k) * 2 + (1 - c if kc else c)
+        move.start(f"gu{kc}{k}", gu_ref.at[owner], gu_out.at[p], peer)
+    for s in range(1, planes - 1):
+        for name, out in outs:
+            chain_arrived(name, s)
+            if s + 1 < planes - 1:
+                chain_step(name, out, s + 1)
+    gather_plane_rest(move, tok_out, half, 2)
+    each = planes // 2
+    swap = pltpu.make_async_remote_copy(
+        src_ref=rows_out.at[pl.ds((1 - c) * each, each)],
+        dst_ref=halves_out.at[:, c],
+        send_sem=send.at[send.shape[0] - 1],
+        recv_sem=recv.at[recv.shape[0] - 1],
+        device_id=pc,
+        device_id_type=MESH,
+    )
+    swap.start()
+    own_halves = keep(6, rows_out.at[pl.ds(c * each, each)], halves_out.at[:, c])
+    for kc, k in plane_peers:
+        move.arrived(f"gu{kc}{k}")
+    for kc in range(2):
+        for kn in range(2):
+            if (kc, kn) != (0, 0):
+                move.arrived(f"st{kc}{kn}")
+    for made in (own_gu, own_tok, own_stream, own_halves):
+        made.wait()
+    swap.wait()
+    for name, s in chains:
+        chain_sent(name, s)
+    for name in [n for n in move.names if not any(n == f"{w}{d}{s}" for w, s in chains for d in "ud")]:
+        move.made[name].wait_send()
+
+
+def start_exchange(tokens, yx, gu, mixer_rows, vec, stream):
+    planes = lax.axis_size("a")
+    hbm = pl.BlockSpec(memory_space=pl.ANY)
+    shapes = [
+        ((8,) + tokens.shape, BF),
+        ((planes,) + yx.shape, BF),
+        (gu.shape, BF),
+        ((planes,) + mixer_rows.shape, BF),
+        ((planes // 2, 2) + mixer_rows.shape, BF),
+        ((planes, 8) + vec.shape, F32),
+        ((2, 2) + stream.shape, F32),
+    ]
+    copies = 7 * 3 + 3 + GATHER_COPIES + 6 * (planes - 1) + 1
+    return pl.pallas_call(
+        start_kernel,
+        in_specs=[hbm] * 6,
+        out_specs=[hbm] * 7,
+        out_shape=[jax.ShapeDtypeStruct(*s) for s in shapes],
+        scratch_shapes=[
+            pltpu.SemaphoreType.DMA((7,)),
+            pltpu.SemaphoreType.DMA((copies,)),
+            pltpu.SemaphoreType.DMA((copies,)),
+        ],
+        compiler_params=pltpu.CompilerParams(
+            collective_id=1, has_side_effects=True, vmem_limit_bytes=VMEM_LIMIT
+        ),
+        cost_estimate=pl.CostEstimate(flops=0, bytes_accessed=100 << 20, transcendentals=0),
+        name="start_exchange",
+    )(tokens, yx, gu, mixer_rows, vec, stream)
+
+
+def norm_product_kernel(info, tok_ref, w_ref, gain_ref, n_ref, gate_ref, lin_ref):
+    rows, d_model = tok_ref.shape[1:]
+    step = min(64, rows)
+
+    @pl.loop(0, rows // step)
+    def _(i):
+        at = pl.ds(pl.multiple_of(i * step, step), step)
+        value = tok_ref[0, at, :].astype(F32)
+        factor = lax.rsqrt(jnp.mean(value * value, axis=-1, keepdims=True) + EPS)
+        n_ref[0, at, :] = (value * factor * gain_ref[...]).astype(BF)
+
+    wide = gate_ref.shape[2]
+    both = mdot(n_ref[0], w_ref[...])
+    gate_ref[0] = both[:, :wide]
+    lin_ref[0] = both[:, wide:].astype(BF)
+
+
+def row_places(info, rows, nseq):
+    i = pl.program_id(0)
+    pos = info[i, 0] + lax.broadcasted_iota(jnp.int32, (rows, 1), 0)
+    begin = jnp.zeros((rows, 1), jnp.int32) + info[i, 1]
+    seg = jnp.zeros((rows, 1), jnp.int32)
+    for s in range(1, nseq):
+        begin = jnp.where(pos >= info[i, 1 + s], info[i, 1 + s], begin)
+        seg = jnp.where(pos >= info[i, 1 + s], s, seg)
+    return pos, begin, seg
+
+
+def inputs_by_tap(ext, lin_ref, rim_ref, conv0_ref, begin_at, seg, taps):
+    rows = lin_ref.shape[1]
+    back = taps - 1
+    ext[0:8, :] = rim_ref[0]
+    ext[8 : 8 + rows, :] = lin_ref[0].astype(F32)
+    slots = conv0_ref.shape[1]
+    column = lax.broadcasted_iota(jnp.int32, (rows, slots), 1)
+    found = [ext[8 : 8 + rows, :]]
+    for k in range(1, taps):
+        hot = (column == seg * back + begin_at - k + back) & (begin_at < k)
+        stored = mdot(jnp.where(hot, 1.0, 0.0).astype(BF), conv0_ref[0])
+        found.append(jnp.where(begin_at >= k, ext[8 - k : 8 - k + rows, :], stored))
+    return found
+
+
+def run_scan(a_s, b_s, p_ref, s_ref, rows, reverse):
+    width = b_s.shape[1]
     groups = rows // 8
-    row = lax.broadcasted_iota(jnp.int32, (blocks, 8, width), 1)
+    row = lax.broadcasted_iota(jnp.int32, (8, width), 0)
     if reverse:
         row = 7 - row
 
@@ -106,38 +570,176 @@
         cp, cs = carry
         g = groups - 1 - i if reverse else i
         at = pl.ds(pl.multiple_of(g * 8, 8), 8)
-        a, b = a_ref[:, at, :], b_ref[:, at, :]
+        a, b = a_s[at, :], b_s[at, :]
         for d in (1, 2, 4):
             by = 8 - d if reverse else d
             inside = row >= d
-            a_far = jnp.where(inside, pltpu.roll(a, by, 1), 1.0)
-            b_far = jnp.where(inside, pltpu.roll(b, by, 1), 0.0)
+            a_far = jnp.where(inside, pltpu.roll(a, by, 0), 1.0)
+            b_far = jnp.where(inside, pltpu.roll(b, by, 0), 0.0)
             b = a * b_far + b
             a = a * a_far
         b = a * cs + b
         a = a * cp
-        p_ref[:, at, :] = a
-        s_ref[:, at, :] = b
+        p_ref[0, at, :] = a
+        s_ref[0, at, :] = b
         last = 0 if reverse else 7
-        return a[:, last : last + 1], b[:, last : last + 1]
-
-    start = (jnp.ones((blocks, 1, width), F32), jnp.zeros((blocks, 1, width), F32))
-    lax.fori_loop(0, groups, step, start)
-
-
-def scan(a, b, reverse):
-    blocks, rows, width = a.shape
-    per = 4
-    spec = pl.BlockSpec((per, rows, width), lambda i: (i, 0, 0))
+        return a[last : last + 1], b[last : last + 1]
+
+    start = (jnp.ones((1, width), F32), jnp.zeros((1, width), F32))
+    lax.fori_loop(0, groups, step, start, unroll=4)
+
+
+V_CBIAS, V_ABIAS, V_IBIAS, V_SOFT = 0, 1, 2, 3
+
+
+def forward_kernel(
+    nseq, taps, info, lin_ref, rim_ref, conv0_ref, state0_ref, wg_ref, vec_ref,
+    conv_ref, retain_ref, admit_ref, p_ref, s_ref, ext, a_s, b_s,
+):
+    i = pl.program_id(0)
+    rows, wide = lin_ref.shape[1:]
+    pos, begin, seg = row_places(info, rows, nseq)
+    at = pos - begin
+
+    def vec(k):
+        return vec_ref[k : k + 1, :]
+
+    by_tap = inputs_by_tap(ext, lin_ref, rim_ref, conv0_ref, at, seg, taps)
+    total = vec(taps + V_CBIAS)
+    for k in range(taps):
+        total = total + vec(k) * by_tap[k]
+    low = total.astype(BF)
+    conv_ref[0] = low
+    conv = low.astype(F32)
+    both = mdot(low, wg_ref[...])
+    retain = jax.nn.sigmoid(both[:, :wide] + vec(taps + V_ABIAS))
+    admit = jax.nn.sigmoid(both[:, wide:] + vec(taps + V_IBIAS))
+    retain_ref[0] = retain
+    admit_ref[0] = admit
+    a = jnp.exp(-8.0 * retain * vec(taps + V_SOFT))
+    mult = jnp.sqrt(jnp.maximum((1.0 - a) * (1.0 + a), FLOOR))
+    drive = mult * admit * conv
+    for s in range(nseq):
+        drive = drive + jnp.where(pos == info[i, 1 + s], a * state0_ref[0, s : s + 1, :], 0.0)
+    a_s[...] = jnp.where(at == 0, 0.0, a)
+    b_s[...] = drive
+    run_scan(a_s, b_s, p_ref, s_ref, rows, False)
+
+
+def gelu_pair(x):
+    root = 0.7978845608028654
+    inner = root * (x + 0.044715 * (x * x * x))
+    th = jnp.tanh(inner)
+    cdf = 0.5 * (1.0 + th)
+    slope = cdf + 0.5 * x * (1.0 - th * th) * (root * (1.0 + 3.0 * 0.044715 * (x * x)))
+    return x * cdf, slope
+
+
+def back_scan_kernel(
+    nseq, taps, info, dres_ref, wo_ref, gate_ref, hidden_ref, retain_ref, vec_ref, *refs
+):
+    dgate_ref, p_ref, s_ref, head_ref, ext, a_s, b_s = refs[-7:]
+    rows = gate_ref.shape[1]
+    pos, begin, _ = row_places(info, rows, nseq)
+    d_mixed = ndot(dres_ref[0], wo_ref[...])
+    gelu, slope = gelu_pair(gate_ref[0])
+    dgate_ref[0] = (d_mixed * hidden_ref[0] * slope).astype(BF)
+    b_s[...] = d_mixed * gelu
+    soft = vec_ref[taps + V_SOFT : taps + V_SOFT + 1, :]
+    a = jnp.where(pos == begin, 0.0, jnp.exp(-8.0 * retain_ref[0] * soft))
+    ext[0:rows, :] = a
+    ext[rows : rows + 8, :] = jnp.ones((8, a.shape[1]), F32)
+    head_ref[0] = ext[0:8, :]
+    a_s[...] = ext[1 : rows + 1, :]
+    run_scan(a_s, b_s, p_ref, s_ref, rows, True)
+
+
+def back_kernel(
+    nseq, taps, info, p_ref, s_ref, grad_in_ref, hidden_ref, state_in_ref, state0_ref, conv_ref,
+    retain_ref, admit_ref, lin_ref, rim_ref, conv0_ref, wg_ref, vec_ref, *refs
+):
+    dconv_ref, wgrad_ref, vgrad_ref, ext = refs[-4:]
+    i = pl.program_id(0)
+    rows, wide = lin_ref.shape[1:]
+    pos, begin, seg = row_places(info, rows, nseq)
+    at = pos - begin
+    conv_low = conv_ref[0]
+    conv = conv_low.astype(F32)
+    retain, admit = retain_ref[0], admit_ref[0]
+    soft = vec_ref[taps + V_SOFT : taps + V_SOFT + 1, :]
+    e = p_ref[0] * grad_in_ref[0, 0:1, :] + s_ref[0]
+    ext[0:8, :] = jnp.broadcast_to(state_in_ref[0], (8, wide))
+    ext[8 : 8 + rows, :] = hidden_ref[0]
+    previous = ext[7 : 7 + rows, :]
+    for s in range(nseq):
+        previous = jnp.where(pos == info[i, 1 + s], state0_ref[0, s : s + 1, :], previous)
+    a = jnp.exp(-8.0 * retain * soft)
+    spread = (1.0 - a) * (1.0 + a)
+    mult = jnp.sqrt(jnp.maximum(spread, FLOOR))
+    d_mult = e * admit * conv
+    d_spread = jnp.where(spread > FLOOR, d_mult * 0.5 / mult, 0.0)
+    d_log = e * previous * a - 2.0 * a * a * d_spread
+    d_rate = (d_log * (-8.0 * soft) * retain * (1.0 - retain)).astype(BF)
+    d_inflow = (e * mult * conv * admit * (1.0 - admit)).astype(BF)
+    d_gates = jnp.concatenate([d_rate, d_inflow], 1)
+    d_conv = e * mult * admit + ndot(d_gates, wg_ref[...])
+    low = d_conv.astype(BF)
+    dconv_ref[0] = low
+    low = low.astype(F32)
+
+    @pl.when(i == 0)
+    def _():
+        wgrad_ref[...] = jnp.zeros_like(wgrad_ref)
+        vgrad_ref[...] = jnp.zeros_like(vgrad_ref)
+
+    wgrad_ref[...] += tdot(conv_low, d_gates)
+    sums = [low * v for v in inputs_by_tap(ext, lin_ref, rim_ref, conv0_ref, at, seg, taps)]
+    sums += [low, d_rate.astype(F32), d_inflow.astype(F32), d_log * (-8.0 * retain)]
+    for k, value in enumerate(sums):
+        vgrad_ref[k : k + 1, :] += jnp.sum(value, axis=0, keepdims=True)
+
+
+def back_conv_kernel(nseq, taps, info, dconv_ref, rim_ref, dgate_ref, vec_ref, out_ref, ext):
+    i = pl.program_id(0)
+    rows, wide = dconv_ref.shape[1:]
+    pos = info[i, 0] + lax.broadcasted_iota(jnp.int32, (rows, 1), 0)
+    ext[0:rows, :] = dconv_ref[0].astype(F32)
+    ext[rows : rows + 8, :] = rim_ref[0]
+    total = vec_ref[0:1, :] * ext[0:rows, :]
+    for k in range(1, taps):
+        cut = jnp.zeros((rows, 1), jnp.int32)
+        for s in range(nseq):
+            start = info[i, 1 + s]
+            cut = jnp.where((pos < start) & (pos + k >= start), 1, cut)
+        total = total + vec_ref[k : k + 1, :] * jnp.where(cut == 0, ext[k : k + rows, :], 0.0)
+    out_ref[0, :, :wide] = dgate_ref[0]
+    out_ref[0, :, wide:] = total.astype(BF)
+
+
+def by_block(body, info, ins, outs, scratch, done=(), name=None, cost=None):
+    blocks = info.shape[0]
+
+    def spec(shape, blocked):
+        zeros = (0,) * (len(shape) - 1)
+        if blocked:
+            return pl.BlockSpec((1,) + tuple(shape[1:]), lambda i, *_: (i,) + zeros)
+        return pl.BlockSpec(tuple(shape), lambda i, *_: (0,) + zeros)
+
+    hbm = pl.BlockSpec(memory_space=pl.ANY)
     return pl.pallas_call(
-        functools.partial(scan_kernel, reverse),
-        grid=(blocks // per,),
-        in_specs=[spec, spec],
-        out_specs=[spec, spec],
-        out_shape=[jax.ShapeDtypeStruct(a.shape, F32)] * 2,
-        compiler_params=pltpu.CompilerParams(vmem_limit_bytes=48 * 1024 * 1024),
-        name="scan",
-    )(a, b)
+        body,
+        grid_spec=pltpu.PrefetchScalarGridSpec(
+            num_scalar_prefetch=1,
+            grid=(blocks,),
+            in_specs=[spec(v.shape, blocked) for v, blocked in ins] + [hbm] * len(done),
+            out_specs=[spec(shape, blocked) for shape, _, blocked in outs],
+            scratch_shapes=[pltpu.VMEM(shape, F32) for shape in scratch],
+        ),
+        out_shape=[jax.ShapeDtypeStruct(shape, kind) for shape, kind, _ in outs],
+        compiler_params=pltpu.CompilerParams(vmem_limit_bytes=VMEM_LIMIT),
+        cost_estimate=cost,
+        name=name,
+    )(info, *[v for v, _ in ins], *done)
 
 
 def on_device(
@@ -175,6 +777,7 @@
     back = taps - 1
     heads_here = planes // 2
     wide_here = heads_here * head_w
+    wp = -(-wide_here // 128) * 128
     hid = w_down.shape[0]
     drows = w_y.shape[0]
     nblocks = 2 * count
@@ -209,8 +812,36 @@
     def scatter_a(value):
         return lax.psum_scatter(value, "a", scatter_dimension=0, tiled=True)
 
-    packed = jnp.concatenate([head_pieces(w_y), head_pieces(w_x)], -1)
-    w_yx = gather_a(row_blocks(by_owner(exchange(packed))))
+    def padded(v, axis=-1):
+        pads = [(0, 0)] * v.ndim
+        pads[axis] = (0, wp - wide_here)
+        return jnp.pad(v, pads)
+
+    def owners(pieces):
+        return pieces.swapaxes(0, 1).reshape((nblocks,) + pieces.shape[2:])
+
+    vectors = jnp.concatenate(
+        [conv_kernel, conv_bias[None], bias_a[None], bias_i[None], decay_param[None]], 0
+    ).reshape(-1)
+    vectors = jnp.concatenate([vectors, norm1_gain, norm2_gain]).astype(F32)
+    lanes = -(-vectors.shape[0] // 1024) * 128
+    vectors = jnp.pad(vectors, (0, 8 * lanes - vectors.shape[0])).reshape(8, lanes)
+    at_start = jnp.concatenate([init_state[0][:, None], init_conv[0].astype(F32)], 1)
+    at_start = at_start.reshape(nseq * taps, width)
+    at_start = jnp.pad(at_start, ((0, 8), (0, 0)))
+    at_start = at_start.at[nseq * taps, :nseq].set(starts[0].astype(F32))
+    all_tokens, w_yx, w_gu, _, gate_rows, canon, at_start = start_exchange(
+        tokens[0],
+        owners(jnp.concatenate([head_pieces(w_y), head_pieces(w_x)], -1)),
+        owners(jnp.concatenate([hidden_pieces(w_gate), hidden_pieces(w_up)], -1)),
+        jnp.concatenate([gate_a, gate_i], 1),
+        vectors,
+        at_start,
+    )
+    w_yx = w_yx.reshape(d_model, 2 * wide_here)
+    w_yx = jnp.concatenate([padded(w_yx[:, :wide_here]), padded(w_yx[:, wide_here:])], 1)
+    w_gu = gather_a(w_gu.reshape(-1, 2 * planes * hid))
+    gate_rows = gate_rows.reshape(wide_here, -1)
 
     def join_halves(mine_all):
         away = swap_c(lax.dynamic_slice_in_dim(mine_all, (1 - c) * heads_here, heads_here, 0))
@@ -219,6 +850,7 @@
         second = jnp.where(c == 0, away, own)
         return jnp.stack([first, second], 1).reshape((wide_here,) + mine_all.shape[2:])
 
+
     def part_halves(full):
         full = full.reshape((heads_here, 2, half) + full.shape[1:])
         own, away = pick(full, c, 1), swap_c(pick(full, 1 - c, 1))
@@ -226,50 +858,33 @@
         second = jnp.where(c == 0, away, own)
         return jnp.concatenate([first, second], 0).reshape((planes * half,) + full.shape[3:])
 
-    mixer_rows = jnp.concatenate([w_out, gate_a, gate_i], 1)
-    mixer_rows = join_halves(gather_a(mixer_rows).reshape(planes, half, -1))
-    w_o = mixer_rows[:, :d_model]
+    w_o = padded(join_halves(gather_a(w_out).reshape(planes, half, d_model)), 0)
 
     def block_diagonal(m):
         m = m.reshape(heads_here, head_w, head_w)
         eye = jnp.eye(heads_here, dtype=m.dtype)
-        return (m[:, :, None, :] * eye[:, None, :, None]).reshape(wide_here, wide_here)
+        full = (m[:, :, None, :] * eye[:, None, :, None]).reshape(wide_here, wide_here)
+        return padded(padded(full), 0)
 
     w_gates = jnp.concatenate(
         [
-            block_diagonal(mixer_rows[:, d_model : d_model + head_w]),
-            block_diagonal(mixer_rows[:, d_model + head_w :]),
+            block_diagonal(gate_rows[:, :head_w]),
+            block_diagonal(gate_rows[:, head_w:]),
         ],
         1,
     )
 
-    packed = jnp.concatenate([hidden_pieces(w_gate), hidden_pieces(w_up)], -1)
-    w_gu = gather_a(row_blocks(by_owner(exchange(packed))))
     w_d = gather_a(w_down)
     f_here = planes * hid
 
-    vectors = jnp.concatenate(
-        [conv_kernel, conv_bias[None], bias_a[None], bias_i[None], decay_param[None]], 0
-    ).reshape(-1)
-    small = jnp.concatenate([vectors, norm1_gain, norm2_gain])
-    small = jnp.stack([small] + [xor_u(small, k) for k in range(1, count)])
-    small = jnp.stack([small, swap_c(small)])
-    small = jnp.stack([small] + [cycle_a(small, d) for d in range(1, planes)])
-    small = small.reshape(planes * nblocks, -1)
-    rel = jnp.arange(planes * nblocks, dtype=jnp.int32)
-    r_a, r_c, r_u = rel // nblocks, (rel // count) % 2, rel % count
-    owner = ((a - r_a + planes) % planes) * nblocks + (u ^ r_u) * 2 + (c ^ r_c)
-    order = (rel[:, None] == owner[None, :]).astype(BF)
-    canon = mdot(order, small)
+    canon = canon.reshape(planes * nblocks, -1)
     nvec = (taps + 4) * half
     gain_one = canon[:, nvec : nvec + drows].reshape(-1)
-    gain_two = canon[:, nvec + drows :].reshape(-1)
+    gain_two = canon[:, nvec + drows : nvec + 2 * drows].reshape(-1)
     mine = pick(canon[:, :nvec].reshape(2, heads_here, count, 2, taps + 4, half), c)
     mine = pick(mine, u, 1).transpose(2, 0, 1, 3).reshape(taps + 4, wide_here)
-    kernel, cbias, abias, ibias, decay_f = (
-        mine[:taps], mine[taps], mine[taps + 1], mine[taps + 2], mine[taps + 3]
-    )
-    gate_bias = jnp.concatenate([abias, ibias])
+    decay_f = mine[taps + 3]
+    vec = padded(jnp.concatenate([mine[: taps + 3], jax.nn.softplus(decay_f)[None]]))
 
     def my_channels(v):
         lead = v.shape[:-1]
@@ -278,14 +893,13 @@
         return pick(v, u, len(lead) + 1).reshape(lead + (wide_here,))
 
     streams = 2 * nn
-    at_start = jnp.concatenate([init_state[0][:, None], init_conv[0].astype(F32)], 1)
-    at_start = jnp.concatenate([at_start.reshape(-1), starts[0].astype(F32)])
-    rel_streams = [at_start] + [xor_stream(at_start, k) for k in range(1, streams)]
-    at_start = jnp.stack([rel_streams[kn * 2 + kc] for kc in range(2) for kn in range(nn)])
-    offsets = at_start[:, -nseq:].astype(jnp.int32)
-    at_start = my_channels(at_start[:, :-nseq].reshape(streams, nseq, taps, width))
-    state_0 = at_start[:, :, 0]
-    conv_0 = at_start[:, :, 1:].reshape(streams, nseq * back, wide_here).astype(BF)
+    at_start = at_start.reshape(streams, -1, width)
+    offsets = at_start[:, nseq * taps, :nseq].astype(jnp.int32)
+    at_start = my_channels(at_start[:, : nseq * taps].reshape(streams, nseq, taps, width))
+    at_start = padded(at_start)
+    state_0 = jnp.pad(at_start[:, :, 0], ((0, 0), (0, -nseq % 8), (0, 0)))
+    conv_0 = at_start[:, :, 1:].reshape(streams, nseq * back, wp).astype(BF)
+    conv_0 = jnp.pad(conv_0, ((0, 0), (0, -(nseq * back) % 16), (0, 0)))
 
     def per_block(v):
         v = v.reshape((2, 1, nn) + v.shape[1:])
@@ -296,23 +910,26 @@
     position = first_row[:, None] + jnp.arange(rows, dtype=jnp.int32)[None]
     off_b = per_block(offsets)
 
-    def segment_of(where_at):
-        return jnp.sum((where_at[:, :, None] >= off_b[:, None, :]).astype(jnp.int32), 2) - 1
-
-    segment = segment_of(position)
-    member = segment[:, :, None] == jnp.arange(nseq, dtype=jnp.int32)
-    begin = jnp.sum(jnp.where(member, off_b[:, None, :], 0), 2)
-    opening = position == begin
-
-    def norm(value, gain):
-        factor = lax.rsqrt(jnp.mean(value * value, axis=-1, keepdims=True) + EPS)
-        return factor, (value * factor * gain).astype(BF)
-
-    inputs = tokens[0].astype(F32)
-    normed = norm(plane_gather(tokens[0]).reshape(nblocks * rows, d_model).astype(F32), gain_one)[1]
-    prod = mdot(normed, w_yx)
-    gate_in = prod[:, :wide_here].reshape(nblocks, rows, wide_here)
-    linear = prod[:, wide_here:].astype(BF).reshape(nblocks, rows, wide_here)
+    info = jnp.concatenate(
+        [first_row[:, None], off_b, jnp.zeros((nblocks, -(nseq + 1) % 8), jnp.int32)], 1
+    )
+
+    grad_low = cotangent[0]
+    grads = plane_gather(grad_low).reshape(nblocks * rows, d_model)
+
+    normed, gate_in, linear = by_block(
+        norm_product_kernel,
+        info,
+        [(all_tokens, True), (w_yx, False), (gain_one[None], False)],
+        [
+            ((nblocks, rows, d_model), BF, True),
+            ((nblocks, rows, wp), F32, True),
+            ((nblocks, rows, wp), BF, True),
+        ],
+        [],
+        name="norm_product",
+    )
+    normed = normed.reshape(nblocks * rows, d_model)
 
     def two(v):
         return v.reshape((2, 2, nn) + v.shape[1:])
@@ -331,42 +948,23 @@
     tail = linear[:, rows - back :]
     rim = per_block(shift_a(of_stream(tail, 1), 1))
     rim = jnp.where(second_half(rim.shape), flip(tail), rim)
-    extended = jnp.concatenate([rim, linear], 1)
-    conv_0b = per_block(conv_0)
-    slots = jnp.arange(back, dtype=jnp.int32)
-    by_tap = [linear.astype(F32)]
-    for k in range(1, taps):
-        offset = position - k - begin
-        hot = member[:, :, :, None] & ((offset + back)[:, :, None, None] == slots)
-        hot = hot.reshape(nblocks, rows, nseq * back).astype(BF)
-        stored = lax.dot_general(
-            hot, conv_0b, (((2,), (1,)), ((0,), (0,))), preferred_element_type=F32
-        )
-        earlier = extended[:, back - k : back - k + rows].astype(F32)
-        by_tap.append(jnp.where((offset >= 0)[:, :, None], earlier, stored))
-    conv_sum = cbias
-    for k in range(taps):
-        conv_sum = conv_sum + kernel[k] * by_tap[k]
-    conv_low = conv_sum.astype(BF)
-    conv_val = conv_low.astype(F32)
-    conv_flat = conv_low.reshape(-1, wide_here)
-    gates = jax.nn.sigmoid(mdot(conv_flat, w_gates) + gate_bias)
-    retain = gates[:, :wide_here].reshape(nblocks, rows, wide_here)
-    admit = gates[:, wide_here:].reshape(nblocks, rows, wide_here)
-    soft_decay = jax.nn.softplus(decay_f)
-    log_a = -8.0 * retain * soft_decay
-    decay_now = jnp.exp(log_a)
-    spread = -jnp.expm1(2.0 * log_a)
-    mult = jnp.sqrt(jnp.maximum(spread, FLOOR))
-    drive = mult * admit * conv_val
-    state_0b = per_block(state_0)
-    state_rows = jnp.zeros_like(drive)
-    for s in range(nseq):
-        state_rows = jnp.where(member[:, :, s, None], state_0b[:, s, None], state_rows)
-    open_3 = opening[:, :, None]
-    a_used = jnp.where(open_3, 0.0, decay_now)
-    b_used = jnp.where(open_3, decay_now * state_rows + drive, drive)
-    carry_mul, carry_add = scan(a_used, b_used, False)
+    rim = jnp.pad(rim.astype(F32), ((0, 0), (8 - back, 0), (0, 0)))
+    conv_0b, state_0b = per_block(conv_0), per_block(state_0)
+    full = (nblocks, rows, wp)
+    conv_low, retain, admit, carry_mul, carry_add = by_block(
+        functools.partial(forward_kernel, nseq, taps),
+        info,
+        [
+            (linear, True), (rim, True), (conv_0b, True), (state_0b, True),
+            (w_gates, False), (vec, False),
+        ],
+        [
+            (full, BF, True), (full, F32, True), (full, F32, True),
+            (full, F32, True), (full, F32, True),
+        ],
+        [(rows + 8, wp), (rows, wp), (rows, wp)],
+        name="mixer_forward",
+    )
 
     def entering(mul, add, reverse):
         pair = jnp.stack([mul, add])
@@ -384,102 +982,112 @@
 
     state_in = entering(carry_mul[:, -1], carry_add[:, -1], False)[:, None]
     hidden = carry_mul * state_in + carry_add
-    gelu_y, gelu_y_back = jax.vjp(jax.nn.gelu, gate_in)
-    mixed_in = (hidden * gelu_y).astype(BF).reshape(-1, wide_here)
-    resid = inputs + plane_scatter(mdot(mixed_in, w_o))
-    scale_two, normed_two = norm(resid, gain_two)
-    normed_two = plane_gather(normed_two).reshape(nblocks * rows, d_model)
-    grad_low = cotangent[0]
-    grads = plane_gather(grad_low).reshape(nblocks * rows, d_model)
+    mixed_in = (hidden * jax.nn.gelu(gate_in)).astype(BF).reshape(-1, wp)
+    resid, normed_two = plane_reduce(
+        2, "fwd", False, mixed_in.reshape(2, count, rows, -1), w_o, gain_two, tokens[0], tokens[0],
+        (grads,),
+    )
+    normed_two = normed_two.reshape(nblocks * rows, d_model)
 
     pair = mdot(normed_two, w_gu)
     gate, upward = pair[:, :f_here], pair[:, f_here:]
     active, gate_back = jax.vjp(jax.nn.gelu, gate)
     inner = (active * upward).astype(BF)
-    result = (resid + plane_scatter(mdot(inner, w_d))).astype(BF)
+    parts = inner.reshape(2, count * rows, f_here)
+    away = swap_c(mdot(parts[1], w_d).astype(BF))
+    low = (mdot(parts[0], w_d) + away.astype(F32)).astype(BF).reshape(count, rows, d_model)
+    result = resid + low[0].astype(F32)
+    for k in range(1, count):
+        result = result + xor_u(low[k], k).astype(F32)
+    result = result.astype(BF)
     d_inner = ndot(grads, w_d)
-    grad_wd = scatter_a(tdot(inner, grads).astype(BF)).astype(F32)
+    sums_d = tdot(inner, grads).astype(BF)
+    grad_wd = scatter_a(sums_d)
     d_gate = gate_back(d_inner * upward)[0].astype(BF)
     d_up = (d_inner * active).astype(BF)
     d_pair = jnp.concatenate([d_gate, d_up], 1)
-    d_normed_two = plane_scatter(ndot(d_pair, w_gu))
-    sums = scatter_a(tdot(normed_two, d_pair).astype(BF))
+    sums_gu = tdot(normed_two, d_pair).astype(BF)
+    sums = scattered_gu = scatter_a(sums_gu)
     sums = by_owner(exchange(to_owner_rows(sums)))
     grad_wg = from_hidden_pieces(sums[..., :f_here]).astype(F32)
     grad_wu = from_hidden_pieces(sums[..., f_here:]).astype(F32)
 
-    def norm_back(value, factor, gain, grad):
-        weighted = grad * gain
-        inner = jnp.mean(weighted * value, axis=-1, keepdims=True)
-        return factor * weighted - value * factor * factor * factor * inner
-
-    d_resid = grad_low.astype(F32) + norm_back(resid, scale_two, gain_two, d_normed_two)
-    d_resid_low = plane_gather(d_resid.astype(BF)).reshape(nblocks * rows, d_model)
-
-    d_mixed = ndot(d_resid_low, w_o).reshape(nblocks, rows, wide_here)
-    sums_o = tdot(mixed_in, d_resid_low).astype(BF)
+    d_resid, d_resid_low = plane_reduce(
+        3, "mid", True, d_pair.reshape(2, count, rows, -1), w_gu, gain_two, grad_low, resid,
+        (sums_gu,),
+    )
+    d_resid_low = d_resid_low.reshape(nblocks * rows, d_model)
+
+    d_gate_in, back_mul, back_add, first = by_block(
+        functools.partial(back_scan_kernel, nseq, taps),
+        info,
+        [
+            (d_resid_low.reshape(nblocks, rows, d_model), True), (w_o, False), (gate_in, True),
+            (hidden, True), (retain, True), (vec, False),
+        ],
+        [(full, BF, True), (full, F32, True), (full, F32, True), ((nblocks, 8, wp), F32, True)],
+        [(rows + 8, wp), (rows, wp), (rows, wp)],
+        name="mixer_back_scan",
+    )
+    sums_o = tdot(mixed_in, d_resid_low)[:wide_here].astype(BF)
     grad_wo = scatter_a(part_halves(sums_o)).astype(F32)
-    d_hidden = d_mixed * gelu_y
-    d_gate_in = gelu_y_back(d_mixed * hidden)[0].astype(BF).reshape(-1, wide_here)
-    forward_mul = jnp.concatenate([a_used[:, 1:], jnp.ones((nblocks, 1, wide_here), F32)], 1)
-    back_mul, back_add = scan(forward_mul, d_hidden, True)
-    grad_in = entering(a_used[:, 0] * back_mul[:, 0], a_used[:, 0] * back_add[:, 0], True)[:, None]
-    total_grad = back_mul * grad_in + back_add
-    previous = jnp.concatenate([state_in, hidden[:, :-1]], 1)
-    previous = jnp.where(open_3, state_rows, previous)
-    d_decay = total_grad * previous
-    d_mult = total_grad * admit * conv_val
-    d_admit = total_grad * mult * conv_val
-    d_conv = total_grad * mult * admit
-    d_spread = jnp.where(spread > FLOOR, d_mult * 0.5 / mult, 0.0)
-    d_log = d_decay * decay_now - 2.0 * decay_now * decay_now * d_spread
-    d_retain = d_log * (-8.0 * soft_decay)
-    grad_decay = jnp.sum(d_log * (-8.0 * retain), axis=(0, 1)) * jax.nn.sigmoid(decay_f)
-    d_rate = (d_retain * retain * (1.0 - retain)).astype(BF)
-    d_inflow = (d_admit * admit * (1.0 - admit)).astype(BF)
-    grad_abias = jnp.sum(d_rate.astype(F32), axis=(0, 1))
-    grad_ibias = jnp.sum(d_inflow.astype(F32), axis=(0, 1))
-    d_gates = jnp.concatenate([d_rate, d_inflow], 2).reshape(-1, 2 * wide_here)
-    d_conv = d_conv + ndot(d_gates, w_gates).reshape(d_conv.shape)
-    sums_gates = tdot(conv_flat, d_gates)
+    grad_in = entering(first[:, 0] * back_mul[:, 0], first[:, 0] * back_add[:, 0], True)[:, None]
+    d_conv_low, sums_gates, vec_grads = by_block(
+        functools.partial(back_kernel, nseq, taps),
+        info,
+        [
+            (back_mul, True), (back_add, True), (grad_in, True), (hidden, True),
+            (state_in, True), (state_0b, True), (conv_low, True), (retain, True),
+            (admit, True), (linear, True), (rim, True), (conv_0b, True), (w_gates, False), (vec, False),
+        ],
+        [(full, BF, True), ((wp, 2 * wp), F32, False), ((taps + 4, wp), F32, False)],
+        [(rows + 8, wp)],
+        (scattered_gu,),
+        name="mixer_back",
+    )
 
     def diagonal(m):
         m = m.reshape(heads_here, head_w, heads_here, head_w)
         return jnp.concatenate([m[h, :, h] for h in range(heads_here)], 0)
 
     grad_gates = jnp.concatenate(
-        [diagonal(sums_gates[:, :wide_here]), diagonal(sums_gates[:, wide_here:])], 1
-    )
-    d_conv_low = d_conv.astype(BF)
-    d_conv_val = d_conv_low.astype(F32)
+        [
+            diagonal(sums_gates[:wide_here, :wide_here]),
+            diagonal(sums_gates[:wide_here, wp : wp + wide_here]),
+        ],
+        1,
+    )
     head = d_conv_low[:, :back]
     rim_back = per_block(shift_a(of_stream(head, 0), -1))
     rim_back = jnp.where(second_half(head.shape), rim_back, flip(head))
-    ahead = jnp.concatenate([d_conv_low, rim_back], 1)
-    d_linear = kernel[0] * d_conv_val
-    kernel_grads = [jnp.sum(d_conv_val * by_tap[0], axis=(0, 1))]
-    for k in range(1, taps):
-        later_rows = ahead[:, k : k + rows].astype(F32)
-        same = (segment_of(position + k) == segment)[:, :, None]
-        d_linear = d_linear + kernel[k] * jnp.where(same, later_rows, 0.0)
-        kernel_grads.append(jnp.sum(d_conv_val * by_tap[k], axis=(0, 1)))
-    grad_cbias = jnp.sum(d_conv_val, axis=(0, 1))
-    vec_grads = jnp.stack(kernel_grads + [grad_cbias, grad_abias, grad_ibias, grad_decay], 1)
+    rim_back = jnp.pad(rim_back.astype(F32), ((0, 0), (0, 8 - back), (0, 0)))
+    d_both = by_block(
+        functools.partial(back_conv_kernel, nseq, taps),
+        info,
+        [(d_conv_low, True), (rim_back, True), (d_gate_in, True), (vec, False)],
+        [((nblocks, rows, 2 * wp), BF, True)],
+        [(rows + 8, wp)],
+        name="mixer_back_conv",
+    )[0]
+    vec_grads = vec_grads[:, :wide_here].T
+    vec_grads = jnp.concatenate(
+        [vec_grads[:, :-1], vec_grads[:, -1:] * jax.nn.sigmoid(decay_f)[:, None]], 1
+    )
     late = jnp.concatenate([grad_gates, vec_grads], 1).astype(BF)
     late = scatter_a(part_halves(late)).astype(F32)
     grad_wa, grad_wi = late[:, :head_w], late[:, head_w : 2 * head_w]
     vec_grads = late[:, 2 * head_w :].T
 
-    d_linear_low = d_linear.astype(BF).reshape(-1, wide_here)
-    d_both = jnp.concatenate([d_gate_in, d_linear_low], 1)
-    d_normed = plane_scatter(ndot(d_both, w_yx))
-    sums = scatter_a(tdot(normed, d_both).astype(BF))
+    sums_yx = tdot(normed, d_both.reshape(nblocks * rows, 2 * wp)).astype(BF)
+    sums_yx = jnp.concatenate([sums_yx[:, :wide_here], sums_yx[:, wp : wp + wide_here]], 1)
+    input_grad = plane_reduce(
+        4, "last", True, d_both.reshape(2, count, rows, -1), w_yx, gain_one, tokens[0], d_resid,
+        (grad_wd, sums_yx, result),
+    )[0]
+    sums = scatter_a(sums_yx)
     sums = by_owner(exchange(to_owner_rows(sums)))
     grad_wy = from_head_pieces(sums[..., :wide_here]).astype(F32)
     grad_wx = from_head_pieces(sums[..., wide_here:]).astype(F32)
-    scale_one = lax.rsqrt(jnp.mean(inputs * inputs, axis=-1, keepdims=True) + EPS)
-    input_grad = (d_resid + norm_back(inputs, scale_one, gain_one, d_normed)).astype(BF)
-
     def gain_grad(gain, *pairs):
         total = sum(jnp.sum(w.astype(F32) * g, axis=1) for w, g in pairs)
         return total / gain.astype(F32)
@@ -495,12 +1103,13 @@
     lasts = lax.dot_general(
         hot, hidden.astype(BF), (((2,), (1,)), ((0,), (0,))), preferred_element_type=F32
     )
+    slots = jnp.arange(back, dtype=jnp.int32)
     where_conv = (end_b[:, :, None] - back + 1 + slots).reshape(nblocks, nseq * back)
     hot = (position[:, None, :] == where_conv[:, :, None]).astype(BF)
     conv_lasts = lax.dot_general(
         hot, linear, (((2,), (1,)), ((0,), (0,))), preferred_element_type=F32
     )
-    lasts = two(jnp.concatenate([lasts, conv_lasts], 1))
+    lasts = two(jnp.concatenate([lasts, conv_lasts], 1)[..., :wide_here])
     lasts = (lasts[:, 0] + lasts[:, 1]).astype(BF)
     came = [cycle_a(lasts, d) for d in range(1, planes)]
     lasts = sum(part.astype(F32) for part in [lasts] + came).astype(BF)
@@ -531,7 +1140,7 @@
         vec_grads[taps + 3],
         grad_wg,
         grad_wu,
-        grad_wd,
+        grad_wd.astype(F32),
         grad_gain_two,
     )
 
@@ -871,7 +1480,7 @@
 def solution(mesh):
     wide, narrow = mesh.shape["wide"], mesh.shape["narrow"]
     def plan(*args):
-        fits = args[6].shape[0] * 2 == args[6].shape[1]
+        fits = args[6].shape[0] * 2 == args[6].shape[1] and narrow == 4
         return (on_device if fits else on_device_any)(*args)
 
     fine = Mesh(mesh.devices.reshape(wide // 2, 2, narrow // 2, 2), ("a", "b", "n", "c"))

time: 1020 us -> 767 us (0.75)
  Pallas kernels: 12.9 us -> 375 us
  waiting for transfers between devices: 318 us -> 73.3 us
  other arithmetic: 180 us -> 55.4 us
  local copies, waits for them, and re-layouts: 216 us -> 94.3 us
  matrix products: 174 us -> 98.4 us
  starting transfers between devices: 88.1 us -> 44.7 us
    pallas_call x2 -> x9, Pallas kernels: 12.9 us -> 375 us  [the longest x3 219 us: plane_reduce(): pl.pallas_call(functools.partial(reduce_kernel, nt, post, len(done)), in_...]
    ppermute x42 -> x15, waiting for transfers between devices: 264 us -> 66.5 us  [xor_u(): return lax.ppermute(value, ('b', 'n'), [(i, i ^ k) for i in range(size)])]
    slice x22 -> x14, local copies, waits for them, and re-layouts: 62.7 us -> 7.83 us  [the longest x1 2.18 us: on_device(): w_yx[:, wide_here:]]
    convert_element_type x10 -> x6, other arithmetic: 63.7 us -> 12.4 us  [the longest x1 6.3 us: on_device(): mixed_in = (hidden * jax.nn.gelu(gate_in)).astype(BF).reshape(-1, wp)]
    dot_general x5 -> x1, matrix products: 67.6 us -> 19.4 us  [ndot(): lax.dot_general(left, right, (((1,), (1,)), ((), ())), preferred_element_...]
    all_gather x4 -> x3, waiting for transfers between devices: 45 us -> 0.02 us  [gather_a(): return lax.all_gather(value, 'a', axis=0, tiled=True)]
    reduce_sum x9 -> x0, other arithmetic: 39.9 us -> none  [the longest x1 11.5 us: on_device(): jnp.sum(d_log * (-8.0 * retain), axis=(0, 1)) * jax.nn.sigmoid(decay_f)]
    ppermute x42 -> x15, starting transfers between devices: 51.4 us -> 18.6 us  [xor_u(): return lax.ppermute(value, ('b', 'n'), [(i, i ^ k) for i in range(size)])]
  transfers between devices with their start and end apart: 85 -> 42, of which waited for: 31 -> 12; matrix products, arithmetic and copies ran while one was open for 47% -> 26% of each run, Pallas kernels for 1% -> 50%
where the time goes in v2:
time: 767 us; the launch traced here: 758 us
  Pallas kernels  375 us (49%)
  matrix products  98.4 us (13%)
  local copies, waits for them, and re-layouts  94.3 us (12%)
  waiting for transfers between devices  73.3 us (10%)
  other arithmetic  55.4 us (7%)
  starting transfers between devices  44.7 us (6%)
  between operations  16.2 us (2%)
    pallas_call x3, Pallas kernels, plane_reduce(): pl.pallas_call(functools.partial(reduce_kernel, nt, post, len(done)), in_...  219 us
    pallas_call x1, Pallas kernels, start_exchange(): pl.pallas_call(start_kernel, in_specs=[hbm] * 6, out_specs=[hbm] * 7, out...  79 us
    pallas_call x5, Pallas kernels, by_block(): pl.pallas_call(body, grid_spec=pltpu.PrefetchScalarGridSpec(num_scalar_pr...  77.3 us
    ppermute x15, waiting for transfers between devices, xor_u(): return lax.ppermute(value, ('b', 'n'), [(i, i ^ k) for i in range(size)])  66.5 us
    dot_general x4, matrix products, tdot(): lax.dot_general(left, right, (((0,), (0,)), ((), ())), preferred_element_...  45.4 us
    dot_general x3, matrix products, mdot(): return jnp.dot(left, right, preferred_element_type=F32)  32.9 us
    dot_general x1, matrix products, ndot(): lax.dot_general(left, right, (((1,), (1,)), ((), ())), preferred_element_...  19.4 us
    ppermute x15, starting transfers between devices, xor_u(): return lax.ppermute(value, ('b', 'n'), [(i, i ^ k) for i in range(size)])  18.6 us
  transfers between devices with their start and end apart: 42, of which 12 were waited for; matrix products, arithmetic and copies ran while one was open for 26% of the time, Pallas kernels for 50%

profile of v2, /device:TPU:0, one launch (start us, length us, event | category | flops | bytes accessed | tf_op | source)
XLA Modules:
  0.0 757.9 jit_solution(2077405079542065513)
XLA Ops:
  24.0 79.0 %start_exchange.1 = (bf16[8,256,2048]{2,1,0:T(8,128)(2,1)}, bf16[4,8,64,640]{3,2,1,0:T(8,128)(2,1)}, bf16[8,64,1536]{2,1,0:T(8,128)(2,1)}, bf16[4,80,320]{2,1,0:...) custom-call(bf16[256,2048]{1,0:T(8,128)(2,1)} %bitcast.268, ...), custom_call_target="tpu_custom_call" | custom-call | bytes 104857600 | tf_op jit(solution)/shard_map/start_exchange/pallas_call | solution.py:501
  115.1 17.1 %norm_product.1 = (bf16[8,256,2048]{2,1,0:T(8,128)(2,1)}, f32[8,256,384]{2,1,0:T(8,128)}, bf16[8,256,384]{2,1,0:T(8,128)(2,1)}) custom-call(s32[8,8]{1,0:T(8,128)} %add_add_fusion.info, bf16[8,256,2048]{2,1,0:T(8,128)(2,1)} %get-tuple-element.57.tok_ref, bf16[2048,768]{1,0:T(8,128)(2,1)} %fusion.17.w_ref.w_hbm, ...), custom_call_target="tpu_custom_call" | custom-call | tf_op jit(solution)/shard_map/norm_product/pallas_call | solution.py:729
  145.5 15.8 %mixer_forward.1 = (bf16[8,256,384]{2,1,0:T(8,128)(2,1)}, f32[8,256,384]{2,1,0:T(8,128)}, f32[8,256,384]{2,1,0:T(8,128)}, f32[8,256,384]{2,1,0:T(8,128)}, f32[8,256,384]{2,1,0:T(8,128)}) custom-call(s32[8,8]{1,0:T(8,128)} %add_add_fusion.info, bf16[8,256,384]{2,1,0:T(8,128)(2,1)} %get-tuple-element.60.lin_ref, f32[8,8,384]{2,1,0:T(8,128)} %pad_convert_fusion.2.rim_ref, ...), custom_call_target="tpu_custom_call" | custom-call | tf_op jit(solution)/shard_map/mixer_forward/pallas_call | solution.py:729
  162.4 3.7 pad_maximum_fusion.1
  169.5 4.7 collective-permute-start.2
  177.5 6.3 fusion.16
  194.4 4.8 constant_dynamic-update-slice_fusion
  199.3 84.7 %plane_reduce_fwd.1 = (f32[256,2048]{1,0:T(8,128)}, bf16[8,256,2048]{2,1,0:T(8,128)(2,1)}) custom-call(bf16[2,4,256,384]{3,2,1,0:T(8,128)(2,1)} %bitcast.277, bf16[384,2048]{1,0:T(8,128)(2,1)} %pad.80.w_hbm.wo_ref, f32[1,2048]{1,0:T(1,128)} %reshape_reshape.13.refs_0_, bf16[256,2048]{1,0:T(8,128)(2,1)} %bitcast.269, bf16[256,2048]{1,0:T(8,128)(2,1)} %bitcast.270, ...), custom_call_target="tpu_custom_call" | custom-call | flops 3221225472 | bytes 3145728 | tf_op jit(solution)/shard_map/plane_reduce_fwd/pallas_call | solution.py:317
  284.0 19.1 %fusion.100 = f32[2048,1536]{0,1:T(8,128)} fusion(bf16[2048,2048]{1,0:T(8,128)(2,1)} %bitcast.369, bf16[2048,1536]{1,0:T(8,128)(2,1)} %all-gather.6.cloned.1.call-done.w_hbm), kind=kOutput, calls=%fused_computation.313 | convolution fusion | flops 12884901888 | bytes 27262976 | tf_op jit(solution)/shard_map/dot_general | solution.py:26
  303.0 19.4 %fusion.6 = (bf16[2048,768]{0,1:T(8,128)(2,1)S(1)}, bf16[2048,768]{0,1:T(8,128)(2,1)S(1)}, bf16[2048,768]{0,1:T(8,128)(2,1)}) fusion(f32[2048,1536]{0,1:T(8,128)} %fusion.100, bf16[2048,2048]{1,0:T(8,128)(2,1)} %bitcast.55.refs_3_, bf16[768,2048]{1,0:T(8,128)(2,1)} %all-gather.8.cloned.1.call-done), kind=kOutput, calls=%fused_computation.10 | convolution fusion | flops 6483345408 | bytes 33554432 | tf_op jit(solution)/shard_map/dot_general | solution.py:22
  325.1 17.4 %convolution_convert_fusion.refs_3_ = bf16[2048,1536]{1,0:T(8,128)(2,1)} fusion(bf16[2048,2048]{1,0:T(8,128)(2,1)} %bitcast.370, bf16[2048,768]{0,1:T(8,128)(2,1)S(1)} %get-tuple-element.187, bf16[2048,768]{0,1:T(8,128)(2,1)S(1)} %get-tuple-element.186), kind=kOutput, calls=%fused_computation.3 | convolution fusion | flops 12900630528 | bytes 20971520 | tf_op jit(solution)/shard_map/dot_general | solution.py:18
  343.2 6.6 pad_maximum_fusion
  349.8 9.1 %copy.176 = bf16[2048,1536]{1,0:T(8,128)(2,1)} copy(bf16[2048,1536]{0,1:T(8,128)(2,1)} %pad_maximum_fusion) | data formatting | bytes 12582912 | tf_op jit(solution)/shard_map/concatenate | solution.py:1008
  358.9 87.1 %plane_reduce_mid.1 = (f32[256,2048]{1,0:T(8,128)}, bf16[8,256,2048]{2,1,0:T(8,128)(2,1)}) custom-call(bf16[2,4,256,1536]{3,2,1,0:T(8,128)(2,1)} %bitcast.274, bf16[2048,1536]{1,0:T(8,128)(2,1)} %all-gather.6.cloned.1.call-done.w_hbm, f32[1,2048]{1,0:T(1,128)} %reshape_reshape.13.refs_0_, bf16[256,2048]{1,0:T(8,128)(2,1)} %bitcast.286, ...), custom_call_target="tpu_custom_call" | custom-call | flops 12884901888 | bytes 12582912 | tf_op jit(solution)/shard_map/plane_reduce_mid/pallas_call | solution.py:317
  446.0 7.5 convolution_bitcast_fusion
  457.2 6.4 collective-permute-start.19
  465.7 4.2 collective-permute-done.18
  470.1 17.4 %mixer_back_scan.1 = (bf16[8,256,384]{2,1,0:T(8,128)(2,1)}, f32[8,256,384]{2,1,0:T(8,128)}, f32[8,256,384]{2,1,0:T(8,128)}, f32[8,8,384]{2,1,0:T(8,128)}) custom-call(s32[8,8]{1,0:T(8,128)} %add_add_fusion.info, bf16[8,256,2048]{2,1,0:T(8,128)(2,1)} %get-tuple-element.68.dres_ref, bf16[384,2048]{1,0:T(8,128)(2,1)} %pad.80.w_hbm.wo_ref, ...), custom_call_target="tpu_custom_call" | custom-call | tf_op jit(solution)/shard_map/mixer_back_scan/pallas_call | solution.py:729
  487.4 10.3 %convolution_convert_fusion.2 = bf16[768,2048]{1,0:T(8,128)(2,1)} fusion(bf16[2048,768]{0,1:T(8,128)(2,1)S(1)} %copy-done.38, bf16[2048,2048]{1,0:T(8,128)(2,1)} %bitcast.55.refs_3_), kind=kOutput, calls=%fused_computation.21 | convolution fusion | flops 6444023808 | bytes 14680064 | tf_op jit(solution)/shard_map/dot_general | solution.py:18
  503.3 8.1 %convolution_convert_fusion.1 = bf16[1024,2048]{1,0:T(8,128)(2,1)} fusion(bf16[768,2048]{1,0:T(8,128)(2,1)} %all-gather.8.cloned.1.call-done, bf16[2048,768]{0,1:T(8,128)(2,1)} %get-tuple-element.188), kind=kOutput, calls=%fused_computation.20 | convolution fusion | flops 3223322624 | bytes 8912896 | tf_op jit(solution)/shard_map/dot_general | solution.py:26
  512.7 17.1 %mixer_back.1 = (bf16[8,256,384]{2,1,0:T(8,128)(2,1)}, f32[384,768]{1,0:T(8,128)}, f32[8,384]{1,0:T(8,128)}) custom-call(s32[8,8]{1,0:T(8,128)} %add_add_fusion.info, f32[8,256,384]{2,1,0:T(8,128)} %get-tuple-element.70.p_ref, f32[8,256,384]{2,1,0:T(8,128)} %get-tuple-element.71.s_ref, f32[8,1,384]{2,1,0:T(1,128)} %broadcast_select_fusion.1.grad_in_ref, ...), custom_call_target="tpu_custom_call" | custom-call | tf_op jit(solution)/shard_map/mixer_back/pallas_call | solution.py:729
  537.3 9.9 %mixer_back_conv.1 = bf16[8,256,768]{2,1,0:T(8,128)(2,1)} custom-call(s32[8,8]{1,0:T(8,128)} %add_add_fusion.info, bf16[8,256,384]{2,1,0:T(8,128)(2,1)} %get-tuple-element.75.dconv_ref, f32[8,8,384]{2,1,0:T(8,128)} %pad_convert_fusion.1.rim_ref, bf16[8,256,384]{2,1,0:T(8,128)(2,1)} %get-tuple-element.76.dgate_ref, f32[8,384]{1,0:T(8,128)} %select_maximum_fusion.vec_ref), custom_call_target="tpu_custom_call" | custom-call | tf_op jit(solution)/shard_map/mixer_back_conv/pallas_call | solution.py:729
  547.2 10.3 %bitcast_convert_fusion = bf16[2048,768]{1,0:T(8,128)(2,1)S(1)} fusion(bf16[8,256,2048]{2,1,0:T(8,128)(2,1)} %get-tuple-element.78, bf16[8,256,768]{2,1,0:T(8,128)(2,1)} %mixer_back_conv.1), kind=kOutput, calls=%fused_computation.13 | convolution fusion | flops 6444023808 | bytes 14680064 | tf_op jit(solution)/shard_map/dot_general | solution.py:18
  561.4 5.8 add_convert_fusion
  576.5 43.1 %collective-permute-done.23 = bf16[2,16,320]{2,1,0:T(8,128)(2,1)S(1)} collective-permute-done((bf16[2,16,320]{2,1,0:T(8,128)(2,1)S(1)}, bf16[2,16,320]{2,1,0:T(8,128)(2,1)S(1)}, u32[]{:S(2)}, u32[]{:S(2)}) %collective-permute-start.23) | collective-permute-done | bytes 20512 | tf_op jit(solution)/shard_map/ppermute | solution.py:39
  628.6 3.7 add_convert_fusion.1.refs_5_
  634.7 47.4 %plane_reduce_last.1 = bf16[256,2048]{1,0:T(8,128)(2,1)} custom-call(bf16[2,4,256,768]{3,2,1,0:T(8,128)(2,1)} %bitcast.292, bf16[2048,768]{1,0:T(8,128)(2,1)} %fusion.17.w_ref.w_hbm, f32[1,2048]{1,0:T(1,128)} %broadcast_in_dim_reshape.4.gain_ref.refs_0_, bf16[256,2048]{1,0:T(8,128)(2,1)} %bitcast.271, f32[256,2048]{1,0:T(8,128)} %get-tuple-element.77.refs_2_, ...), custom_call_target="tpu_custom_call" | custom-call | flops 6442450944 | bytes 6291456 | tf_op jit(solution)/shard_map/plane_reduce_last/pallas_call | solution.py:317
  688.9 7.3 collective-permute-done.33
  696.2 5.8 collective-permute-done.32
  711.4 4.2 reshape.998
  721.3 3.5 reshape.999
  732.6 3.9 collective-permute-done.27
  (382 shorter events, 151.1 us)
Async XLA Ops:
  7.2 179.7 %all-gather.4.cloned.1.call-start = ((), (), s32[]{:S(2)}) async-start(), calls=%async_computation.5 | async-start | bytes 1638400 | tf_op jit(solution)/shard_map/all_gather | solution.py:810
  7.9 276.0 %all-gather.6.cloned.1.call-start = ((), (), s32[]{:S(2)}) async-start(), calls=%async_computation.6 | async-start | bytes 7864320 | tf_op jit(solution)/shard_map/all_gather | solution.py:810
  103.0 200.0 %all-gather.8.cloned.1.call-start = ((), (), s32[]{:S(2)}) async-start(), calls=%async_computation.7 | async-start | bytes 3932160 | tf_op jit(solution)/shard_map/all_gather | solution.py:810
  103.3 59.1 %collective-permute-start.5 = (bf16[256,2048]{1,0:T(8,128)(2,1)S(1)}, bf16[256,2048]{1,0:T(8,128)(2,1)}, u32[]{:S(2)}, u32[]{:S(2)}) collective-permute-start(bf16[256,2048]{1,0:T(8,128)(2,1)S(1)} %bitcast.287), channel_id=1, source_target_pairs={{0,2},{2,0},{4,6},{6,4},{1,3},{3,1},{5,7},{7,5},{8,10},{10,8},{12,... | collective-permute-start | bytes 3145736 | tf_op jit(solution)/shard_map/ppermute | solution.py:39
  104.0 58.3 %collective-permute-start.6 = (bf16[256,2048]{1,0:T(8,128)(2,1)S(1)}, bf16[256,2048]{1,0:T(8,128)(2,1)}, u32[]{:S(2)}, u32[]{:S(2)}) collective-permute-start(bf16[256,2048]{1,0:T(8,128)(2,1)S(1)} %bitcast.288), channel_id=1, source_target_pairs={{0,4},{2,6},{4,0},{6,2},{1,5},{3,7},{5,1},{7,3},{8,12},{10,14},{12... | collective-permute-start | bytes 3145736 | tf_op jit(solution)/shard_map/ppermute | solution.py:39
  105.4 57.0 %collective-permute-start.7 = (bf16[256,2048]{1,0:T(8,128)(2,1)S(1)}, bf16[256,2048]{1,0:T(8,128)(2,1)}, u32[]{:S(2)}, u32[]{:S(2)}) collective-permute-start(bf16[256,2048]{1,0:T(8,128)(2,1)S(1)} %bitcast.289), channel_id=1, source_target_pairs={{0,6},{2,4},{4,2},{6,0},{1,7},{3,5},{5,3},{7,1},{8,14},{10,12},{12... | collective-permute-start | bytes 3145736 | tf_op jit(solution)/shard_map/ppermute | solution.py:39
  133.1 10.3 %collective-permute-start = (bf16[4,3,384]{2,1,0:T(4,128)(2,1)S(1)}, bf16[4,3,384]{2,1,0:T(4,128)(2,1)S(1)}, u32[]{:S(2)}, u32[]{:S(2)}) collective-permute-start(bf16[4,3,384]{2,1,0:T(4,128)(2,1)S(1)} %bitcast.358), channel_id=1, source_target_pairs={{0,8},{8,16},{16,24},{1,9},{9,17},{17,25},{2,10},{10,18},{18,26},{... | collective-permute-start | bytes 27656 | tf_op jit(solution)/shard_map/ppermute | solution.py:44
  135.4 377.3 %reduce-scatter.6.cloned.1.call-start = ((), (), s32[]{:S(2)}) async-start(), calls=%async_computation.8 | async-start | bytes 7864320 | tf_op jit(solution)/shard_map/reduce_scatter | solution.py:813
  166.1 28.3 %collective-permute-start.8 = (bf16[4,256,2048]{2,1,0:T(8,128)(2,1)}, bf16[4,256,2048]{2,1,0:T(8,128)(2,1)}, u32[]{:S(2)}, u32[]{:S(2)}) collective-permute-start(bf16[4,256,2048]{2,1,0:T(8,128)(2,1)} %pad_maximum_fusion.1), channel_id=1, source_target_pairs={{0,1},{1,0},{2,3},{3,2},{4,5},{5,4},{6,7},{7,6},{8,9},{9,8},{10,11... | collective-permute-start | bytes 12582920 | tf_op jit(solution)/shard_map/ppermute | solution.py:34
  167.1 10.2 %collective-permute-start.1 = (f32[2,4,384]{2,0,1:T(2,128)S(1)}, f32[2,4,384]{2,0,1:T(2,128)S(1)}, u32[]{:S(2)}, u32[]{:S(2)}) collective-permute-start(f32[2,4,384]{2,0,1:T(2,128)S(1)} %pad_maximum_fusion.25), channel_id=1, source_target_pairs={{0,8},{8,16},{16,24},{1,9},{9,17},{17,25},{2,10},{10,18},{18,26},{... | collective-permute-start | bytes 36872 | tf_op jit(solution)/shard_map/ppermute | solution.py:44
  342.5 283.0 %reduce-scatter.14.cloned.1.call-start = ((), (), s32[]{:S(2)}) async-start(), calls=%async_computation.12 | async-start | bytes 1638400 | tf_op jit(solution)/shard_map/reduce_scatter | solution.py:813
  457.1 175.1 %reduce-scatter.8.cloned.1.call-start = ((), (), s32[]{:S(2)}) async-start(), calls=%async_computation.9 | async-start | bytes 3932160 | tf_op jit(solution)/shard_map/reduce_scatter | solution.py:813
  457.2 8.5 %collective-permute-start.19 = (bf16[2,2,16,320]{3,2,1,0:T(8,128)(2,1)S(1)}, bf16[2,2,16,320]{3,2,1,0:T(8,128)(2,1)S(1)}, u32[]{:S(2)}, u32[]{:S(2)}) collective-permute-start(bf16[2,2,16,320]{3,2,1,0:T(8,128)(2,1)S(1)} %fusion.56), channel_id=1, source_target_pairs={{0,24},{8,0},{16,8},{24,16},{1,25},{9,1},{17,9},{25,17},{2,26},{10... | collective-permute-start | bytes 122888 | tf_op jit(solution)/shard_map/ppermute | solution.py:49
  470.0 103.7 %collective-permute-start.20 = (bf16[2,16,320]{2,1,0:T(8,128)(2,1)S(1)}, bf16[2,16,320]{2,1,0:T(8,128)(2,1)S(1)}, u32[]{:S(2)}, u32[]{:S(2)}) collective-permute-start(bf16[2,16,320]{2,1,0:T(8,128)(2,1)S(1)} %get-tuple-element.252), channel_id=1, source_target_pairs={{0,1},{1,0},{2,3},{3,2},{4,5},{5,4},{6,7},{7,6},{8,9},{9,8},{10,11... | collective-permute-start | bytes 61448 | tf_op jit(solution)/shard_map/ppermute | solution.py:34
  497.7 184.4 %reduce-scatter.12.cloned.1.call-start = ((), (), s32[]{:S(2)}) async-start(), calls=%async_computation.11 | async-start | bytes 307200 | tf_op jit(solution)/shard_map/reduce_scatter | solution.py:813
  499.4 12.5 %collective-permute-start.13 = (f32[2,4,384]{2,0,1:T(2,128)S(1)}, f32[2,4,384]{2,0,1:T(2,128)S(1)}, u32[]{:S(2)}, u32[]{:S(2)}) collective-permute-start(f32[2,4,384]{2,0,1:T(2,128)S(1)} %pad_maximum_fusion.26), channel_id=1, source_target_pairs={{8,0},{16,8},{24,16},{9,1},{17,9},{25,17},{10,2},{18,10},{26,18},{... | collective-permute-start | bytes 36872 | tf_op jit(solution)/shard_map/ppermute | solution.py:44
  500.7 11.2 %collective-permute-start.14 = (f32[2,4,384]{2,0,1:T(2,128)S(1)}, f32[2,4,384]{2,0,1:T(2,128)S(1)}, u32[]{:S(2)}, u32[]{:S(2)}) collective-permute-start(f32[2,4,384]{2,0,1:T(2,128)S(1)} %pad_maximum_fusion.26), channel_id=1, source_target_pairs={{16,0},{24,8},{17,1},{25,9},{18,2},{26,10},{19,3},{27,11},{20,4},{... | collective-permute-start | bytes 36872 | tf_op jit(solution)/shard_map/ppermute | solution.py:44
  502.0 9.9 %collective-permute-start.15 = (f32[2,4,384]{2,0,1:T(2,128)S(1)}, f32[2,4,384]{2,0,1:T(2,128)S(1)}, u32[]{:S(2)}, u32[]{:S(2)}) collective-permute-start(f32[2,4,384]{2,0,1:T(2,128)S(1)} %pad_maximum_fusion.26), channel_id=1, source_target_pairs={{24,0},{25,1},{26,2},{27,3},{28,4},{29,5},{30,6},{31,7}} | collective-permute-start | bytes 36872 | tf_op jit(solution)/shard_map/ppermute | solution.py:44
  511.4 50.0 %collective-permute-start.9 = (bf16[1024,2048]{1,0:T(8,128)(2,1)}, bf16[1024,2048]{1,0:T(8,128)(2,1)}, u32[]{:S(2)}, u32[]{:S(2)}) collective-permute-start(bf16[1024,2048]{1,0:T(8,128)(2,1)} %convolution_convert_fusion.1), channel_id=1, source_target_pairs={{0,1},{1,0},{2,3},{3,2},{4,5},{5,4},{6,7},{7,6},{8,9},{9,8},{10,11... | collective-permute-start | bytes 12582920 | tf_op jit(solution)/shard_map/ppermute | solution.py:34
  535.6 21.9 %collective-permute-start.28 = (bf16[2,80,328]{2,1,0:T(8,128)(2,1)S(1)}, bf16[2,80,328]{2,1,0:T(8,128)(2,1)S(1)}, u32[]{:S(2)}, u32[]{:S(2)}) collective-permute-start(bf16[2,80,328]{2,1,0:T(8,128)(2,1)S(1)} %dynamic-slice_bitcast_fusion.5), channel_id=1, source_target_pairs={{0,1},{1,0},{2,3},{3,2},{4,5},{5,4},{6,7},{7,6},{8,9},{9,8},{10,11... | collective-permute-start | bytes 314888 | tf_op jit(solution)/shard_map/ppermute | solution.py:34
  558.3 166.5 %reduce-scatter.10.cloned.1.call-start = ((), (), s32[]{:S(2)}) async-start(), calls=%async_computation.10 | async-start | bytes 3276800 | tf_op jit(solution)/shard_map/reduce_scatter | solution.py:813
  570.2 58.4 %collective-permute-start.12 = (bf16[256,2048]{1,0:T(8,128)(2,1)}, bf16[256,2048]{1,0:T(8,128)(2,1)S(1)}, u32[]{:S(2)}, u32[]{:S(2)}) collective-permute-start(bf16[256,2048]{1,0:T(8,128)(2,1)} %get-tuple-element.190), channel_id=1, source_target_pairs={{0,6},{2,4},{4,2},{6,0},{1,7},{3,5},{5,3},{7,1},{8,14},{10,12},{12... | collective-permute-start | bytes 3145736 | tf_op jit(solution)/shard_map/ppermute | solution.py:39
  572.1 56.4 %collective-permute-start.11 = (bf16[256,2048]{1,0:T(8,128)(2,1)}, bf16[256,2048]{1,0:T(8,128)(2,1)}, u32[]{:S(2)}, u32[]{:S(2)}) collective-permute-start(bf16[256,2048]{1,0:T(8,128)(2,1)} %get-tuple-element.191), channel_id=1, source_target_pairs={{0,4},{2,6},{4,0},{6,2},{1,5},{3,7},{5,1},{7,3},{8,12},{10,14},{12... | collective-permute-start | bytes 3145736 | tf_op jit(solution)/shard_map/ppermute | solution.py:39
  573.0 55.6 %collective-permute-start.10 = (bf16[256,2048]{1,0:T(8,128)(2,1)}, bf16[256,2048]{1,0:T(8,128)(2,1)}, u32[]{:S(2)}, u32[]{:S(2)}) collective-permute-start(bf16[256,2048]{1,0:T(8,128)(2,1)} %get-tuple-element.189), channel_id=1, source_target_pairs={{0,2},{2,0},{4,6},{6,4},{1,3},{3,1},{5,7},{7,5},{8,10},{10,8},{12,... | collective-permute-start | bytes 3145736 | tf_op jit(solution)/shard_map/ppermute | solution.py:39
  573.7 46.0 %collective-permute-start.23 = (bf16[2,16,320]{2,1,0:T(8,128)(2,1)S(1)}, bf16[2,16,320]{2,1,0:T(8,128)(2,1)S(1)}, u32[]{:S(2)}, u32[]{:S(2)}) collective-permute-start(bf16[2,16,320]{2,1,0:T(8,128)(2,1)S(1)} %get-tuple-element.249), channel_id=1, source_target_pairs={{0,6},{2,4},{4,2},{6,0},{1,7},{3,5},{5,3},{7,1},{8,14},{10,12},{12... | collective-permute-start | bytes 61448 | tf_op jit(solution)/shard_map/ppermute | solution.py:39
  575.7 45.6 %collective-permute-start.22 = (bf16[2,16,320]{2,1,0:T(8,128)(2,1)S(1)}, bf16[2,16,320]{2,1,0:T(8,128)(2,1)S(1)}, u32[]{:S(2)}, u32[]{:S(2)}) collective-permute-start(bf16[2,16,320]{2,1,0:T(8,128)(2,1)S(1)} %get-tuple-element.250), channel_id=1, source_target_pairs={{0,4},{2,6},{4,0},{6,2},{1,5},{3,7},{5,1},{7,3},{8,12},{10,14},{12... | collective-permute-start | bytes 61448 | tf_op jit(solution)/shard_map/ppermute | solution.py:39
  628.5 54.5 %collective-permute-start.30 = (bf16[4,64,1536]{2,1,0:T(8,128)(2,1)}, bf16[4,64,1536]{2,1,0:T(8,128)(2,1)S(1)}, u32[]{:S(2)}, u32[]{:S(2)}) collective-permute-start(bf16[4,64,1536]{2,1,0:T(8,128)(2,1)} %get-tuple-element.210), channel_id=1, source_target_pairs={{0,1},{1,0},{2,3},{3,2},{4,5},{5,4},{6,7},{7,6},{8,9},{9,8},{10,11... | collective-permute-start | bytes 2359304 | tf_op jit(solution)/shard_map/ppermute | solution.py:34
  683.2 13.1 %collective-permute-start.33 = (bf16[2,64,1536]{2,1,0:T(8,128)(2,1)S(1)}, bf16[2,64,1536]{2,1,0:T(8,128)(2,1)S(1)}, u32[]{:S(2)}, u32[]{:S(2)}) collective-permute-start(bf16[2,64,1536]{2,1,0:T(8,128)(2,1)S(1)} %get-tuple-element.209), channel_id=1, source_target_pairs={{0,6},{2,4},{4,2},{6,0},{1,7},{3,5},{5,3},{7,1},{8,14},{10,12},{12... | collective-permute-start | bytes 1179656 | tf_op jit(solution)/shard_map/ppermute | solution.py:39
  684.6 17.5 %collective-permute-start.32 = (bf16[2,64,1536]{2,1,0:T(8,128)(2,1)S(1)}, bf16[2,64,1536]{2,1,0:T(8,128)(2,1)S(1)}, u32[]{:S(2)}, u32[]{:S(2)}) collective-permute-start(bf16[2,64,1536]{2,1,0:T(8,128)(2,1)S(1)} %get-tuple-element.208), channel_id=1, source_target_pairs={{0,4},{2,6},{4,0},{6,2},{1,5},{3,7},{5,1},{7,3},{8,12},{10,14},{12... | collective-permute-start | bytes 1179656 | tf_op jit(solution)/shard_map/ppermute | solution.py:39
  685.2 17.9 %collective-permute-start.31 = (bf16[2,64,1536]{2,1,0:T(8,128)(2,1)S(1)}, bf16[2,64,1536]{2,1,0:T(8,128)(2,1)S(1)}, u32[]{:S(2)}, u32[]{:S(2)}) collective-permute-start(bf16[2,64,1536]{2,1,0:T(8,128)(2,1)S(1)} %get-tuple-element.207), channel_id=1, source_target_pairs={{0,2},{2,0},{4,6},{6,4},{1,3},{3,1},{5,7},{7,5},{8,10},{10,8},{12,... | collective-permute-start | bytes 1179656 | tf_op jit(solution)/shard_map/ppermute | solution.py:39
  729.9 8.8 %collective-permute-start.26 = (bf16[2,64,640]{2,1,0:T(8,128)(2,1)S(1)}, bf16[2,64,640]{2,1,0:T(8,128)(2,1)S(1)}, u32[]{:S(2)}, u32[]{:S(2)}) collective-permute-start(bf16[2,64,640]{2,1,0:T(8,128)(2,1)S(1)} %get-tuple-element.224), channel_id=1, source_target_pairs={{0,4},{2,6},{4,0},{6,2},{1,5},{3,7},{5,1},{7,3},{8,12},{10,14},{12... | collective-permute-start | bytes 491528 | tf_op jit(solution)/shard_map/ppermute | solution.py:39
  730.6 8.9 %collective-permute-start.25 = (bf16[2,64,640]{2,1,0:T(8,128)(2,1)S(1)}, bf16[2,64,640]{2,1,0:T(8,128)(2,1)S(1)}, u32[]{:S(2)}, u32[]{:S(2)}) collective-permute-start(bf16[2,64,640]{2,1,0:T(8,128)(2,1)S(1)} %get-tuple-element.223), channel_id=1, source_target_pairs={{0,2},{2,0},{4,6},{6,4},{1,3},{3,1},{5,7},{7,5},{8,10},{10,8},{12,... | collective-permute-start | bytes 491528 | tf_op jit(solution)/shard_map/ppermute | solution.py:39
  (49 other events, 612.1 us)
Sparse Core Ops, SparseCore 0:
  9.6 36.5 all-gather.3
  103.1 116.8 all-gather.5
  221.6 62.7 all-gather.7
  342.6 113.2 reduce-scatter.5
  458.0 33.5 reduce-scatter.13
  497.9 60.6 reduce-scatter.7
  561.4 19.4 reduce-scatter.11
  583.3 50.3 reduce-scatter.9

commit v3 on v2

--- a/solution.py
+++ b/solution.py
@@ -44,38 +44,12 @@
     return lax.ppermute(value, "a", [(i, i + by) for i in range(size) if 0 <= i + by < size])
 
 
-def cycle_a(value, by):
-    size = lax.axis_size("a")
-    return lax.ppermute(value, "a", [(i, (i + by) % size) for i in range(size)])
-
-
 def chips():
     return lax.axis_size("b") * lax.axis_size("n")
 
 
 def chip():
     return lax.axis_index("b") * lax.axis_size("n") + lax.axis_index("n")
-
-
-def plane_gather(value):
-    mine = jnp.stack([value] + [xor_u(value, k) for k in range(1, chips())])
-    return jnp.concatenate([mine, swap_c(mine)])
-
-
-def exchange(pieces):
-    c, u = lax.axis_index("c"), chip()
-    both = jnp.stack([pick(pieces, c), swap_c(pick(pieces, 1 - c))])
-    out = []
-    for k in range(chips()):
-        piece = pick(both, u ^ k, 1)
-        out.append(piece if k == 0 else xor_u(piece, k))
-    return jnp.stack(out, 1)
-
-
-def by_owner(rel):
-    c, u = lax.axis_index("c"), chip()
-    rel = jnp.stack([pick(rel, c), pick(rel, 1 - c)])
-    return jnp.stack([pick(rel, u ^ q, 1) for q in range(chips())], 1)
 
 
 MESH = pl.DeviceIdType.MESH
@@ -168,13 +142,47 @@
 GATHER_COPIES = 14
 
 
-def reduce_kernel(nt, post, waits, x_hbm, w_hbm, *refs):
-    gain_ref, first_ref, second_ref = refs[:3]
-    out_ref, refs = refs[3 + waits], refs[4 + waits :]
+def plane_peers_of():
+    a, b, n, c = places()
+    peers = {}
+    for kc in range(2):
+        for k in range(4):
+            if (kc, k) != (0, 0):
+                there = (a, 1 - b if k & 2 else b, 1 - n if k & 1 else n, 1 - c if kc else c)
+                peers[kc, k] = there
+    return peers
+
+
+def peer_owner(kc, k):
+    _, b, n, c = places()
+    return ((b * 2 + n) ^ k) * 2 + (1 - c if kc else c)
+
+
+def set_side_by_side(pieces, order, width):
+    group = 1
+    while group * width % 128 and group < len(order):
+        group += 1
+    for i in range(0, len(order), group):
+        runs = [pieces[p, :, o : o + width].astype(F32) for p, o in order[i : i + group]]
+        yield slice(i * width, (i + len(runs)) * width), jnp.concatenate(runs, 1)
+
+
+def reduce_kernel(nt, post, nx, extra, waits, hid, *refs):
+    x_hbm, refs = refs[:nx], refs[nx:]
+    w_hbm, gain_ref, first_ref, second_ref = refs[:4]
+    extra_in, refs = refs[4 : 4 + extra], refs[4 + extra :]
+    if post == "last":
+        lasts_ref, refs = refs[0], refs[1:]
+    refs = refs[waits:]
+    out_ref, refs = refs[0], refs[1:]
     if post == "last":
         everyone = mine = None
+        extra_out, lasts_out = refs[:extra], refs[extra]
+        extra_buf, lasts_buf, lasts_mine, lasts_far, refs = *refs[extra + 1 : extra + 5], refs[extra + 5 :]
     else:
         everyone, refs = refs[0], refs[1:]
+        if extra:
+            extra_out, refs = refs[0], refs[1:]
         mine, refs = refs[0], refs[1:]
     x_v, w_v, away_s, away_r, acc, out_b, in_b, local, send, recv = refs
     rows, d_model = acc.shape[1:]
@@ -183,13 +191,32 @@
     px, py, pc = neighbours()
     move = Mover(send, recv)
 
-    w_copy = pltpu.make_async_copy(w_hbm, w_v, local.at[8])
-    w_copy.start()
+    slots = iter(range(local.shape[0]))
+
+    def keep(src, dst):
+        made = pltpu.make_async_copy(src, dst, local.at[next(slots)])
+        made.start()
+        return made
+
+    w_copy = keep(w_hbm, w_v)
     loads = {}
-    for i, (k, kc) in enumerate((k, kc) for k in (3, 2, 1, 0) for kc in (1, 0)):
-        loads[kc, k] = pltpu.make_async_copy(x_hbm.at[kc, k], x_v.at[kc, k], local.at[i])
-        loads[kc, k].start()
-    greet((px, py, pc))
+    each = x_v.shape[3] // nx
+    for k in (3, 2, 1, 0):
+        for kc in (1, 0):
+            loads[kc, k] = [
+                keep(x.at[kc, k], x_v.at[kc, k, :, pl.ds(i * each, each)])
+                for i, x in enumerate(x_hbm)
+            ]
+    if post == "last":
+        a, b, n, c = places()
+        planes = lasts_far.shape[0] + 1
+        columns = [(lax.rem(a + d, planes), b, n, c) for d in range(1, planes)]
+        peers = plane_peers_of()
+        greet([*peers.values(), *columns])
+        for (kc, k), peer in peers.items():
+            move.start(f"l{kc}{k}", lasts_ref.at[kc, k % 2], lasts_buf.at[kc, k], peer)
+    else:
+        greet((px, py, pc))
     w_copy.wait()
 
     def product(kc, k, t):
@@ -217,7 +244,8 @@
         move.start(name, out_b.at[slot], in_b.at[slot], peer)
 
     for k in (3, 2, 1, 0):
-        loads[1, k].wait()
+        for load in loads[1, k]:
+            load.wait()
 
         @pl.loop(0, d_model // tile)
         def _(t):
@@ -225,7 +253,8 @@
             away_s[k, :, at] = value.astype(BF)
 
         move.start(f"away{k}", away_s.at[k], away_r.at[k], pc)
-        loads[0, k].wait()
+        for load in loads[0, k]:
+            load.wait()
 
         @pl.loop(0, d_model // tile)
         def _(t):
@@ -245,10 +274,38 @@
             hand_on("x0", 2, 2, 0, px)
         elif k == 1:
             hand_on("y1", 5, 1, 1, py)
+    kept = []
+    if extra and post == "fwd":
+        for k in range(4):
+            kept.append(keep(extra_in[k], extra_out.at[k]))
+            move.start(f"e{k}", extra_in[k], extra_out.at[4 + k], pc)
     move.arrived("d0")
     hand_on("y0", 4, 1, 0, py, 0)
     move.arrived("d1")
     hand_on("x1", 3, 2, 1, px, 1)
+    if extra and post == "last":
+        lasts_buf[0, 0] = lasts_ref[0, 0]
+        for kc, k in peers:
+            move.arrived(f"l{kc}{k}")
+        u = b * 2 + n
+        me = u * 2 + c
+        for kc in range(2):
+            for q in range(4):
+                found = lasts_buf[kc, 0]
+                for k in range(1, 4):
+                    found = jnp.where((u ^ k) == q, lasts_buf[kc, k], found)
+                lasts_mine[jnp.bitwise_xor(c, kc), q] = found
+        for i, peer in enumerate(columns):
+            move.start(f"z{i}", lasts_mine, lasts_far.at[i], peer)
+        each_rows = extra_buf.shape[2]
+        for i in range(extra):
+            def part(owner, i=i):
+                at = pl.multiple_of(owner * each_rows, each_rows)
+                return extra_in[i].at[pl.ds(at, each_rows)]
+
+            kept.append(keep(part(me), extra_buf.at[i, me]))
+            for (kc, k), peer in plane_peers_of().items():
+                move.start(f"e{i}{kc}{k}", part(peer_owner(kc, k)), extra_buf.at[i, me], peer)
 
     for h in range(2):
         move.arrived(f"x{h}")
@@ -281,14 +338,29 @@
         if everyone is not None:
             gather_plane_start(move, mine, everyone, h, half)
     if everyone is not None:
-        own = pltpu.make_async_copy(mine, everyone.at[0], local.at[9])
-        own.start()
+        kept.append(keep(mine, everyone.at[0]))
         gather_plane_rest(move, everyone, half)
-        own.wait()
+    if extra and post == "fwd":
+        for k in range(4):
+            move.arrived(f"e{k}")
+    for made in kept:
+        made.wait()
+    if extra and post == "last":
+        total = lasts_mine[...].astype(F32)
+        for i in range(len(columns)):
+            move.arrived(f"z{i}")
+            total = total + lasts_far[i].astype(F32)
+        lasts_out[...] = total.astype(BF)
+        order = [(p, z * hid) for z in range(extra_buf.shape[3] // hid) for p in range(8)]
+        for i in range(extra):
+            for kc, k in plane_peers_of():
+                move.arrived(f"e{i}{kc}{k}")
+            for at, value in set_side_by_side(extra_buf.at[i], order, hid):
+                extra_out[i][:, at] = value
     move.sent()
 
 
-def plane_reduce(ident, post, nt, x, w, gain, first, second, done=()):
+def plane_reduce(ident, post, nt, xs, w, gain, first, second, extra=(), done=(), hid=0, lasts=None):
     rows, d_model = first.shape
     vmem = pl.BlockSpec(memory_space=pltpu.VMEM)
     hbm = pl.BlockSpec(memory_space=pl.ANY)
@@ -300,54 +372,72 @@
     if post != "last":
         out_shape.append(jax.ShapeDtypeStruct((8, rows, d_model), BF))
         out_specs.append(hbm)
+        copies += GATHER_COPIES
+        if extra:
+            out_shape.append(jax.ShapeDtypeStruct((8, rows, d_model), BF))
+            out_specs.append(hbm)
+            copies += 4
         scratch.append(pltpu.VMEM((rows, d_model), BF))
-        copies += GATHER_COPIES
+    else:
+        each = extra[0].shape[0] // 8, extra[0].shape[1]
+        for _ in extra:
+            out_shape.append(jax.ShapeDtypeStruct((each[0], 8 * each[1]), F32))
+            out_specs.append(vmem)
+        planes = lax.axis_size("a")
+        copies += 7 * len(extra) + 7 + planes - 1
+        block = (2, 4) + lasts.shape[2:]
+        out_shape.append(jax.ShapeDtypeStruct(block, BF))
+        out_specs.append(vmem)
+        scratch.append(pltpu.VMEM((len(extra), 8) + each, BF))
+        scratch += [pltpu.VMEM(block, BF)] * 2 + [pltpu.VMEM((planes - 1,) + block, BF)]
+    wide = sum(x.shape[3] for x in xs)
     scratch += [
-        pltpu.VMEM(x.shape, BF),
+        pltpu.VMEM((2, 4, rows, wide), BF),
         pltpu.VMEM(w.shape, BF),
         pltpu.VMEM((4, rows, d_model), BF),
         pltpu.VMEM((4, rows, d_model), BF),
         pltpu.VMEM((4, rows, d_model), F32),
         pltpu.VMEM((6, rows // 2, d_model), BF),
         pltpu.VMEM((6, rows // 2, d_model), BF),
-        pltpu.SemaphoreType.DMA((10,)),
+        pltpu.SemaphoreType.DMA((2 + 8 * len(xs) + len(extra),)),
         pltpu.SemaphoreType.DMA((copies,)),
         pltpu.SemaphoreType.DMA((copies,)),
     ]
     return pl.pallas_call(
-        functools.partial(reduce_kernel, nt, post, len(done)),
-        in_specs=[hbm, hbm, vmem, vmem, vmem] + [hbm] * len(done),
+        functools.partial(reduce_kernel, nt, post, len(xs), len(extra), len(done), hid),
+        in_specs=[hbm] * (len(xs) + 1)
+        + [vmem] * 3
+        + [hbm if post == "last" else vmem] * len(extra)
+        + [vmem] * (lasts is not None)
+        + [hbm] * len(done),
         out_specs=out_specs,
         out_shape=out_shape,
         scratch_shapes=scratch,
         compiler_params=pltpu.CompilerParams(
             collective_id=ident, has_side_effects=True, vmem_limit_bytes=VMEM_LIMIT
         ),
-        cost_estimate=pl.CostEstimate(
-            flops=2 * x.size * d_model, bytes_accessed=2 * (x.size + w.size), transcendentals=0
-        ),
+        cost_estimate=pl.CostEstimate(flops=0, bytes_accessed=8 << 20, transcendentals=0),
         name=f"plane_reduce_{post}",
-    )(x, w, gain.reshape(1, -1), first, second, *done)
+    )(*xs, w, gain.reshape(1, -1), first, second, *extra, *([] if lasts is None else [lasts]), *done)
 
 
 def start_kernel(
-    tokens_ref, yx_ref, gu_ref, rows_ref, vec_ref, stream_ref,
+    head_w, hid, tokens_ref, wy_ref, wx_ref, wg_ref, wu_ref, rows_ref, vec_ref, stream_ref,
     tok_out, yx_out, gu_out, rows_out, halves_out, vec_out, stream_out,
-    local, send, recv,
+    yx_ref, gu_ref, local, send, recv,
 ):
     a, b, n, c = places()
     planes = yx_out.shape[0]
-    u = b * 2 + n
-    p = u * 2 + c
-    px, py, pc = neighbours()
-    plane_peers = {}
-    for kc in range(2):
-        for k in range(4):
-            if (kc, k) != (0, 0):
-                b2 = 1 - b if k & 2 else b
-                n2 = 1 - n if k & 1 else n
-                plane_peers[kc, k] = (a, b2, n2, 1 - c if kc else c)
+    p = (b * 2 + n) * 2 + c
+    pc = neighbours()[2]
+    plane_peers = plane_peers_of()
     up, down = (a + 1, b, n, c), (a - 1, b, n, c)
+    each = planes // 2
+
+    def pack(out, sources, columns, width):
+        for owner in range(8):
+            runs = [w[:, o : o + width] for w in sources for o in columns(owner)]
+            out[owner] = jnp.concatenate(runs, 1)
 
     barrier = pltpu.get_barrier_semaphore()
     for peer in plane_peers.values():
@@ -361,12 +451,15 @@
     def _():
         pl.semaphore_signal(barrier, inc=1, device_id=down, device_id_type=MESH)
 
+    def head_columns(owner):
+        return [((owner % 2 * each + j) * 4 + owner // 2) * head_w for j in range(each)]
+
+    pack(yx_ref, (wy_ref, wx_ref), head_columns, head_w)
     others = len(plane_peers) + jnp.minimum(planes - 1 - a, 1) + jnp.minimum(a, 1)
     pl.semaphore_wait(barrier, others)
 
     move = Mover(send, recv)
     half = tokens_ref.shape[0] // 2
-    locals_ = []
 
     def keep(i, src, dst):
         made = pltpu.make_async_copy(src, dst, local.at[i])
@@ -375,8 +468,7 @@
 
     def to_owners(name, pieces, out):
         for (kc, k), peer in plane_peers.items():
-            owner = (u ^ k) * 2 + (1 - c if kc else c)
-            move.start(f"{name}{kc}{k}", pieces.at[owner], out.at[a, p], peer)
+            move.start(f"{name}{kc}{k}", pieces.at[peer_owner(kc, k)], out.at[a, p], peer)
 
     chains = {}
 
@@ -427,7 +519,6 @@
     own_yx = keep(1, yx_ref.at[p], yx_out.at[a, p])
     own_vec = keep(2, vec_ref, vec_out.at[a, p])
     own_rows = keep(0, rows_ref, rows_out.at[a])
-    own_gu = keep(3, gu_ref.at[p], gu_out.at[p])
     own_tok = keep(4, tokens_ref, tok_out.at[0])
     own_stream = keep(5, stream_ref, stream_out.at[0, 0])
     own_yx.wait()
@@ -441,6 +532,8 @@
         chain_step(name, out, 0)
     for h in range(2):
         gather_plane_start(move, tokens_ref, tok_out, h, half)
+    pack(gu_ref, (wg_ref, wu_ref), lambda o: [(z * 8 + o) * hid for z in range(planes)], hid)
+    own_gu = keep(3, gu_ref.at[p], gu_out.at[p])
     gather_plane_rest(move, tok_out, half, 0)
     for kc in range(2):
         for kn in range(2):
@@ -451,15 +544,13 @@
         chain_step(name, out, 1)
     gather_plane_rest(move, tok_out, half, 1)
     for (kc, k), peer in plane_peers.items():
-        owner = (u ^ k) * 2 + (1 - c if kc else c)
-        move.start(f"gu{kc}{k}", gu_ref.at[owner], gu_out.at[p], peer)
+        move.start(f"gu{kc}{k}", gu_ref.at[peer_owner(kc, k)], gu_out.at[p], peer)
     for s in range(1, planes - 1):
         for name, out in outs:
             chain_arrived(name, s)
             if s + 1 < planes - 1:
                 chain_step(name, out, s + 1)
     gather_plane_rest(move, tok_out, half, 2)
-    each = planes // 2
     swap = pltpu.make_async_remote_copy(
         src_ref=rows_out.at[pl.ds((1 - c) * each, each)],
         dst_ref=halves_out.at[:, c],
@@ -485,25 +576,31 @@
         move.made[name].wait_send()
 
 
-def start_exchange(tokens, yx, gu, mixer_rows, vec, stream):
+def start_exchange(tokens, w_y, w_x, w_gate, w_up, gate_rows, vec, stream):
     planes = lax.axis_size("a")
+    head_w, hid = gate_rows.shape[1] // 2, w_gate.shape[1] // (planes * 8)
+    vmem = pl.BlockSpec(memory_space=pltpu.VMEM)
     hbm = pl.BlockSpec(memory_space=pl.ANY)
+    yx = (8, w_y.shape[0], 2 * w_y.shape[1] // 8)
+    gu = (8, w_gate.shape[0], 2 * w_gate.shape[1] // 8)
     shapes = [
         ((8,) + tokens.shape, BF),
-        ((planes,) + yx.shape, BF),
-        (gu.shape, BF),
-        ((planes,) + mixer_rows.shape, BF),
-        ((planes // 2, 2) + mixer_rows.shape, BF),
+        ((planes,) + yx, BF),
+        (gu, BF),
+        ((planes,) + gate_rows.shape, BF),
+        ((planes // 2, 2) + gate_rows.shape, BF),
         ((planes, 8) + vec.shape, F32),
         ((2, 2) + stream.shape, F32),
     ]
     copies = 7 * 3 + 3 + GATHER_COPIES + 6 * (planes - 1) + 1
     return pl.pallas_call(
-        start_kernel,
-        in_specs=[hbm] * 6,
+        functools.partial(start_kernel, head_w, hid),
+        in_specs=[vmem] * 8,
         out_specs=[hbm] * 7,
-        out_shape=[jax.ShapeDtypeStruct(*s) for s in shapes],
+        out_shape=[jax.ShapeDtypeStruct(*shape) for shape in shapes],
         scratch_shapes=[
+            pltpu.VMEM(yx, BF),
+            pltpu.VMEM(gu, BF),
             pltpu.SemaphoreType.DMA((7,)),
             pltpu.SemaphoreType.DMA((copies,)),
             pltpu.SemaphoreType.DMA((copies,)),
@@ -511,12 +608,202 @@
         compiler_params=pltpu.CompilerParams(
             collective_id=1, has_side_effects=True, vmem_limit_bytes=VMEM_LIMIT
         ),
-        cost_estimate=pl.CostEstimate(flops=0, bytes_accessed=100 << 20, transcendentals=0),
+        cost_estimate=pl.CostEstimate(flops=0, bytes_accessed=8 << 20, transcendentals=0),
         name="start_exchange",
-    )(tokens, yx, gu, mixer_rows, vec, stream)
-
-
-def norm_product_kernel(info, tok_ref, w_ref, gain_ref, n_ref, gate_ref, lin_ref):
+    )(tokens, w_y, w_x, w_gate, w_up, gate_rows, vec, stream)
+
+
+def finish_kernel(head_w, sums_ref, y_ref, x_ref, buf, local, send, recv):
+    _, b, n, c = places()
+    me = (b * 2 + n) * 2 + c
+    peers = plane_peers_of()
+    greet(list(peers.values()))
+    move = Mover(send, recv)
+    each_rows = buf.shape[1]
+
+    def part(owner):
+        return sums_ref.at[pl.ds(pl.multiple_of(owner * each_rows, each_rows), each_rows)]
+
+    for (kc, k), peer in peers.items():
+        move.start(f"e{kc}{k}", part(peer_owner(kc, k)), buf.at[me], peer)
+    own = pltpu.make_async_copy(part(me), buf.at[me], local.at[0])
+    own.start()
+    own.wait()
+    for kc, k in peers:
+        move.arrived(f"e{kc}{k}")
+    wide = buf.shape[2] // 2
+    each = wide // head_w
+    order = [(q * 2 + i, j * head_w) for i in range(2) for j in range(each) for q in range(4)]
+    for first, out in ((0, y_ref), (wide, x_ref)):
+        for at, value in set_side_by_side(buf, [(p, o + first) for p, o in order], head_w):
+            out[:, at] = value
+    move.sent()
+
+
+def finish(sums, head_w):
+    each = sums.shape[0] // 8, sums.shape[1]
+    vmem = pl.BlockSpec(memory_space=pltpu.VMEM)
+    return pl.pallas_call(
+        functools.partial(finish_kernel, head_w),
+        in_specs=[pl.BlockSpec(memory_space=pl.ANY)],
+        out_specs=[vmem, vmem],
+        out_shape=[jax.ShapeDtypeStruct((each[0], 4 * each[1]), F32)] * 2,
+        scratch_shapes=[
+            pltpu.VMEM((8,) + each, BF),
+            pltpu.SemaphoreType.DMA((1,)),
+            pltpu.SemaphoreType.DMA((7,)),
+            pltpu.SemaphoreType.DMA((7,)),
+        ],
+        compiler_params=pltpu.CompilerParams(
+            collective_id=5, has_side_effects=True, vmem_limit_bytes=VMEM_LIMIT
+        ),
+        name="finish",
+    )(sums)
+
+
+def column_peers(planes):
+    a, b, n, c = places()
+    return [(lax.rem(a + d, planes), b, n, c) for d in range(1, planes)]
+
+
+def earlier_blocks(ref, want, row=0, count=1):
+    _, b, _, _ = places()
+    return [
+        jnp.where(
+            b == want,
+            ref[kc * 4 + kn, row : row + count, :],
+            ref[kc * 4 + 2 + kn, row : row + count, :],
+        )
+        for kc in range(2)
+        for kn in range(2)
+    ]
+
+
+def pass_state_kernel(reverse, mul_ref, add_ref, out_ref, whole, came, send, recv):
+    a, b, n, c = places()
+    planes = came.shape[0] + 1
+    row = 0 if reverse else 7
+    near_at, far_at = (1, 0) if reverse else (0, 1)
+    came[...] = jnp.zeros_like(came)
+    near_mul, near_add = earlier_blocks(mul_ref, near_at, row), earlier_blocks(add_ref, near_at, row)
+    far_mul, far_add = earlier_blocks(mul_ref, far_at, row), earlier_blocks(add_ref, far_at, row)
+    for i in range(4):
+        whole[0, i : i + 1, :] = near_mul[i] * far_mul[i]
+        whole[1, i : i + 1, :] = far_mul[i] * near_add[i] + far_add[i]
+    greet(column_peers(planes))
+
+    def copy(d):
+        return pltpu.make_async_remote_copy(
+            src_ref=whole,
+            dst_ref=came.at[d - 1],
+            send_sem=send.at[d - 1],
+            recv_sem=recv.at[d - 1],
+            device_id=(a - d if reverse else a + d, b, n, c),
+            device_id_type=MESH,
+        )
+
+    def sends(d):
+        return a >= d if reverse else a + d < planes
+
+    def receives(d):
+        return a + d < planes if reverse else a >= d
+
+    for d in range(1, planes):
+        @pl.when(sends(d))
+        def _():
+            copy(d).start()
+
+    for d in range(1, planes):
+        @pl.when(receives(d))
+        def _():
+            copy(d).wait_recv()
+
+    for i in range(4):
+        at = slice(i, i + 1)
+        value = came[planes - 2, 1, at, :]
+        for d in range(planes - 2, 0, -1):
+            value = came[d - 1, 0, at, :] * value + came[d - 1, 1, at, :]
+        to_far = near_mul[i] * value + near_add[i]
+        for kb in range(2):
+            is_far = (b if kb == 0 else 1 - b) == far_at
+            at = (i // 2) * 4 + kb * 2 + i % 2
+            out_ref[at] = jnp.where(is_far, to_far, value)
+
+    for d in range(1, planes):
+        @pl.when(sends(d))
+        def _():
+            copy(d).wait_send()
+
+
+def pass_rows_kernel(reverse, edge_ref, out_ref, leaving, came, send, recv):
+    a, b, n, c = places()
+    planes = lax.axis_size("a")
+    near_at, far_at = (1, 0) if reverse else (0, 1)
+    came[...] = jnp.zeros_like(came)
+    out_ref[...] = jnp.zeros_like(out_ref)
+    first = 0 if reverse else 4
+    for i, value in enumerate(earlier_blocks(edge_ref, far_at, first, 4)):
+        leaving[i * 4 : i * 4 + 4, :] = value
+    greet(column_peers(planes))
+    copy = pltpu.make_async_remote_copy(
+        src_ref=leaving,
+        dst_ref=came,
+        send_sem=send.at[0],
+        recv_sem=recv.at[0],
+        device_id=(a - 1 if reverse else a + 1, b, n, c),
+        device_id_type=MESH,
+    )
+    sends = a >= 1 if reverse else a + 1 < planes
+    receives = a + 1 < planes if reverse else a >= 1
+
+    @pl.when(sends)
+    def _():
+        copy.start()
+
+    @pl.when(receives)
+    def _():
+        copy.wait_recv()
+
+    for i in range(4):
+        for kb in range(2):
+            is_far = (b if kb == 0 else 1 - b) == far_at
+            at = (i // 2) * 4 + kb * 2 + i % 2
+            other = (i // 2) * 4 + (1 - kb) * 2 + i % 2
+            out_ref[at, first : first + 4, :] = jnp.where(
+                is_far, edge_ref[other, first : first + 4, :], came[i * 4 : i * 4 + 4, :]
+            )
+
+    @pl.when(sends)
+    def _():
+        copy.wait_send()
+
+
+def pass_along(ident, name, reverse, *edges):
+    shape = edges[0].shape
+    planes = lax.axis_size("a")
+    vmem = pl.BlockSpec(memory_space=pltpu.VMEM)
+    if len(edges) == 2:
+        body, out = pass_state_kernel, (shape[0], 1, shape[2])
+        buffers = [(2, 4) + shape[2:], (planes - 1, 2, 4) + shape[2:]]
+    else:
+        body, out = pass_rows_kernel, shape
+        buffers = [(16,) + shape[2:]] * 2
+    return pl.pallas_call(
+        functools.partial(body, reverse),
+        in_specs=[vmem] * len(edges),
+        out_specs=vmem,
+        out_shape=jax.ShapeDtypeStruct(out, F32),
+        scratch_shapes=[pltpu.VMEM(shape, F32) for shape in buffers]
+        + [pltpu.SemaphoreType.DMA((planes - 1,))] * 2,
+        compiler_params=pltpu.CompilerParams(
+            collective_id=ident, has_side_effects=True, vmem_limit_bytes=VMEM_LIMIT
+        ),
+        cost_estimate=pl.CostEstimate(flops=0, bytes_accessed=1 << 20, transcendentals=0),
+        name=name,
+    )(*edges)
+
+
+def norm_product_kernel(info, tok_ref, w_ref, gain_ref, n_ref, gate_ref, lin_ref, tail_ref):
     rows, d_model = tok_ref.shape[1:]
     step = min(64, rows)
 
@@ -529,8 +816,12 @@
 
     wide = gate_ref.shape[2]
     both = mdot(n_ref[0], w_ref[...])
-    gate_ref[0] = both[:, :wide]
-    lin_ref[0] = both[:, wide:].astype(BF)
+    used = both.shape[1] // 2
+    pad = [jnp.zeros((rows, wide - used), F32)] if wide > used else []
+    gate_ref[0] = jnp.concatenate([both[:, :used]] + pad, 1)
+    low = jnp.concatenate([both[:, used:]] + pad, 1).astype(BF)
+    lin_ref[0] = low
+    tail_ref[0] = low.astype(F32)[rows - 8 :, :]
 
 
 def row_places(info, rows, nseq):
@@ -594,7 +885,7 @@
 
 def forward_kernel(
     nseq, taps, info, lin_ref, rim_ref, conv0_ref, state0_ref, wg_ref, vec_ref,
-    conv_ref, retain_ref, admit_ref, p_ref, s_ref, ext, a_s, b_s,
+    conv_ref, retain_ref, admit_ref, p_ref, s_ref, pe_ref, se_ref, ext, a_s, b_s,
 ):
     i = pl.program_id(0)
     rows, wide = lin_ref.shape[1:]
@@ -624,6 +915,8 @@
     a_s[...] = jnp.where(at == 0, 0.0, a)
     b_s[...] = drive
     run_scan(a_s, b_s, p_ref, s_ref, rows, False)
+    pe_ref[0] = p_ref[0, rows - 8 : rows, :]
+    se_ref[0] = s_ref[0, rows - 8 : rows, :]
 
 
 def gelu_pair(x):
@@ -638,7 +931,7 @@
 def back_scan_kernel(
     nseq, taps, info, dres_ref, wo_ref, gate_ref, hidden_ref, retain_ref, vec_ref, *refs
 ):
-    dgate_ref, p_ref, s_ref, head_ref, ext, a_s, b_s = refs[-7:]
+    dgate_ref, p_ref, s_ref, pe_ref, se_ref, ext, a_s, b_s = refs[-8:]
     rows = gate_ref.shape[1]
     pos, begin, _ = row_places(info, rows, nseq)
     d_mixed = ndot(dres_ref[0], wo_ref[...])
@@ -649,16 +942,17 @@
     a = jnp.where(pos == begin, 0.0, jnp.exp(-8.0 * retain_ref[0] * soft))
     ext[0:rows, :] = a
     ext[rows : rows + 8, :] = jnp.ones((8, a.shape[1]), F32)
-    head_ref[0] = ext[0:8, :]
     a_s[...] = ext[1 : rows + 1, :]
     run_scan(a_s, b_s, p_ref, s_ref, rows, True)
+    pe_ref[0] = ext[0:8, :] * p_ref[0, 0:8, :]
+    se_ref[0] = ext[0:8, :] * s_ref[0, 0:8, :]
 
 
 def back_kernel(
     nseq, taps, info, p_ref, s_ref, grad_in_ref, hidden_ref, state_in_ref, state0_ref, conv_ref,
     retain_ref, admit_ref, lin_ref, rim_ref, conv0_ref, wg_ref, vec_ref, *refs
 ):
-    dconv_ref, wgrad_ref, vgrad_ref, ext = refs[-4:]
+    dconv_ref, head_ref, wgrad_ref, vgrad_ref, ext = refs[-5:]
     i = pl.program_id(0)
     rows, wide = lin_ref.shape[1:]
     pos, begin, seg = row_places(info, rows, nseq)
@@ -686,6 +980,7 @@
     low = d_conv.astype(BF)
     dconv_ref[0] = low
     low = low.astype(F32)
+    head_ref[0] = low[0:8, :]
 
     @pl.when(i == 0)
     def _():
@@ -699,7 +994,8 @@
         vgrad_ref[k : k + 1, :] += jnp.sum(value, axis=0, keepdims=True)
 
 
-def back_conv_kernel(nseq, taps, info, dconv_ref, rim_ref, dgate_ref, vec_ref, out_ref, ext):
+def back_conv_kernel(nseq, taps, info, dconv_ref, rim_ref, dgate_ref, vec_ref, *refs):
+    out_ref, ext = refs[-2:]
     i = pl.program_id(0)
     rows, wide = dconv_ref.shape[1:]
     pos = info[i, 0] + lax.broadcasted_iota(jnp.int32, (rows, 1), 0)
@@ -712,11 +1008,12 @@
             start = info[i, 1 + s]
             cut = jnp.where((pos < start) & (pos + k >= start), 1, cut)
         total = total + vec_ref[k : k + 1, :] * jnp.where(cut == 0, ext[k : k + rows, :], 0.0)
-    out_ref[0, :, :wide] = dgate_ref[0]
-    out_ref[0, :, wide:] = total.astype(BF)
-
-
-def by_block(body, info, ins, outs, scratch, done=(), name=None, cost=None):
+    used = out_ref.shape[2] // 2
+    both = [dgate_ref[0].astype(F32)[:, :used], total[:, :used]]
+    out_ref[0] = jnp.concatenate(both, 1).astype(BF)
+
+
+def by_block(body, info, ins, outs, scratch, done=(), name=None):
     blocks = info.shape[0]
 
     def spec(shape, blocked):
@@ -737,7 +1034,7 @@
         ),
         out_shape=[jax.ShapeDtypeStruct(shape, kind) for shape, kind, _ in outs],
         compiler_params=pltpu.CompilerParams(vmem_limit_bytes=VMEM_LIMIT),
-        cost_estimate=cost,
+        cost_estimate=pl.CostEstimate(flops=0, bytes_accessed=1 << 20, transcendentals=0),
         name=name,
     )(info, *[v for v, _ in ins], *done)
 
@@ -782,30 +1079,6 @@
     drows = w_y.shape[0]
     nblocks = 2 * count
 
-    def head_pieces(w):
-        w = w.reshape(w.shape[0], 2, heads_here, count, head_w)
-        return w.transpose(1, 3, 0, 2, 4).reshape(2, count, w.shape[0], wide_here)
-
-    def from_head_pieces(pieces):
-        r = pieces.shape[2]
-        pieces = pieces.reshape(2, count, r, heads_here, head_w)
-        return pieces.transpose(2, 0, 3, 1, 4).reshape(r, width)
-
-    def hidden_pieces(w):
-        w = w.reshape(w.shape[0], planes, count, 2, hid)
-        return w.transpose(3, 2, 0, 1, 4).reshape(2, count, w.shape[0], planes * hid)
-
-    def from_hidden_pieces(pieces):
-        r = pieces.shape[2]
-        pieces = pieces.reshape(2, count, r, planes, hid)
-        return pieces.transpose(2, 3, 1, 0, 4).reshape(r, planes * count * 2 * hid)
-
-    def row_blocks(owned):
-        return owned.swapaxes(0, 1).reshape((-1,) + owned.shape[3:])
-
-    def to_owner_rows(full):
-        return full.reshape((count, 2, -1) + full.shape[1:]).swapaxes(0, 1)
-
     def gather_a(value):
         return lax.all_gather(value, "a", axis=0, tiled=True)
 
@@ -816,9 +1089,6 @@
         pads = [(0, 0)] * v.ndim
         pads[axis] = (0, wp - wide_here)
         return jnp.pad(v, pads)
-
-    def owners(pieces):
-        return pieces.swapaxes(0, 1).reshape((nblocks,) + pieces.shape[2:])
 
     vectors = jnp.concatenate(
         [conv_kernel, conv_bias[None], bias_a[None], bias_i[None], decay_param[None]], 0
@@ -832,14 +1102,15 @@
     at_start = at_start.at[nseq * taps, :nseq].set(starts[0].astype(F32))
     all_tokens, w_yx, w_gu, _, gate_rows, canon, at_start = start_exchange(
         tokens[0],
-        owners(jnp.concatenate([head_pieces(w_y), head_pieces(w_x)], -1)),
-        owners(jnp.concatenate([hidden_pieces(w_gate), hidden_pieces(w_up)], -1)),
+        w_y,
+        w_x,
+        w_gate,
+        w_up,
         jnp.concatenate([gate_a, gate_i], 1),
         vectors,
         at_start,
     )
     w_yx = w_yx.reshape(d_model, 2 * wide_here)
-    w_yx = jnp.concatenate([padded(w_yx[:, :wide_here]), padded(w_yx[:, wide_here:])], 1)
     w_gu = gather_a(w_gu.reshape(-1, 2 * planes * hid))
     gate_rows = gate_rows.reshape(wide_here, -1)
 
@@ -915,9 +1186,10 @@
     )
 
     grad_low = cotangent[0]
-    grads = plane_gather(grad_low).reshape(nblocks * rows, d_model)
-
-    normed, gate_in, linear = by_block(
+    grads = [grad_low] + [xor_u(grad_low, k) for k in range(1, count)]
+
+    edge = ((nblocks, 8, wp), F32, True)
+    normed, gate_in, linear, tail = by_block(
         norm_product_kernel,
         info,
         [(all_tokens, True), (w_yx, False), (gain_one[None], False)],
@@ -925,6 +1197,7 @@
             ((nblocks, rows, d_model), BF, True),
             ((nblocks, rows, wp), F32, True),
             ((nblocks, rows, wp), BF, True),
+            edge,
         ],
         [],
         name="norm_product",
@@ -934,24 +1207,10 @@
     def two(v):
         return v.reshape((2, 2, nn) + v.shape[1:])
 
-    def flip(v):
-        v = two(v)
-        return jnp.stack([v[:, 1], v[:, 0]], 1).reshape((nblocks,) + v.shape[3:])
-
-    def of_stream(v, which):
-        v = two(v)
-        return jnp.where(b == which, v[:, 0], v[:, 1]).reshape((streams,) + v.shape[3:])
-
-    def second_half(shape):
-        return ((b ^ block_b) == 1).reshape((nblocks,) + (1,) * (len(shape) - 1))
-
-    tail = linear[:, rows - back :]
-    rim = per_block(shift_a(of_stream(tail, 1), 1))
-    rim = jnp.where(second_half(rim.shape), flip(tail), rim)
-    rim = jnp.pad(rim.astype(F32), ((0, 0), (8 - back, 0), (0, 0)))
+    rim = pass_along(6, "pass_rows", False, tail)
     conv_0b, state_0b = per_block(conv_0), per_block(state_0)
     full = (nblocks, rows, wp)
-    conv_low, retain, admit, carry_mul, carry_add = by_block(
+    conv_low, retain, admit, carry_mul, carry_add, end_mul, end_add = by_block(
         functools.partial(forward_kernel, nseq, taps),
         info,
         [
@@ -960,79 +1219,67 @@
         ],
         [
             (full, BF, True), (full, F32, True), (full, F32, True),
-            (full, F32, True), (full, F32, True),
+            (full, F32, True), (full, F32, True), edge, edge,
         ],
         [(rows + 8, wp), (rows, wp), (rows, wp)],
         name="mixer_forward",
     )
 
-    def entering(mul, add, reverse):
-        pair = jnp.stack([mul, add])
-        near = of_stream(pair.swapaxes(0, 1), 1 if reverse else 0)
-        far = of_stream(pair.swapaxes(0, 1), 0 if reverse else 1)
-        whole = jnp.stack([near[:, 0] * far[:, 0], far[:, 0] * near[:, 1] + far[:, 1]])
-        came = [shift_a(whole, -d if reverse else d) for d in range(1, planes)]
-        value = came[-1][1]
-        for part in came[-2::-1]:
-            value = part[0] * value + part[1]
-        to_far = near[:, 0] * value + near[:, 1]
-        value, to_far = per_block(value), per_block(to_far)
-        is_far = second_half(value.shape)
-        return jnp.where(is_far != reverse, to_far, value)
-
-    state_in = entering(carry_mul[:, -1], carry_add[:, -1], False)[:, None]
+    (end_mul, end_add), grads = lax.optimization_barrier(((end_mul, end_add), grads))
+    state_in = pass_along(7, "pass_state", False, end_mul, end_add)
     hidden = carry_mul * state_in + carry_add
     mixed_in = (hidden * jax.nn.gelu(gate_in)).astype(BF).reshape(-1, wp)
-    resid, normed_two = plane_reduce(
-        2, "fwd", False, mixed_in.reshape(2, count, rows, -1), w_o, gain_two, tokens[0], tokens[0],
-        (grads,),
+    resid, normed_two, grads = plane_reduce(
+        2, "fwd", False, (mixed_in.reshape(2, count, rows, -1),), w_o, gain_two, tokens[0],
+        tokens[0], grads,
     )
     normed_two = normed_two.reshape(nblocks * rows, d_model)
+    grads = grads.reshape(nblocks * rows, d_model)
 
     pair = mdot(normed_two, w_gu)
     gate, upward = pair[:, :f_here], pair[:, f_here:]
     active, gate_back = jax.vjp(jax.nn.gelu, gate)
     inner = (active * upward).astype(BF)
+    sums_d = tdot(inner, grads).astype(BF)
+    grad_wd = scatter_a(sums_d)
+    grads, _ = lax.optimization_barrier((grads, sums_d))
+    d_inner = ndot(grads, w_d)
+    d_gate = gate_back(d_inner * upward)[0].astype(BF)
+    d_up = (d_inner * active).astype(BF)
+    sums_g = tdot(normed_two, d_gate).astype(BF)
+    sums_u = tdot(normed_two, d_up).astype(BF)
+    sent_g, sent_u = scatter_a(sums_g), scatter_a(sums_u)
     parts = inner.reshape(2, count * rows, f_here)
     away = swap_c(mdot(parts[1], w_d).astype(BF))
-    low = (mdot(parts[0], w_d) + away.astype(F32)).astype(BF).reshape(count, rows, d_model)
+    d_resid, d_resid_low = plane_reduce(
+        3, "mid", True, (d_gate.reshape(2, count, rows, -1), d_up.reshape(2, count, rows, -1)), w_gu,
+        gain_two, grad_low, resid, (), (grad_wd, sums_g, sums_u, away),
+    )
+    d_resid_low = d_resid_low.reshape(nblocks * rows, d_model)
+
+    sums_o = tdot(mixed_in, d_resid_low)[:wide_here].astype(BF)
+    grad_wo = scatter_a(part_halves(sums_o))
+    own, _ = lax.optimization_barrier((parts[0], sums_o))
+    low = (mdot(own, w_d) + away.astype(F32)).astype(BF).reshape(count, rows, d_model)
     result = resid + low[0].astype(F32)
     for k in range(1, count):
         result = result + xor_u(low[k], k).astype(F32)
     result = result.astype(BF)
-    d_inner = ndot(grads, w_d)
-    sums_d = tdot(inner, grads).astype(BF)
-    grad_wd = scatter_a(sums_d)
-    d_gate = gate_back(d_inner * upward)[0].astype(BF)
-    d_up = (d_inner * active).astype(BF)
-    d_pair = jnp.concatenate([d_gate, d_up], 1)
-    sums_gu = tdot(normed_two, d_pair).astype(BF)
-    sums = scattered_gu = scatter_a(sums_gu)
-    sums = by_owner(exchange(to_owner_rows(sums)))
-    grad_wg = from_hidden_pieces(sums[..., :f_here]).astype(F32)
-    grad_wu = from_hidden_pieces(sums[..., f_here:]).astype(F32)
-
-    d_resid, d_resid_low = plane_reduce(
-        3, "mid", True, d_pair.reshape(2, count, rows, -1), w_gu, gain_two, grad_low, resid,
-        (sums_gu,),
-    )
-    d_resid_low = d_resid_low.reshape(nblocks * rows, d_model)
-
-    d_gate_in, back_mul, back_add, first = by_block(
+
+    d_gate_in, back_mul, back_add, end_mul, end_add = by_block(
         functools.partial(back_scan_kernel, nseq, taps),
         info,
         [
             (d_resid_low.reshape(nblocks, rows, d_model), True), (w_o, False), (gate_in, True),
             (hidden, True), (retain, True), (vec, False),
         ],
-        [(full, BF, True), (full, F32, True), (full, F32, True), ((nblocks, 8, wp), F32, True)],
+        [(full, BF, True), (full, F32, True), (full, F32, True), edge, edge],
         [(rows + 8, wp), (rows, wp), (rows, wp)],
+        (low, sent_g),
         name="mixer_back_scan",
     )
-    sums_o = tdot(mixed_in, d_resid_low)[:wide_here].astype(BF)
-    grad_wo = scatter_a(part_halves(sums_o)).astype(F32)
-    grad_in = entering(first[:, 0] * back_mul[:, 0], first[:, 0] * back_add[:, 0], True)[:, None]
-    d_conv_low, sums_gates, vec_grads = by_block(
+    grad_in = pass_along(8, "pass_state_back", True, end_mul, end_add)
+    d_conv_low, head, sums_gates, vec_grads = by_block(
         functools.partial(back_kernel, nseq, taps),
         info,
         [
@@ -1040,9 +1287,9 @@
             (state_in, True), (state_0b, True), (conv_low, True), (retain, True),
             (admit, True), (linear, True), (rim, True), (conv_0b, True), (w_gates, False), (vec, False),
         ],
-        [(full, BF, True), ((wp, 2 * wp), F32, False), ((taps + 4, wp), F32, False)],
+        [(full, BF, True), edge, ((wp, 2 * wp), F32, False), ((taps + 4, wp), F32, False)],
         [(rows + 8, wp)],
-        (scattered_gu,),
+        (result, sent_u),
         name="mixer_back",
     )
 
@@ -1057,16 +1304,14 @@
         ],
         1,
     )
-    head = d_conv_low[:, :back]
-    rim_back = per_block(shift_a(of_stream(head, 0), -1))
-    rim_back = jnp.where(second_half(head.shape), rim_back, flip(head))
-    rim_back = jnp.pad(rim_back.astype(F32), ((0, 0), (0, 8 - back), (0, 0)))
+    rim_back = pass_along(9, "pass_rows_back", True, head)
     d_both = by_block(
         functools.partial(back_conv_kernel, nseq, taps),
         info,
         [(d_conv_low, True), (rim_back, True), (d_gate_in, True), (vec, False)],
-        [((nblocks, rows, 2 * wp), BF, True)],
+        [((nblocks, rows, 2 * wide_here), BF, True)],
         [(rows + 8, wp)],
+        (grad_wo,),
         name="mixer_back_conv",
     )[0]
     vec_grads = vec_grads[:, :wide_here].T
@@ -1078,23 +1323,7 @@
     grad_wa, grad_wi = late[:, :head_w], late[:, head_w : 2 * head_w]
     vec_grads = late[:, 2 * head_w :].T
 
-    sums_yx = tdot(normed, d_both.reshape(nblocks * rows, 2 * wp)).astype(BF)
-    sums_yx = jnp.concatenate([sums_yx[:, :wide_here], sums_yx[:, wp : wp + wide_here]], 1)
-    input_grad = plane_reduce(
-        4, "last", True, d_both.reshape(2, count, rows, -1), w_yx, gain_one, tokens[0], d_resid,
-        (grad_wd, sums_yx, result),
-    )[0]
-    sums = scatter_a(sums_yx)
-    sums = by_owner(exchange(to_owner_rows(sums)))
-    grad_wy = from_head_pieces(sums[..., :wide_here]).astype(F32)
-    grad_wx = from_head_pieces(sums[..., wide_here:]).astype(F32)
-    def gain_grad(gain, *pairs):
-        total = sum(jnp.sum(w.astype(F32) * g, axis=1) for w, g in pairs)
-        return total / gain.astype(F32)
-
-    grad_gain_one = gain_grad(norm1_gain, (w_y, grad_wy), (w_x, grad_wx))
-    grad_gain_two = gain_grad(norm2_gain, (w_gate, grad_wg), (w_up, grad_wu))
-
+    sums_yx = tdot(normed, d_both.reshape(nblocks * rows, 2 * wide_here)).astype(BF)
     end = jnp.concatenate(
         [offsets[:, 1:], jnp.full((streams, 1), planes * 2 * rows, jnp.int32)], 1
     )
@@ -1111,13 +1340,20 @@
     )
     lasts = two(jnp.concatenate([lasts, conv_lasts], 1)[..., :wide_here])
     lasts = (lasts[:, 0] + lasts[:, 1]).astype(BF)
-    came = [cycle_a(lasts, d) for d in range(1, planes)]
-    lasts = sum(part.astype(F32) for part in [lasts] + came).astype(BF)
-    both = jnp.stack([lasts[0], swap_c(lasts[1])])
-    found = jnp.stack(
-        [both[:, k % nn] if k == 0 else xor_u(both[:, k % nn], k) for k in range(count)], 1
-    )
-    found = by_owner(found).reshape(2, count, nseq * taps, heads_here, head_w)
+    input_grad, grad_wg, grad_wu, found = plane_reduce(
+        4, "last", True, (d_both.reshape(2, count, rows, -1),), w_yx, gain_one, tokens[0], d_resid,
+        (sent_g, sent_u), (sums_yx, result), hid, lasts,
+    )
+    grad_wy, grad_wx = finish(scatter_a(sums_yx), head_w)
+
+    def gain_grad(gain, *pairs):
+        total = sum(jnp.sum(w.astype(F32) * g, axis=1) for w, g in pairs)
+        return total / gain.astype(F32)
+
+    grad_gain_one = gain_grad(norm1_gain, (w_y, grad_wy), (w_x, grad_wx))
+    grad_gain_two = gain_grad(norm2_gain, (w_gate, grad_wg), (w_up, grad_wu))
+
+    found = found.reshape(2, count, nseq * taps, heads_here, head_w)
     found = found.transpose(2, 0, 3, 1, 4).reshape(nseq * taps, width)
     final_state = found[:nseq].astype(F32)
     final_conv = found[nseq:].reshape(nseq, back, width)
@@ -1131,7 +1367,7 @@
         grad_wx,
         grad_wa,
         grad_wi,
-        grad_wo,
+        grad_wo.astype(F32),
         grad_gain_one,
         vec_grads[:taps],
         vec_grads[taps],

time: 767 us -> 684 us (0.89)
  Pallas kernels: 375 us -> 442 us
  local copies, waits for them, and re-layouts: 94.3 us -> 42.9 us
  waiting for transfers between devices: 73.3 us -> 34.4 us
  starting transfers between devices: 44.7 us -> 9.86 us
  other arithmetic: 55.4 us -> 35.6 us
    pallas_call x4 -> x9, Pallas kernels: 298 us -> 365 us  [the longest x3 238 us: plane_reduce(): pl.pallas_call(functools.partial(reduce_kernel, nt, post, len(xs), len(ex...]
    ppermute x15 -> x6, waiting for transfers between devices: 66.5 us -> 18.6 us  [xor_u(): return lax.ppermute(value, ('b', 'n'), [(i, i ^ k) for i in range(size)])]
    convert_element_type x12 -> x0, local copies, waits for them, and re-layouts: 24 us -> none  [the longest x3 9.84 us: on_device(): grad_wg = from_hidden_pieces(sums[..., :f_here]).astype(F32)]
    ppermute x11 -> x0, starting transfers between devices: 22.8 us -> none  [the longest x8 15.8 us: shift_a(): lax.ppermute(value, 'a', [(i, i + by) for i in range(size) if 0 <= i + by...]
    reduce_scatter x5 -> x6, waiting for transfers between devices: 0.05 us -> 14.9 us  [scatter_a(): return lax.psum_scatter(value, 'a', scatter_dimension=0, tiled=True)]
    concatenate x5 -> x0, other arithmetic: 14.5 us -> none  [the longest x1 6.6 us: on_device(): d_pair = jnp.concatenate([d_gate, d_up], 1)]
    concatenate x2 -> x0, local copies, waits for them, and re-layouts: 13.9 us -> none  [the longest x1 9.11 us: on_device(): d_pair = jnp.concatenate([d_gate, d_up], 1)]
    ppermute x15 -> x6, starting transfers between devices: 18.6 us -> 7.04 us  [xor_u(): return lax.ppermute(value, ('b', 'n'), [(i, i ^ k) for i in range(size)])]
  transfers between devices with their start and end apart: 42 -> 19, of which waited for: 12 -> 2; matrix products, arithmetic and copies ran while one was open for 26% -> 23% of each run, Pallas kernels for 50% -> 63%
where the time goes in v3:
time: 684 us; the launch traced here: 677 us
  Pallas kernels  442 us (65%)
  matrix products  97.6 us (14%)
  local copies, waits for them, and re-layouts  42.9 us (6%)
  other arithmetic  35.6 us (5%)
  waiting for transfers between devices  34.4 us (5%)
  between operations  15 us (2%)
  starting transfers between devices  9.86 us (1%)
    pallas_call x3, Pallas kernels, plane_reduce(): pl.pallas_call(functools.partial(reduce_kernel, nt, post, len(xs), len(ex...  238 us
    pallas_call x1, Pallas kernels, start_exchange(): pl.pallas_call(functools.partial(start_kernel, head_w, hid), in_specs=[vm...  84.9 us
    pallas_call x5, Pallas kernels, by_block(): pl.pallas_call(body, grid_spec=pltpu.PrefetchScalarGridSpec(num_scalar_pr...  76.8 us
    dot_general x5, matrix products, tdot(): lax.dot_general(left, right, (((0,), (0,)), ((), ())), preferred_element_...  47.8 us
    pallas_call x4, Pallas kernels, pass_along(): pl.pallas_call(functools.partial(body, reverse), in_specs=[vmem] * len(ed...  30.1 us
    dot_general x3, matrix products, mdot(): return jnp.dot(left, right, preferred_element_type=F32)  29.7 us
    unnamed x73, local copies, waits for them, and re-layouts  18.6 us
    ppermute x6, waiting for transfers between devices, xor_u(): return lax.ppermute(value, ('b', 'n'), [(i, i ^ k) for i in range(size)])  18.6 us
  transfers between devices with their start and end apart: 19, of which 2 were waited for; matrix products, arithmetic and copies ran while one was open for 23% of the time, Pallas kernels for 63%

profile of v3, /device:TPU:0, one launch (start us, length us, event | category | flops | bytes accessed | tf_op | source)
XLA Modules:
  0.0 677.3 jit_solution(10741926536081235643)
XLA Ops:
  14.5 84.9 %start_exchange.1 = (bf16[8,256,2048]{2,1,0:T(8,128)(2,1)}, bf16[4,8,64,640]{3,2,1,0:T(8,128)(2,1)}, bf16[8,64,1536]{2,1,0:T(8,128)(2,1)}, bf16[4,80,320]{2,1,0:...) custom-call(bf16[256,2048]{1,0:T(8,128)(2,1)} %bitcast.142, ...), custom_call_target="tpu_custom_call" | custom-call | bytes 8388608 | tf_op jit(solution)/shard_map/start_exchange/pallas_call | solution.py:596
  110.6 2.0 constant_dynamic-slice_fusion
  115.0 17.6 %norm_product.1 = (bf16[8,256,2048]{2,1,0:T(8,128)(2,1)}, f32[8,256,384]{2,1,0:T(8,128)}, bf16[8,256,384]{2,1,0:T(8,128)(2,1)}, f32[8,8,384]{2,1,0:T(8,128)}) custom-call(s32[8,8]{1,0:T(8,128)} %add_add_fusion.info, bf16[8,256,2048]{2,1,0:T(8,128)(2,1)} %get-tuple-element.77.tok_ref, bf16[2048,640]{1,0:T(8,128)(2,1)} %bitcast.147, ...), custom_call_target="tpu_custom_call" | custom-call | bytes 1048576 | tf_op jit(solution)/shard_map/norm_product/pallas_call | solution.py:1026
  132.6 5.7 pass_rows.1.rim_ref
  140.2 15.9 %mixer_forward.1 = (bf16[8,256,384]{2,1,0:T(8,128)(2,1)}, f32[8,256,384]{2,1,0:T(8,128)}, f32[8,256,384]{2,1,0:T(8,128)}, f32[8,256,384]{2,1,0:T(8,128)}, f32[8,...) custom-call(s32[8,8]{1,0:T(8,128)} %add_add_fusion.info, ...), custom_call_target="tpu_custom_call" | custom-call | bytes 1048576 | tf_op jit(solution)/shard_map/mixer_forward/pallas_call | solution.py:1026
  156.2 10.6 %pass_state.1.state_in_ref = f32[8,1,384]{2,1,0:T(1,128)} custom-call(f32[8,8,384]{2,1,0:T(8,128)} %get-tuple-element.86.mul_ref, f32[8,8,384]{2,1,0:T(8,128)} %get-tuple-element.87.add_ref), custom_call_target="tpu_custom_call" | custom-call | bytes 1048576 | tf_op jit(solution)/shard_map/pass_state/pallas_call | solution.py:791
  167.5 6.5 fusion.15
  176.7 85.1 %plane_reduce_fwd.1 = (f32[256,2048]{1,0:T(8,128)}, bf16[8,256,2048]{2,1,0:T(8,128)(2,1)}, bf16[8,256,2048]{2,1,0:T(8,128)(2,1)}) custom-call(bf16[2,4,256,384]{3,2,1,0:T(8,128)(2,1)} %bitcast.150, bf16[384,2048]{1,0:T(8,128)(2,1)} %pad.57.refs_1_.wo_ref, f32[1,2048]{1,0:T(1,128)} %reshape_reshape.13.refs_2_.refs_3_, bf16[256,2048]{1,0:T(8,128)(2,1)} %bitcast.143, ...), custom_call_target="tpu_custom_call" | custom-call | bytes 8388608 | tf_op jit(solution)/shard_map/plane_reduce_fwd/pallas_call | solution.py:406
  261.8 17.4 %fusion.59 = f32[2048,1536]{1,0:T(8,128)S(1)} fusion(bf16[2048,2048]{1,0:T(8,128)(2,1)} %bitcast.200, bf16[2048,1536]{1,0:T(8,128)(2,1)} %all-gather.6.cloned.1.call-done.refs_2_), kind=kOutput, calls=%fused_computation.156 | convolution fusion | flops 12884901888 | bytes 27262976 | tf_op jit(solution)/shard_map/dot_general | solution.py:26
  279.2 2.2 multiply_convert_fusion.1
  281.5 4.1 copy-done.2
  285.6 2.7 copy-done.29
  288.3 8.6 %convolution_convert_fusion.1 = bf16[768,2048]{1,0:T(8,128)(2,1)} fusion(bf16[2048,768]{1,0:T(8,128)(2,1)S(1)} %multiply_convert_fusion.1, bf16[2048,2048]{1,0:T(8,128)(2,1)S(1)} %bitcast.204), kind=kOutput, calls=%fused_computation.16 | convolution fusion | flops 6444023808 | bytes 14680064 | tf_op jit(solution)/shard_map/dot_general | solution.py:18
  297.0 17.7 %multiply_convert_fusion = (bf16[2048,768]{1,0:T(8,128)(2,1)}, bf16[2048,768]{1,0:T(8,128)(2,1)S(1)}) fusion(f32[2048,1536]{1,0:T(8,128)} %copy-done.2, bf16[2048,2048]{1,0:T(8,128)(2,1)} %bitcast.203, bf16[768,2048]{1,0:T(8,128)(2,1)} %all-gather.8.cloned.1.call-done), kind=kOutput, calls=%fused_computation.10 | convolution fusion | flops 6480199680 | bytes 30408704 | tf_op jit(solution)/shard_map/dot_general | solution.py:22
  316.4 10.5 %convolution_convert_fusion.3.refs_7_ = bf16[2048,768]{1,0:T(8,128)(2,1)} fusion(bf16[2048,2048]{1,0:T(8,128)(2,1)} %bitcast.201, bf16[2048,768]{1,0:T(8,128)(2,1)S(1)} %get-tuple-element.185), kind=kOutput, calls=%fused_computation.18 | convolution fusion | flops 6444023808 | bytes 14680064 | tf_op jit(solution)/shard_map/dot_general | solution.py:18
  327.0 7.1 %convolution_convert_fusion = bf16[1024,2048]{1,0:T(8,128)(2,1)} fusion(bf16[768,2048]{1,0:T(8,128)(2,1)} %all-gather.8.cloned.1.call-done, bf16[2048,768]{1,0:T(8,128)(2,1)S(1)} %multiply_convert_fusion.1), kind=kOutput, calls=%fused_computation.15 | convolution fusion | flops 3223322624 | bytes 8912896 | tf_op jit(solution)/shard_map/dot_general | solution.py:26
  334.4 10.5 %convolution_convert_fusion.2.refs_8_ = bf16[2048,768]{1,0:T(8,128)(2,1)} fusion(bf16[2048,2048]{1,0:T(8,128)(2,1)} %bitcast.202, bf16[2048,768]{1,0:T(8,128)(2,1)S(1)} %copy-done.10), kind=kOutput, calls=%fused_computation.17 | convolution fusion | flops 6444023808 | bytes 14680064 | tf_op jit(solution)/shard_map/dot_general | solution.py:18
  345.1 14.9 %reduce-scatter.7.cloned.1.call-done.refs_6_ = bf16[192,2048]{1,0:T(8,128)(2,1)} async-done(((bf16[768,2048]{1,0:T(8,128)(2,1)}), bf16[192,2048]{1,0:T(8,128)(2,1)}) %reduce-scatter.7.cloned.1.call-update) | async-done | bytes 786448 | tf_op jit(solution)/shard_map/reduce_scatter | solution.py:1086
  360.0 88.1 %plane_reduce_mid.1 = (f32[256,2048]{1,0:T(8,128)}, bf16[8,256,2048]{2,1,0:T(8,128)(2,1)}) custom-call(bf16[2,4,256,768]{3,2,1,0:T(8,128)(2,1)} %bitcast.156, bf16[2,4,256,768]{3,2,1,0:T(8,128)(2,1)} %bitcast.155, bf16[2048,1536]{1,0:T(8,128)(2,1)} %all-gather.6.cloned.1.call-done.refs_2_, f32[1,2048]{1,0:T(1,128)} %reshape_reshape.13.refs_2_.refs_3_, ...), custom_call_target="tpu_custom_call" | custom-call | bytes 8388608 | tf_op jit(solution)/shard_map/plane_reduce_mid/pallas_call | solution.py:406
  448.1 7.0 %convolution_bitcast_fusion = bf16[384,2048]{1,0:T(8,128)(2,1)S(1)} fusion(bf16[8,256,384]{2,1,0:T(8,128)(2,1)S(1)} %copy-done.8, bf16[8,256,2048]{2,1,0:T(8,128)(2,1)} %get-tuple-element.99.dres_ref), kind=kOutput, calls=%fused_computation.29 | convolution fusion | flops 3221225472 | bytes 11534336 | tf_op jit(solution)/shard_map/dot_general | solution.py:18
  456.8 5.3 add_convert_fusion
  468.7 17.1 %mixer_back_scan.1 = (bf16[8,256,384]{2,1,0:T(8,128)(2,1)}, f32[8,256,384]{2,1,0:T(8,128)}, f32[8,256,384]{2,1,0:T(8,128)}, f32[8,8,384]{2,1,0:T(8,128)}, f32[8,8,384]{2,1,0:T(8,128)}) custom-call(s32[8,8]{1,0:T(8,128)} %add_add_fusion.info, bf16[8,256,2048]{2,1,0:T(8,128)(2,1)} %get-tuple-element.99.dres_ref, bf16[384,2048]{1,0:T(8,128)(2,1)} %pad.57.refs_1_.wo_ref, ...), custom_call_target="tpu_custom_call" | custom-call | bytes 1048576 | tf_op jit(solution)/shard_map/mixer_back_scan/pallas_call | solution.py:1026
  485.8 7.5 %pass_state_back.1.grad_in_ref = f32[8,1,384]{2,1,0:T(1,128)} custom-call(f32[8,8,384]{2,1,0:T(8,128)} %get-tuple-element.104.mul_ref, f32[8,8,384]{2,1,0:T(8,128)} %get-tuple-element.105.add_ref), custom_call_target="tpu_custom_call" | custom-call | bytes 1048576 | tf_op jit(solution)/shard_map/pass_state_back/pallas_call | solution.py:791
  495.9 18.6 %collective-permute-done.7 = bf16[256,2048]{1,0:T(8,128)(2,1)} collective-permute-done((bf16[256,2048]{1,0:T(8,128)(2,1)}, bf16[256,2048]{1,0:T(8,128)(2,1)}, u32[]{:S(2)}, u32[]{:S(2)}) %collective-permute-start.7) | collective-permute-done | bytes 1048608 | tf_op jit(solution)/shard_map/ppermute | solution.py:39
  514.5 4.0 add_convert_fusion.1.refs_0_.refs_9_
  518.6 17.4 %mixer_back.1 = (bf16[8,256,384]{2,1,0:T(8,128)(2,1)}, f32[8,8,384]{2,1,0:T(8,128)}, f32[384,768]{1,0:T(8,128)}, f32[8,384]{1,0:T(8,128)}) custom-call(s32[8,8]{1,0:T(8,128)} %add_add_fusion.info, f32[8,256,384]{2,1,0:T(8,128)} %get-tuple-element.102.p_ref, f32[8,256,384]{2,1,0:T(8,128)} %get-tuple-element.103.s_ref, ...), custom_call_target="tpu_custom_call" | custom-call | bytes 1048576 | tf_op jit(solution)/shard_map/mixer_back/pallas_call | solution.py:1026
  539.6 6.4 pass_rows_back.1.rim_ref
  547.0 8.8 %mixer_back_conv.1 = bf16[8,256,640]{2,1,0:T(8,128)(2,1)} custom-call(s32[8,8]{1,0:T(8,128)} %add_add_fusion.info, bf16[8,256,384]{2,1,0:T(8,128)(2,1)} %get-tuple-element.108.dconv_ref, f32[8,8,384]{2,1,0:T(8,128)} %pass_rows_back.1.rim_ref, bf16[8,256,384]{2,1,0:T(8,128)(2,1)} %get-tuple-element.110.dgate_ref, f32[8,384]{1,0:T(8,128)} %select_maximum_fusion.vec_ref, ...), custom_call_target="tpu_custom_call" | custom-call | bytes 1048576 | tf_op jit(solution)/shard_map/mixer_back_conv/pallas_call | solution.py:1026
  555.8 11.1 %bitcast_convert_fusion.refs_8_ = bf16[2048,640]{1,0:T(8,128)(2,1)} fusion(bf16[8,256,2048]{2,1,0:T(8,128)(2,1)} %get-tuple-element.112, bf16[8,256,640]{2,1,0:T(8,128)(2,1)} %mixer_back_conv.1), kind=kOutput, calls=%fused_computation.13 | convolution fusion | flops 5370019840 | bytes 13631488 | tf_op jit(solution)/shard_map/dot_general | solution.py:18
  567.4 2.1 fusion.22
  575.8 64.5 %plane_reduce_last.1 = (bf16[256,2048]{1,0:T(8,128)(2,1)}, f32[64,6144]{1,0:T(8,128)}, f32[64,6144]{1,0:T(8,128)}, bf16[2,4,16,320]{3,2,1,0:T(8,128)(2,1)}) custom-call(bf16[2,4,256,640]{3,2,1,0:T(8,128)(2,1)} %bitcast.146, bf16[2048,640]{1,0:T(8,128)(2,1)} %bitcast.148, f32[1,2048]{1,0:T(1,128)} %broadcast_in_dim_reshape.4.gain_ref.refs_2_, ...), custom_call_target="tpu_custom_call" | custom-call | bytes 8388608 | tf_op jit(solution)/shard_map/plane_reduce_last/pallas_call | solution.py:406
  651.0 12.2 %finish.1 = (f32[64,2560]{1,0:T(8,128)}, f32[64,2560]{1,0:T(8,128)}) custom-call(bf16[512,640]{1,0:T(8,128)(2,1)} %reduce-scatter.15.cloned.1.call-done.sums_ref), custom_call_target="tpu_custom_call" | custom-call | tf_op jit(solution)/shard_map/finish/pallas_call | solution.py:646
  (227 shorter events, 68.1 us)
Async XLA Ops:
  7.2 103.4 %all-gather.4.cloned.1.call-start = ((), (), s32[]{:S(2)}) async-start(), calls=%async_computation.6 | async-start | bytes 1638400 | tf_op jit(solution)/shard_map/all_gather | solution.py:1083
  7.9 253.9 %all-gather.6.cloned.1.call-start = ((), (), s32[]{:S(2)}) async-start(), calls=%async_computation.7 | async-start | bytes 7864320 | tf_op jit(solution)/shard_map/all_gather | solution.py:1083
  99.5 197.6 %all-gather.8.cloned.1.call-start = ((), (), s32[]{:S(2)}) async-start(), calls=%async_computation.8 | async-start | bytes 3932160 | tf_op jit(solution)/shard_map/all_gather | solution.py:1083
  99.5 56.6 %collective-permute-start = (bf16[256,2048]{1,0:T(8,128)(2,1)}, bf16[256,2048]{1,0:T(8,128)(2,1)}, u32[]{:S(2)}, u32[]{:S(2)}) collective-permute-start(bf16[256,2048]{1,0:T(8,128)(2,1)} %bitcast.23.refs_5_.refs_4_), channel_id=1, source_target_pairs={{0,2},{2,0},{4,6},{6,4},{1,3},{3,1},{5,7},{7,5},{8,10},{10,8},{12,... | collective-permute-start | bytes 3145736 | tf_op jit(solution)/shard_map/ppermute | solution.py:39
  101.0 55.1 %collective-permute-start.1 = (bf16[256,2048]{1,0:T(8,128)(2,1)}, bf16[256,2048]{1,0:T(8,128)(2,1)}, u32[]{:S(2)}, u32[]{:S(2)}) collective-permute-start(bf16[256,2048]{1,0:T(8,128)(2,1)} %bitcast.23.refs_5_.refs_4_), channel_id=1, source_target_pairs={{0,4},{2,6},{4,0},{6,2},{1,5},{3,7},{5,1},{7,3},{8,12},{10,14},{12... | collective-permute-start | bytes 3145736 | tf_op jit(solution)/shard_map/ppermute | solution.py:39
  102.5 53.7 %collective-permute-start.2 = (bf16[256,2048]{1,0:T(8,128)(2,1)}, bf16[256,2048]{1,0:T(8,128)(2,1)}, u32[]{:S(2)}, u32[]{:S(2)}) collective-permute-start(bf16[256,2048]{1,0:T(8,128)(2,1)} %bitcast.23.refs_5_.refs_4_), channel_id=1, source_target_pairs={{0,6},{2,4},{4,2},{6,0},{1,7},{3,5},{5,3},{7,1},{8,14},{10,12},{12... | collective-permute-start | bytes 3145736 | tf_op jit(solution)/shard_map/ppermute | solution.py:39
  103.1 256.9 %reduce-scatter.7.cloned.1.call-start = ((), (), s32[]{:S(2)}) async-start(), calls=%async_computation.9 | async-start | bytes 3932160 | tf_op jit(solution)/shard_map/reduce_scatter | solution.py:1086
  112.6 61.3 %collective-permute-start.3 = (bf16[2,80,2048]{2,1,0:T(8,128)(2,1)}, bf16[2,80,2048]{2,1,0:T(8,128)(2,1)}, u32[]{:S(2)}, u32[]{:S(2)}) collective-permute-start(bf16[2,80,2048]{2,1,0:T(8,128)(2,1)} %constant_dynamic-slice_fusion), channel_id=1, source_target_pairs={{0,1},{1,0},{2,3},{3,2},{4,5},{5,4},{6,7},{7,6},{8,9},{9,8},{10,11... | collective-permute-start | bytes 1966088 | tf_op jit(solution)/shard_map/ppermute | solution.py:34
  132.6 34.9 %copy-start.3 = (f32[8,256,384]{2,1,0:T(8,128)S(1)}, f32[8,256,384]{2,1,0:T(8,128)}, u32[]{:S(2)}) copy-start(f32[8,256,384]{2,1,0:T(8,128)} %get-tuple-element.89.gate_ref) | copy-start | bytes 9437188
  279.2 9.1 %copy-start.29 = (bf16[8,256,2048]{2,1,0:T(8,128)(2,1)S(1)}, bf16[8,256,2048]{2,1,0:T(8,128)(2,1)}, u32[]{:S(2)}) copy-start(bf16[8,256,2048]{2,1,0:T(8,128)(2,1)} %get-tuple-element.97) | copy-start | bytes 25165828
  285.6 59.5 %copy-start.5 = (bf16[2048,768]{1,0:T(8,128)(2,1)}, bf16[2048,768]{1,0:T(8,128)(2,1)S(1)}, u32[]{:S(2)}) copy-start(bf16[2048,768]{1,0:T(8,128)(2,1)S(1)} %multiply_convert_fusion.1) | copy-start | bytes 9437188
  297.0 171.7 %reduce-scatter.9.cloned.1.call-start = ((), (), s32[]{:S(2)}) async-start(), calls=%async_computation.10 | async-start | bytes 3932160 | tf_op jit(solution)/shard_map/reduce_scatter | solution.py:1086
  327.0 191.6 %reduce-scatter.11.cloned.1.call-start = ((), (), s32[]{:S(2)}) async-start(), calls=%async_computation.11 | async-start | bytes 3932160 | tf_op jit(solution)/shard_map/reduce_scatter | solution.py:1086
  334.1 11.0 %collective-permute-start.4 = (bf16[1024,2048]{1,0:T(8,128)(2,1)}, bf16[1024,2048]{1,0:T(8,128)(2,1)}, u32[]{:S(2)}, u32[]{:S(2)}) collective-permute-start(bf16[1024,2048]{1,0:T(8,128)(2,1)} %convolution_convert_fusion), channel_id=1, source_target_pairs={{0,1},{1,0},{2,3},{3,2},{4,5},{5,4},{6,7},{7,6},{8,9},{9,8},{10,11... | collective-permute-start | bytes 12582920 | tf_op jit(solution)/shard_map/ppermute | solution.py:34
  345.0 202.0 %reduce-scatter.13.cloned.1.call-start = ((), (), s32[]{:S(2)}) async-start(), calls=%async_computation.12 | async-start | bytes 1638400 | tf_op jit(solution)/shard_map/reduce_scatter | solution.py:1086
  360.0 88.1 %copy-start.8 = (bf16[8,256,384]{2,1,0:T(8,128)(2,1)S(1)}, bf16[8,256,384]{2,1,0:T(8,128)(2,1)}, u32[]{:S(2)}) copy-start(bf16[8,256,384]{2,1,0:T(8,128)(2,1)} %get-tuple-element.182) | copy-start | bytes 4718596
  448.1 8.5 %copy-start.30 = (bf16[768,2048]{1,0:T(8,128)(2,1)S(1)}, bf16[768,2048]{1,0:T(8,128)(2,1)}, u32[]{:S(2)}) copy-start(bf16[768,2048]{1,0:T(8,128)(2,1)} %all-gather.8.cloned.1.call-done) | copy-start | bytes 9437188
  456.2 37.1 %collective-permute-start.8 = (bf16[2,80,2048]{2,1,0:T(8,128)(2,1)}, bf16[2,80,2048]{2,1,0:T(8,128)(2,1)}, u32[]{:S(2)}, u32[]{:S(2)}) collective-permute-start(bf16[2,80,2048]{2,1,0:T(8,128)(2,1)} %dynamic-slice_bitcast_fusion), channel_id=1, source_target_pairs={{0,1},{1,0},{2,3},{3,2},{4,5},{5,4},{6,7},{7,6},{8,9},{9,8},{10,11... | collective-permute-start | bytes 1966088 | tf_op jit(solution)/shard_map/ppermute | solution.py:34
  465.1 30.8 %collective-permute-start.5 = (bf16[256,2048]{1,0:T(8,128)(2,1)}, bf16[256,2048]{1,0:T(8,128)(2,1)}, u32[]{:S(2)}, u32[]{:S(2)}) collective-permute-start(bf16[256,2048]{1,0:T(8,128)(2,1)} %get-tuple-element.186), channel_id=1, source_target_pairs={{0,2},{2,0},{4,6},{6,4},{1,3},{3,1},{5,7},{7,5},{8,10},{10,8},{12,... | collective-permute-start | bytes 3145736 | tf_op jit(solution)/shard_map/ppermute | solution.py:39
  466.6 29.3 %collective-permute-start.6 = (bf16[256,2048]{1,0:T(8,128)(2,1)}, bf16[256,2048]{1,0:T(8,128)(2,1)}, u32[]{:S(2)}, u32[]{:S(2)}) collective-permute-start(bf16[256,2048]{1,0:T(8,128)(2,1)} %get-tuple-element.188), channel_id=1, source_target_pairs={{0,4},{2,6},{4,0},{6,2},{1,5},{3,7},{5,1},{7,3},{8,12},{10,14},{12... | collective-permute-start | bytes 3145736 | tf_op jit(solution)/shard_map/ppermute | solution.py:39
  467.1 47.4 %collective-permute-start.7 = (bf16[256,2048]{1,0:T(8,128)(2,1)}, bf16[256,2048]{1,0:T(8,128)(2,1)}, u32[]{:S(2)}, u32[]{:S(2)}) collective-permute-start(bf16[256,2048]{1,0:T(8,128)(2,1)} %get-tuple-element.187), channel_id=1, source_target_pairs={{0,6},{2,4},{4,2},{6,0},{1,7},{3,5},{5,3},{7,1},{8,14},{10,12},{12... | collective-permute-start | bytes 3145736 | tf_op jit(solution)/shard_map/ppermute | solution.py:39
  493.3 21.2 %copy-start.4 = (f32[256,2048]{1,0:T(8,128)S(1)}, f32[256,2048]{1,0:T(8,128)}, u32[]{:S(2)}) copy-start(f32[256,2048]{1,0:T(8,128)} %get-tuple-element.94.refs_5_) | copy-start | bytes 6291460
  495.9 76.0 %reduce-scatter.17.cloned.1.call-start = ((), (), s32[]{:S(2)}) async-start(), calls=%async_computation.14 | async-start | bytes 307200 | tf_op jit(solution)/shard_map/reduce_scatter | solution.py:1086
  539.6 6.5 collective-permute-start.9
  546.9 104.1 %reduce-scatter.15.cloned.1.call-start = ((), (), s32[]{:S(2)}) async-start(), calls=%async_computation.13 | async-start | bytes 3276800 | tf_op jit(solution)/shard_map/reduce_scatter | solution.py:1086
  555.8 11.1 %copy-start.25 = (f32[4,1,4]{2,1,0:T(1,128)S(1)}, f32[4,1,4]{2,1,0:T(1,128)}, u32[]{:S(2)}) copy-start(f32[4,1,4]{2,1,0:T(1,128)} %copy-done.24) | copy-start | bytes 196
  575.8 71.9 %copy-start.16 = (bf16[80,2048]{1,0:T(8,128)(2,1)S(1)}, bf16[80,2048]{1,0:T(8,128)(2,1)}, u32[]{:S(2)}) copy-start(bf16[80,2048]{1,0:T(8,128)(2,1)} %reduce-scatter.13.cloned.1.call-done.refs_0_) | copy-start | bytes 983044
  575.8 72.8 %copy-start.12 = (bf16[64,6144]{1,0:T(8,128)(2,1)S(1)}, bf16[64,6144]{1,0:T(8,128)(2,1)}, u32[]{:S(2)}) copy-start(bf16[64,6144]{1,0:T(8,128)(2,1)} %wg_ref.1) | copy-start | bytes 2359300
  575.8 72.8 %copy-start.13 = (bf16[64,6144]{1,0:T(8,128)(2,1)S(1)}, bf16[64,6144]{1,0:T(8,128)(2,1)}, u32[]{:S(2)}) copy-start(bf16[64,6144]{1,0:T(8,128)(2,1)} %wu_ref.1) | copy-start | bytes 2359300
  648.6 14.7 %copy-start.17 = (bf16[64,2560]{1,0:T(8,128)(2,1)S(1)}, bf16[64,2560]{1,0:T(8,128)(2,1)}, u32[]{:S(2)}) copy-start(bf16[64,2560]{1,0:T(8,128)(2,1)} %wy_ref.1) | copy-start | bytes 983044
  648.6 16.5 %copy-start.28 = (bf16[64]{0:T(256)(128)(2,1)S(1)}, bf16[64]{0:T(256)(128)(2,1)}, u32[]{:S(2)}) copy-start(bf16[64]{0:T(256)(128)(2,1)} %param.31) | copy-start | bytes 388
  650.4 15.1 %copy-start.19 = (bf16[256,2048]{1,0:T(8,128)(2,1)S(1)}, bf16[256,2048]{1,0:T(8,128)(2,1)}, u32[]{:S(2)}) copy-start(bf16[256,2048]{1,0:T(8,128)(2,1)} %get-tuple-element.113) | copy-start | bytes 3145732
  (19 other events, 80.4 us)
Sparse Core Ops, SparseCore 0:
  9.6 42.8 all-gather.3
  99.6 117.0 all-gather.5
  218.3 63.1 all-gather.7
  297.1 62.8 reduce-scatter.6
  362.1 60.2 reduce-scatter.8
  424.6 60.2 reduce-scatter.10
  496.0 28.4 reduce-scatter.12
  547.0 17.7 reduce-scatter.16
  567.2 56.5 reduce-scatter.14

commit v4 on v3

--- a/solution.py
+++ b/solution.py
@@ -177,13 +177,16 @@
     out_ref, refs = refs[0], refs[1:]
     if post == "last":
         everyone = mine = None
-        extra_out, lasts_out = refs[:extra], refs[extra]
-        extra_buf, lasts_buf, lasts_mine, lasts_far, refs = *refs[extra + 1 : extra + 5], refs[extra + 5 :]
+        extra_out, lasts_out = refs[:2], refs[2]
+        extra_buf, lasts_buf, lasts_mine, lasts_far = refs[3:7]
+        refs = refs[7:]
     else:
         everyone, refs = refs[0], refs[1:]
         if extra:
             extra_out, refs = refs[0], refs[1:]
         mine, refs = refs[0], refs[1:]
+        if post == "mid":
+            (side_x, side_w, side_s, side_r), refs = refs[:4], refs[4:]
     x_v, w_v, away_s, away_r, acc, out_b, in_b, local, send, recv = refs
     rows, d_model = acc.shape[1:]
     half = rows // 2
@@ -207,6 +210,8 @@
                 keep(x.at[kc, k], x_v.at[kc, k, :, pl.ds(i * each, each)])
                 for i, x in enumerate(x_hbm)
             ]
+    if post == "mid":
+        side_loads = [keep(extra_in[0], side_x), keep(extra_in[1], side_w)]
     if post == "last":
         a, b, n, c = places()
         planes = lasts_far.shape[0] + 1
@@ -283,6 +288,28 @@
     hand_on("y0", 4, 1, 0, py, 0)
     move.arrived("d1")
     hand_on("x1", 3, 2, 1, px, 1)
+    if post == "mid":
+        for load in side_loads:
+            load.wait()
+        for k in range(4):
+
+            @pl.loop(0, d_model // tile)
+            def _(t):
+                at = pl.ds(pl.multiple_of(t * tile, tile), tile)
+                side_s[k, :, at] = mdot(side_x[1, k], side_w[:, at]).astype(BF)
+
+            move.start(f"s{k}", side_s.at[k], side_r.at[k], pc)
+        for k in range(4):
+            move.arrived(f"s{k}")
+            move.made.pop(f"s{k}").wait_send()
+
+            @pl.loop(0, d_model // tile)
+            def _(t):
+                at = pl.ds(pl.multiple_of(t * tile, tile), tile)
+                value = mdot(side_x[0, k], side_w[:, at]) + side_r[k, :, at].astype(F32)
+                side_s[k, :, at] = value.astype(BF)
+
+            kept.append(keep(side_s.at[k], extra_out.at[k]))
     if extra and post == "last":
         lasts_buf[0, 0] = lasts_ref[0, 0]
         for kc, k in peers:
@@ -297,15 +324,15 @@
                 lasts_mine[jnp.bitwise_xor(c, kc), q] = found
         for i, peer in enumerate(columns):
             move.start(f"z{i}", lasts_mine, lasts_far.at[i], peer)
-        each_rows = extra_buf.shape[2]
-        for i in range(extra):
-            def part(owner, i=i):
-                at = pl.multiple_of(owner * each_rows, each_rows)
-                return extra_in[i].at[pl.ds(at, each_rows)]
-
-            kept.append(keep(part(me), extra_buf.at[i, me]))
-            for (kc, k), peer in plane_peers_of().items():
-                move.start(f"e{i}{kc}{k}", part(peer_owner(kc, k)), extra_buf.at[i, me], peer)
+        each_rows = extra_buf.shape[1]
+
+        def part(owner):
+            at = pl.multiple_of(owner * each_rows, each_rows)
+            return extra_in[0].at[pl.ds(at, each_rows)]
+
+        kept.append(keep(part(me), extra_buf.at[me]))
+        for (kc, k), peer in peers.items():
+            move.start(f"e{kc}{k}", part(peer_owner(kc, k)), extra_buf.at[me], peer)
 
     for h in range(2):
         move.arrived(f"x{h}")
@@ -351,11 +378,12 @@
             move.arrived(f"z{i}")
             total = total + lasts_far[i].astype(F32)
         lasts_out[...] = total.astype(BF)
-        order = [(p, z * hid) for z in range(extra_buf.shape[3] // hid) for p in range(8)]
-        for i in range(extra):
-            for kc, k in plane_peers_of():
-                move.arrived(f"e{i}{kc}{k}")
-            for at, value in set_side_by_side(extra_buf.at[i], order, hid):
+        for kc, k in peers:
+            move.arrived(f"e{kc}{k}")
+        wide = extra_buf.shape[2] // 2
+        for i in range(2):
+            order = [(p, i * wide + z * hid) for z in range(wide // hid) for p in range(8)]
+            for at, value in set_side_by_side(extra_buf, order, hid):
                 extra_out[i][:, at] = value
     move.sent()
 
@@ -374,21 +402,25 @@
         out_specs.append(hbm)
         copies += GATHER_COPIES
         if extra:
-            out_shape.append(jax.ShapeDtypeStruct((8, rows, d_model), BF))
+            blocks = 8 if post == "fwd" else 4
+            out_shape.append(jax.ShapeDtypeStruct((blocks, rows, d_model), BF))
             out_specs.append(hbm)
             copies += 4
         scratch.append(pltpu.VMEM((rows, d_model), BF))
+        if post == "mid":
+            scratch += [pltpu.VMEM(v.shape, BF) for v in extra]
+            scratch += [pltpu.VMEM((4, rows, d_model), BF)] * 2
     else:
         each = extra[0].shape[0] // 8, extra[0].shape[1]
-        for _ in extra:
-            out_shape.append(jax.ShapeDtypeStruct((each[0], 8 * each[1]), F32))
+        for _ in range(2):
+            out_shape.append(jax.ShapeDtypeStruct((each[0], 4 * each[1]), F32))
             out_specs.append(vmem)
         planes = lax.axis_size("a")
         copies += 7 * len(extra) + 7 + planes - 1
         block = (2, 4) + lasts.shape[2:]
         out_shape.append(jax.ShapeDtypeStruct(block, BF))
         out_specs.append(vmem)
-        scratch.append(pltpu.VMEM((len(extra), 8) + each, BF))
+        scratch.append(pltpu.VMEM((8,) + each, BF))
         scratch += [pltpu.VMEM(block, BF)] * 2 + [pltpu.VMEM((planes - 1,) + block, BF)]
     wide = sum(x.shape[3] for x in xs)
     scratch += [
@@ -399,7 +431,7 @@
         pltpu.VMEM((4, rows, d_model), F32),
         pltpu.VMEM((6, rows // 2, d_model), BF),
         pltpu.VMEM((6, rows // 2, d_model), BF),
-        pltpu.SemaphoreType.DMA((2 + 8 * len(xs) + len(extra),)),
+        pltpu.SemaphoreType.DMA((8 + 8 * len(xs),)),
         pltpu.SemaphoreType.DMA((copies,)),
         pltpu.SemaphoreType.DMA((copies,)),
     ]
@@ -407,7 +439,7 @@
         functools.partial(reduce_kernel, nt, post, len(xs), len(extra), len(done), hid),
         in_specs=[hbm] * (len(xs) + 1)
         + [vmem] * 3
-        + [hbm if post == "last" else vmem] * len(extra)
+        + [vmem if post == "fwd" else hbm] * len(extra)
         + [vmem] * (lasts is not None)
         + [hbm] * len(done),
         out_specs=out_specs,
@@ -928,6 +960,24 @@
     return x * cdf, slope
 
 
+def ffn_forward_kernel(info, n_ref, w_ref, inner_ref, by_gate_ref, by_up_ref):
+    pair = mdot(n_ref[0], w_ref[...])
+    hidden = inner_ref.shape[2]
+    upward = pair[:, hidden:]
+    active, slope = gelu_pair(pair[:, :hidden])
+    inner_ref[0] = (active * upward).astype(BF)
+    by_gate_ref[0] = (slope * upward).astype(BF)
+    by_up_ref[0] = active.astype(BF)
+
+
+def ffn_back_kernel(info, g_ref, w_ref, by_gate_ref, by_up_ref, *refs):
+    out_ref = refs[-1]
+    hidden = w_ref.shape[0]
+    d_inner = ndot(g_ref[0], w_ref[...])
+    out_ref[0, :, :hidden] = (d_inner * by_gate_ref[0].astype(F32)).astype(BF)
+    out_ref[0, :, hidden:] = (d_inner * by_up_ref[0].astype(F32)).astype(BF)
+
+
 def back_scan_kernel(
     nseq, taps, info, dres_ref, wo_ref, gate_ref, hidden_ref, retain_ref, vec_ref, *refs
 ):
@@ -1236,31 +1286,43 @@
     normed_two = normed_two.reshape(nblocks * rows, d_model)
     grads = grads.reshape(nblocks * rows, d_model)
 
-    pair = mdot(normed_two, w_gu)
-    gate, upward = pair[:, :f_here], pair[:, f_here:]
-    active, gate_back = jax.vjp(jax.nn.gelu, gate)
-    inner = (active * upward).astype(BF)
-    sums_d = tdot(inner, grads).astype(BF)
-    grad_wd = scatter_a(sums_d)
-    grads, _ = lax.optimization_barrier((grads, sums_d))
-    d_inner = ndot(grads, w_d)
-    d_gate = gate_back(d_inner * upward)[0].astype(BF)
-    d_up = (d_inner * active).astype(BF)
-    sums_g = tdot(normed_two, d_gate).astype(BF)
-    sums_u = tdot(normed_two, d_up).astype(BF)
-    sent_g, sent_u = scatter_a(sums_g), scatter_a(sums_u)
-    parts = inner.reshape(2, count * rows, f_here)
-    away = swap_c(mdot(parts[1], w_d).astype(BF))
-    d_resid, d_resid_low = plane_reduce(
-        3, "mid", True, (d_gate.reshape(2, count, rows, -1), d_up.reshape(2, count, rows, -1)), w_gu,
-        gain_two, grad_low, resid, (), (grad_wd, sums_g, sums_u, away),
+    hid_full = (nblocks, rows, f_here)
+    inner, by_gate, by_up = by_block(
+        ffn_forward_kernel,
+        info,
+        [(normed_two.reshape(nblocks, rows, d_model), True), (w_gu, False)],
+        [(hid_full, BF, True)] * 3,
+        [],
+        name="ffn_forward",
+    )
+    inner = inner.reshape(nblocks * rows, f_here)
+    cut = d_model // 2
+    first_d = tdot(inner, grads[:, :cut]).astype(BF)
+    second_d = tdot(inner, grads[:, cut:]).astype(BF)
+    sent_d = scatter_a(first_d), scatter_a(second_d)
+    d_pair = by_block(
+        ffn_back_kernel,
+        info,
+        [
+            (grads.reshape(nblocks, rows, d_model), True), (w_d, False), (by_gate, True),
+            (by_up, True),
+        ],
+        [((nblocks, rows, 2 * f_here), BF, True)],
+        [],
+        (first_d, second_d),
+        name="ffn_back",
+    )[0]
+    sums_gu = tdot(normed_two, d_pair.reshape(nblocks * rows, -1)).astype(BF)
+    sent_gu = scatter_a(sums_gu)
+    d_resid, d_resid_low, low = plane_reduce(
+        3, "mid", True, (d_pair.reshape(2, count, rows, -1),), w_gu,
+        gain_two, grad_low, resid, (inner.reshape(2, count, rows, f_here), w_d), (sent_d[0], sums_gu),
     )
     d_resid_low = d_resid_low.reshape(nblocks * rows, d_model)
 
     sums_o = tdot(mixed_in, d_resid_low)[:wide_here].astype(BF)
     grad_wo = scatter_a(part_halves(sums_o))
-    own, _ = lax.optimization_barrier((parts[0], sums_o))
-    low = (mdot(own, w_d) + away.astype(F32)).astype(BF).reshape(count, rows, d_model)
+    low, sums_o = lax.optimization_barrier((low, sums_o))
     result = resid + low[0].astype(F32)
     for k in range(1, count):
         result = result + xor_u(low[k], k).astype(F32)
@@ -1275,7 +1337,7 @@
         ],
         [(full, BF, True), (full, F32, True), (full, F32, True), edge, edge],
         [(rows + 8, wp), (rows, wp), (rows, wp)],
-        (low, sent_g),
+        (sent_d[1], sums_o),
         name="mixer_back_scan",
     )
     grad_in = pass_along(8, "pass_state_back", True, end_mul, end_add)
@@ -1289,7 +1351,7 @@
         ],
         [(full, BF, True), edge, ((wp, 2 * wp), F32, False), ((taps + 4, wp), F32, False)],
         [(rows + 8, wp)],
-        (result, sent_u),
+        (result, sent_gu),
         name="mixer_back",
     )
 
@@ -1342,7 +1404,7 @@
     lasts = (lasts[:, 0] + lasts[:, 1]).astype(BF)
     input_grad, grad_wg, grad_wu, found = plane_reduce(
         4, "last", True, (d_both.reshape(2, count, rows, -1),), w_yx, gain_one, tokens[0], d_resid,
-        (sent_g, sent_u), (sums_yx, result), hid, lasts,
+        (sent_gu,), (sums_yx, result), hid, lasts,
     )
     grad_wy, grad_wx = finish(scatter_a(sums_yx), head_w)
 
@@ -1376,7 +1438,7 @@
         vec_grads[taps + 3],
         grad_wg,
         grad_wu,
-        grad_wd.astype(F32),
+        jnp.concatenate(sent_d, 1).astype(F32),
         grad_gain_two,
     )
 

time: 684 us -> 644 us (0.942)
  matrix products: 97.6 us -> 54.8 us
  Pallas kernels: 442 us -> 480 us
  waiting for transfers between devices: 34.4 us -> 19.1 us
  local copies, waits for them, and re-layouts: 42.9 us -> 28 us
    dot_general x4 -> x0, matrix products: 47.4 us -> none  [the longest x3 29.7 us: mdot(): return jnp.dot(left, right, preferred_element_type=F32)]
    pallas_call x5 -> x7, Pallas kernels: 76.8 us -> 112 us  [by_block(): pl.pallas_call(body, grid_spec=pltpu.PrefetchScalarGridSpec(num_scalar_pr...]
    reduce_scatter x6, waiting for transfers between devices: 14.9 us -> 0.05 us  [scatter_a(): return lax.psum_scatter(value, 'a', scatter_dimension=0, tiled=True)]
    unnamed x73 -> x63, local copies, waits for them, and re-layouts: 18.6 us -> 8.01 us
  transfers between devices with their start and end apart: 19 -> 18, of which waited for: 2 -> 2; matrix products, arithmetic and copies ran while one was open for 23% -> 17% of each run, Pallas kernels for 63% -> 73%
where the time goes in v4:
time: 644 us; the launch traced here: 637 us
  Pallas kernels  480 us (75%)
  matrix products  54.8 us (9%)
  other arithmetic  30.7 us (5%)
  local copies, waits for them, and re-layouts  28 us (4%)
  waiting for transfers between devices  19.1 us (3%)
  between operations  14.9 us (2%)
  starting transfers between devices  9.52 us (1%)
    pallas_call x3, Pallas kernels, plane_reduce(): pl.pallas_call(functools.partial(reduce_kernel, nt, post, len(xs), len(ex...  239 us
    pallas_call x7, Pallas kernels, by_block(): pl.pallas_call(body, grid_spec=pltpu.PrefetchScalarGridSpec(num_scalar_pr...  112 us
    pallas_call x1, Pallas kernels, start_exchange(): pl.pallas_call(functools.partial(start_kernel, head_w, hid), in_specs=[vm...  84.9 us
    dot_general x5, matrix products, tdot(): lax.dot_general(left, right, (((0,), (0,)), ((), ())), preferred_element_...  52.4 us
    pallas_call x4, Pallas kernels, pass_along(): pl.pallas_call(functools.partial(body, reverse), in_specs=[vmem] * len(ed...  31 us
    ppermute x6, waiting for transfers between devices, xor_u(): return lax.ppermute(value, ('b', 'n'), [(i, i ^ k) for i in range(size)])  17.5 us
  transfers between devices with their start and end apart: 18, of which 2 were waited for; matrix products, arithmetic and copies ran while one was open for 17% of the time, Pallas kernels for 73%

profile of v4, /device:TPU:0, one launch (start us, length us, event | category | flops | bytes accessed | tf_op | source)
XLA Modules:
  0.0 636.6 jit_solution(4173518915175240638)
XLA Ops:
  14.5 84.9 %start_exchange.1 = (bf16[8,256,2048]{2,1,0:T(8,128)(2,1)}, bf16[4,8,64,640]{3,2,1,0:T(8,128)(2,1)}, bf16[8,64,1536]{2,1,0:T(8,128)(2,1)}, bf16[4,80,320]{2,1,0:...) custom-call(bf16[256,2048]{1,0:T(8,128)(2,1)} %bitcast.143, ...), custom_call_target="tpu_custom_call" | custom-call | bytes 8388608 | tf_op jit(solution)/shard_map/start_exchange/pallas_call | solution.py:628
  110.4 2.0 constant_dynamic-slice_fusion
  112.4 1.6 collective-permute-start.3
  114.7 17.7 %norm_product.1 = (bf16[8,256,2048]{2,1,0:T(8,128)(2,1)}, f32[8,256,384]{2,1,0:T(8,128)}, bf16[8,256,384]{2,1,0:T(8,128)(2,1)}, f32[8,8,384]{2,1,0:T(8,128)}) custom-call(s32[8,8]{1,0:T(8,128)} %add_add_fusion.info, bf16[8,256,2048]{2,1,0:T(8,128)(2,1)} %get-tuple-element.81.tok_ref, bf16[2048,640]{1,0:T(8,128)(2,1)} %bitcast.150, ...), custom_call_target="tpu_custom_call" | custom-call | bytes 1048576 | tf_op jit(solution)/shard_map/norm_product/pallas_call | solution.py:1076
  132.4 5.7 pass_rows.1.rim_ref
  140.2 15.9 %mixer_forward.1 = (bf16[8,256,384]{2,1,0:T(8,128)(2,1)}, f32[8,256,384]{2,1,0:T(8,128)}, f32[8,256,384]{2,1,0:T(8,128)}, f32[8,256,384]{2,1,0:T(8,128)}, f32[8,...) custom-call(s32[8,8]{1,0:T(8,128)} %add_add_fusion.info, ...), custom_call_target="tpu_custom_call" | custom-call | bytes 1048576 | tf_op jit(solution)/shard_map/mixer_forward/pallas_call | solution.py:1076
  156.1 8.0 %pass_state.1.state_in_ref = f32[8,1,384]{2,1,0:T(1,128)} custom-call(f32[8,8,384]{2,1,0:T(8,128)} %get-tuple-element.90.mul_ref, f32[8,8,384]{2,1,0:T(8,128)} %get-tuple-element.91.add_ref), custom_call_target="tpu_custom_call" | custom-call | bytes 1048576 | tf_op jit(solution)/shard_map/pass_state/pallas_call | solution.py:823
  164.8 6.4 %fusion.12 = (bf16[8,256,384]{2,1,0:T(8,128)(2,1)}, f32[8,256,384]{2,1,0:T(8,128)}) fusion(f32[8,256,384]{2,1,0:T(8,128)S(1)} %copy-done.1, f32[8,256,384]{2,1,0:T(8,128)} %get-tuple-element.92, f32[8,256,384]{2,1,0:T(8,128)} %get-tuple-element.87, f32[8,384]{1,0:T(8,128)S(1)} %bitcast.190), kind=kLoop, calls=%fused_computation.15 | loop fusion | flops 9437184 | bytes 14168064 | tf_op jit(solution)/shard_map/convert_element_type | solution.py:1281
  174.0 86.3 %plane_reduce_fwd.1 = (f32[256,2048]{1,0:T(8,128)}, bf16[8,256,2048]{2,1,0:T(8,128)(2,1)}, bf16[8,256,2048]{2,1,0:T(8,128)(2,1)}) custom-call(bf16[2,4,256,384]{3,2,1,0:T(8,128)(2,1)} %bitcast.155, bf16[384,2048]{1,0:T(8,128)(2,1)} %pad.57.refs_1_.wo_ref, f32[1,2048]{1,0:T(1,128)} %reshape_reshape.16.refs_2_, bf16[256,2048]{1,0:T(8,128)(2,1)} %bitcast.144, ...), custom_call_target="tpu_custom_call" | custom-call | bytes 8388608 | tf_op jit(solution)/shard_map/plane_reduce_fwd/pallas_call | solution.py:438
  260.3 19.8 %ffn_forward.1 = (bf16[8,256,768]{2,1,0:T(8,128)(2,1)}, bf16[8,256,768]{2,1,0:T(8,128)(2,1)}, bf16[8,256,768]{2,1,0:T(8,128)(2,1)}) custom-call(s32[8,8]{1,0:T(8,128)} %add_add_fusion.info, bf16[8,256,2048]{2,1,0:T(8,128)(2,1)} %get-tuple-element.100.n_ref, bf16[2048,1536]{1,0:T(8,128)(2,1)} %all-gather.8.cloned.1.call-done.w_ref.refs_1_), custom_call_target="tpu_custom_call" | custom-call | bytes 1048576 | tf_op jit(solution)/shard_map/ffn_forward/pallas_call | solution.py:1076
  280.2 7.9 %fusion.17.refs_0_ = bf16[768,1024]{1,0:T(8,128)(2,1)} fusion(bf16[2048,768]{1,0:T(8,128)(2,1)} %bitcast.158, bf16[2048,2048]{1,0:T(8,128)(2,1)} %bitcast.153), kind=kOutput, calls=%fused_computation.24 | convolution fusion | flops 3222011904 | bytes 8912896 | tf_op jit(solution)/shard_map/dot_general | solution.py:18
  288.2 7.0 %fusion.20.refs_1_ = bf16[768,1024]{1,0:T(8,128)(2,1)} fusion(bf16[2048,768]{1,0:T(8,128)(2,1)S(1)} %bitcast.160, bf16[2048,2048]{1,0:T(8,128)(2,1)} %bitcast.154), kind=kOutput, calls=%fused_computation.25 | convolution fusion | flops 3222011904 | bytes 8912896 | tf_op jit(solution)/shard_map/dot_general | solution.py:18
  295.3 15.0 %ffn_back.1 = bf16[8,256,1536]{2,1,0:T(8,128)(2,1)} custom-call(s32[8,8]{1,0:T(8,128)} %add_add_fusion.info, bf16[8,256,2048]{2,1,0:T(8,128)(2,1)} %get-tuple-element.99.g_ref, bf16[768,2048]{1,0:T(8,128)(2,1)} %all-gather.6.cloned.1.call-done.w_ref.refs_6_, bf16[8,256,768]{2,1,0:T(8,128)(2,1)} %get-tuple-element.102.by_gate_ref, ...), custom_call_target="tpu_custom_call" | custom-call | bytes 1048576 | tf_op jit(solution)/shard_map/ffn_back/pallas_call | solution.py:1076
  310.3 19.2 %bitcast_convert_fusion.refs_8_ = bf16[2048,1536]{1,0:T(8,128)(2,1)} fusion(bf16[8,256,2048]{2,1,0:T(8,128)(2,1)} %get-tuple-element.100.n_ref, bf16[8,256,1536]{2,1,0:T(8,128)(2,1)} %ffn_back.1), kind=kOutput, calls=%fused_computation | convolution fusion | flops 12888047616 | bytes 20971520 | tf_op jit(solution)/shard_map/dot_general | solution.py:18
  329.7 88.5 %plane_reduce_mid.1 = (f32[256,2048]{1,0:T(8,128)}, bf16[8,256,2048]{2,1,0:T(8,128)(2,1)}, bf16[4,256,2048]{2,1,0:T(8,128)(2,1)}) custom-call(bf16[2,4,256,1536]{3,2,1,0:T(8,128)(2,1)} %bitcast.142, bf16[2048,1536]{1,0:T(8,128)(2,1)} %all-gather.8.cloned.1.call-done.w_ref.refs_1_, f32[1,2048]{1,0:T(1,128)} %reshape_reshape.16.refs_2_, ...), custom_call_target="tpu_custom_call" | custom-call | bytes 8388608 | tf_op jit(solution)/shard_map/plane_reduce_mid/pallas_call | solution.py:438
  418.1 7.1 %convolution_bitcast_fusion = bf16[384,2048]{1,0:T(8,128)(2,1)S(1)} fusion(bf16[8,256,384]{2,1,0:T(8,128)(2,1)S(1)} %copy-done.7, bf16[8,256,2048]{2,1,0:T(8,128)(2,1)} %get-tuple-element.106.dres_ref), kind=kOutput, calls=%fused_computation.17 | convolution fusion | flops 3221225472 | bytes 11534336 | tf_op jit(solution)/shard_map/dot_general | solution.py:18
  425.9 1.7 slice_bitcast_fusion.2
  427.7 1.8 collective-permute-start.6
  431.3 17.3 %mixer_back_scan.1 = (bf16[8,256,384]{2,1,0:T(8,128)(2,1)}, f32[8,256,384]{2,1,0:T(8,128)}, f32[8,256,384]{2,1,0:T(8,128)}, f32[8,8,384]{2,1,0:T(8,128)}, f32[8,8,384]{2,1,0:T(8,128)}) custom-call(s32[8,8]{1,0:T(8,128)} %add_add_fusion.info, bf16[8,256,2048]{2,1,0:T(8,128)(2,1)} %get-tuple-element.106.dres_ref, bf16[384,2048]{1,0:T(8,128)(2,1)} %pad.57.refs_1_.wo_ref, ...), custom_call_target="tpu_custom_call" | custom-call | bytes 1048576 | tf_op jit(solution)/shard_map/mixer_back_scan/pallas_call | solution.py:1076
  448.6 9.2 %pass_state_back.1.grad_in_ref = f32[8,1,384]{2,1,0:T(1,128)} custom-call(f32[8,8,384]{2,1,0:T(8,128)} %get-tuple-element.112.mul_ref, f32[8,8,384]{2,1,0:T(8,128)} %get-tuple-element.113.add_ref), custom_call_target="tpu_custom_call" | custom-call | bytes 1048576 | tf_op jit(solution)/shard_map/pass_state_back/pallas_call | solution.py:823
  459.2 17.2 %collective-permute-done.5 = bf16[256,2048]{1,0:T(8,128)(2,1)} collective-permute-done((bf16[256,2048]{1,0:T(8,128)(2,1)}, bf16[256,2048]{1,0:T(8,128)(2,1)}, u32[]{:S(2)}, u32[]{:S(2)}) %collective-permute-start.5) | collective-permute-done | bytes 1048608 | tf_op jit(solution)/shard_map/ppermute | solution.py:39
  476.7 3.6 fusion.16.refs_0_.refs_8_
  480.3 17.5 %mixer_back.1 = (bf16[8,256,384]{2,1,0:T(8,128)(2,1)}, f32[8,8,384]{2,1,0:T(8,128)}, f32[384,768]{1,0:T(8,128)}, f32[8,384]{1,0:T(8,128)}) custom-call(s32[8,8]{1,0:T(8,128)} %add_add_fusion.info, f32[8,256,384]{2,1,0:T(8,128)} %get-tuple-element.110.p_ref, f32[8,256,384]{2,1,0:T(8,128)} %get-tuple-element.111.s_ref, ...), custom_call_target="tpu_custom_call" | custom-call | bytes 1048576 | tf_op jit(solution)/shard_map/mixer_back/pallas_call | solution.py:1076
  501.5 8.2 %pass_rows_back.1.rim_ref = f32[8,8,384]{2,1,0:T(8,128)} custom-call(f32[8,8,384]{2,1,0:T(8,128)} %get-tuple-element.117.edge_ref), custom_call_target="tpu_custom_call" | custom-call | bytes 1048576 | tf_op jit(solution)/shard_map/pass_rows_back/pallas_call | solution.py:823
  509.7 8.8 %mixer_back_conv.1 = bf16[8,256,640]{2,1,0:T(8,128)(2,1)} custom-call(s32[8,8]{1,0:T(8,128)} %add_add_fusion.info, bf16[8,256,384]{2,1,0:T(8,128)(2,1)} %get-tuple-element.116.dconv_ref, f32[8,8,384]{2,1,0:T(8,128)} %pass_rows_back.1.rim_ref, bf16[8,256,384]{2,1,0:T(8,128)(2,1)} %get-tuple-element.118.dgate_ref, f32[8,384]{1,0:T(8,128)} %select_maximum_fusion.vec_ref, ...), custom_call_target="tpu_custom_call" | custom-call | bytes 1048576 | tf_op jit(solution)/shard_map/mixer_back_conv/pallas_call | solution.py:1076
  519.3 11.1 %bitcast_convert_fusion.1.refs_7_ = bf16[2048,640]{1,0:T(8,128)(2,1)} fusion(bf16[8,256,2048]{2,1,0:T(8,128)(2,1)} %get-tuple-element.120, bf16[8,256,640]{2,1,0:T(8,128)(2,1)} %mixer_back_conv.1), kind=kOutput, calls=%fused_computation.1 | convolution fusion | flops 5370019840 | bytes 13631488 | tf_op jit(solution)/shard_map/dot_general | solution.py:18
  531.0 2.1 fusion.28
  536.4 64.6 %plane_reduce_last.1 = (bf16[256,2048]{1,0:T(8,128)(2,1)}, f32[64,6144]{1,0:T(8,128)}, f32[64,6144]{1,0:T(8,128)}, bf16[2,4,16,320]{3,2,1,0:T(8,128)(2,1)}) custom-call(bf16[2,4,256,640]{3,2,1,0:T(8,128)(2,1)} %bitcast.149, bf16[2048,640]{1,0:T(8,128)(2,1)} %bitcast.151, f32[1,2048]{1,0:T(1,128)} %broadcast_in_dim_reshape.4.gain_ref.refs_2_, ...), custom_call_target="tpu_custom_call" | custom-call | bytes 8388608 | tf_op jit(solution)/shard_map/plane_reduce_last/pallas_call | solution.py:438
  603.8 2.4 multiply_reduce_fusion
  609.0 1.6 fusion.63
  610.6 12.2 %finish.1 = (f32[64,2560]{1,0:T(8,128)}, f32[64,2560]{1,0:T(8,128)}) custom-call(bf16[512,640]{1,0:T(8,128)(2,1)} %reduce-scatter.15.cloned.1.call-done.sums_ref), custom_call_target="tpu_custom_call" | custom-call | tf_op jit(solution)/shard_map/finish/pallas_call | solution.py:678
  622.8 1.6 multiply_reduce_fusion.2
  (210 shorter events, 47.6 us)
Async XLA Ops:
  7.2 103.2 %all-gather.4.cloned.1.call-start = ((), (), s32[]{:S(2)}) async-start(), calls=%async_computation.6 | async-start | bytes 1638400 | tf_op jit(solution)/shard_map/all_gather | solution.py:1133
  7.9 252.4 %all-gather.8.cloned.1.call-start = ((), (), s32[]{:S(2)}) async-start(), calls=%async_computation.8 | async-start | bytes 7864320 | tf_op jit(solution)/shard_map/all_gather | solution.py:1133
  99.5 7.3 %copy-start.23 = (bf16[2,2,80,320]{3,2,1,0:T(8,128)(2,1)S(1)}, bf16[2,2,80,320]{3,2,1,0:T(8,128)(2,1)}, u32[]{:S(2)}) copy-start(bf16[2,2,80,320]{3,2,1,0:T(8,128)(2,1)} %get-tuple-element.86) | copy-start | bytes 614404
  99.5 195.8 %all-gather.6.cloned.1.call-start = ((), (), s32[]{:S(2)}) async-start(), calls=%async_computation.7 | async-start | bytes 3932160 | tf_op jit(solution)/shard_map/all_gather | solution.py:1133
  100.2 229.4 %reduce-scatter.7.cloned.1.call-start = ((), (), s32[]{:S(2)}) async-start(), calls=%async_computation.9 | async-start | bytes 1966080 | tf_op jit(solution)/shard_map/reduce_scatter | solution.py:1136
  100.3 55.8 %collective-permute-start = (bf16[256,2048]{1,0:T(8,128)(2,1)}, bf16[256,2048]{1,0:T(8,128)(2,1)}, u32[]{:S(2)}, u32[]{:S(2)}) collective-permute-start(bf16[256,2048]{1,0:T(8,128)(2,1)} %bitcast.23.refs_5_.refs_3_), channel_id=1, source_target_pairs={{0,2},{2,0},{4,6},{6,4},{1,3},{3,1},{5,7},{7,5},{8,10},{10,8},{12,... | collective-permute-start | bytes 3145736 | tf_op jit(solution)/shard_map/ppermute | solution.py:39
  101.8 54.3 %collective-permute-start.1 = (bf16[256,2048]{1,0:T(8,128)(2,1)}, bf16[256,2048]{1,0:T(8,128)(2,1)}, u32[]{:S(2)}, u32[]{:S(2)}) collective-permute-start(bf16[256,2048]{1,0:T(8,128)(2,1)} %bitcast.23.refs_5_.refs_3_), channel_id=1, source_target_pairs={{0,4},{2,6},{4,0},{6,2},{1,5},{3,7},{5,1},{7,3},{8,12},{10,14},{12... | collective-permute-start | bytes 3145736 | tf_op jit(solution)/shard_map/ppermute | solution.py:39
  103.3 52.8 %collective-permute-start.2 = (bf16[256,2048]{1,0:T(8,128)(2,1)}, bf16[256,2048]{1,0:T(8,128)(2,1)}, u32[]{:S(2)}, u32[]{:S(2)}) collective-permute-start(bf16[256,2048]{1,0:T(8,128)(2,1)} %bitcast.23.refs_5_.refs_3_), channel_id=1, source_target_pairs={{0,6},{2,4},{4,2},{6,0},{1,7},{3,5},{5,3},{7,1},{8,14},{10,12},{12... | collective-permute-start | bytes 3145736 | tf_op jit(solution)/shard_map/ppermute | solution.py:39
  112.4 58.8 %collective-permute-start.3 = (bf16[2,80,2048]{2,1,0:T(8,128)(2,1)}, bf16[2,80,2048]{2,1,0:T(8,128)(2,1)}, u32[]{:S(2)}, u32[]{:S(2)}) collective-permute-start(bf16[2,80,2048]{2,1,0:T(8,128)(2,1)} %constant_dynamic-slice_fusion), channel_id=1, source_target_pairs={{0,1},{1,0},{2,3},{3,2},{4,5},{5,4},{6,7},{7,6},{8,9},{9,8},{10,11... | collective-permute-start | bytes 1966088 | tf_op jit(solution)/shard_map/ppermute | solution.py:34
  132.4 32.4 %copy-start.1 = (f32[8,256,384]{2,1,0:T(8,128)S(1)}, f32[8,256,384]{2,1,0:T(8,128)}, u32[]{:S(2)}) copy-start(f32[8,256,384]{2,1,0:T(8,128)} %get-tuple-element.93.gate_ref) | copy-start | bytes 9437188
  164.8 6.5 %copy-start.19 = (bf16[320,2048]{1,0:T(8,128)(2,1)S(1)}, bf16[320,2048]{1,0:T(8,128)(2,1)}, u32[]{:S(2)}) copy-start(bf16[320,2048]{1,0:T(8,128)(2,1)} %all-gather.4.cloned.1.call-done) | copy-start | bytes 3932164
  280.2 8.0 %copy-start.11 = (bf16[8,256,768]{2,1,0:T(8,128)(2,1)S(1)}, bf16[8,256,768]{2,1,0:T(8,128)(2,1)}, u32[]{:S(2)}) copy-start(bf16[8,256,768]{2,1,0:T(8,128)(2,1)} %get-tuple-element.104) | copy-start | bytes 9437188
  288.1 143.1 %reduce-scatter.9.cloned.1.call-start = ((), (), s32[]{:S(2)}) async-start(), calls=%async_computation.10 | async-start | bytes 1966080 | tf_op jit(solution)/shard_map/reduce_scatter | solution.py:1136
  295.2 185.1 %reduce-scatter.11.cloned.1.call-start = ((), (), s32[]{:S(2)}) async-start(), calls=%async_computation.11 | async-start | bytes 7864320 | tf_op jit(solution)/shard_map/reduce_scatter | solution.py:1136
  329.6 180.1 %reduce-scatter.13.cloned.1.call-start = ((), (), s32[]{:S(2)}) async-start(), calls=%async_computation.12 | async-start | bytes 1638400 | tf_op jit(solution)/shard_map/reduce_scatter | solution.py:1136
  329.6 88.5 %copy-start.7 = (bf16[8,256,384]{2,1,0:T(8,128)(2,1)S(1)}, bf16[8,256,384]{2,1,0:T(8,128)(2,1)}, u32[]{:S(2)}) copy-start(bf16[8,256,384]{2,1,0:T(8,128)(2,1)} %get-tuple-element.190) | copy-start | bytes 4718596
  418.1 7.8 %copy-start.8 = (bf16[4,256,2048]{2,1,0:T(8,128)(2,1)S(1)}, bf16[4,256,2048]{2,1,0:T(8,128)(2,1)}, u32[]{:S(2)}) copy-start(bf16[4,256,2048]{2,1,0:T(8,128)(2,1)} %get-tuple-element.107) | copy-start | bytes 12582916
  425.5 32.3 %collective-permute-start.7 = (bf16[2,80,2048]{2,1,0:T(8,128)(2,1)S(1)}, bf16[2,80,2048]{2,1,0:T(8,128)(2,1)S(1)}, u32[]{:S(2)}, u32[]{:S(2)}) collective-permute-start(bf16[2,80,2048]{2,1,0:T(8,128)(2,1)S(1)} %dynamic-slice_bitcast_fusion), channel_id=1, source_target_pairs={{0,1},{1,0},{2,3},{3,2},{4,5},{5,4},{6,7},{7,6},{8,9},{9,8},{10,11... | collective-permute-start | bytes 1966088 | tf_op jit(solution)/shard_map/ppermute | solution.py:34
  427.7 31.5 %collective-permute-start.6 = (bf16[256,2048]{1,0:T(8,128)(2,1)}, bf16[256,2048]{1,0:T(8,128)(2,1)S(1)}, u32[]{:S(2)}, u32[]{:S(2)}) collective-permute-start(bf16[256,2048]{1,0:T(8,128)(2,1)} %get-tuple-element.193), channel_id=1, source_target_pairs={{0,6},{2,4},{4,2},{6,0},{1,7},{3,5},{5,3},{7,1},{8,14},{10,12},{12... | collective-permute-start | bytes 3145736 | tf_op jit(solution)/shard_map/ppermute | solution.py:39
  429.5 46.9 %collective-permute-start.5 = (bf16[256,2048]{1,0:T(8,128)(2,1)}, bf16[256,2048]{1,0:T(8,128)(2,1)}, u32[]{:S(2)}, u32[]{:S(2)}) collective-permute-start(bf16[256,2048]{1,0:T(8,128)(2,1)} %get-tuple-element.194), channel_id=1, source_target_pairs={{0,4},{2,6},{4,0},{6,2},{1,5},{3,7},{5,1},{7,3},{8,12},{10,14},{12... | collective-permute-start | bytes 3145736 | tf_op jit(solution)/shard_map/ppermute | solution.py:39
  430.3 46.3 %collective-permute-start.4 = (bf16[256,2048]{1,0:T(8,128)(2,1)}, bf16[256,2048]{1,0:T(8,128)(2,1)}, u32[]{:S(2)}, u32[]{:S(2)}) collective-permute-start(bf16[256,2048]{1,0:T(8,128)(2,1)} %get-tuple-element.192), channel_id=1, source_target_pairs={{0,2},{2,0},{4,6},{6,4},{1,3},{3,1},{5,7},{7,5},{8,10},{10,8},{12,... | collective-permute-start | bytes 3145736 | tf_op jit(solution)/shard_map/ppermute | solution.py:39
  431.3 26.5 %copy-start.3 = (bf16[320,2048]{1,0:T(8,128)(2,1)S(1)}, bf16[320,2048]{1,0:T(8,128)(2,1)}, u32[]{:S(2)}) copy-start(bf16[320,2048]{1,0:T(8,128)(2,1)} %copy-done.2) | copy-start | bytes 3932164
  457.9 18.7 %copy-start.4 = (f32[256,2048]{1,0:T(8,128)S(1)}, f32[256,2048]{1,0:T(8,128)}, u32[]{:S(2)}) copy-start(f32[256,2048]{1,0:T(8,128)} %get-tuple-element.98.refs_4_) | copy-start | bytes 6291460
  459.1 147.6 %reduce-scatter.17.cloned.1.call-start = ((), (), s32[]{:S(2)}) async-start(), calls=%async_computation.14 | async-start | bytes 307200 | tf_op jit(solution)/shard_map/reduce_scatter | solution.py:1136
  501.4 17.0 %collective-permute-start.8 = (bf16[2,80,328]{2,1,0:T(8,128)(2,1)S(1)}, bf16[2,80,328]{2,1,0:T(8,128)(2,1)S(1)}, u32[]{:S(2)}, u32[]{:S(2)}) collective-permute-start(bf16[2,80,328]{2,1,0:T(8,128)(2,1)S(1)} %dynamic-slice_bitcast_fusion.1), channel_id=1, source_target_pairs={{0,1},{1,0},{2,3},{3,2},{4,5},{5,4},{6,7},{7,6},{8,9},{9,8},{10,11... | collective-permute-start | bytes 314888 | tf_op jit(solution)/shard_map/ppermute | solution.py:34
  519.3 91.3 %reduce-scatter.15.cloned.1.call-start = ((), (), s32[]{:S(2)}) async-start(), calls=%async_computation.13 | async-start | bytes 3276800 | tf_op jit(solution)/shard_map/reduce_scatter | solution.py:1136
  536.4 67.4 %copy-start.9 = (bf16[64,6144]{1,0:T(8,128)(2,1)S(1)}, bf16[64,6144]{1,0:T(8,128)(2,1)}, u32[]{:S(2)}) copy-start(bf16[64,6144]{1,0:T(8,128)(2,1)} %wg_ref.1) | copy-start | bytes 2359300
  536.4 67.4 %copy-start.10 = (bf16[64,6144]{1,0:T(8,128)(2,1)S(1)}, bf16[64,6144]{1,0:T(8,128)(2,1)}, u32[]{:S(2)}) copy-start(bf16[64,6144]{1,0:T(8,128)(2,1)} %wu_ref.1) | copy-start | bytes 2359300
  603.8 19.0 %copy-start.17 = (bf16[64,2560]{1,0:T(8,128)(2,1)S(1)}, bf16[64,2560]{1,0:T(8,128)(2,1)}, u32[]{:S(2)}) copy-start(bf16[64,2560]{1,0:T(8,128)(2,1)} %wy_ref.1) | copy-start | bytes 983044
  603.8 19.0 %copy-start.18 = (bf16[64,2560]{1,0:T(8,128)(2,1)S(1)}, bf16[64,2560]{1,0:T(8,128)(2,1)}, u32[]{:S(2)}) copy-start(bf16[64,2560]{1,0:T(8,128)(2,1)} %wx_ref.1) | copy-start | bytes 983044
  606.1 18.3 %copy-start.25 = (bf16[64]{0:T(256)(128)(2,1)S(1)}, bf16[64]{0:T(256)(128)(2,1)}, u32[]{:S(2)}) copy-start(bf16[64]{0:T(256)(128)(2,1)} %param.31) | copy-start | bytes 388
  606.1 18.8 %copy-start.20 = (bf16[256,2048]{1,0:T(8,128)(2,1)S(1)}, bf16[256,2048]{1,0:T(8,128)(2,1)}, u32[]{:S(2)}) copy-start(bf16[256,2048]{1,0:T(8,128)(2,1)} %get-tuple-element.121) | copy-start | bytes 3145732
  (12 other events, 39.0 us)
Sparse Core Ops, SparseCore 0:
  9.6 42.8 all-gather.3
  99.6 117.0 all-gather.7
  218.3 63.1 all-gather.5
  288.2 36.2 reduce-scatter.6
  326.7 34.2 reduce-scatter.8
  363.1 110.4 reduce-scatter.10
  476.0 31.7 reduce-scatter.12
  519.4 17.4 reduce-scatter.16
  539.3 56.5 reduce-scatter.14

commit v5 on v4

--- a/solution.py
+++ b/solution.py
@@ -167,19 +167,25 @@
         yield slice(i * width, (i + len(runs)) * width), jnp.concatenate(runs, 1)
 
 
-def reduce_kernel(nt, post, nx, extra, waits, hid, *refs):
+def gain_sum(pairs, gain):
+    total = sum(jnp.sum(w[...].astype(F32) * g[...], axis=-1, keepdims=True) for w, g in pairs)
+    return total / gain[...]
+
+
+def reduce_kernel(nt, post, nx, extra, waits, hid, head_w, *refs):
     x_hbm, refs = refs[:nx], refs[nx:]
     w_hbm, gain_ref, first_ref, second_ref = refs[:4]
     extra_in, refs = refs[4 : 4 + extra], refs[4 + extra :]
     if post == "last":
-        lasts_ref, refs = refs[0], refs[1:]
+        lasts_ref, wg_ref, wu_ref, gain_two_ref = refs[:4]
+        refs = refs[4:]
     refs = refs[waits:]
     out_ref, refs = refs[0], refs[1:]
     if post == "last":
         everyone = mine = None
-        extra_out, lasts_out = refs[:2], refs[2]
-        extra_buf, lasts_buf, lasts_mine, lasts_far = refs[3:7]
-        refs = refs[7:]
+        extra_out, lasts_out, gain_out = refs[:2], refs[2], refs[3]
+        extra_buf, lasts_buf, lasts_mine, lasts_far, lasts_sent, lasts_sum = refs[4:10]
+        refs = refs[10:]
     else:
         everyone, refs = refs[0], refs[1:]
         if extra:
@@ -218,8 +224,13 @@
         columns = [(lax.rem(a + d, planes), b, n, c) for d in range(1, planes)]
         peers = plane_peers_of()
         greet([*peers.values(), *columns])
+        for kc in range(2):
+            for kn in range(2):
+                lasts_sent[kc, kn] = (
+                    lasts_ref[kc * 4 + kn].astype(F32) + lasts_ref[kc * 4 + 2 + kn].astype(F32)
+                ).astype(BF)
         for (kc, k), peer in peers.items():
-            move.start(f"l{kc}{k}", lasts_ref.at[kc, k % 2], lasts_buf.at[kc, k], peer)
+            move.start(f"l{kc}{k}", lasts_sent.at[kc, k % 2], lasts_buf.at[kc, k], peer)
     else:
         greet((px, py, pc))
     w_copy.wait()
@@ -311,7 +322,7 @@
 
             kept.append(keep(side_s.at[k], extra_out.at[k]))
     if extra and post == "last":
-        lasts_buf[0, 0] = lasts_ref[0, 0]
+        lasts_buf[0, 0] = lasts_sent[0, 0]
         for kc, k in peers:
             move.arrived(f"l{kc}{k}")
         u = b * 2 + n
@@ -377,7 +388,13 @@
         for i in range(len(columns)):
             move.arrived(f"z{i}")
             total = total + lasts_far[i].astype(F32)
-        lasts_out[...] = total.astype(BF)
+        lasts_sum[...] = total.reshape(lasts_sum.shape)
+        heads = extra_buf.shape[2] // (2 * hid) // 2
+        order = [
+            (i * 4 + q, j * head_w) for i in range(2) for j in range(heads) for q in range(4)
+        ]
+        for at, value in set_side_by_side(lasts_sum, order, head_w):
+            lasts_out[:, at] = value
         for kc, k in peers:
             move.arrived(f"e{kc}{k}")
         wide = extra_buf.shape[2] // 2
@@ -385,10 +402,11 @@
             order = [(p, i * wide + z * hid) for z in range(wide // hid) for p in range(8)]
             for at, value in set_side_by_side(extra_buf, order, hid):
                 extra_out[i][:, at] = value
+        gain_out[...] = gain_sum(((wg_ref, extra_out[0]), (wu_ref, extra_out[1])), gain_two_ref)
     move.sent()
 
 
-def plane_reduce(ident, post, nt, xs, w, gain, first, second, extra=(), done=(), hid=0, lasts=None):
+def plane_reduce(ident, post, nt, xs, w, gain, first, second, extra=(), done=(), hid=0, lasts=None, weights=(), head_w=0):
     rows, d_model = first.shape
     vmem = pl.BlockSpec(memory_space=pltpu.VMEM)
     hbm = pl.BlockSpec(memory_space=pl.ANY)
@@ -417,11 +435,14 @@
             out_specs.append(vmem)
         planes = lax.axis_size("a")
         copies += 7 * len(extra) + 7 + planes - 1
-        block = (2, 4) + lasts.shape[2:]
-        out_shape.append(jax.ShapeDtypeStruct(block, BF))
-        out_specs.append(vmem)
+        block = (2, 4) + lasts.shape[1:]
+        wide = lax.axis_size("a") * 4 * head_w
+        out_shape.append(jax.ShapeDtypeStruct((lasts.shape[1], wide), F32))
+        out_shape.append(jax.ShapeDtypeStruct((each[0], 1), F32))
+        out_specs += [vmem, vmem]
         scratch.append(pltpu.VMEM((8,) + each, BF))
         scratch += [pltpu.VMEM(block, BF)] * 2 + [pltpu.VMEM((planes - 1,) + block, BF)]
+        scratch += [pltpu.VMEM((2, 2) + block[2:], BF), pltpu.VMEM((8,) + block[2:], F32)]
     wide = sum(x.shape[3] for x in xs)
     scratch += [
         pltpu.VMEM((2, 4, rows, wide), BF),
@@ -435,12 +456,15 @@
         pltpu.SemaphoreType.DMA((copies,)),
         pltpu.SemaphoreType.DMA((copies,)),
     ]
+    last = []
+    if post == "last":
+        last = [lasts, *weights[:2], weights[2].astype(F32).reshape(-1, 1)]
     return pl.pallas_call(
-        functools.partial(reduce_kernel, nt, post, len(xs), len(extra), len(done), hid),
+        functools.partial(reduce_kernel, nt, post, len(xs), len(extra), len(done), hid, head_w),
         in_specs=[hbm] * (len(xs) + 1)
         + [vmem] * 3
         + [vmem if post == "fwd" else hbm] * len(extra)
-        + [vmem] * (lasts is not None)
+        + [vmem] * (4 if post == "last" else 0)
         + [hbm] * len(done),
         out_specs=out_specs,
         out_shape=out_shape,
@@ -450,7 +474,7 @@
         ),
         cost_estimate=pl.CostEstimate(flops=0, bytes_accessed=8 << 20, transcendentals=0),
         name=f"plane_reduce_{post}",
-    )(*xs, w, gain.reshape(1, -1), first, second, *extra, *([] if lasts is None else [lasts]), *done)
+    )(*xs, w, gain.reshape(1, -1), first, second, *extra, *last, *done)
 
 
 def start_kernel(
@@ -645,7 +669,9 @@
     )(tokens, w_y, w_x, w_gate, w_up, gate_rows, vec, stream)
 
 
-def finish_kernel(head_w, sums_ref, y_ref, x_ref, buf, local, send, recv):
+def finish_kernel(
+    head_w, sums_ref, wy_ref, wx_ref, gain_ref, y_ref, x_ref, gain_out, buf, local, send, recv
+):
     _, b, n, c = places()
     me = (b * 2 + n) * 2 + c
     peers = plane_peers_of()
@@ -669,17 +695,19 @@
     for first, out in ((0, y_ref), (wide, x_ref)):
         for at, value in set_side_by_side(buf, [(p, o + first) for p, o in order], head_w):
             out[:, at] = value
+    gain_out[...] = gain_sum(((wy_ref, y_ref), (wx_ref, x_ref)), gain_ref)
     move.sent()
 
 
-def finish(sums, head_w):
+def finish(sums, w_y, w_x, gain, head_w):
     each = sums.shape[0] // 8, sums.shape[1]
     vmem = pl.BlockSpec(memory_space=pltpu.VMEM)
     return pl.pallas_call(
         functools.partial(finish_kernel, head_w),
-        in_specs=[pl.BlockSpec(memory_space=pl.ANY)],
-        out_specs=[vmem, vmem],
-        out_shape=[jax.ShapeDtypeStruct((each[0], 4 * each[1]), F32)] * 2,
+        in_specs=[pl.BlockSpec(memory_space=pl.ANY), vmem, vmem, vmem],
+        out_specs=[vmem] * 3,
+        out_shape=[jax.ShapeDtypeStruct((each[0], 4 * each[1]), F32)] * 2
+        + [jax.ShapeDtypeStruct((each[0], 1), F32)],
         scratch_shapes=[
             pltpu.VMEM((8,) + each, BF),
             pltpu.SemaphoreType.DMA((1,)),
@@ -690,7 +718,7 @@
             collective_id=5, has_side_effects=True, vmem_limit_bytes=VMEM_LIMIT
         ),
         name="finish",
-    )(sums)
+    )(sums, w_y, w_x, gain.astype(F32).reshape(-1, 1))
 
 
 def column_peers(planes):
@@ -711,7 +739,42 @@
     ]
 
 
-def pass_state_kernel(reverse, mul_ref, add_ref, out_ref, whole, came, send, recv):
+def split_refs(refs):
+    if len(refs) == 5:
+        return None, refs[:1], refs[1:], None
+    return refs[0], refs[1:3], refs[3:7], refs[7:]
+
+
+def swap_halves(rows_ref, out_ref, local, send, recv):
+    _, _, _, c = places()
+    planes, half = out_ref.shape[:2]
+    each = planes // 2
+    made = []
+    for j in range(each):
+        away = pl.multiple_of((2 * j + 1 - c) * half, half)
+        own = pl.multiple_of((2 * j + c) * half, half)
+        made.append(
+            pltpu.make_async_remote_copy(
+                src_ref=rows_ref.at[pl.ds(away, half)],
+                dst_ref=out_ref.at[c * each + j],
+                send_sem=send.at[j],
+                recv_sem=recv.at[j],
+                device_id=neighbours()[2],
+                device_id_type=MESH,
+            )
+        )
+        made.append(
+            pltpu.make_async_copy(
+                rows_ref.at[pl.ds(own, half)], out_ref.at[c * each + j], local.at[j]
+            )
+        )
+    for copy in made:
+        copy.start()
+    return made
+
+
+def pass_state_kernel(reverse, mul_ref, add_ref, *refs):
+    rows_ref, (out_ref, *halves), (whole, came, send, recv), swaps = split_refs(refs)
     a, b, n, c = places()
     planes = came.shape[0] + 1
     row = 0 if reverse else 7
@@ -722,7 +785,8 @@
     for i in range(4):
         whole[0, i : i + 1, :] = near_mul[i] * far_mul[i]
         whole[1, i : i + 1, :] = far_mul[i] * near_add[i] + far_add[i]
-    greet(column_peers(planes))
+    greet(column_peers(planes) + ([neighbours()[2]] if swaps else []))
+    swapped = swap_halves(rows_ref, halves[0], *swaps) if swaps else []
 
     def copy(d):
         return pltpu.make_async_remote_copy(
@@ -766,8 +830,12 @@
         def _():
             copy(d).wait_send()
 
-
-def pass_rows_kernel(reverse, edge_ref, out_ref, leaving, came, send, recv):
+    for made in swapped:
+        made.wait()
+
+
+def pass_rows_kernel(reverse, edge_ref, *refs):
+    rows_ref, (out_ref, *halves), (leaving, came, send, recv), swaps = split_refs(refs)
     a, b, n, c = places()
     planes = lax.axis_size("a")
     near_at, far_at = (1, 0) if reverse else (0, 1)
@@ -776,7 +844,8 @@
     first = 0 if reverse else 4
     for i, value in enumerate(earlier_blocks(edge_ref, far_at, first, 4)):
         leaving[i * 4 : i * 4 + 4, :] = value
-    greet(column_peers(planes))
+    greet(column_peers(planes) + ([neighbours()[2]] if swaps else []))
+    swapped = swap_halves(rows_ref, halves[0], *swaps) if swaps else []
     copy = pltpu.make_async_remote_copy(
         src_ref=leaving,
         dst_ref=came,
@@ -809,8 +878,11 @@
     def _():
         copy.wait_send()
 
-
-def pass_along(ident, name, reverse, *edges):
+    for made in swapped:
+        made.wait()
+
+
+def pass_along(ident, name, reverse, *edges, halves=None):
     shape = edges[0].shape
     planes = lax.axis_size("a")
     vmem = pl.BlockSpec(memory_space=pltpu.VMEM)
@@ -820,19 +892,26 @@
     else:
         body, out = pass_rows_kernel, shape
         buffers = [(16,) + shape[2:]] * 2
+    given, out_shape = list(edges), [jax.ShapeDtypeStruct(out, F32)]
+    scratch = [pltpu.VMEM(shape, F32) for shape in buffers]
+    scratch += [pltpu.SemaphoreType.DMA((planes - 1,))] * 2
+    if halves is not None:
+        given.append(halves[0])
+        to = (planes, halves[1], halves[0].shape[1])
+        out_shape.append(jax.ShapeDtypeStruct(to, BF))
+        scratch += [pltpu.SemaphoreType.DMA((planes // 2,))] * 3
     return pl.pallas_call(
         functools.partial(body, reverse),
-        in_specs=[vmem] * len(edges),
-        out_specs=vmem,
-        out_shape=jax.ShapeDtypeStruct(out, F32),
-        scratch_shapes=[pltpu.VMEM(shape, F32) for shape in buffers]
-        + [pltpu.SemaphoreType.DMA((planes - 1,))] * 2,
+        in_specs=[vmem] * len(given),
+        out_specs=[vmem] * len(out_shape),
+        out_shape=out_shape,
+        scratch_shapes=scratch,
         compiler_params=pltpu.CompilerParams(
             collective_id=ident, has_side_effects=True, vmem_limit_bytes=VMEM_LIMIT
         ),
         cost_estimate=pl.CostEstimate(flops=0, bytes_accessed=1 << 20, transcendentals=0),
         name=name,
-    )(*edges)
+    )(*given)
 
 
 def norm_product_kernel(info, tok_ref, w_ref, gain_ref, n_ref, gate_ref, lin_ref, tail_ref):
@@ -979,10 +1058,22 @@
 
 
 def back_scan_kernel(
-    nseq, taps, info, dres_ref, wo_ref, gate_ref, hidden_ref, retain_ref, vec_ref, *refs
+    nseq, taps, info, dres_ref, wo_ref, gate_ref, hidden_ref, retain_ref, vec_ref, mixed_ref, *refs
 ):
-    dgate_ref, p_ref, s_ref, pe_ref, se_ref, ext, a_s, b_s = refs[-8:]
+    dgate_ref, p_ref, s_ref, pe_ref, se_ref, wgrad_ref, ext, a_s, b_s, wgrad = refs[-10:]
     rows = gate_ref.shape[1]
+    i = pl.program_id(0)
+
+    @pl.when(i == 0)
+    def _():
+        wgrad[...] = jnp.zeros_like(wgrad)
+
+    wgrad[...] += tdot(mixed_ref[0], dres_ref[0])
+
+    @pl.when(i == pl.num_programs(0) - 1)
+    def _():
+        wgrad_ref[...] = wgrad[...].astype(BF)
+
     pos, begin, _ = row_places(info, rows, nseq)
     d_mixed = ndot(dres_ref[0], wo_ref[...])
     gelu, slope = gelu_pair(gate_ref[0])
@@ -999,10 +1090,10 @@
 
 
 def back_kernel(
-    nseq, taps, info, p_ref, s_ref, grad_in_ref, hidden_ref, state_in_ref, state0_ref, conv_ref,
-    retain_ref, admit_ref, lin_ref, rim_ref, conv0_ref, wg_ref, vec_ref, *refs
+    nseq, taps, length, info, p_ref, s_ref, grad_in_ref, hidden_ref, state_in_ref, state0_ref, conv_ref,
+    retain_ref, admit_ref, lin_ref, rim_ref, conv0_ref, wg_ref, vec_ref, sums_o_ref, *refs
 ):
-    dconv_ref, head_ref, wgrad_ref, vgrad_ref, ext = refs[-5:]
+    dconv_ref, head_ref, late_ref, lasts_ref, ext, wgrad_ref, vgrad_ref = refs[-7:]
     i = pl.program_id(0)
     rows, wide = lin_ref.shape[1:]
     pos, begin, seg = row_places(info, rows, nseq)
@@ -1042,6 +1133,38 @@
     sums += [low, d_rate.astype(F32), d_inflow.astype(F32), d_log * (-8.0 * retain)]
     for k, value in enumerate(sums):
         vgrad_ref[k : k + 1, :] += jnp.sum(value, axis=0, keepdims=True)
+
+    slots = lasts_ref.shape[1]
+    column = lax.broadcasted_iota(jnp.int32, (1, slots), 1)
+    wanted = jnp.full((1, slots), -1, jnp.int32)
+    for q in range(nseq):
+        end = (info[i, 2 + q] if q + 1 < nseq else length) - 1
+        wanted = jnp.where(column == q, end, wanted)
+        for j in range(taps - 1):
+            wanted = jnp.where(column == nseq + q * (taps - 1) + j, end - (taps - 2) + j, wanted)
+    hot = jnp.where(pos == wanted, 1.0, 0.0).astype(BF)
+    states, convs = tdot(hot, hidden_ref[0].astype(BF)), tdot(hot, lin_ref[0])
+    row = lax.broadcasted_iota(jnp.int32, states.shape, 0)
+    lasts_ref[0] = jnp.where(row < nseq, states, convs).astype(BF)
+
+    @pl.when(i == pl.num_programs(0) - 1)
+    def _():
+        used = late_ref.shape[0]
+        before = sums_o_ref.shape[1]
+        late_ref[:, :before] = sums_o_ref[:used, :]
+        head_w = (late_ref.shape[1] - before - len(sums)) // 2
+        last = len(sums) - 1
+        vgrad_ref[last : last + 1, :] *= vec_ref[last + 1 : last + 2, :]
+        count = vgrad_ref.shape[0]
+        row = lax.broadcasted_iota(jnp.int32, (count, count), 0)
+        column = lax.broadcasted_iota(jnp.int32, (count, count), 1)
+        eye = jnp.where(row == column, 1.0, 0.0).astype(BF)
+        turned = tdot(vgrad_ref[...].astype(BF), eye)
+        for h in range(used // head_w):
+            at = slice(h * head_w, (h + 1) * head_w)
+            parts = [wgrad_ref[at, o + h * head_w : o + (h + 1) * head_w] for o in (0, wide)]
+            parts.append(turned[at, : len(sums)])
+            late_ref[at, before:] = jnp.concatenate(parts, 1).astype(BF)
 
 
 def back_conv_kernel(nseq, taps, info, dconv_ref, rim_ref, dgate_ref, vec_ref, *refs):
@@ -1172,13 +1295,6 @@
         return jnp.stack([first, second], 1).reshape((wide_here,) + mine_all.shape[2:])
 
 
-    def part_halves(full):
-        full = full.reshape((heads_here, 2, half) + full.shape[1:])
-        own, away = pick(full, c, 1), swap_c(pick(full, 1 - c, 1))
-        first = jnp.where(c == 0, own, away)
-        second = jnp.where(c == 0, away, own)
-        return jnp.concatenate([first, second], 0).reshape((planes * half,) + full.shape[3:])
-
     w_o = padded(join_halves(gather_a(w_out).reshape(planes, half, d_model)), 0)
 
     def block_diagonal(m):
@@ -1205,7 +1321,8 @@
     mine = pick(canon[:, :nvec].reshape(2, heads_here, count, 2, taps + 4, half), c)
     mine = pick(mine, u, 1).transpose(2, 0, 1, 3).reshape(taps + 4, wide_here)
     decay_f = mine[taps + 3]
-    vec = padded(jnp.concatenate([mine[: taps + 3], jax.nn.softplus(decay_f)[None]]))
+    vec = [mine[: taps + 3], jax.nn.softplus(decay_f)[None], jax.nn.sigmoid(decay_f)[None]]
+    vec = padded(jnp.concatenate(vec))
 
     def my_channels(v):
         lead = v.shape[:-1]
@@ -1257,7 +1374,7 @@
     def two(v):
         return v.reshape((2, 2, nn) + v.shape[1:])
 
-    rim = pass_along(6, "pass_rows", False, tail)
+    rim = pass_along(6, "pass_rows", False, tail)[0]
     conv_0b, state_0b = per_block(conv_0), per_block(state_0)
     full = (nblocks, rows, wp)
     conv_low, retain, admit, carry_mul, carry_add, end_mul, end_add = by_block(
@@ -1276,7 +1393,7 @@
     )
 
     (end_mul, end_add), grads = lax.optimization_barrier(((end_mul, end_add), grads))
-    state_in = pass_along(7, "pass_state", False, end_mul, end_add)
+    state_in = pass_along(7, "pass_state", False, end_mul, end_add)[0]
     hidden = carry_mul * state_in + carry_add
     mixed_in = (hidden * jax.nn.gelu(gate_in)).astype(BF).reshape(-1, wp)
     resid, normed_two, grads = plane_reduce(
@@ -1320,105 +1437,70 @@
     )
     d_resid_low = d_resid_low.reshape(nblocks * rows, d_model)
 
-    sums_o = tdot(mixed_in, d_resid_low)[:wide_here].astype(BF)
-    grad_wo = scatter_a(part_halves(sums_o))
-    low, sums_o = lax.optimization_barrier((low, sums_o))
     result = resid + low[0].astype(F32)
     for k in range(1, count):
         result = result + xor_u(low[k], k).astype(F32)
     result = result.astype(BF)
 
-    d_gate_in, back_mul, back_add, end_mul, end_add = by_block(
+    d_gate_in, back_mul, back_add, end_mul, end_add, sums_o = by_block(
         functools.partial(back_scan_kernel, nseq, taps),
         info,
         [
             (d_resid_low.reshape(nblocks, rows, d_model), True), (w_o, False), (gate_in, True),
-            (hidden, True), (retain, True), (vec, False),
+            (hidden, True), (retain, True), (vec, False), (mixed_in.reshape(full), True),
         ],
-        [(full, BF, True), (full, F32, True), (full, F32, True), edge, edge],
-        [(rows + 8, wp), (rows, wp), (rows, wp)],
-        (sent_d[1], sums_o),
+        [
+            (full, BF, True), (full, F32, True), (full, F32, True), edge, edge,
+            ((wp, d_model), BF, False),
+        ],
+        [(rows + 8, wp), (rows, wp), (rows, wp), (wp, d_model)],
+        (sent_d[1],),
         name="mixer_back_scan",
     )
-    grad_in = pass_along(8, "pass_state_back", True, end_mul, end_add)
-    d_conv_low, head, sums_gates, vec_grads = by_block(
-        functools.partial(back_kernel, nseq, taps),
+    grad_in = pass_along(8, "pass_state_back", True, end_mul, end_add)[0]
+    d_conv_low, head, late, lasts = by_block(
+        functools.partial(back_kernel, nseq, taps, planes * 2 * rows),
         info,
         [
             (back_mul, True), (back_add, True), (grad_in, True), (hidden, True),
             (state_in, True), (state_0b, True), (conv_low, True), (retain, True),
             (admit, True), (linear, True), (rim, True), (conv_0b, True), (w_gates, False), (vec, False),
+            (sums_o, False),
         ],
-        [(full, BF, True), edge, ((wp, 2 * wp), F32, False), ((taps + 4, wp), F32, False)],
-        [(rows + 8, wp)],
-        (result, sent_gu),
+        [
+            (full, BF, True), edge, ((wide_here, d_model + 2 * head_w + taps + 4), BF, False),
+            ((nblocks, nseq * taps, wp), BF, True),
+        ],
+        [(rows + 8, wp), (wp, 2 * wp), (taps + 4, wp)],
+        (),
         name="mixer_back",
     )
 
-    def diagonal(m):
-        m = m.reshape(heads_here, head_w, heads_here, head_w)
-        return jnp.concatenate([m[h, :, h] for h in range(heads_here)], 0)
-
-    grad_gates = jnp.concatenate(
-        [
-            diagonal(sums_gates[:wide_here, :wide_here]),
-            diagonal(sums_gates[:wide_here, wp : wp + wide_here]),
-        ],
-        1,
-    )
-    rim_back = pass_along(9, "pass_rows_back", True, head)
+    rim_back, late = pass_along(9, "pass_rows_back", True, head, halves=(late, half))
     d_both = by_block(
         functools.partial(back_conv_kernel, nseq, taps),
         info,
         [(d_conv_low, True), (rim_back, True), (d_gate_in, True), (vec, False)],
         [((nblocks, rows, 2 * wide_here), BF, True)],
         [(rows + 8, wp)],
-        (grad_wo,),
+        (result, sent_gu),
         name="mixer_back_conv",
     )[0]
-    vec_grads = vec_grads[:, :wide_here].T
-    vec_grads = jnp.concatenate(
-        [vec_grads[:, :-1], vec_grads[:, -1:] * jax.nn.sigmoid(decay_f)[:, None]], 1
-    )
-    late = jnp.concatenate([grad_gates, vec_grads], 1).astype(BF)
-    late = scatter_a(part_halves(late)).astype(F32)
-    grad_wa, grad_wi = late[:, :head_w], late[:, head_w : 2 * head_w]
-    vec_grads = late[:, 2 * head_w :].T
-
+    late = scatter_a(late.reshape(planes * half, -1))
     sums_yx = tdot(normed, d_both.reshape(nblocks * rows, 2 * wide_here)).astype(BF)
-    end = jnp.concatenate(
-        [offsets[:, 1:], jnp.full((streams, 1), planes * 2 * rows, jnp.int32)], 1
-    )
-    end_b = per_block(end) - 1
-    hot = (position[:, None, :] == end_b[:, :, None]).astype(BF)
-    lasts = lax.dot_general(
-        hot, hidden.astype(BF), (((2,), (1,)), ((0,), (0,))), preferred_element_type=F32
-    )
-    slots = jnp.arange(back, dtype=jnp.int32)
-    where_conv = (end_b[:, :, None] - back + 1 + slots).reshape(nblocks, nseq * back)
-    hot = (position[:, None, :] == where_conv[:, :, None]).astype(BF)
-    conv_lasts = lax.dot_general(
-        hot, linear, (((2,), (1,)), ((0,), (0,))), preferred_element_type=F32
-    )
-    lasts = two(jnp.concatenate([lasts, conv_lasts], 1)[..., :wide_here])
-    lasts = (lasts[:, 0] + lasts[:, 1]).astype(BF)
-    input_grad, grad_wg, grad_wu, found = plane_reduce(
+    input_grad, grad_wg, grad_wu, found, grad_gain_two = plane_reduce(
         4, "last", True, (d_both.reshape(2, count, rows, -1),), w_yx, gain_one, tokens[0], d_resid,
-        (sent_gu,), (sums_yx, result), hid, lasts,
-    )
-    grad_wy, grad_wx = finish(scatter_a(sums_yx), head_w)
-
-    def gain_grad(gain, *pairs):
-        total = sum(jnp.sum(w.astype(F32) * g, axis=1) for w, g in pairs)
-        return total / gain.astype(F32)
-
-    grad_gain_one = gain_grad(norm1_gain, (w_y, grad_wy), (w_x, grad_wx))
-    grad_gain_two = gain_grad(norm2_gain, (w_gate, grad_wg), (w_up, grad_wu))
-
-    found = found.reshape(2, count, nseq * taps, heads_here, head_w)
-    found = found.transpose(2, 0, 3, 1, 4).reshape(nseq * taps, width)
-    final_state = found[:nseq].astype(F32)
-    final_conv = found[nseq:].reshape(nseq, back, width)
+        (sent_gu,), (sums_yx,), hid, lasts, (w_gate, w_up, norm2_gain), head_w,
+    )
+    late, input_grad = lax.optimization_barrier((late, input_grad))
+    late = late.astype(F32)
+    grad_wo, grad_gates, vec_grads = jnp.split(late, [d_model, d_model + 2 * head_w], 1)
+    grad_wa, grad_wi, vec_grads = grad_gates[:, :head_w], grad_gates[:, head_w:], vec_grads.T
+    grad_wy, grad_wx, grad_gain_one = finish(scatter_a(sums_yx), w_y, w_x, norm1_gain, head_w)
+    grad_gain_one, grad_gain_two = grad_gain_one[:, 0], grad_gain_two[:, 0]
+
+    final_state = found[:nseq]
+    final_conv = found[nseq:].astype(BF).reshape(nseq, back, width)
 
     return (
         result[None],
@@ -1429,7 +1511,7 @@
         grad_wx,
         grad_wa,
         grad_wi,
-        grad_wo.astype(F32),
+        grad_wo,
         grad_gain_one,
         vec_grads[:taps],
         vec_grads[taps],

time: 644 us -> 626 us (0.972)
  waiting for transfers between devices: 19.1 us -> 9.59 us
  matrix products: 54.8 us -> 45.3 us
  other arithmetic: 30.7 us -> 23 us
    ppermute x6, waiting for transfers between devices: 17.5 us -> 0.02 us  [xor_u(): return lax.ppermute(value, ('b', 'n'), [(i, i ^ k) for i in range(size)])]
    unnamed x9, waiting for transfers between devices: 1.48 us -> 9.5 us
    dot_general x5 -> x4, matrix products: 52.4 us -> 45.3 us  [tdot(): lax.dot_general(left, right, (((0,), (0,)), ((), ())), preferred_element_...]
    unnamed x63 -> x45, local copies, waits for them, and re-layouts: 8.01 us -> 13.2 us
  transfers between devices with their start and end apart: 18 -> 15, of which waited for: 2 -> 1; matrix products, arithmetic and copies ran while one was open for 17% -> 15% of each run, Pallas kernels for 73% -> 76%
where the time goes in v5:
time: 626 us; the launch traced here: 619 us
  Pallas kernels  486 us (78%)
  matrix products  45.3 us (7%)
  local copies, waits for them, and re-layouts  31.3 us (5%)
  other arithmetic  23 us (4%)
  between operations  14.9 us (2%)
  waiting for transfers between devices  9.59 us (2%)
  starting transfers between devices  8.92 us (1%)
    pallas_call x3, Pallas kernels, plane_reduce(): pl.pallas_call(functools.partial(reduce_kernel, nt, post, len(xs), len(ex...  240 us
    pallas_call x7, Pallas kernels, by_block(): pl.pallas_call(body, grid_spec=pltpu.PrefetchScalarGridSpec(num_scalar_pr...  118 us
    pallas_call x1, Pallas kernels, start_exchange(): pl.pallas_call(functools.partial(start_kernel, head_w, hid), in_specs=[vm...  84.9 us
    dot_general x4, matrix products, tdot(): lax.dot_general(left, right, (((0,), (0,)), ((), ())), preferred_element_...  45.3 us
    pallas_call x4, Pallas kernels, pass_along(): pl.pallas_call(functools.partial(body, reverse), in_specs=[vmem] * len(gi...  30 us
    pallas_call x1, Pallas kernels, finish(): pl.pallas_call(functools.partial(finish_kernel, head_w), in_specs=[pl.Blo...  13.4 us
    unnamed x45, local copies, waits for them, and re-layouts  13.2 us
  transfers between devices with their start and end apart: 15, of which 1 were waited for; matrix products, arithmetic and copies ran while one was open for 15% of the time, Pallas kernels for 76%

profile of v5, /device:TPU:0, one launch (start us, length us, event | category | flops | bytes accessed | tf_op | source)
XLA Modules:
  0.0 619.4 jit_solution(3439811018947878457)
XLA Ops:
  13.0 1.5 pad_maximum_fusion.2.rows_ref
  14.5 84.9 %start_exchange.1 = (bf16[8,256,2048]{2,1,0:T(8,128)(2,1)}, bf16[4,8,64,640]{3,2,1,0:T(8,128)(2,1)}, bf16[8,64,1536]{2,1,0:T(8,128)(2,1)}, bf16[4,80,320]{2,1,0:...) custom-call(bf16[256,2048]{1,0:T(8,128)(2,1)} %bitcast.100, ...), custom_call_target="tpu_custom_call" | custom-call | bytes 8388608 | tf_op jit(solution)/shard_map/start_exchange/pallas_call | solution.py:652
  100.3 1.5 collective-permute-start
  101.8 1.5 collective-permute-start.1
  110.4 2.0 constant_dynamic-slice_fusion
  112.4 1.6 collective-permute-start.3
  114.7 17.7 %norm_product.1 = (bf16[8,256,2048]{2,1,0:T(8,128)(2,1)}, f32[8,256,384]{2,1,0:T(8,128)}, bf16[8,256,384]{2,1,0:T(8,128)(2,1)}, f32[8,8,384]{2,1,0:T(8,128)}) custom-call(s32[8,8]{1,0:T(8,128)} %add_add_fusion.info, bf16[8,256,2048]{2,1,0:T(8,128)(2,1)} %get-tuple-element.86.tok_ref, bf16[2048,640]{1,0:T(8,128)(2,1)} %bitcast.106, ...), custom_call_target="tpu_custom_call" | custom-call | bytes 1048576 | tf_op jit(solution)/shard_map/norm_product/pallas_call | solution.py:1199
  132.4 5.7 pass_rows.1.rim_ref
  140.1 15.9 %mixer_forward.1 = (bf16[8,256,384]{2,1,0:T(8,128)(2,1)}, f32[8,256,384]{2,1,0:T(8,128)}, f32[8,256,384]{2,1,0:T(8,128)}, f32[8,256,384]{2,1,0:T(8,128)}, f32[8,...) custom-call(s32[8,8]{1,0:T(8,128)} %add_add_fusion.info, ...), custom_call_target="tpu_custom_call" | custom-call | bytes 1048576 | tf_op jit(solution)/shard_map/mixer_forward/pallas_call | solution.py:1199
  156.1 8.0 %pass_state.1.state_in_ref = f32[8,1,384]{2,1,0:T(1,128)} custom-call(f32[8,8,384]{2,1,0:T(8,128)} %get-tuple-element.95.mul_ref, f32[8,8,384]{2,1,0:T(8,128)} %get-tuple-element.96.add_ref), custom_call_target="tpu_custom_call" | custom-call | bytes 1048576 | tf_op jit(solution)/shard_map/pass_state/pallas_call | solution.py:903
  164.8 6.5 %fusion.12 = (bf16[8,256,384]{2,1,0:T(8,128)(2,1)}, f32[8,256,384]{2,1,0:T(8,128)}) fusion(f32[8,256,384]{2,1,0:T(8,128)S(1)} %copy-done, f32[8,256,384]{2,1,0:T(8,128)} %get-tuple-element.97, f32[8,256,384]{2,1,0:T(8,128)} %get-tuple-element.92, f32[8,384]{1,0:T(8,128)S(1)} %bitcast.137), kind=kLoop, calls=%fused_computation.15 | loop fusion | flops 9437184 | bytes 14168064 | tf_op jit(solution)/shard_map/convert_element_type | solution.py:1398
  173.9 86.3 %plane_reduce_fwd.1 = (f32[256,2048]{1,0:T(8,128)}, bf16[8,256,2048]{2,1,0:T(8,128)(2,1)}, bf16[8,256,2048]{2,1,0:T(8,128)(2,1)}) custom-call(bf16[2,4,256,384]{3,2,1,0:T(8,128)(2,1)} %bitcast.104, bf16[384,2048]{1,0:T(8,128)(2,1)} %pad.56.refs_1_.wo_ref, f32[1,2048]{1,0:T(1,128)} %reshape_reshape.16.refs_2_, bf16[256,2048]{1,0:T(8,128)(2,1)} %bitcast.101, ...), custom_call_target="tpu_custom_call" | custom-call | bytes 8388608 | tf_op jit(solution)/shard_map/plane_reduce_fwd/pallas_call | solution.py:462
  260.3 19.8 %ffn_forward.1 = (bf16[8,256,768]{2,1,0:T(8,128)(2,1)}, bf16[8,256,768]{2,1,0:T(8,128)(2,1)}, bf16[8,256,768]{2,1,0:T(8,128)(2,1)}) custom-call(s32[8,8]{1,0:T(8,128)} %add_add_fusion.info, bf16[8,256,2048]{2,1,0:T(8,128)(2,1)} %get-tuple-element.105.n_ref, bf16[2048,1536]{1,0:T(8,128)(2,1)} %all-gather.8.cloned.1.call-done.w_ref.refs_1_), custom_call_target="tpu_custom_call" | custom-call | bytes 1048576 | tf_op jit(solution)/shard_map/ffn_forward/pallas_call | solution.py:1199
  280.1 7.9 %fusion.17.refs_0_ = bf16[768,1024]{1,0:T(8,128)(2,1)} fusion(bf16[2048,768]{1,0:T(8,128)(2,1)} %bitcast.112, bf16[2048,2048]{1,0:T(8,128)(2,1)} %bitcast.108), kind=kOutput, calls=%fused_computation.22 | convolution fusion | flops 3222011904 | bytes 8912896 | tf_op jit(solution)/shard_map/dot_general | solution.py:18
  288.1 7.0 %fusion.20.refs_1_ = bf16[768,1024]{1,0:T(8,128)(2,1)} fusion(bf16[2048,768]{1,0:T(8,128)(2,1)S(1)} %bitcast.114, bf16[2048,2048]{1,0:T(8,128)(2,1)} %bitcast.109), kind=kOutput, calls=%fused_computation.23 | convolution fusion | flops 3222011904 | bytes 8912896 | tf_op jit(solution)/shard_map/dot_general | solution.py:18
  295.2 15.0 %ffn_back.1 = bf16[8,256,1536]{2,1,0:T(8,128)(2,1)} custom-call(s32[8,8]{1,0:T(8,128)} %add_add_fusion.info, bf16[8,256,2048]{2,1,0:T(8,128)(2,1)} %get-tuple-element.104.g_ref, bf16[768,2048]{1,0:T(8,128)(2,1)} %all-gather.6.cloned.1.call-done.w_ref.refs_6_, bf16[8,256,768]{2,1,0:T(8,128)(2,1)} %get-tuple-element.107.by_gate_ref, ...), custom_call_target="tpu_custom_call" | custom-call | bytes 1048576 | tf_op jit(solution)/shard_map/ffn_back/pallas_call | solution.py:1199
  310.2 19.2 %bitcast_convert_fusion.refs_8_ = bf16[2048,1536]{1,0:T(8,128)(2,1)} fusion(bf16[8,256,2048]{2,1,0:T(8,128)(2,1)} %get-tuple-element.105.n_ref, bf16[8,256,1536]{2,1,0:T(8,128)(2,1)} %ffn_back.1), kind=kOutput, calls=%fused_computation | convolution fusion | flops 12888047616 | bytes 20971520 | tf_op jit(solution)/shard_map/dot_general | solution.py:18
  329.5 88.4 %plane_reduce_mid.1 = (f32[256,2048]{1,0:T(8,128)}, bf16[8,256,2048]{2,1,0:T(8,128)(2,1)}, bf16[4,256,2048]{2,1,0:T(8,128)(2,1)}) custom-call(bf16[2,4,256,1536]{3,2,1,0:T(8,128)(2,1)} %bitcast.99, bf16[2048,1536]{1,0:T(8,128)(2,1)} %all-gather.8.cloned.1.call-done.w_ref.refs_1_, f32[1,2048]{1,0:T(1,128)} %reshape_reshape.16.refs_2_, ...), custom_call_target="tpu_custom_call" | custom-call | bytes 8388608 | tf_op jit(solution)/shard_map/plane_reduce_mid/pallas_call | solution.py:462
  417.9 3.7 slice_bitcast_fusion.2
  421.6 1.7 collective-permute-start.6
  425.1 21.3 %mixer_back_scan.1 = (bf16[8,256,384]{2,1,0:T(8,128)(2,1)}, f32[8,256,384]{2,1,0:T(8,128)}, f32[8,256,384]{2,1,0:T(8,128)}, f32[8,8,384]{2,1,0:T(8,128)}, f32[8,...) custom-call(s32[8,8]{1,0:T(8,128)} %add_add_fusion.info, bf16[8,256,2048]{2,1,0:T(8,128)(2,1)} %get-tuple-element.111.dres_ref, ...), custom_call_target="tpu_custom_call" | custom-call | bytes 1048576 | tf_op jit(solution)/shard_map/mixer_back_scan/pallas_call | solution.py:1199
  446.4 9.2 %pass_state_back.1.grad_in_ref = f32[8,1,384]{2,1,0:T(1,128)} custom-call(f32[8,8,384]{2,1,0:T(8,128)} %get-tuple-element.115.mul_ref, f32[8,8,384]{2,1,0:T(8,128)} %get-tuple-element.116.add_ref), custom_call_target="tpu_custom_call" | custom-call | bytes 1048576 | tf_op jit(solution)/shard_map/pass_state_back/pallas_call | solution.py:903
  455.6 18.7 %mixer_back.1 = (bf16[8,256,384]{2,1,0:T(8,128)(2,1)}, f32[8,8,384]{2,1,0:T(8,128)}, bf16[320,2376]{1,0:T(8,128)(2,1)}, bf16[8,16,384]{2,1,0:T(8,128)(2,1)}) custom-call(s32[8,8]{1,0:T(8,128)} %add_add_fusion.info, f32[8,256,384]{2,1,0:T(8,128)} %get-tuple-element.113.p_ref, f32[8,256,384]{2,1,0:T(8,128)} %get-tuple-element.114.s_ref, ...), custom_call_target="tpu_custom_call" | custom-call | bytes 1048576 | tf_op jit(solution)/shard_map/mixer_back/pallas_call | solution.py:1199
  474.3 7.1 %pass_rows_back.1 = (f32[8,8,384]{2,1,0:T(8,128)}, bf16[4,80,2376]{2,1,0:T(8,128)(2,1)}) custom-call(f32[8,8,384]{2,1,0:T(8,128)} %get-tuple-element.120.edge_ref, bf16[320,2376]{1,0:T(8,128)(2,1)} %get-tuple-element.121.refs_0_), custom_call_target="tpu_custom_call" | custom-call | bytes 1048576 | tf_op jit(solution)/shard_map/pass_rows_back/pallas_call | solution.py:903
  481.5 3.6 fusion.16.refs_0_
  485.2 9.1 %mixer_back_conv.1 = bf16[8,256,640]{2,1,0:T(8,128)(2,1)} custom-call(s32[8,8]{1,0:T(8,128)} %add_add_fusion.info, bf16[8,256,384]{2,1,0:T(8,128)(2,1)} %get-tuple-element.123.dconv_ref, f32[8,8,384]{2,1,0:T(8,128)} %get-tuple-element.124.rim_ref, bf16[8,256,384]{2,1,0:T(8,128)(2,1)} %get-tuple-element.125.dgate_ref, f32[9,384]{1,0:T(8,128)} %select_maximum_fusion.vec_ref, ...), custom_call_target="tpu_custom_call" | custom-call | bytes 1048576 | tf_op jit(solution)/shard_map/mixer_back_conv/pallas_call | solution.py:1199
  494.3 11.2 %bitcast_convert_fusion.1.refs_10_ = bf16[2048,640]{1,0:T(8,128)(2,1)} fusion(bf16[8,256,2048]{2,1,0:T(8,128)(2,1)} %get-tuple-element.128, bf16[8,256,640]{2,1,0:T(8,128)(2,1)} %mixer_back_conv.1), kind=kOutput, calls=%fused_computation.1 | convolution fusion | flops 5370019840 | bytes 13631488 | tf_op jit(solution)/shard_map/dot_general | solution.py:18
  508.2 8.0 %reduce-scatter.16.cloned.1.call-done = bf16[80,2376]{1,0:T(8,128)(2,1)} async-done(((bf16[320,2376]{1,0:T(8,128)(2,1)}), bf16[80,2376]{1,0:T(8,128)(2,1)}) %reduce-scatter.16.cloned.1.call-update) | async-done | bytes 380176
  517.6 65.8 %plane_reduce_last.1 = (bf16[256,2048]{1,0:T(8,128)(2,1)}, f32[64,6144]{1,0:T(8,128)}, f32[64,6144]{1,0:T(8,128)}, f32[16,2560]{1,0:T(8,128)}, f32[64,1]{1,0:T(8,128)}) custom-call(bf16[2,4,256,640]{3,2,1,0:T(8,128)(2,1)} %bitcast.105, bf16[2048,640]{1,0:T(8,128)(2,1)} %bitcast.107, f32[1,2048]{1,0:T(1,128)} %broadcast_in_dim_reshape.8.gain_ref.refs_2_, ...), custom_call_target="tpu_custom_call" | custom-call | bytes 8388608 | tf_op jit(solution)/shard_map/plane_reduce_last/pallas_call | solution.py:462
  590.0 13.4 %finish.1 = (f32[64,2560]{1,0:T(8,128)}, f32[64,2560]{1,0:T(8,128)}, f32[64,1]{1,0:T(8,128)}) custom-call(bf16[512,640]{1,0:T(8,128)(2,1)} %reduce-scatter.14.cloned.1.call-done.sums_ref, bf16[64,2560]{1,0:T(8,128)(2,1)} %wy_ref.3, bf16[64,2560]{1,0:T(8,128)(2,1)} %wx_ref.3, f32[64,1]{1,0:T(8,128)} %copy.91.gain_ref), custom_call_target="tpu_custom_call" | custom-call | tf_op jit(solution)/shard_map/finish/pallas_call | solution.py:705
  604.9 2.3 copy.119
  607.2 2.1 copy.120
  (142 shorter events, 36.9 us)
Async XLA Ops:
  7.2 103.2 %all-gather.4.cloned.1.call-start = ((), (), s32[]{:S(2)}) async-start(), calls=%async_computation.5 | async-start | bytes 1638400 | tf_op jit(solution)/shard_map/all_gather | solution.py:1256
  7.9 252.3 %all-gather.8.cloned.1.call-start = ((), (), s32[]{:S(2)}) async-start(), calls=%async_computation.7 | async-start | bytes 7864320 | tf_op jit(solution)/shard_map/all_gather | solution.py:1256
  11.5 2.9 copy-start.8
  99.4 5.5 copy-start.10
  99.4 8.0 %copy-start.11 = (bf16[2,2,80,320]{3,2,1,0:T(8,128)(2,1)S(1)}, bf16[2,2,80,320]{3,2,1,0:T(8,128)(2,1)}, u32[]{:S(2)}) copy-start(bf16[2,2,80,320]{3,2,1,0:T(8,128)(2,1)} %get-tuple-element.91) | copy-start | bytes 614404
  99.5 195.7 %all-gather.6.cloned.1.call-start = ((), (), s32[]{:S(2)}) async-start(), calls=%async_computation.6 | async-start | bytes 3932160 | tf_op jit(solution)/shard_map/all_gather | solution.py:1256
  100.2 229.3 %reduce-scatter.8.cloned.1.call-start = ((), (), s32[]{:S(2)}) async-start(), calls=%async_computation.8 | async-start | bytes 1966080 | tf_op jit(solution)/shard_map/reduce_scatter | solution.py:1259
  100.3 55.8 %collective-permute-start = (bf16[256,2048]{1,0:T(8,128)(2,1)}, bf16[256,2048]{1,0:T(8,128)(2,1)}, u32[]{:S(2)}, u32[]{:S(2)}) collective-permute-start(bf16[256,2048]{1,0:T(8,128)(2,1)} %bitcast.23.refs_5_.refs_3_), channel_id=1, source_target_pairs={{0,2},{2,0},{4,6},{6,4},{1,3},{3,1},{5,7},{7,5},{8,10},{10,8},{12,... | collective-permute-start | bytes 3145736 | tf_op jit(solution)/shard_map/ppermute | solution.py:39
  101.8 54.3 %collective-permute-start.1 = (bf16[256,2048]{1,0:T(8,128)(2,1)}, bf16[256,2048]{1,0:T(8,128)(2,1)}, u32[]{:S(2)}, u32[]{:S(2)}) collective-permute-start(bf16[256,2048]{1,0:T(8,128)(2,1)} %bitcast.23.refs_5_.refs_3_), channel_id=1, source_target_pairs={{0,4},{2,6},{4,0},{6,2},{1,5},{3,7},{5,1},{7,3},{8,12},{10,14},{12... | collective-permute-start | bytes 3145736 | tf_op jit(solution)/shard_map/ppermute | solution.py:39
  103.3 52.8 %collective-permute-start.2 = (bf16[256,2048]{1,0:T(8,128)(2,1)}, bf16[256,2048]{1,0:T(8,128)(2,1)}, u32[]{:S(2)}, u32[]{:S(2)}) collective-permute-start(bf16[256,2048]{1,0:T(8,128)(2,1)} %bitcast.23.refs_5_.refs_3_), channel_id=1, source_target_pairs={{0,6},{2,4},{4,2},{6,0},{1,7},{3,5},{5,3},{7,1},{8,14},{10,12},{12... | collective-permute-start | bytes 3145736 | tf_op jit(solution)/shard_map/ppermute | solution.py:39
  112.4 58.9 %collective-permute-start.3 = (bf16[2,80,2048]{2,1,0:T(8,128)(2,1)}, bf16[2,80,2048]{2,1,0:T(8,128)(2,1)}, u32[]{:S(2)}, u32[]{:S(2)}) collective-permute-start(bf16[2,80,2048]{2,1,0:T(8,128)(2,1)} %constant_dynamic-slice_fusion), channel_id=1, source_target_pairs={{0,1},{1,0},{2,3},{3,2},{4,5},{5,4},{6,7},{7,6},{8,9},{9,8},{10,11... | collective-permute-start | bytes 1966088 | tf_op jit(solution)/shard_map/ppermute | solution.py:34
  132.4 32.5 %copy-start = (f32[8,256,384]{2,1,0:T(8,128)S(1)}, f32[8,256,384]{2,1,0:T(8,128)}, u32[]{:S(2)}) copy-start(f32[8,256,384]{2,1,0:T(8,128)} %get-tuple-element.98.gate_ref) | copy-start | bytes 9437188
  164.8 6.5 %copy-start.7 = (bf16[320,2048]{1,0:T(8,128)(2,1)S(1)}, bf16[320,2048]{1,0:T(8,128)(2,1)}, u32[]{:S(2)}) copy-start(bf16[320,2048]{1,0:T(8,128)(2,1)} %all-gather.4.cloned.1.call-done) | copy-start | bytes 3932164
  280.1 8.0 %copy-start.2 = (bf16[8,256,768]{2,1,0:T(8,128)(2,1)S(1)}, bf16[8,256,768]{2,1,0:T(8,128)(2,1)}, u32[]{:S(2)}) copy-start(bf16[8,256,768]{2,1,0:T(8,128)(2,1)} %get-tuple-element.109) | copy-start | bytes 9437188
  288.0 137.0 %reduce-scatter.10.cloned.1.call-start = ((), (), s32[]{:S(2)}) async-start(), calls=%async_computation.9 | async-start | bytes 1966080 | tf_op jit(solution)/shard_map/reduce_scatter | solution.py:1259
  295.1 190.1 %reduce-scatter.12.cloned.1.call-start = ((), (), s32[]{:S(2)}) async-start(), calls=%async_computation.10 | async-start | bytes 7864320 | tf_op jit(solution)/shard_map/reduce_scatter | solution.py:1259
  329.5 186.8 %reduce-scatter.16.cloned.1.call-start = ((), (), s32[]{:S(2)}) async-start(), calls=%async_computation.12 | async-start | bytes 1945600
  421.6 59.9 %collective-permute-start.6 = (bf16[256,2048]{1,0:T(8,128)(2,1)}, bf16[256,2048]{1,0:T(8,128)(2,1)S(1)}, u32[]{:S(2)}, u32[]{:S(2)}) collective-permute-start(bf16[256,2048]{1,0:T(8,128)(2,1)} %get-tuple-element.218), channel_id=1, source_target_pairs={{0,6},{2,4},{4,2},{6,0},{1,7},{3,5},{5,3},{7,1},{8,14},{10,12},{12... | collective-permute-start | bytes 3145736 | tf_op jit(solution)/shard_map/ppermute | solution.py:39
  423.3 58.2 %collective-permute-start.5 = (bf16[256,2048]{1,0:T(8,128)(2,1)}, bf16[256,2048]{1,0:T(8,128)(2,1)}, u32[]{:S(2)}, u32[]{:S(2)}) collective-permute-start(bf16[256,2048]{1,0:T(8,128)(2,1)} %get-tuple-element.219), channel_id=1, source_target_pairs={{0,4},{2,6},{4,0},{6,2},{1,5},{3,7},{5,1},{7,3},{8,12},{10,14},{12... | collective-permute-start | bytes 3145736 | tf_op jit(solution)/shard_map/ppermute | solution.py:39
  424.2 57.4 %collective-permute-start.4 = (bf16[256,2048]{1,0:T(8,128)(2,1)}, bf16[256,2048]{1,0:T(8,128)(2,1)}, u32[]{:S(2)}, u32[]{:S(2)}) collective-permute-start(bf16[256,2048]{1,0:T(8,128)(2,1)} %get-tuple-element.217), channel_id=1, source_target_pairs={{0,2},{2,0},{4,6},{6,4},{1,3},{3,1},{5,7},{7,5},{8,10},{10,8},{12,... | collective-permute-start | bytes 3145736 | tf_op jit(solution)/shard_map/ppermute | solution.py:39
  474.3 7.2 %copy-start.1 = (f32[256,2048]{1,0:T(8,128)S(1)}, f32[256,2048]{1,0:T(8,128)}, u32[]{:S(2)}) copy-start(f32[256,2048]{1,0:T(8,128)} %get-tuple-element.103.refs_4_) | copy-start | bytes 6291460
  481.5 108.6 %reduce-scatter.14.cloned.1.call-start = ((), (), s32[]{:S(2)}) async-start(), calls=%async_computation.11 | async-start | bytes 3276800 | tf_op jit(solution)/shard_map/reduce_scatter | solution.py:1259
  494.3 11.2 %copy-start.14 = (bf16[64]{0:T(256)(128)(2,1)S(1)}, bf16[64]{0:T(256)(128)(2,1)}, u32[]{:S(2)}) copy-start(bf16[64]{0:T(256)(128)(2,1)} %param.40) | copy-start | bytes 388
  494.3 11.9 %copy-start.15 = (bf16[64]{0:T(256)(128)(2,1)S(1)}, bf16[64]{0:T(256)(128)(2,1)}, u32[]{:S(2)}) copy-start(bf16[64]{0:T(256)(128)(2,1)} %param.31) | copy-start | bytes 388
  494.3 12.7 %copy-start.3 = (bf16[192,1024]{1,0:T(8,128)(2,1)S(1)}, bf16[192,1024]{1,0:T(8,128)(2,1)}, u32[]{:S(2)}) copy-start(bf16[192,1024]{1,0:T(8,128)(2,1)} %reduce-scatter.8.cloned.1.call-done.refs_7_) | copy-start | bytes 1179652
  494.3 12.7 %copy-start.6 = (bf16[192,1024]{1,0:T(8,128)(2,1)S(1)}, bf16[192,1024]{1,0:T(8,128)(2,1)}, u32[]{:S(2)}) copy-start(bf16[192,1024]{1,0:T(8,128)(2,1)} %reduce-scatter.10.cloned.1.call-done.refs_0_) | copy-start | bytes 1179652
  583.4 0.9 copy-start.12
  583.4 4.8 copy-start.13
  587.7 22.5 %copy-start.5 = (f32[64,6144]{1,0:T(8,128)S(1)}, f32[64,6144]{1,0:T(8,128)}, u32[]{:S(2)}) copy-start(f32[64,6144]{1,0:T(8,128)} %get-tuple-element.270) | copy-start | bytes 4718596
  603.4 5.9 copy-start.9
  607.2 4.1 copy-start.4
Sparse Core Ops, SparseCore 0:
  9.6 42.8 all-gather.3
  99.6 117.0 all-gather.7
  218.3 63.1 all-gather.5
  288.2 36.2 reduce-scatter.7
  326.6 34.2 reduce-scatter.9
  363.1 110.5 reduce-scatter.11
  481.6 34.6 reduce-scatter.15
  518.6 57.3 reduce-scatter.13

commit v6 on v5

--- a/solution.py
+++ b/solution.py
@@ -169,23 +169,25 @@
 
 def gain_sum(pairs, gain):
     total = sum(jnp.sum(w[...].astype(F32) * g[...], axis=-1, keepdims=True) for w, g in pairs)
-    return total / gain[...]
-
-
-def reduce_kernel(nt, post, nx, extra, waits, hid, head_w, *refs):
+    size = total.shape[0]
+    row = lax.broadcasted_iota(jnp.int32, (size, size), 0)
+    column = lax.broadcasted_iota(jnp.int32, (size, size), 1)
+    return jnp.sum(jnp.where(row == column, total, 0.0), axis=0, keepdims=True) / gain[...]
+
+
+def reduce_kernel(nt, post, nx, extra, waits, *refs):
     x_hbm, refs = refs[:nx], refs[nx:]
     w_hbm, gain_ref, first_ref, second_ref = refs[:4]
     extra_in, refs = refs[4 : 4 + extra], refs[4 + extra :]
     if post == "last":
-        lasts_ref, wg_ref, wu_ref, gain_two_ref = refs[:4]
-        refs = refs[4:]
+        lasts_ref, refs = refs[0], refs[1:]
     refs = refs[waits:]
     out_ref, refs = refs[0], refs[1:]
     if post == "last":
         everyone = mine = None
-        extra_out, lasts_out, gain_out = refs[:2], refs[2], refs[3]
-        extra_buf, lasts_buf, lasts_mine, lasts_far, lasts_sent, lasts_sum = refs[4:10]
-        refs = refs[10:]
+        extra_buf, lasts_sum = refs[:2]
+        lasts_buf, lasts_mine, lasts_far, lasts_sent = refs[2:6]
+        refs = refs[6:]
     else:
         everyone, refs = refs[0], refs[1:]
         if extra:
@@ -389,24 +391,12 @@
             move.arrived(f"z{i}")
             total = total + lasts_far[i].astype(F32)
         lasts_sum[...] = total.reshape(lasts_sum.shape)
-        heads = extra_buf.shape[2] // (2 * hid) // 2
-        order = [
-            (i * 4 + q, j * head_w) for i in range(2) for j in range(heads) for q in range(4)
-        ]
-        for at, value in set_side_by_side(lasts_sum, order, head_w):
-            lasts_out[:, at] = value
         for kc, k in peers:
             move.arrived(f"e{kc}{k}")
-        wide = extra_buf.shape[2] // 2
-        for i in range(2):
-            order = [(p, i * wide + z * hid) for z in range(wide // hid) for p in range(8)]
-            for at, value in set_side_by_side(extra_buf, order, hid):
-                extra_out[i][:, at] = value
-        gain_out[...] = gain_sum(((wg_ref, extra_out[0]), (wu_ref, extra_out[1])), gain_two_ref)
     move.sent()
 
 
-def plane_reduce(ident, post, nt, xs, w, gain, first, second, extra=(), done=(), hid=0, lasts=None, weights=(), head_w=0):
+def plane_reduce(ident, post, nt, xs, w, gain, first, second, extra=(), done=(), lasts=None):
     rows, d_model = first.shape
     vmem = pl.BlockSpec(memory_space=pltpu.VMEM)
     hbm = pl.BlockSpec(memory_space=pl.ANY)
@@ -430,19 +420,14 @@
             scratch += [pltpu.VMEM((4, rows, d_model), BF)] * 2
     else:
         each = extra[0].shape[0] // 8, extra[0].shape[1]
-        for _ in range(2):
-            out_shape.append(jax.ShapeDtypeStruct((each[0], 4 * each[1]), F32))
-            out_specs.append(vmem)
         planes = lax.axis_size("a")
-        copies += 7 * len(extra) + 7 + planes - 1
+        copies += 7 + 7 + planes - 1
         block = (2, 4) + lasts.shape[1:]
-        wide = lax.axis_size("a") * 4 * head_w
-        out_shape.append(jax.ShapeDtypeStruct((lasts.shape[1], wide), F32))
-        out_shape.append(jax.ShapeDtypeStruct((each[0], 1), F32))
-        out_specs += [vmem, vmem]
-        scratch.append(pltpu.VMEM((8,) + each, BF))
+        out_shape.append(jax.ShapeDtypeStruct((8,) + each, BF))
+        out_shape.append(jax.ShapeDtypeStruct((8,) + block[2:], F32))
+        out_specs += [hbm, vmem]
         scratch += [pltpu.VMEM(block, BF)] * 2 + [pltpu.VMEM((planes - 1,) + block, BF)]
-        scratch += [pltpu.VMEM((2, 2) + block[2:], BF), pltpu.VMEM((8,) + block[2:], F32)]
+        scratch.append(pltpu.VMEM((2, 2) + block[2:], BF))
     wide = sum(x.shape[3] for x in xs)
     scratch += [
         pltpu.VMEM((2, 4, rows, wide), BF),
@@ -456,15 +441,13 @@
         pltpu.SemaphoreType.DMA((copies,)),
         pltpu.SemaphoreType.DMA((copies,)),
     ]
-    last = []
-    if post == "last":
-        last = [lasts, *weights[:2], weights[2].astype(F32).reshape(-1, 1)]
+    last = [] if lasts is None else [lasts]
     return pl.pallas_call(
-        functools.partial(reduce_kernel, nt, post, len(xs), len(extra), len(done), hid, head_w),
+        functools.partial(reduce_kernel, nt, post, len(xs), len(extra), len(done)),
         in_specs=[hbm] * (len(xs) + 1)
         + [vmem] * 3
         + [vmem if post == "fwd" else hbm] * len(extra)
-        + [vmem] * (4 if post == "last" else 0)
+        + [vmem] * (lasts is not None)
         + [hbm] * len(done),
         out_specs=out_specs,
         out_shape=out_shape,
@@ -669,9 +652,7 @@
     )(tokens, w_y, w_x, w_gate, w_up, gate_rows, vec, stream)
 
 
-def finish_kernel(
-    head_w, sums_ref, wy_ref, wx_ref, gain_ref, y_ref, x_ref, gain_out, buf, local, send, recv
-):
+def finish_kernel(sums_ref, buf, local, send, recv):
     _, b, n, c = places()
     me = (b * 2 + n) * 2 + c
     peers = plane_peers_of()
@@ -689,6 +670,77 @@
     own.wait()
     for kc, k in peers:
         move.arrived(f"e{kc}{k}")
+    move.sent()
+
+
+def finish(sums, done):
+    vmem = pl.BlockSpec(memory_space=pltpu.VMEM)
+
+    def body(sums_ref, *refs):
+        finish_kernel(sums_ref, *refs[len(done) :])
+
+    return pl.pallas_call(
+        body,
+        in_specs=[vmem] + [pl.BlockSpec(memory_space=pl.ANY)] * len(done),
+        out_specs=vmem,
+        out_shape=jax.ShapeDtypeStruct((8, sums.shape[0] // 8, sums.shape[1]), BF),
+        scratch_shapes=[
+            pltpu.SemaphoreType.DMA((1,)),
+            pltpu.SemaphoreType.DMA((7,)),
+            pltpu.SemaphoreType.DMA((7,)),
+        ],
+        compiler_params=pltpu.CompilerParams(
+            collective_id=5, has_side_effects=True, vmem_limit_bytes=VMEM_LIMIT
+        ),
+        cost_estimate=pl.CostEstimate(flops=0, bytes_accessed=1 << 20, transcendentals=0),
+        name="finish",
+    )(sums, *done)
+
+
+def in_place(body, ins, outs, name):
+    vmem = pl.BlockSpec(memory_space=pltpu.VMEM)
+    return pl.pallas_call(
+        body,
+        in_specs=[vmem] * len(ins),
+        out_specs=[vmem] * len(outs),
+        out_shape=[jax.ShapeDtypeStruct(*out) for out in outs],
+        compiler_params=pltpu.CompilerParams(vmem_limit_bytes=VMEM_LIMIT),
+        cost_estimate=pl.CostEstimate(flops=0, bytes_accessed=1 << 20, transcendentals=0),
+        name=name,
+    )(*ins)
+
+
+def order_hidden_kernel(
+    hid, head_w, buf, wg_ref, wu_ref, gain_ref, late_ref, lasts_ref,
+    g_ref, u_ref, gain_out, out_ref, a_ref, i_ref, state_ref, conv_ref, *vec_refs,
+):
+    wide = buf.shape[2] // 2
+    for i, out in enumerate((g_ref, u_ref)):
+        order = [(p, i * wide + z * hid) for z in range(wide // hid) for p in range(8)]
+        for at, value in set_side_by_side(buf, order, hid):
+            out[:, at] = value
+    gain_out[...] = gain_sum(((wg_ref, g_ref), (wu_ref, u_ref)), gain_ref)
+    heads = wide // hid // 2
+    order = [(i * 4 + q, j * head_w) for i in range(2) for j in range(heads) for q in range(4)]
+    for at, value in set_side_by_side(lasts_ref, order, head_w):
+        nseq = state_ref.shape[0]
+        state_ref[:, at] = value[:nseq]
+        conv_ref[:, at] = value[nseq:].astype(BF)
+    wide_out, half = out_ref.shape[1], late_ref.shape[0]
+    out_ref[...] = late_ref[:, :wide_out].astype(F32)
+    a_ref[...] = late_ref[:, wide_out : wide_out + head_w].astype(F32)
+    i_ref[...] = late_ref[:, wide_out + head_w : wide_out + 2 * head_w].astype(F32)
+    row = lax.broadcasted_iota(jnp.int32, (half, half), 0)
+    column = lax.broadcasted_iota(jnp.int32, (half, half), 1)
+    eye = jnp.where(row == column, 1.0, 0.0).astype(BF)
+    turned = tdot(late_ref[:, wide_out + 2 * head_w :], eye)
+    taps = vec_refs[0].shape[0]
+    vec_refs[0][...] = turned[:taps]
+    for i, vec_ref in enumerate(vec_refs[1:]):
+        vec_ref[...] = turned[taps + i : taps + i + 1]
+
+
+def order_heads_kernel(head_w, buf, wy_ref, wx_ref, gain_ref, y_ref, x_ref, gain_out):
     wide = buf.shape[2] // 2
     each = wide // head_w
     order = [(q * 2 + i, j * head_w) for i in range(2) for j in range(each) for q in range(4)]
@@ -696,29 +748,6 @@
         for at, value in set_side_by_side(buf, [(p, o + first) for p, o in order], head_w):
             out[:, at] = value
     gain_out[...] = gain_sum(((wy_ref, y_ref), (wx_ref, x_ref)), gain_ref)
-    move.sent()
-
-
-def finish(sums, w_y, w_x, gain, head_w):
-    each = sums.shape[0] // 8, sums.shape[1]
-    vmem = pl.BlockSpec(memory_space=pltpu.VMEM)
-    return pl.pallas_call(
-        functools.partial(finish_kernel, head_w),
-        in_specs=[pl.BlockSpec(memory_space=pl.ANY), vmem, vmem, vmem],
-        out_specs=[vmem] * 3,
-        out_shape=[jax.ShapeDtypeStruct((each[0], 4 * each[1]), F32)] * 2
-        + [jax.ShapeDtypeStruct((each[0], 1), F32)],
-        scratch_shapes=[
-            pltpu.VMEM((8,) + each, BF),
-            pltpu.SemaphoreType.DMA((1,)),
-            pltpu.SemaphoreType.DMA((7,)),
-            pltpu.SemaphoreType.DMA((7,)),
-        ],
-        compiler_params=pltpu.CompilerParams(
-            collective_id=5, has_side_effects=True, vmem_limit_bytes=VMEM_LIMIT
-        ),
-        name="finish",
-    )(sums, w_y, w_x, gain.astype(F32).reshape(-1, 1))
 
 
 def column_peers(planes):
@@ -1488,19 +1517,34 @@
     )[0]
     late = scatter_a(late.reshape(planes * half, -1))
     sums_yx = tdot(normed, d_both.reshape(nblocks * rows, 2 * wide_here)).astype(BF)
-    input_grad, grad_wg, grad_wu, found, grad_gain_two = plane_reduce(
+    input_grad, pieces, lasts = plane_reduce(
         4, "last", True, (d_both.reshape(2, count, rows, -1),), w_yx, gain_one, tokens[0], d_resid,
-        (sent_gu,), (sums_yx,), hid, lasts, (w_gate, w_up, norm2_gain), head_w,
-    )
-    late, input_grad = lax.optimization_barrier((late, input_grad))
-    late = late.astype(F32)
-    grad_wo, grad_gates, vec_grads = jnp.split(late, [d_model, d_model + 2 * head_w], 1)
-    grad_wa, grad_wi, vec_grads = grad_gates[:, :head_w], grad_gates[:, head_w:], vec_grads.T
-    grad_wy, grad_wx, grad_gain_one = finish(scatter_a(sums_yx), w_y, w_x, norm1_gain, head_w)
-    grad_gain_one, grad_gain_two = grad_gain_one[:, 0], grad_gain_two[:, 0]
-
-    final_state = found[:nseq]
-    final_conv = found[nseq:].astype(BF).reshape(nseq, back, width)
+        (sent_gu,), (sums_yx,), lasts,
+    )
+    gain_shape = ((1, drows), F32)
+    (
+        grad_wg, grad_wu, grad_gain_two, grad_wo, grad_wa, grad_wi, final_state, final_conv,
+        grad_taps, *vec_grads,
+    ) = in_place(
+        functools.partial(order_hidden_kernel, hid, head_w),
+        (pieces, w_gate, w_up, norm2_gain.astype(F32)[None], late, lasts),
+        [
+            (w_gate.shape, F32), (w_up.shape, F32), gain_shape, (w_out.shape, F32),
+            (gate_a.shape, F32), (gate_i.shape, F32), ((nseq, width), F32),
+            ((nseq * back, width), BF), ((taps, half), F32),
+        ]
+        + [((1, half), F32)] * 4,
+        "order_hidden",
+    )
+    pieces = finish(scatter_a(sums_yx), (grad_wg,))
+    grad_wy, grad_wx, grad_gain_one = in_place(
+        functools.partial(order_heads_kernel, head_w),
+        (pieces, w_y, w_x, norm1_gain.astype(F32)[None]),
+        [(w_y.shape, F32), (w_x.shape, F32), gain_shape],
+        "order_heads",
+    )
+    grad_gain_one, grad_gain_two = grad_gain_one[0], grad_gain_two[0]
+    final_conv = final_conv.reshape(nseq, back, width)
 
     return (
         result[None],
@@ -1513,11 +1557,8 @@
         grad_wi,
         grad_wo,
         grad_gain_one,
-        vec_grads[:taps],
-        vec_grads[taps],
-        vec_grads[taps + 1],
-        vec_grads[taps + 2],
-        vec_grads[taps + 3],
+        grad_taps,
+        *[v[0] for v in vec_grads],
         grad_wg,
         grad_wu,
         jnp.concatenate(sent_d, 1).astype(F32),

time: 626 us -> 607 us (0.970)
  local copies, waits for them, and re-layouts: 31.3 us -> 17.9 us
  waiting for transfers between devices: 9.59 us -> 1.57 us
    unnamed x45 -> x30, local copies, waits for them, and re-layouts: 13.2 us -> 3.33 us
    unnamed x9 -> x8, waiting for transfers between devices: 9.5 us -> 1.46 us
    pallas_call x1 -> x3, Pallas kernels: 13.4 us -> 19.7 us  [the longest x1 12.6 us: finish(): pl.pallas_call(body, in_specs=[vmem] + [pl.BlockSpec(memory_space=pl.ANY)...]
  transfers between devices with their start and end apart: 15 -> 15, of which waited for: 1 -> 0; matrix products, arithmetic and copies ran while one was open for 15% -> 14% of each run, Pallas kernels for 76% -> 79%
where the time goes in v6:
time: 607 us; the launch traced here: 601 us
  Pallas kernels  491 us (81%)
  matrix products  45.3 us (7%)
  other arithmetic  21.9 us (4%)
  local copies, waits for them, and re-layouts  17.9 us (3%)
  between operations  14.9 us (2%)
  starting transfers between devices  8.92 us (1%)
    pallas_call x3, Pallas kernels, plane_reduce(): pl.pallas_call(functools.partial(reduce_kernel, nt, post, len(xs), len(ex...  238 us
    pallas_call x7, Pallas kernels, by_block(): pl.pallas_call(body, grid_spec=pltpu.PrefetchScalarGridSpec(num_scalar_pr...  117 us
    pallas_call x1, Pallas kernels, start_exchange(): pl.pallas_call(functools.partial(start_kernel, head_w, hid), in_specs=[vm...  84.9 us
    dot_general x4, matrix products, tdot(): lax.dot_general(left, right, (((0,), (0,)), ((), ())), preferred_element_...  45.3 us
    pallas_call x4, Pallas kernels, pass_along(): pl.pallas_call(functools.partial(body, reverse), in_specs=[vmem] * len(gi...  30.1 us
    pallas_call x1, Pallas kernels, finish(): pl.pallas_call(body, in_specs=[vmem] + [pl.BlockSpec(memory_space=pl.ANY)...  12.6 us
  transfers between devices with their start and end apart: 15, of which 0 were waited for; matrix products, arithmetic and copies ran while one was open for 14% of the time, Pallas kernels for 79%

profile of v6, /device:TPU:0, one launch (start us, length us, event | category | flops | bytes accessed | tf_op | source)
XLA Modules:
  0.0 601.0 jit_solution(13531721941217559215)
XLA Ops:
  11.5 1.4 fusion.39.vec_ref
  13.0 1.5 pad_maximum_fusion.2.rows_ref
  14.5 84.9 %start_exchange.1 = (bf16[8,256,2048]{2,1,0:T(8,128)(2,1)}, bf16[4,8,64,640]{3,2,1,0:T(8,128)(2,1)}, bf16[8,64,1536]{2,1,0:T(8,128)(2,1)}, bf16[4,80,320]{2,1,0:...) custom-call(bf16[256,2048]{1,0:T(8,128)(2,1)} %bitcast.94, ...), custom_call_target="tpu_custom_call" | custom-call | bytes 8388608 | tf_op jit(solution)/shard_map/start_exchange/pallas_call | solution.py:635
  100.3 1.5 collective-permute-start
  101.8 1.5 collective-permute-start.1
  110.4 2.0 constant_dynamic-slice_fusion
  112.4 1.6 collective-permute-start.3
  114.7 17.7 %norm_product.1 = (bf16[8,256,2048]{2,1,0:T(8,128)(2,1)}, f32[8,256,384]{2,1,0:T(8,128)}, bf16[8,256,384]{2,1,0:T(8,128)(2,1)}, f32[8,8,384]{2,1,0:T(8,128)}) custom-call(s32[8,8]{1,0:T(8,128)} %add_add_fusion.info, bf16[8,256,2048]{2,1,0:T(8,128)(2,1)} %get-tuple-element.95.tok_ref, bf16[2048,640]{1,0:T(8,128)(2,1)} %bitcast.100, ...), custom_call_target="tpu_custom_call" | custom-call | bytes 1048576 | tf_op jit(solution)/shard_map/norm_product/pallas_call | solution.py:1228
  132.4 5.7 pass_rows.1.rim_ref
  140.1 15.9 %mixer_forward.1 = (bf16[8,256,384]{2,1,0:T(8,128)(2,1)}, f32[8,256,384]{2,1,0:T(8,128)}, f32[8,256,384]{2,1,0:T(8,128)}, f32[8,256,384]{2,1,0:T(8,128)}, f32[8,...) custom-call(s32[8,8]{1,0:T(8,128)} %add_add_fusion.info, ...), custom_call_target="tpu_custom_call" | custom-call | bytes 1048576 | tf_op jit(solution)/shard_map/mixer_forward/pallas_call | solution.py:1228
  156.1 8.1 %pass_state.1.state_in_ref = f32[8,1,384]{2,1,0:T(1,128)} custom-call(f32[8,8,384]{2,1,0:T(8,128)} %get-tuple-element.104.mul_ref, f32[8,8,384]{2,1,0:T(8,128)} %get-tuple-element.105.add_ref), custom_call_target="tpu_custom_call" | custom-call | bytes 1048576 | tf_op jit(solution)/shard_map/pass_state/pallas_call | solution.py:932
  164.9 6.5 %fusion.12 = (bf16[8,256,384]{2,1,0:T(8,128)(2,1)}, f32[8,256,384]{2,1,0:T(8,128)}) fusion(f32[8,256,384]{2,1,0:T(8,128)S(1)} %copy-done, f32[8,256,384]{2,1,0:T(8,128)} %get-tuple-element.106, f32[8,256,384]{2,1,0:T(8,128)} %get-tuple-element.101, f32[8,384]{1,0:T(8,128)S(1)} %bitcast.131), kind=kLoop, calls=%fused_computation.15 | loop fusion | flops 9437184 | bytes 14168064 | tf_op jit(solution)/shard_map/convert_element_type | solution.py:1427
  174.0 86.3 %plane_reduce_fwd.1 = (f32[256,2048]{1,0:T(8,128)}, bf16[8,256,2048]{2,1,0:T(8,128)(2,1)}, bf16[8,256,2048]{2,1,0:T(8,128)(2,1)}) custom-call(bf16[2,4,256,384]{3,2,1,0:T(8,128)(2,1)} %bitcast.98, bf16[384,2048]{1,0:T(8,128)(2,1)} %pad.56.refs_1_.wo_ref, f32[1,2048]{1,0:T(1,128)} %reshape_reshape.16.refs_2_, bf16[256,2048]{1,0:T(8,128)(2,1)} %bitcast.95, ...), custom_call_target="tpu_custom_call" | custom-call | bytes 8388608 | tf_op jit(solution)/shard_map/plane_reduce_fwd/pallas_call | solution.py:445
  260.3 19.8 %ffn_forward.1 = (bf16[8,256,768]{2,1,0:T(8,128)(2,1)}, bf16[8,256,768]{2,1,0:T(8,128)(2,1)}, bf16[8,256,768]{2,1,0:T(8,128)(2,1)}) custom-call(s32[8,8]{1,0:T(8,128)} %add_add_fusion.info, bf16[8,256,2048]{2,1,0:T(8,128)(2,1)} %get-tuple-element.114.n_ref, bf16[2048,1536]{1,0:T(8,128)(2,1)} %all-gather.8.cloned.1.call-done.w_ref.refs_1_), custom_call_target="tpu_custom_call" | custom-call | bytes 1048576 | tf_op jit(solution)/shard_map/ffn_forward/pallas_call | solution.py:1228
  280.1 7.9 %fusion.17.refs_0_ = bf16[768,1024]{1,0:T(8,128)(2,1)} fusion(bf16[2048,768]{1,0:T(8,128)(2,1)} %bitcast.106, bf16[2048,2048]{1,0:T(8,128)(2,1)} %bitcast.102), kind=kOutput, calls=%fused_computation.22 | convolution fusion | flops 3222011904 | bytes 8912896 | tf_op jit(solution)/shard_map/dot_general | solution.py:18
  288.1 7.0 %fusion.20.refs_1_ = bf16[768,1024]{1,0:T(8,128)(2,1)} fusion(bf16[2048,768]{1,0:T(8,128)(2,1)S(1)} %bitcast.108, bf16[2048,2048]{1,0:T(8,128)(2,1)} %bitcast.103), kind=kOutput, calls=%fused_computation.23 | convolution fusion | flops 3222011904 | bytes 8912896 | tf_op jit(solution)/shard_map/dot_general | solution.py:18
  295.2 15.0 %ffn_back.1 = bf16[8,256,1536]{2,1,0:T(8,128)(2,1)} custom-call(s32[8,8]{1,0:T(8,128)} %add_add_fusion.info, bf16[8,256,2048]{2,1,0:T(8,128)(2,1)} %get-tuple-element.113.g_ref, bf16[768,2048]{1,0:T(8,128)(2,1)} %all-gather.6.cloned.1.call-done.w_ref.refs_6_, bf16[8,256,768]{2,1,0:T(8,128)(2,1)} %get-tuple-element.116.by_gate_ref, ...), custom_call_target="tpu_custom_call" | custom-call | bytes 1048576 | tf_op jit(solution)/shard_map/ffn_back/pallas_call | solution.py:1228
  310.2 19.2 %bitcast_convert_fusion.refs_8_ = bf16[2048,1536]{1,0:T(8,128)(2,1)} fusion(bf16[8,256,2048]{2,1,0:T(8,128)(2,1)} %get-tuple-element.114.n_ref, bf16[8,256,1536]{2,1,0:T(8,128)(2,1)} %ffn_back.1), kind=kOutput, calls=%fused_computation | convolution fusion | flops 12888047616 | bytes 20971520 | tf_op jit(solution)/shard_map/dot_general | solution.py:18
  329.6 88.3 %plane_reduce_mid.1 = (f32[256,2048]{1,0:T(8,128)}, bf16[8,256,2048]{2,1,0:T(8,128)(2,1)}, bf16[4,256,2048]{2,1,0:T(8,128)(2,1)}) custom-call(bf16[2,4,256,1536]{3,2,1,0:T(8,128)(2,1)} %bitcast.93, bf16[2048,1536]{1,0:T(8,128)(2,1)} %all-gather.8.cloned.1.call-done.w_ref.refs_1_, f32[1,2048]{1,0:T(1,128)} %reshape_reshape.16.refs_2_, ...), custom_call_target="tpu_custom_call" | custom-call | bytes 8388608 | tf_op jit(solution)/shard_map/plane_reduce_mid/pallas_call | solution.py:445
  417.9 3.7 slice_bitcast_fusion.2
  421.6 1.7 collective-permute-start.6
  425.1 21.3 %mixer_back_scan.1 = (bf16[8,256,384]{2,1,0:T(8,128)(2,1)}, f32[8,256,384]{2,1,0:T(8,128)}, f32[8,256,384]{2,1,0:T(8,128)}, f32[8,8,384]{2,1,0:T(8,128)}, f32[8,...) custom-call(s32[8,8]{1,0:T(8,128)} %add_add_fusion.info, bf16[8,256,2048]{2,1,0:T(8,128)(2,1)} %get-tuple-element.120.dres_ref, ...), custom_call_target="tpu_custom_call" | custom-call | bytes 1048576 | tf_op jit(solution)/shard_map/mixer_back_scan/pallas_call | solution.py:1228
  446.4 9.2 %pass_state_back.1.grad_in_ref = f32[8,1,384]{2,1,0:T(1,128)} custom-call(f32[8,8,384]{2,1,0:T(8,128)} %get-tuple-element.124.mul_ref, f32[8,8,384]{2,1,0:T(8,128)} %get-tuple-element.125.add_ref), custom_call_target="tpu_custom_call" | custom-call | bytes 1048576 | tf_op jit(solution)/shard_map/pass_state_back/pallas_call | solution.py:932
  455.6 18.7 %mixer_back.1 = (bf16[8,256,384]{2,1,0:T(8,128)(2,1)}, f32[8,8,384]{2,1,0:T(8,128)}, bf16[320,2376]{1,0:T(8,128)(2,1)}, bf16[8,16,384]{2,1,0:T(8,128)(2,1)}) custom-call(s32[8,8]{1,0:T(8,128)} %add_add_fusion.info, f32[8,256,384]{2,1,0:T(8,128)} %get-tuple-element.122.p_ref, f32[8,256,384]{2,1,0:T(8,128)} %get-tuple-element.123.s_ref, ...), custom_call_target="tpu_custom_call" | custom-call | bytes 1048576 | tf_op jit(solution)/shard_map/mixer_back/pallas_call | solution.py:1228
  474.3 7.1 %pass_rows_back.1 = (f32[8,8,384]{2,1,0:T(8,128)}, bf16[4,80,2376]{2,1,0:T(8,128)(2,1)}) custom-call(f32[8,8,384]{2,1,0:T(8,128)} %get-tuple-element.130.edge_ref, bf16[320,2376]{1,0:T(8,128)(2,1)} %get-tuple-element.131.refs_0_), custom_call_target="tpu_custom_call" | custom-call | bytes 1048576 | tf_op jit(solution)/shard_map/pass_rows_back/pallas_call | solution.py:932
  481.6 3.6 fusion.16.refs_0_
  485.2 9.0 %mixer_back_conv.1 = bf16[8,256,640]{2,1,0:T(8,128)(2,1)} custom-call(s32[8,8]{1,0:T(8,128)} %add_add_fusion.info, bf16[8,256,384]{2,1,0:T(8,128)(2,1)} %get-tuple-element.129.dconv_ref, f32[8,8,384]{2,1,0:T(8,128)} %get-tuple-element.132.rim_ref, bf16[8,256,384]{2,1,0:T(8,128)(2,1)} %get-tuple-element.133.dgate_ref, f32[9,384]{1,0:T(8,128)} %select_maximum_fusion.vec_ref, ...), custom_call_target="tpu_custom_call" | custom-call | bytes 1048576 | tf_op jit(solution)/shard_map/mixer_back_conv/pallas_call | solution.py:1228
  494.2 11.2 %bitcast_convert_fusion.1.refs_7_ = bf16[2048,640]{1,0:T(8,128)(2,1)} fusion(bf16[8,256,2048]{2,1,0:T(8,128)(2,1)} %get-tuple-element.136, bf16[8,256,640]{2,1,0:T(8,128)(2,1)} %mixer_back_conv.1), kind=kOutput, calls=%fused_computation.1 | convolution fusion | flops 5370019840 | bytes 13631488 | tf_op jit(solution)/shard_map/dot_general | solution.py:18
  507.8 63.7 %plane_reduce_last.1 = (bf16[256,2048]{1,0:T(8,128)(2,1)}, bf16[8,64,1536]{2,1,0:T(8,128)(2,1)}, f32[8,16,384]{2,1,0:T(8,128)}) custom-call(bf16[2,4,256,640]{3,2,1,0:T(8,128)(2,1)} %bitcast.99, bf16[2048,640]{1,0:T(8,128)(2,1)} %bitcast.101, f32[1,2048]{1,0:T(1,128)} %broadcast_in_dim_reshape.8.gain_ref.refs_2_, bf16[256,2048]{1,0:T(8,128)(2,1)} %bitcast.97, ...), custom_call_target="tpu_custom_call" | custom-call | bytes 8388608 | tf_op jit(solution)/shard_map/plane_reduce_last/pallas_call | solution.py:445
  571.6 4.7 order_hidden.1
  577.9 12.6 %finish.1.buf = bf16[8,64,640]{2,1,0:T(8,128)(2,1)} custom-call(bf16[512,640]{1,0:T(8,128)(2,1)} %reduce-scatter.14.cloned.1.call-done.sums_ref, f32[64,6144]{1,0:T(8,128)} %get-tuple-element.263.refs_0_), custom_call_target="tpu_custom_call" | custom-call | bytes 1048576 | tf_op jit(solution)/shard_map/finish/pallas_call | solution.py:682
  590.5 2.5 order_heads.1
  (116 shorter events, 25.2 us)
Async XLA Ops:
  7.2 103.2 %all-gather.4.cloned.1.call-start = ((), (), s32[]{:S(2)}) async-start(), calls=%async_computation.5 | async-start | bytes 1638400 | tf_op jit(solution)/shard_map/all_gather | solution.py:1285
  7.9 252.3 %all-gather.8.cloned.1.call-start = ((), (), s32[]{:S(2)}) async-start(), calls=%async_computation.7 | async-start | bytes 7864320 | tf_op jit(solution)/shard_map/all_gather | solution.py:1285
  11.5 2.9 copy-start.7
  99.4 5.5 copy-start.8
  99.4 8.0 %copy-start.9 = (bf16[2,2,80,320]{3,2,1,0:T(8,128)(2,1)S(1)}, bf16[2,2,80,320]{3,2,1,0:T(8,128)(2,1)}, u32[]{:S(2)}) copy-start(bf16[2,2,80,320]{3,2,1,0:T(8,128)(2,1)} %get-tuple-element.100) | copy-start | bytes 614404
  99.5 195.7 %all-gather.6.cloned.1.call-start = ((), (), s32[]{:S(2)}) async-start(), calls=%async_computation.6 | async-start | bytes 3932160 | tf_op jit(solution)/shard_map/all_gather | solution.py:1285
  100.2 229.3 %reduce-scatter.6.cloned.1.call-start = ((), (), s32[]{:S(2)}) async-start(), calls=%async_computation.8 | async-start | bytes 1966080 | tf_op jit(solution)/shard_map/reduce_scatter | solution.py:1288
  100.3 55.8 %collective-permute-start = (bf16[256,2048]{1,0:T(8,128)(2,1)}, bf16[256,2048]{1,0:T(8,128)(2,1)}, u32[]{:S(2)}, u32[]{:S(2)}) collective-permute-start(bf16[256,2048]{1,0:T(8,128)(2,1)} %bitcast.23.refs_5_.refs_3_), channel_id=1, source_target_pairs={{0,2},{2,0},{4,6},{6,4},{1,3},{3,1},{5,7},{7,5},{8,10},{10,8},{12,... | collective-permute-start | bytes 3145736 | tf_op jit(solution)/shard_map/ppermute | solution.py:39
  101.8 54.3 %collective-permute-start.1 = (bf16[256,2048]{1,0:T(8,128)(2,1)}, bf16[256,2048]{1,0:T(8,128)(2,1)}, u32[]{:S(2)}, u32[]{:S(2)}) collective-permute-start(bf16[256,2048]{1,0:T(8,128)(2,1)} %bitcast.23.refs_5_.refs_3_), channel_id=1, source_target_pairs={{0,4},{2,6},{4,0},{6,2},{1,5},{3,7},{5,1},{7,3},{8,12},{10,14},{12... | collective-permute-start | bytes 3145736 | tf_op jit(solution)/shard_map/ppermute | solution.py:39
  103.3 52.8 %collective-permute-start.2 = (bf16[256,2048]{1,0:T(8,128)(2,1)}, bf16[256,2048]{1,0:T(8,128)(2,1)}, u32[]{:S(2)}, u32[]{:S(2)}) collective-permute-start(bf16[256,2048]{1,0:T(8,128)(2,1)} %bitcast.23.refs_5_.refs_3_), channel_id=1, source_target_pairs={{0,6},{2,4},{4,2},{6,0},{1,7},{3,5},{5,3},{7,1},{8,14},{10,12},{12... | collective-permute-start | bytes 3145736 | tf_op jit(solution)/shard_map/ppermute | solution.py:39
  112.4 58.9 %collective-permute-start.3 = (bf16[2,80,2048]{2,1,0:T(8,128)(2,1)}, bf16[2,80,2048]{2,1,0:T(8,128)(2,1)}, u32[]{:S(2)}, u32[]{:S(2)}) collective-permute-start(bf16[2,80,2048]{2,1,0:T(8,128)(2,1)} %constant_dynamic-slice_fusion), channel_id=1, source_target_pairs={{0,1},{1,0},{2,3},{3,2},{4,5},{5,4},{6,7},{7,6},{8,9},{9,8},{10,11... | collective-permute-start | bytes 1966088 | tf_op jit(solution)/shard_map/ppermute | solution.py:34
  132.4 32.5 %copy-start = (f32[8,256,384]{2,1,0:T(8,128)S(1)}, f32[8,256,384]{2,1,0:T(8,128)}, u32[]{:S(2)}) copy-start(f32[8,256,384]{2,1,0:T(8,128)} %get-tuple-element.107.gate_ref) | copy-start | bytes 9437188
  164.9 6.5 %copy-start.5 = (bf16[320,2048]{1,0:T(8,128)(2,1)S(1)}, bf16[320,2048]{1,0:T(8,128)(2,1)}, u32[]{:S(2)}) copy-start(bf16[320,2048]{1,0:T(8,128)(2,1)} %all-gather.4.cloned.1.call-done) | copy-start | bytes 3932164
  280.1 8.0 %copy-start.2 = (bf16[8,256,768]{2,1,0:T(8,128)(2,1)S(1)}, bf16[8,256,768]{2,1,0:T(8,128)(2,1)}, u32[]{:S(2)}) copy-start(bf16[8,256,768]{2,1,0:T(8,128)(2,1)} %get-tuple-element.118) | copy-start | bytes 9437188
  288.0 137.0 %reduce-scatter.8.cloned.1.call-start = ((), (), s32[]{:S(2)}) async-start(), calls=%async_computation.9 | async-start | bytes 1966080 | tf_op jit(solution)/shard_map/reduce_scatter | solution.py:1288
  295.1 190.1 %reduce-scatter.10.cloned.1.call-start = ((), (), s32[]{:S(2)}) async-start(), calls=%async_computation.10 | async-start | bytes 7864320 | tf_op jit(solution)/shard_map/reduce_scatter | solution.py:1288
  329.5 242.1 %reduce-scatter.12.cloned.1.call-start = ((), (), s32[]{:S(2)}) async-start(), calls=%async_computation.11 | async-start | bytes 1945600 | tf_op jit(solution)/shard_map/reduce_scatter | solution.py:1288
  421.6 59.9 %collective-permute-start.6 = (bf16[256,2048]{1,0:T(8,128)(2,1)}, bf16[256,2048]{1,0:T(8,128)(2,1)S(1)}, u32[]{:S(2)}, u32[]{:S(2)}) collective-permute-start(bf16[256,2048]{1,0:T(8,128)(2,1)} %get-tuple-element.217), channel_id=1, source_target_pairs={{0,6},{2,4},{4,2},{6,0},{1,7},{3,5},{5,3},{7,1},{8,14},{10,12},{12... | collective-permute-start | bytes 3145736 | tf_op jit(solution)/shard_map/ppermute | solution.py:39
  423.3 58.2 %collective-permute-start.5 = (bf16[256,2048]{1,0:T(8,128)(2,1)}, bf16[256,2048]{1,0:T(8,128)(2,1)}, u32[]{:S(2)}, u32[]{:S(2)}) collective-permute-start(bf16[256,2048]{1,0:T(8,128)(2,1)} %get-tuple-element.218), channel_id=1, source_target_pairs={{0,4},{2,6},{4,0},{6,2},{1,5},{3,7},{5,1},{7,3},{8,12},{10,14},{12... | collective-permute-start | bytes 3145736 | tf_op jit(solution)/shard_map/ppermute | solution.py:39
  424.2 57.4 %collective-permute-start.4 = (bf16[256,2048]{1,0:T(8,128)(2,1)}, bf16[256,2048]{1,0:T(8,128)(2,1)}, u32[]{:S(2)}, u32[]{:S(2)}) collective-permute-start(bf16[256,2048]{1,0:T(8,128)(2,1)} %get-tuple-element.216), channel_id=1, source_target_pairs={{0,2},{2,0},{4,6},{6,4},{1,3},{3,1},{5,7},{7,5},{8,10},{10,8},{12,... | collective-permute-start | bytes 3145736 | tf_op jit(solution)/shard_map/ppermute | solution.py:39
  474.3 7.2 %copy-start.1 = (f32[256,2048]{1,0:T(8,128)S(1)}, f32[256,2048]{1,0:T(8,128)}, u32[]{:S(2)}) copy-start(f32[256,2048]{1,0:T(8,128)} %get-tuple-element.112.refs_4_) | copy-start | bytes 6291460
  481.5 96.4 %reduce-scatter.14.cloned.1.call-start = ((), (), s32[]{:S(2)}) async-start(), calls=%async_computation.12 | async-start | bytes 3276800 | tf_op jit(solution)/shard_map/reduce_scatter | solution.py:1288
  494.2 11.2 %copy-start.10 = (bf16[64]{0:T(256)(128)(2,1)S(1)}, bf16[64]{0:T(256)(128)(2,1)}, u32[]{:S(2)}) copy-start(bf16[64]{0:T(256)(128)(2,1)} %param.40) | copy-start | bytes 388
  494.2 11.7 %copy-start.11 = (bf16[64]{0:T(256)(128)(2,1)S(1)}, bf16[64]{0:T(256)(128)(2,1)}, u32[]{:S(2)}) copy-start(bf16[64]{0:T(256)(128)(2,1)} %param.31) | copy-start | bytes 388
  494.2 12.3 %copy-start.3 = (bf16[192,1024]{1,0:T(8,128)(2,1)S(1)}, bf16[192,1024]{1,0:T(8,128)(2,1)}, u32[]{:S(2)}) copy-start(bf16[192,1024]{1,0:T(8,128)(2,1)} %reduce-scatter.6.cloned.1.call-done.refs_7_) | copy-start | bytes 1179652
  494.2 12.3 %copy-start.4 = (bf16[192,1024]{1,0:T(8,128)(2,1)S(1)}, bf16[192,1024]{1,0:T(8,128)(2,1)}, u32[]{:S(2)}) copy-start(bf16[192,1024]{1,0:T(8,128)(2,1)} %reduce-scatter.8.cloned.1.call-done.refs_0_) | copy-start | bytes 1179652
  576.2 16.8 %copy-start.6 = (bf16[256,2048]{1,0:T(8,128)(2,1)S(1)}, bf16[256,2048]{1,0:T(8,128)(2,1)}, u32[]{:S(2)}) copy-start(bf16[256,2048]{1,0:T(8,128)(2,1)} %get-tuple-element.137) | copy-start | bytes 3145732
Sparse Core Ops, SparseCore 0:
  9.6 42.8 all-gather.3
  99.6 117.0 all-gather.7
  218.3 63.1 all-gather.5
  288.2 36.2 reduce-scatter.5
  326.6 34.2 reduce-scatter.7
  363.1 110.5 reduce-scatter.9
  481.6 34.6 reduce-scatter.11
  518.6 57.3 reduce-scatter.13

commit v7 on v6

--- a/solution.py
+++ b/solution.py
@@ -190,8 +190,10 @@
         refs = refs[6:]
     else:
         everyone, refs = refs[0], refs[1:]
-        if extra:
+        if extra and post == "fwd":
             extra_out, refs = refs[0], refs[1:]
+        elif extra:
+            extra_out, refs = refs[:4], refs[4:]
         mine, refs = refs[0], refs[1:]
         if post == "mid":
             (side_x, side_w, side_s, side_r), refs = refs[:4], refs[4:]
@@ -322,7 +324,7 @@
                 value = mdot(side_x[0, k], side_w[:, at]) + side_r[k, :, at].astype(F32)
                 side_s[k, :, at] = value.astype(BF)
 
-            kept.append(keep(side_s.at[k], extra_out.at[k]))
+            kept.append(keep(side_s.at[k], extra_out[k]))
     if extra and post == "last":
         lasts_buf[0, 0] = lasts_sent[0, 0]
         for kc, k in peers:
@@ -410,9 +412,9 @@
         out_specs.append(hbm)
         copies += GATHER_COPIES
         if extra:
-            blocks = 8 if post == "fwd" else 4
-            out_shape.append(jax.ShapeDtypeStruct((blocks, rows, d_model), BF))
-            out_specs.append(hbm)
+            shapes = [(8, rows, d_model)] if post == "fwd" else [(rows, d_model)] * 4
+            out_shape += [jax.ShapeDtypeStruct(shape, BF) for shape in shapes]
+            out_specs += [hbm] * len(shapes)
             copies += 4
         scratch.append(pltpu.VMEM((rows, d_model), BF))
         if post == "mid":
@@ -943,25 +945,54 @@
     )(*given)
 
 
-def norm_product_kernel(info, tok_ref, w_ref, gain_ref, n_ref, gate_ref, lin_ref, tail_ref):
-    rows, d_model = tok_ref.shape[1:]
-    step = min(64, rows)
-
-    @pl.loop(0, rows // step)
-    def _(i):
-        at = pl.ds(pl.multiple_of(i * step, step), step)
-        value = tok_ref[0, at, :].astype(F32)
-        factor = lax.rsqrt(jnp.mean(value * value, axis=-1, keepdims=True) + EPS)
-        n_ref[0, at, :] = (value * factor * gain_ref[...]).astype(BF)
-
+def norm_product_kernel(tok_ref, w_ref, gain_ref, n_ref, gate_ref, lin_ref, tail_ref, held):
+    i = pl.program_id(0)
+    rows = tok_ref.shape[1]
     wide = gate_ref.shape[2]
-    both = mdot(n_ref[0], w_ref[...])
+    both = mdot(held[(i + 1) % 2], w_ref[...])
     used = both.shape[1] // 2
     pad = [jnp.zeros((rows, wide - used), F32)] if wide > used else []
     gate_ref[0] = jnp.concatenate([both[:, :used]] + pad, 1)
     low = jnp.concatenate([both[:, used:]] + pad, 1).astype(BF)
     lin_ref[0] = low
     tail_ref[0] = low.astype(F32)[rows - 8 :, :]
+    step = min(64, rows)
+    for k in range(rows // step):
+        at = slice(k * step, (k + 1) * step)
+        value = tok_ref[0, at, :].astype(F32)
+        factor = lax.rsqrt(jnp.mean(value * value, axis=-1, keepdims=True) + EPS)
+        low = (value * factor * gain_ref[...]).astype(BF)
+        n_ref[0, at, :] = low
+        held[i % 2, at, :] = low
+
+
+def norm_product(tokens, w, gain, wide):
+    blocks, rows, d_model = tokens.shape
+
+    def now(i):
+        return (jnp.minimum(i, blocks - 1), 0, 0)
+
+    def last(i):
+        return (jnp.maximum(i - 1, 0), 0, 0)
+
+    shapes = [(rows, d_model, BF), (rows, wide, F32), (rows, wide, BF), (8, wide, F32)]
+    return pl.pallas_call(
+        norm_product_kernel,
+        grid=(blocks + 1,),
+        in_specs=[
+            pl.BlockSpec((1, rows, d_model), now),
+            pl.BlockSpec(w.shape, lambda i: (0, 0)),
+            pl.BlockSpec(gain.shape, lambda i: (0, 0)),
+        ],
+        out_specs=[
+            pl.BlockSpec((1,) + shape[:2], last if k else now) for k, shape in enumerate(shapes)
+        ],
+        out_shape=[jax.ShapeDtypeStruct((blocks,) + s[:2], s[2]) for s in shapes],
+        scratch_shapes=[pltpu.VMEM((2, rows, d_model), BF)],
+        compiler_params=pltpu.CompilerParams(vmem_limit_bytes=VMEM_LIMIT),
+        cost_estimate=pl.CostEstimate(flops=0, bytes_accessed=1 << 20, transcendentals=0),
+        name="norm_product",
+    )(tokens, w, gain)
 
 
 def row_places(info, rows, nseq):
@@ -1385,19 +1416,7 @@
     grads = [grad_low] + [xor_u(grad_low, k) for k in range(1, count)]
 
     edge = ((nblocks, 8, wp), F32, True)
-    normed, gate_in, linear, tail = by_block(
-        norm_product_kernel,
-        info,
-        [(all_tokens, True), (w_yx, False), (gain_one[None], False)],
-        [
-            ((nblocks, rows, d_model), BF, True),
-            ((nblocks, rows, wp), F32, True),
-            ((nblocks, rows, wp), BF, True),
-            edge,
-        ],
-        [],
-        name="norm_product",
-    )
+    normed, gate_in, linear, tail = norm_product(all_tokens, w_yx, gain_one[None], wp)
     normed = normed.reshape(nblocks * rows, d_model)
 
     def two(v):
@@ -1442,9 +1461,9 @@
         name="ffn_forward",
     )
     inner = inner.reshape(nblocks * rows, f_here)
-    cut = d_model // 2
-    first_d = tdot(inner, grads[:, :cut]).astype(BF)
-    second_d = tdot(inner, grads[:, cut:]).astype(BF)
+    cut = d_model * 3 // 8
+    sums_d = tdot(inner, grads).astype(BF)
+    first_d, second_d = sums_d[:, :cut], sums_d[:, cut:]
     sent_d = scatter_a(first_d), scatter_a(second_d)
     d_pair = by_block(
         ffn_back_kernel,
@@ -1455,12 +1474,12 @@
         ],
         [((nblocks, rows, 2 * f_here), BF, True)],
         [],
-        (first_d, second_d),
+        (sums_d,),
         name="ffn_back",
     )[0]
     sums_gu = tdot(normed_two, d_pair.reshape(nblocks * rows, -1)).astype(BF)
     sent_gu = scatter_a(sums_gu)
-    d_resid, d_resid_low, low = plane_reduce(
+    d_resid, d_resid_low, *low = plane_reduce(
         3, "mid", True, (d_pair.reshape(2, count, rows, -1),), w_gu,
         gain_two, grad_low, resid, (inner.reshape(2, count, rows, f_here), w_d), (sent_d[0], sums_gu),
     )

time: 607 us -> 608 us (level)
    pallas_call x7 -> x6, Pallas kernels: 117 us -> 100 us  [by_block(): pl.pallas_call(body, grid_spec=pltpu.PrefetchScalarGridSpec(num_scalar_pr...]
    pallas_call x0 -> x1, Pallas kernels: none -> 15.1 us  [norm_product(): pl.pallas_call(norm_product_kernel, grid=(blocks + 1,), in_specs=[pl.Bloc...]
    dot_general x4 -> x3, matrix products: 45.3 us -> 40.5 us  [tdot(): lax.dot_general(left, right, (((0,), (0,)), ((), ())), preferred_element_...]
  transfers between devices with their start and end apart: 15 -> 15, of which waited for: 0 -> 1; matrix products, arithmetic and copies ran while one was open for 14% -> 13% of each run, Pallas kernels for 79% -> 80%
where the time goes in v7:
time: 608 us; the launch traced here: 597 us
  Pallas kernels  491 us (81%)
  matrix products  40.5 us (7%)
  other arithmetic  22 us (4%)
  local copies, waits for them, and re-layouts  16.9 us (3%)
  between operations  14.9 us (2%)
  starting transfers between devices  8.99 us (1%)
    pallas_call x3, Pallas kernels, plane_reduce(): pl.pallas_call(functools.partial(reduce_kernel, nt, post, len(xs), len(ex...  238 us
    pallas_call x6, Pallas kernels, by_block(): pl.pallas_call(body, grid_spec=pltpu.PrefetchScalarGridSpec(num_scalar_pr...  100 us
    pallas_call x1, Pallas kernels, start_exchange(): pl.pallas_call(functools.partial(start_kernel, head_w, hid), in_specs=[vm...  84.9 us
    dot_general x3, matrix products, tdot(): lax.dot_general(left, right, (((0,), (0,)), ((), ())), preferred_element_...  40.5 us
    pallas_call x4, Pallas kernels, pass_along(): pl.pallas_call(functools.partial(body, reverse), in_specs=[vmem] * len(gi...  33.2 us
    pallas_call x1, Pallas kernels, norm_product(): pl.pallas_call(norm_product_kernel, grid=(blocks + 1,), in_specs=[pl.Bloc...  15.1 us
    pallas_call x1, Pallas kernels, finish(): pl.pallas_call(body, in_specs=[vmem] + [pl.BlockSpec(memory_space=pl.ANY)...  12.6 us
  transfers between devices with their start and end apart: 15, of which 1 were waited for; matrix products, arithmetic and copies ran while one was open for 13% of the time, Pallas kernels for 80%

profile of v7, /device:TPU:0, one launch (start us, length us, event | category | flops | bytes accessed | tf_op | source)
XLA Modules:
  0.0 596.9 jit_solution(17246901219275703633)
XLA Ops:
  11.5 1.4 fusion.25.vec_ref
  13.0 1.5 pad_maximum_fusion.2.rows_ref
  14.5 84.9 %start_exchange.1 = (bf16[8,256,2048]{2,1,0:T(8,128)(2,1)}, bf16[4,8,64,640]{3,2,1,0:T(8,128)(2,1)}, bf16[8,64,1536]{2,1,0:T(8,128)(2,1)}, bf16[4,80,320]{2,1,0:...) custom-call(bf16[256,2048]{1,0:T(8,128)(2,1)} %bitcast.85, ...), custom_call_target="tpu_custom_call" | custom-call | bytes 8388608 | tf_op jit(solution)/shard_map/start_exchange/pallas_call | solution.py:637
  99.5 1.5 collective-permute-start
  101.0 1.5 collective-permute-start.1
  109.8 2.0 constant_dynamic-slice_fusion
  111.8 1.6 collective-permute-start.3
  114.0 15.1 %norm_product.1 = (bf16[8,256,2048]{2,1,0:T(8,128)(2,1)}, f32[8,256,384]{2,1,0:T(8,128)}, bf16[8,256,384]{2,1,0:T(8,128)(2,1)}, f32[8,8,384]{2,1,0:T(8,128)}) custom-call(bf16[8,256,2048]{2,1,0:T(8,128)(2,1)} %get-tuple-element.98.tok_ref, bf16[2048,640]{1,0:T(8,128)(2,1)} %bitcast.91, f32[1,2048]{1,0:T(1,128)} %broadcast_in_dim_reshape.8.gain_ref.refs_2_), custom_call_target="tpu_custom_call" | custom-call | bytes 1048576 | tf_op jit(solution)/shard_map/norm_product/pallas_call | solution.py:979
  129.1 5.8 pass_rows.1.rim_ref
  137.0 15.9 %mixer_forward.1 = (bf16[8,256,384]{2,1,0:T(8,128)(2,1)}, f32[8,256,384]{2,1,0:T(8,128)}, f32[8,256,384]{2,1,0:T(8,128)}, f32[8,256,384]{2,1,0:T(8,128)}, f32[8,...) custom-call(s32[8,8]{1,0:T(8,128)} %add_add_fusion.info, ...), custom_call_target="tpu_custom_call" | custom-call | bytes 1048576 | tf_op jit(solution)/shard_map/mixer_forward/pallas_call | solution.py:1259
  152.9 10.8 %pass_state.1.state_in_ref = f32[8,1,384]{2,1,0:T(1,128)} custom-call(f32[8,8,384]{2,1,0:T(8,128)} %get-tuple-element.107.mul_ref, f32[8,8,384]{2,1,0:T(8,128)} %get-tuple-element.108.add_ref), custom_call_target="tpu_custom_call" | custom-call | bytes 1048576 | tf_op jit(solution)/shard_map/pass_state/pallas_call | solution.py:934
  164.5 6.4 %fusion.8 = (bf16[8,256,384]{2,1,0:T(8,128)(2,1)}, f32[8,256,384]{2,1,0:T(8,128)}) fusion(f32[8,256,384]{2,1,0:T(8,128)S(1)} %copy-done, f32[8,256,384]{2,1,0:T(8,128)} %get-tuple-element.109, f32[8,256,384]{2,1,0:T(8,128)} %get-tuple-element.104, f32[8,384]{1,0:T(8,128)S(1)} %bitcast.118), kind=kLoop, calls=%fused_computation.12 | loop fusion | flops 9437184 | bytes 14168064 | tf_op jit(solution)/shard_map/convert_element_type | solution.py:1446
  173.5 85.6 %plane_reduce_fwd.1 = (f32[256,2048]{1,0:T(8,128)}, bf16[8,256,2048]{2,1,0:T(8,128)(2,1)}, bf16[8,256,2048]{2,1,0:T(8,128)(2,1)}) custom-call(bf16[2,4,256,384]{3,2,1,0:T(8,128)(2,1)} %bitcast.89, bf16[384,2048]{1,0:T(8,128)(2,1)} %pad.56.refs_1_.wo_ref, f32[1,2048]{1,0:T(1,128)} %reshape_reshape.16.refs_2_, bf16[256,2048]{1,0:T(8,128)(2,1)} %bitcast.86, ...), custom_call_target="tpu_custom_call" | custom-call | bytes 8388608 | tf_op jit(solution)/shard_map/plane_reduce_fwd/pallas_call | solution.py:447
  259.2 19.8 %ffn_forward.1 = (bf16[8,256,768]{2,1,0:T(8,128)(2,1)}, bf16[8,256,768]{2,1,0:T(8,128)(2,1)}, bf16[8,256,768]{2,1,0:T(8,128)(2,1)}) custom-call(s32[8,8]{1,0:T(8,128)} %add_add_fusion.info, bf16[8,256,2048]{2,1,0:T(8,128)(2,1)} %get-tuple-element.117.n_ref, bf16[2048,1536]{1,0:T(8,128)(2,1)} %all-gather.8.cloned.1.call-done.w_ref.refs_1_), custom_call_target="tpu_custom_call" | custom-call | bytes 1048576 | tf_op jit(solution)/shard_map/ffn_forward/pallas_call | solution.py:1259
  279.0 10.1 %bitcast_convert_fusion.1.refs_0_ = bf16[768,2048]{1,0:T(8,128)(2,1)S(1)} fusion(bf16[8,256,768]{2,1,0:T(8,128)(2,1)} %get-tuple-element.121, bf16[8,256,2048]{2,1,0:T(8,128)(2,1)} %get-tuple-element.116.g_ref), kind=kOutput, calls=%fused_computation.1 | convolution fusion | flops 6444023808 | bytes 14680064 | tf_op jit(solution)/shard_map/dot_general | solution.py:18
  290.5 1.5 slice.87
  292.1 15.2 %ffn_back.1 = bf16[8,256,1536]{2,1,0:T(8,128)(2,1)} custom-call(s32[8,8]{1,0:T(8,128)} %add_add_fusion.info, bf16[8,256,2048]{2,1,0:T(8,128)(2,1)} %get-tuple-element.116.g_ref, bf16[768,2048]{1,0:T(8,128)(2,1)} %all-gather.6.cloned.1.call-done.w_ref.refs_6_, bf16[8,256,768]{2,1,0:T(8,128)(2,1)} %get-tuple-element.119.by_gate_ref, ...), custom_call_target="tpu_custom_call" | custom-call | bytes 1048576 | tf_op jit(solution)/shard_map/ffn_back/pallas_call | solution.py:1259
  307.3 19.2 %bitcast_convert_fusion.refs_8_ = bf16[2048,1536]{1,0:T(8,128)(2,1)} fusion(bf16[8,256,2048]{2,1,0:T(8,128)(2,1)} %get-tuple-element.117.n_ref, bf16[8,256,1536]{2,1,0:T(8,128)(2,1)} %ffn_back.1), kind=kOutput, calls=%fused_computation | convolution fusion | flops 12888047616 | bytes 20971520 | tf_op jit(solution)/shard_map/dot_general | solution.py:18
  326.6 88.2 %plane_reduce_mid.1 = (f32[256,2048]{1,0:T(8,128)}, bf16[8,256,2048]{2,1,0:T(8,128)(2,1)}, bf16[256,2048]{1,0:T(8,128)(2,1)}, bf16[256,2048]{1,0:T(8,128)(2,1)},...) custom-call(bf16[2,4,256,1536]{3,2,1,0:T(8,128)(2,1)} %bitcast.84, ...), custom_call_target="tpu_custom_call" | custom-call | bytes 8388608 | tf_op jit(solution)/shard_map/plane_reduce_mid/pallas_call | solution.py:447
  415.4 1.7 collective-permute-start.5
  418.4 21.3 %mixer_back_scan.1 = (bf16[8,256,384]{2,1,0:T(8,128)(2,1)}, f32[8,256,384]{2,1,0:T(8,128)}, f32[8,256,384]{2,1,0:T(8,128)}, f32[8,8,384]{2,1,0:T(8,128)}, f32[8,...) custom-call(s32[8,8]{1,0:T(8,128)} %add_add_fusion.info, bf16[8,256,2048]{2,1,0:T(8,128)(2,1)} %get-tuple-element.126.dres_ref, ...), custom_call_target="tpu_custom_call" | custom-call | bytes 1048576 | tf_op jit(solution)/shard_map/mixer_back_scan/pallas_call | solution.py:1259
  439.7 8.8 %pass_state_back.1.grad_in_ref = f32[8,1,384]{2,1,0:T(1,128)} custom-call(f32[8,8,384]{2,1,0:T(8,128)} %get-tuple-element.130.mul_ref, f32[8,8,384]{2,1,0:T(8,128)} %get-tuple-element.131.add_ref), custom_call_target="tpu_custom_call" | custom-call | bytes 1048576 | tf_op jit(solution)/shard_map/pass_state_back/pallas_call | solution.py:934
  448.5 18.7 %mixer_back.1 = (bf16[8,256,384]{2,1,0:T(8,128)(2,1)}, f32[8,8,384]{2,1,0:T(8,128)}, bf16[320,2376]{1,0:T(8,128)(2,1)}, bf16[8,16,384]{2,1,0:T(8,128)(2,1)}) custom-call(s32[8,8]{1,0:T(8,128)} %add_add_fusion.info, f32[8,256,384]{2,1,0:T(8,128)} %get-tuple-element.128.p_ref, f32[8,256,384]{2,1,0:T(8,128)} %get-tuple-element.129.s_ref, ...), custom_call_target="tpu_custom_call" | custom-call | bytes 1048576 | tf_op jit(solution)/shard_map/mixer_back/pallas_call | solution.py:1259
  467.2 7.8 %pass_rows_back.1 = (f32[8,8,384]{2,1,0:T(8,128)}, bf16[4,80,2376]{2,1,0:T(8,128)(2,1)}) custom-call(f32[8,8,384]{2,1,0:T(8,128)} %get-tuple-element.136.edge_ref, bf16[320,2376]{1,0:T(8,128)(2,1)} %get-tuple-element.137.refs_0_), custom_call_target="tpu_custom_call" | custom-call | bytes 1048576 | tf_op jit(solution)/shard_map/pass_rows_back/pallas_call | solution.py:934
  475.1 3.8 add_convert_fusion.refs_0_
  478.9 9.3 %mixer_back_conv.1 = bf16[8,256,640]{2,1,0:T(8,128)(2,1)} custom-call(s32[8,8]{1,0:T(8,128)} %add_add_fusion.info, bf16[8,256,384]{2,1,0:T(8,128)(2,1)} %get-tuple-element.135.dconv_ref, f32[8,8,384]{2,1,0:T(8,128)} %get-tuple-element.138.rim_ref, bf16[8,256,384]{2,1,0:T(8,128)(2,1)} %get-tuple-element.139.dgate_ref, f32[9,384]{1,0:T(8,128)} %select_maximum_fusion.vec_ref, ...), custom_call_target="tpu_custom_call" | custom-call | bytes 1048576 | tf_op jit(solution)/shard_map/mixer_back_conv/pallas_call | solution.py:1259
  488.2 11.1 %bitcast_convert_fusion.2.refs_7_ = bf16[2048,640]{1,0:T(8,128)(2,1)} fusion(bf16[8,256,2048]{2,1,0:T(8,128)(2,1)} %get-tuple-element.142, bf16[8,256,640]{2,1,0:T(8,128)(2,1)} %mixer_back_conv.1), kind=kOutput, calls=%fused_computation.2 | convolution fusion | flops 5370019840 | bytes 13631488 | tf_op jit(solution)/shard_map/dot_general | solution.py:18
  501.7 63.9 %plane_reduce_last.1 = (bf16[256,2048]{1,0:T(8,128)(2,1)}, bf16[8,64,1536]{2,1,0:T(8,128)(2,1)}, f32[8,16,384]{2,1,0:T(8,128)}) custom-call(bf16[2,4,256,640]{3,2,1,0:T(8,128)(2,1)} %bitcast.90, bf16[2048,640]{1,0:T(8,128)(2,1)} %bitcast.92, f32[1,2048]{1,0:T(1,128)} %broadcast_in_dim_reshape.8.gain_ref.refs_2_, bf16[256,2048]{1,0:T(8,128)(2,1)} %bitcast.88, ...), custom_call_target="tpu_custom_call" | custom-call | bytes 8388608 | tf_op jit(solution)/shard_map/plane_reduce_last/pallas_call | solution.py:447
  565.6 4.7 order_hidden.1
  572.0 1.9 reduce-scatter.14.cloned.1.call-done.sums_ref
  573.8 12.6 %finish.1.buf = bf16[8,64,640]{2,1,0:T(8,128)(2,1)} custom-call(bf16[512,640]{1,0:T(8,128)(2,1)} %reduce-scatter.14.cloned.1.call-done.sums_ref, f32[64,6144]{1,0:T(8,128)} %get-tuple-element.266.refs_0_), custom_call_target="tpu_custom_call" | custom-call | bytes 1048576 | tf_op jit(solution)/shard_map/finish/pallas_call | solution.py:684
  586.4 2.5 order_heads.1
  (118 shorter events, 26.0 us)
Async XLA Ops:
  7.2 102.6 %all-gather.4.cloned.1.call-start = ((), (), s32[]{:S(2)}) async-start(), calls=%async_computation.5 | async-start | bytes 1638400 | tf_op jit(solution)/shard_map/all_gather | solution.py:1316
  7.9 251.3 %all-gather.8.cloned.1.call-start = ((), (), s32[]{:S(2)}) async-start(), calls=%async_computation.7 | async-start | bytes 7864320 | tf_op jit(solution)/shard_map/all_gather | solution.py:1316
  11.5 2.9 copy-start.8
  99.4 4.9 copy-start.9
  99.4 7.3 %copy-start.10 = (bf16[2,2,80,320]{3,2,1,0:T(8,128)(2,1)S(1)}, bf16[2,2,80,320]{3,2,1,0:T(8,128)(2,1)}, u32[]{:S(2)}) copy-start(bf16[2,2,80,320]{3,2,1,0:T(8,128)(2,1)} %get-tuple-element.103) | copy-start | bytes 614404
  99.5 192.6 %all-gather.6.cloned.1.call-start = ((), (), s32[]{:S(2)}) async-start(), calls=%async_computation.6 | async-start | bytes 3932160 | tf_op jit(solution)/shard_map/all_gather | solution.py:1316
  99.5 53.4 %collective-permute-start = (bf16[256,2048]{1,0:T(8,128)(2,1)}, bf16[256,2048]{1,0:T(8,128)(2,1)}, u32[]{:S(2)}, u32[]{:S(2)}) collective-permute-start(bf16[256,2048]{1,0:T(8,128)(2,1)} %bitcast.23.refs_5_.refs_3_), channel_id=1, source_target_pairs={{0,2},{2,0},{4,6},{6,4},{1,3},{3,1},{5,7},{7,5},{8,10},{10,8},{12,... | collective-permute-start | bytes 3145736 | tf_op jit(solution)/shard_map/ppermute | solution.py:39
  101.0 51.9 %collective-permute-start.1 = (bf16[256,2048]{1,0:T(8,128)(2,1)}, bf16[256,2048]{1,0:T(8,128)(2,1)}, u32[]{:S(2)}, u32[]{:S(2)}) collective-permute-start(bf16[256,2048]{1,0:T(8,128)(2,1)} %bitcast.23.refs_5_.refs_3_), channel_id=1, source_target_pairs={{0,4},{2,6},{4,0},{6,2},{1,5},{3,7},{5,1},{7,3},{8,12},{10,14},{12... | collective-permute-start | bytes 3145736 | tf_op jit(solution)/shard_map/ppermute | solution.py:39
  102.5 50.4 %collective-permute-start.2 = (bf16[256,2048]{1,0:T(8,128)(2,1)}, bf16[256,2048]{1,0:T(8,128)(2,1)}, u32[]{:S(2)}, u32[]{:S(2)}) collective-permute-start(bf16[256,2048]{1,0:T(8,128)(2,1)} %bitcast.23.refs_5_.refs_3_), channel_id=1, source_target_pairs={{0,6},{2,4},{4,2},{6,0},{1,7},{3,5},{5,3},{7,1},{8,14},{10,12},{12... | collective-permute-start | bytes 3145736 | tf_op jit(solution)/shard_map/ppermute | solution.py:39
  103.1 223.5 %reduce-scatter.6.cloned.1.call-start = ((), (), s32[]{:S(2)}) async-start(), calls=%async_computation.8 | async-start | bytes 1474560 | tf_op jit(solution)/shard_map/reduce_scatter | solution.py:1319
  111.8 59.1 %collective-permute-start.3 = (bf16[2,80,2048]{2,1,0:T(8,128)(2,1)}, bf16[2,80,2048]{2,1,0:T(8,128)(2,1)}, u32[]{:S(2)}, u32[]{:S(2)}) collective-permute-start(bf16[2,80,2048]{2,1,0:T(8,128)(2,1)} %constant_dynamic-slice_fusion), channel_id=1, source_target_pairs={{0,1},{1,0},{2,3},{3,2},{4,5},{5,4},{6,7},{7,6},{8,9},{9,8},{10,11... | collective-permute-start | bytes 1966088 | tf_op jit(solution)/shard_map/ppermute | solution.py:34
  129.1 35.4 %copy-start = (f32[8,256,384]{2,1,0:T(8,128)S(1)}, f32[8,256,384]{2,1,0:T(8,128)}, u32[]{:S(2)}) copy-start(f32[8,256,384]{2,1,0:T(8,128)} %get-tuple-element.110.gate_ref) | copy-start | bytes 9437188
  164.5 6.4 %copy-start.4 = (bf16[320,2048]{1,0:T(8,128)(2,1)S(1)}, bf16[320,2048]{1,0:T(8,128)(2,1)}, u32[]{:S(2)}) copy-start(bf16[320,2048]{1,0:T(8,128)(2,1)} %all-gather.4.cloned.1.call-done) | copy-start | bytes 3932164
  289.1 2.8 copy-start.1
  290.5 127.9 %reduce-scatter.8.cloned.1.call-start = ((), (), s32[]{:S(2)}) async-start(), calls=%async_computation.9 | async-start | bytes 2457600 | tf_op jit(solution)/shard_map/reduce_scatter | solution.py:1319
  292.0 186.9 %reduce-scatter.10.cloned.1.call-start = ((), (), s32[]{:S(2)}) async-start(), calls=%async_computation.10 | async-start | bytes 7864320 | tf_op jit(solution)/shard_map/reduce_scatter | solution.py:1319
  326.5 239.1 %reduce-scatter.12.cloned.1.call-start = ((), (), s32[]{:S(2)}) async-start(), calls=%async_computation.11 | async-start | bytes 1945600 | tf_op jit(solution)/shard_map/reduce_scatter | solution.py:1319
  414.8 60.2 %collective-permute-start.6 = (bf16[256,2048]{1,0:T(8,128)(2,1)}, bf16[256,2048]{1,0:T(8,128)(2,1)}, u32[]{:S(2)}, u32[]{:S(2)}) collective-permute-start(bf16[256,2048]{1,0:T(8,128)(2,1)} %get-tuple-element.125), channel_id=1, source_target_pairs={{0,6},{2,4},{4,2},{6,0},{1,7},{3,5},{5,3},{7,1},{8,14},{10,12},{12... | collective-permute-start | bytes 3145736 | tf_op jit(solution)/shard_map/ppermute | solution.py:39
  415.4 59.7 %collective-permute-start.5 = (bf16[256,2048]{1,0:T(8,128)(2,1)}, bf16[256,2048]{1,0:T(8,128)(2,1)}, u32[]{:S(2)}, u32[]{:S(2)}) collective-permute-start(bf16[256,2048]{1,0:T(8,128)(2,1)} %get-tuple-element.124), channel_id=1, source_target_pairs={{0,4},{2,6},{4,0},{6,2},{1,5},{3,7},{5,1},{7,3},{8,12},{10,14},{12... | collective-permute-start | bytes 3145736 | tf_op jit(solution)/shard_map/ppermute | solution.py:39
  417.1 58.1 %collective-permute-start.4 = (bf16[256,2048]{1,0:T(8,128)(2,1)}, bf16[256,2048]{1,0:T(8,128)(2,1)}, u32[]{:S(2)}, u32[]{:S(2)}) collective-permute-start(bf16[256,2048]{1,0:T(8,128)(2,1)} %get-tuple-element.123), channel_id=1, source_target_pairs={{0,2},{2,0},{4,6},{6,4},{1,3},{3,1},{5,7},{7,5},{8,10},{10,8},{12,... | collective-permute-start | bytes 3145736 | tf_op jit(solution)/shard_map/ppermute | solution.py:39
  467.2 7.9 %copy-start.2 = (f32[256,2048]{1,0:T(8,128)S(1)}, f32[256,2048]{1,0:T(8,128)}, u32[]{:S(2)}) copy-start(f32[256,2048]{1,0:T(8,128)} %get-tuple-element.115.refs_4_) | copy-start | bytes 6291460
  467.2 7.9 %copy-start.6 = (bf16[256,2048]{1,0:T(8,128)(2,1)S(1)}, bf16[256,2048]{1,0:T(8,128)(2,1)}, u32[]{:S(2)}) copy-start(bf16[256,2048]{1,0:T(8,128)(2,1)} %get-tuple-element.122) | copy-start | bytes 3145732
  475.0 98.8 %reduce-scatter.14.cloned.1.call-start = ((), (), s32[]{:S(2)}) async-start(), calls=%async_computation.12 | async-start | bytes 3276800 | tf_op jit(solution)/shard_map/reduce_scatter | solution.py:1319
  488.2 11.2 %copy-start.11 = (bf16[64]{0:T(256)(128)(2,1)S(1)}, bf16[64]{0:T(256)(128)(2,1)}, u32[]{:S(2)}) copy-start(bf16[64]{0:T(256)(128)(2,1)} %param.40) | copy-start | bytes 388
  488.2 11.7 %copy-start.12 = (bf16[64]{0:T(256)(128)(2,1)S(1)}, bf16[64]{0:T(256)(128)(2,1)}, u32[]{:S(2)}) copy-start(bf16[64]{0:T(256)(128)(2,1)} %param.31) | copy-start | bytes 388
  488.2 12.2 %copy-start.3 = (bf16[192,1280]{1,0:T(8,128)(2,1)S(1)}, bf16[192,1280]{1,0:T(8,128)(2,1)}, u32[]{:S(2)}) copy-start(bf16[192,1280]{1,0:T(8,128)(2,1)} %reduce-scatter.8.cloned.1.call-done.refs_0_) | copy-start | bytes 1474564
  488.2 12.2 %copy-start.5 = (bf16[192,768]{1,0:T(8,128)(2,1)S(1)}, bf16[192,768]{1,0:T(8,128)(2,1)}, u32[]{:S(2)}) copy-start(bf16[192,768]{1,0:T(8,128)(2,1)} %reduce-scatter.6.cloned.1.call-done.refs_7_) | copy-start | bytes 884740
  570.3 18.7 %copy-start.7 = (bf16[256,2048]{1,0:T(8,128)(2,1)S(1)}, bf16[256,2048]{1,0:T(8,128)(2,1)}, u32[]{:S(2)}) copy-start(bf16[256,2048]{1,0:T(8,128)(2,1)} %get-tuple-element.143) | copy-start | bytes 3145732
Sparse Core Ops, SparseCore 0:
  9.6 42.8 all-gather.3
  99.6 117.0 all-gather.7
  218.3 63.0 all-gather.5
  290.6 29.6 reduce-scatter.5
  322.4 40.1 reduce-scatter.7
  364.8 111.2 reduce-scatter.9
  478.4 35.7 reduce-scatter.11
  516.5 57.3 reduce-scatter.13

commit v8 on v7

--- a/solution.py
+++ b/solution.py
@@ -70,6 +70,10 @@
     for peer in peers:
         pl.semaphore_signal(barrier, inc=1, device_id=peer, device_id_type=MESH)
     pl.semaphore_wait(barrier, len(peers))
+
+
+PARTS = 2
+IN_PARTS = frozenset("d0 d1 x0 x1 y0 y1 gx0 gx1 gy0 gy1 fx fy".split(" "))
 
 
 class Mover:
@@ -93,10 +97,17 @@
         return made
 
     def start(self, name, src, dst, peer):
-        self.copy(name, src, dst, peer).start()
+        if name not in IN_PARTS:
+            self.copy(name, src, dst, peer).start()
+            return
+        rows = src.shape[0] // PARTS
+        for i in range(PARTS):
+            at = pl.ds(i * rows, rows)
+            self.copy(f"{name}.{i}", src.at[at], dst.at[at], peer).start()
 
     def arrived(self, name):
-        self.made[name].wait_recv()
+        for part in [f"{name}.{i}" for i in range(PARTS)] if name in IN_PARTS else [name]:
+            self.made[part].wait_recv()
 
     def sent(self):
         for made in self.made.values():
@@ -139,7 +150,7 @@
             move.arrived(name)
 
 
-GATHER_COPIES = 14
+GATHER_COPIES = 14 + 6 * (PARTS - 1)
 
 
 def plane_peers_of():
@@ -406,7 +417,7 @@
     out_shape = [jax.ShapeDtypeStruct((rows, d_model), out_type)]
     out_specs = [vmem]
     scratch = []
-    copies = 10
+    copies = 10 + 6 * (PARTS - 1)
     if post != "last":
         out_shape.append(jax.ShapeDtypeStruct((8, rows, d_model), BF))
         out_specs.append(hbm)
@@ -1461,9 +1472,9 @@
         name="ffn_forward",
     )
     inner = inner.reshape(nblocks * rows, f_here)
-    cut = d_model * 3 // 8
-    sums_d = tdot(inner, grads).astype(BF)
-    first_d, second_d = sums_d[:, :cut], sums_d[:, cut:]
+    cut = d_model // 2
+    first_d = tdot(inner, grads[:, :cut]).astype(BF)
+    second_d = tdot(inner, grads[:, cut:]).astype(BF)
     sent_d = scatter_a(first_d), scatter_a(second_d)
     d_pair = by_block(
         ffn_back_kernel,
@@ -1474,7 +1485,7 @@
         ],
         [((nblocks, rows, 2 * f_here), BF, True)],
         [],
-        (sums_d,),
+        (first_d, second_d),
         name="ffn_back",
     )[0]
     sums_gu = tdot(normed_two, d_pair.reshape(nblocks * rows, -1)).astype(BF)

time: 608 us -> 607 us (level)
    dot_general x3 -> x4, matrix products: 40.5 us -> 45.3 us  [tdot(): lax.dot_general(left, right, (((0,), (0,)), ((), ())), preferred_element_...]
  transfers between devices with their start and end apart: 15 -> 15, of which waited for: 1 -> 0; matrix products, arithmetic and copies ran while one was open for 13% -> 13% of each run, Pallas kernels for 80% -> 80%
where the time goes in v8:
time: 607 us; the launch traced here: 601 us
  Pallas kernels  494 us (81%)
  matrix products  45.3 us (7%)
  other arithmetic  21.9 us (4%)
  between operations  14.9 us (2%)
  local copies, waits for them, and re-layouts  14.2 us (2%)
  starting transfers between devices  8.99 us (1%)
    pallas_call x3, Pallas kernels, plane_reduce(): pl.pallas_call(functools.partial(reduce_kernel, nt, post, len(xs), len(ex...  239 us
    pallas_call x6, Pallas kernels, by_block(): pl.pallas_call(body, grid_spec=pltpu.PrefetchScalarGridSpec(num_scalar_pr...  99.7 us
    pallas_call x1, Pallas kernels, start_exchange(): pl.pallas_call(functools.partial(start_kernel, head_w, hid), in_specs=[vm...  85.1 us
    dot_general x4, matrix products, tdot(): lax.dot_general(left, right, (((0,), (0,)), ((), ())), preferred_element_...  45.3 us
    pallas_call x4, Pallas kernels, pass_along(): pl.pallas_call(functools.partial(body, reverse), in_specs=[vmem] * len(gi...  35.2 us
    pallas_call x1, Pallas kernels, norm_product(): pl.pallas_call(norm_product_kernel, grid=(blocks + 1,), in_specs=[pl.Bloc...  15.1 us
    pallas_call x1, Pallas kernels, finish(): pl.pallas_call(body, in_specs=[vmem] + [pl.BlockSpec(memory_space=pl.ANY)...  12.6 us
  transfers between devices with their start and end apart: 15, of which 0 were waited for; matrix products, arithmetic and copies ran while one was open for 13% of the time, Pallas kernels for 80%

profile of v8, /device:TPU:0, one launch (start us, length us, event | category | flops | bytes accessed | tf_op | source)
XLA Modules:
  0.0 601.0 jit_solution(2881124588947475611)
XLA Ops:
  11.5 1.4 fusion.35.vec_ref
  13.0 1.5 pad_maximum_fusion.2.rows_ref
  14.5 85.1 %start_exchange.1 = (bf16[8,256,2048]{2,1,0:T(8,128)(2,1)}, bf16[4,8,64,640]{3,2,1,0:T(8,128)(2,1)}, bf16[8,64,1536]{2,1,0:T(8,128)(2,1)}, bf16[4,80,320]{2,1,0:...) custom-call(bf16[256,2048]{1,0:T(8,128)(2,1)} %bitcast.85, ...), custom_call_target="tpu_custom_call" | custom-call | bytes 8388608 | tf_op jit(solution)/shard_map/start_exchange/pallas_call | solution.py:648
  100.4 1.5 collective-permute-start
  101.9 1.5 collective-permute-start.1
  110.5 2.0 constant_dynamic-slice_fusion
  112.6 1.6 collective-permute-start.3
  114.8 15.1 %norm_product.1 = (bf16[8,256,2048]{2,1,0:T(8,128)(2,1)}, f32[8,256,384]{2,1,0:T(8,128)}, bf16[8,256,384]{2,1,0:T(8,128)(2,1)}, f32[8,8,384]{2,1,0:T(8,128)}) custom-call(bf16[8,256,2048]{2,1,0:T(8,128)(2,1)} %get-tuple-element.98.tok_ref, bf16[2048,640]{1,0:T(8,128)(2,1)} %bitcast.91, f32[1,2048]{1,0:T(1,128)} %broadcast_in_dim_reshape.8.gain_ref.refs_2_), custom_call_target="tpu_custom_call" | custom-call | bytes 1048576 | tf_op jit(solution)/shard_map/norm_product/pallas_call | solution.py:990
  129.9 5.7 pass_rows.1.rim_ref
  137.6 15.9 %mixer_forward.1 = (bf16[8,256,384]{2,1,0:T(8,128)(2,1)}, f32[8,256,384]{2,1,0:T(8,128)}, f32[8,256,384]{2,1,0:T(8,128)}, f32[8,256,384]{2,1,0:T(8,128)}, f32[8,...) custom-call(s32[8,8]{1,0:T(8,128)} %add_add_fusion.info, ...), custom_call_target="tpu_custom_call" | custom-call | bytes 1048576 | tf_op jit(solution)/shard_map/mixer_forward/pallas_call | solution.py:1270
  153.6 10.6 %pass_state.1.state_in_ref = f32[8,1,384]{2,1,0:T(1,128)} custom-call(f32[8,8,384]{2,1,0:T(8,128)} %get-tuple-element.107.mul_ref, f32[8,8,384]{2,1,0:T(8,128)} %get-tuple-element.108.add_ref), custom_call_target="tpu_custom_call" | custom-call | bytes 1048576 | tf_op jit(solution)/shard_map/pass_state/pallas_call | solution.py:945
  164.9 6.4 %fusion.12 = (bf16[8,256,384]{2,1,0:T(8,128)(2,1)}, f32[8,256,384]{2,1,0:T(8,128)}) fusion(f32[8,256,384]{2,1,0:T(8,128)S(1)} %copy-done, f32[8,256,384]{2,1,0:T(8,128)} %get-tuple-element.109, f32[8,256,384]{2,1,0:T(8,128)} %get-tuple-element.104, f32[8,384]{1,0:T(8,128)S(1)} %bitcast.122), kind=kLoop, calls=%fused_computation.15 | loop fusion | flops 9437184 | bytes 14168064 | tf_op jit(solution)/shard_map/convert_element_type | solution.py:1457
  172.7 1.4 pad.56.refs_1_.wo_ref
  174.0 86.4 %plane_reduce_fwd.1 = (f32[256,2048]{1,0:T(8,128)}, bf16[8,256,2048]{2,1,0:T(8,128)(2,1)}, bf16[8,256,2048]{2,1,0:T(8,128)(2,1)}) custom-call(bf16[2,4,256,384]{3,2,1,0:T(8,128)(2,1)} %bitcast.89, bf16[384,2048]{1,0:T(8,128)(2,1)} %pad.56.refs_1_.wo_ref, f32[1,2048]{1,0:T(1,128)} %reshape_reshape.16.refs_2_, bf16[256,2048]{1,0:T(8,128)(2,1)} %bitcast.86, ...), custom_call_target="tpu_custom_call" | custom-call | bytes 8388608 | tf_op jit(solution)/shard_map/plane_reduce_fwd/pallas_call | solution.py:458
  260.4 19.8 %ffn_forward.1 = (bf16[8,256,768]{2,1,0:T(8,128)(2,1)}, bf16[8,256,768]{2,1,0:T(8,128)(2,1)}, bf16[8,256,768]{2,1,0:T(8,128)(2,1)}) custom-call(s32[8,8]{1,0:T(8,128)} %add_add_fusion.info, bf16[8,256,2048]{2,1,0:T(8,128)(2,1)} %get-tuple-element.117.n_ref, bf16[2048,1536]{1,0:T(8,128)(2,1)} %all-gather.8.cloned.1.call-done.w_ref.refs_1_), custom_call_target="tpu_custom_call" | custom-call | bytes 1048576 | tf_op jit(solution)/shard_map/ffn_forward/pallas_call | solution.py:1270
  280.2 7.9 %fusion.13.refs_0_ = bf16[768,1024]{1,0:T(8,128)(2,1)} fusion(bf16[2048,768]{1,0:T(8,128)(2,1)} %bitcast.97, bf16[2048,2048]{1,0:T(8,128)(2,1)} %bitcast.93), kind=kOutput, calls=%fused_computation.18 | convolution fusion | flops 3222011904 | bytes 8912896 | tf_op jit(solution)/shard_map/dot_general | solution.py:18
  288.2 7.0 %fusion.16.refs_1_ = bf16[768,1024]{1,0:T(8,128)(2,1)} fusion(bf16[2048,768]{1,0:T(8,128)(2,1)S(1)} %bitcast.99, bf16[2048,2048]{1,0:T(8,128)(2,1)} %bitcast.94), kind=kOutput, calls=%fused_computation.19 | convolution fusion | flops 3222011904 | bytes 8912896 | tf_op jit(solution)/shard_map/dot_general | solution.py:18
  295.3 15.0 %ffn_back.1 = bf16[8,256,1536]{2,1,0:T(8,128)(2,1)} custom-call(s32[8,8]{1,0:T(8,128)} %add_add_fusion.info, bf16[8,256,2048]{2,1,0:T(8,128)(2,1)} %get-tuple-element.116.g_ref, bf16[768,2048]{1,0:T(8,128)(2,1)} %all-gather.6.cloned.1.call-done.w_ref.refs_6_, bf16[8,256,768]{2,1,0:T(8,128)(2,1)} %get-tuple-element.119.by_gate_ref, ...), custom_call_target="tpu_custom_call" | custom-call | bytes 1048576 | tf_op jit(solution)/shard_map/ffn_back/pallas_call | solution.py:1270
  310.4 19.2 %bitcast_convert_fusion.refs_8_ = bf16[2048,1536]{1,0:T(8,128)(2,1)} fusion(bf16[8,256,2048]{2,1,0:T(8,128)(2,1)} %get-tuple-element.117.n_ref, bf16[8,256,1536]{2,1,0:T(8,128)(2,1)} %ffn_back.1), kind=kOutput, calls=%fused_computation | convolution fusion | flops 12888047616 | bytes 20971520 | tf_op jit(solution)/shard_map/dot_general | solution.py:18
  329.7 88.6 %plane_reduce_mid.1 = (f32[256,2048]{1,0:T(8,128)}, bf16[8,256,2048]{2,1,0:T(8,128)(2,1)}, bf16[256,2048]{1,0:T(8,128)(2,1)}, bf16[256,2048]{1,0:T(8,128)(2,1)},...) custom-call(bf16[2,4,256,1536]{3,2,1,0:T(8,128)(2,1)} %bitcast.84, ...), custom_call_target="tpu_custom_call" | custom-call | bytes 8388608 | tf_op jit(solution)/shard_map/plane_reduce_mid/pallas_call | solution.py:458
  418.3 1.8 collective-permute-start.6
  421.8 21.3 %mixer_back_scan.1 = (bf16[8,256,384]{2,1,0:T(8,128)(2,1)}, f32[8,256,384]{2,1,0:T(8,128)}, f32[8,256,384]{2,1,0:T(8,128)}, f32[8,8,384]{2,1,0:T(8,128)}, f32[8,...) custom-call(s32[8,8]{1,0:T(8,128)} %add_add_fusion.info, bf16[8,256,2048]{2,1,0:T(8,128)(2,1)} %get-tuple-element.126.dres_ref, ...), custom_call_target="tpu_custom_call" | custom-call | bytes 1048576 | tf_op jit(solution)/shard_map/mixer_back_scan/pallas_call | solution.py:1270
  443.2 11.8 %pass_state_back.1.grad_in_ref = f32[8,1,384]{2,1,0:T(1,128)} custom-call(f32[8,8,384]{2,1,0:T(8,128)} %get-tuple-element.130.mul_ref, f32[8,8,384]{2,1,0:T(8,128)} %get-tuple-element.131.add_ref), custom_call_target="tpu_custom_call" | custom-call | bytes 1048576 | tf_op jit(solution)/shard_map/pass_state_back/pallas_call | solution.py:945
  455.0 18.7 %mixer_back.1 = (bf16[8,256,384]{2,1,0:T(8,128)(2,1)}, f32[8,8,384]{2,1,0:T(8,128)}, bf16[320,2376]{1,0:T(8,128)(2,1)}, bf16[8,16,384]{2,1,0:T(8,128)(2,1)}) custom-call(s32[8,8]{1,0:T(8,128)} %add_add_fusion.info, f32[8,256,384]{2,1,0:T(8,128)} %get-tuple-element.128.p_ref, f32[8,256,384]{2,1,0:T(8,128)} %get-tuple-element.129.s_ref, ...), custom_call_target="tpu_custom_call" | custom-call | bytes 1048576 | tf_op jit(solution)/shard_map/mixer_back/pallas_call | solution.py:1270
  473.7 7.1 %pass_rows_back.1 = (f32[8,8,384]{2,1,0:T(8,128)}, bf16[4,80,2376]{2,1,0:T(8,128)(2,1)}) custom-call(f32[8,8,384]{2,1,0:T(8,128)} %get-tuple-element.136.edge_ref, bf16[320,2376]{1,0:T(8,128)(2,1)} %get-tuple-element.137.refs_0_), custom_call_target="tpu_custom_call" | custom-call | bytes 1048576 | tf_op jit(solution)/shard_map/pass_rows_back/pallas_call | solution.py:945
  481.0 3.6 add_convert_fusion.refs_0_
  484.6 9.0 %mixer_back_conv.1 = bf16[8,256,640]{2,1,0:T(8,128)(2,1)} custom-call(s32[8,8]{1,0:T(8,128)} %add_add_fusion.info, bf16[8,256,384]{2,1,0:T(8,128)(2,1)} %get-tuple-element.135.dconv_ref, f32[8,8,384]{2,1,0:T(8,128)} %get-tuple-element.138.rim_ref, bf16[8,256,384]{2,1,0:T(8,128)(2,1)} %get-tuple-element.139.dgate_ref, f32[9,384]{1,0:T(8,128)} %select_maximum_fusion.vec_ref, ...), custom_call_target="tpu_custom_call" | custom-call | bytes 1048576 | tf_op jit(solution)/shard_map/mixer_back_conv/pallas_call | solution.py:1270
  493.6 11.2 %bitcast_convert_fusion.1.refs_7_ = bf16[2048,640]{1,0:T(8,128)(2,1)} fusion(bf16[8,256,2048]{2,1,0:T(8,128)(2,1)} %get-tuple-element.142, bf16[8,256,640]{2,1,0:T(8,128)(2,1)} %mixer_back_conv.1), kind=kOutput, calls=%fused_computation.1 | convolution fusion | flops 5370019840 | bytes 13631488 | tf_op jit(solution)/shard_map/dot_general | solution.py:18
  507.2 64.3 %plane_reduce_last.1 = (bf16[256,2048]{1,0:T(8,128)(2,1)}, bf16[8,64,1536]{2,1,0:T(8,128)(2,1)}, f32[8,16,384]{2,1,0:T(8,128)}) custom-call(bf16[2,4,256,640]{3,2,1,0:T(8,128)(2,1)} %bitcast.90, bf16[2048,640]{1,0:T(8,128)(2,1)} %bitcast.92, f32[1,2048]{1,0:T(1,128)} %broadcast_in_dim_reshape.8.gain_ref.refs_2_, bf16[256,2048]{1,0:T(8,128)(2,1)} %bitcast.88, ...), custom_call_target="tpu_custom_call" | custom-call | bytes 8388608 | tf_op jit(solution)/shard_map/plane_reduce_last/pallas_call | solution.py:458
  571.5 4.6 order_hidden.1
  577.9 12.6 %finish.1.buf = bf16[8,64,640]{2,1,0:T(8,128)(2,1)} custom-call(bf16[512,640]{1,0:T(8,128)(2,1)} %reduce-scatter.14.cloned.1.call-done.sums_ref, f32[64,6144]{1,0:T(8,128)} %get-tuple-element.266.refs_0_), custom_call_target="tpu_custom_call" | custom-call | bytes 1048576 | tf_op jit(solution)/shard_map/finish/pallas_call | solution.py:695
  590.4 2.5 order_heads.1
  (117 shorter events, 23.9 us)
Async XLA Ops:
  7.2 103.3 %all-gather.4.cloned.1.call-start = ((), (), s32[]{:S(2)}) async-start(), calls=%async_computation.5 | async-start | bytes 1638400 | tf_op jit(solution)/shard_map/all_gather | solution.py:1327
  7.9 252.5 %all-gather.8.cloned.1.call-start = ((), (), s32[]{:S(2)}) async-start(), calls=%async_computation.7 | async-start | bytes 7864320 | tf_op jit(solution)/shard_map/all_gather | solution.py:1327
  11.5 2.9 copy-start.8
  99.5 5.5 copy-start.9
  99.6 8.0 %copy-start.10 = (bf16[2,2,80,320]{3,2,1,0:T(8,128)(2,1)S(1)}, bf16[2,2,80,320]{3,2,1,0:T(8,128)(2,1)}, u32[]{:S(2)}) copy-start(bf16[2,2,80,320]{3,2,1,0:T(8,128)(2,1)} %get-tuple-element.103) | copy-start | bytes 614404
  99.6 195.7 %all-gather.6.cloned.1.call-start = ((), (), s32[]{:S(2)}) async-start(), calls=%async_computation.6 | async-start | bytes 3932160 | tf_op jit(solution)/shard_map/all_gather | solution.py:1327
  100.3 229.3 %reduce-scatter.6.cloned.1.call-start = ((), (), s32[]{:S(2)}) async-start(), calls=%async_computation.8 | async-start | bytes 1966080 | tf_op jit(solution)/shard_map/reduce_scatter | solution.py:1330
  100.4 53.2 %collective-permute-start = (bf16[256,2048]{1,0:T(8,128)(2,1)}, bf16[256,2048]{1,0:T(8,128)(2,1)}, u32[]{:S(2)}, u32[]{:S(2)}) collective-permute-start(bf16[256,2048]{1,0:T(8,128)(2,1)} %bitcast.23.refs_5_.refs_3_), channel_id=1, source_target_pairs={{0,2},{2,0},{4,6},{6,4},{1,3},{3,1},{5,7},{7,5},{8,10},{10,8},{12,... | collective-permute-start | bytes 3145736 | tf_op jit(solution)/shard_map/ppermute | solution.py:39
  101.9 51.7 %collective-permute-start.1 = (bf16[256,2048]{1,0:T(8,128)(2,1)}, bf16[256,2048]{1,0:T(8,128)(2,1)}, u32[]{:S(2)}, u32[]{:S(2)}) collective-permute-start(bf16[256,2048]{1,0:T(8,128)(2,1)} %bitcast.23.refs_5_.refs_3_), channel_id=1, source_target_pairs={{0,4},{2,6},{4,0},{6,2},{1,5},{3,7},{5,1},{7,3},{8,12},{10,14},{12... | collective-permute-start | bytes 3145736 | tf_op jit(solution)/shard_map/ppermute | solution.py:39
  103.4 50.2 %collective-permute-start.2 = (bf16[256,2048]{1,0:T(8,128)(2,1)}, bf16[256,2048]{1,0:T(8,128)(2,1)}, u32[]{:S(2)}, u32[]{:S(2)}) collective-permute-start(bf16[256,2048]{1,0:T(8,128)(2,1)} %bitcast.23.refs_5_.refs_3_), channel_id=1, source_target_pairs={{0,6},{2,4},{4,2},{6,0},{1,7},{3,5},{5,3},{7,1},{8,14},{10,12},{12... | collective-permute-start | bytes 3145736 | tf_op jit(solution)/shard_map/ppermute | solution.py:39
  112.6 58.8 %collective-permute-start.3 = (bf16[2,80,2048]{2,1,0:T(8,128)(2,1)}, bf16[2,80,2048]{2,1,0:T(8,128)(2,1)}, u32[]{:S(2)}, u32[]{:S(2)}) collective-permute-start(bf16[2,80,2048]{2,1,0:T(8,128)(2,1)} %constant_dynamic-slice_fusion), channel_id=1, source_target_pairs={{0,1},{1,0},{2,3},{3,2},{4,5},{5,4},{6,7},{7,6},{8,9},{9,8},{10,11... | collective-permute-start | bytes 1966088 | tf_op jit(solution)/shard_map/ppermute | solution.py:34
  129.9 35.0 %copy-start = (f32[8,256,384]{2,1,0:T(8,128)S(1)}, f32[8,256,384]{2,1,0:T(8,128)}, u32[]{:S(2)}) copy-start(f32[8,256,384]{2,1,0:T(8,128)} %get-tuple-element.110.gate_ref) | copy-start | bytes 9437188
  164.9 6.5 %copy-start.5 = (bf16[320,2048]{1,0:T(8,128)(2,1)S(1)}, bf16[320,2048]{1,0:T(8,128)(2,1)}, u32[]{:S(2)}) copy-start(bf16[320,2048]{1,0:T(8,128)(2,1)} %all-gather.4.cloned.1.call-done) | copy-start | bytes 3932164
  280.2 8.0 %copy-start.2 = (bf16[8,256,768]{2,1,0:T(8,128)(2,1)S(1)}, bf16[8,256,768]{2,1,0:T(8,128)(2,1)}, u32[]{:S(2)}) copy-start(bf16[8,256,768]{2,1,0:T(8,128)(2,1)} %get-tuple-element.121) | copy-start | bytes 9437188
  288.2 133.7 %reduce-scatter.8.cloned.1.call-start = ((), (), s32[]{:S(2)}) async-start(), calls=%async_computation.9 | async-start | bytes 1966080 | tf_op jit(solution)/shard_map/reduce_scatter | solution.py:1330
  295.2 189.4 %reduce-scatter.10.cloned.1.call-start = ((), (), s32[]{:S(2)}) async-start(), calls=%async_computation.10 | async-start | bytes 7864320 | tf_op jit(solution)/shard_map/reduce_scatter | solution.py:1330
  329.6 241.9 %reduce-scatter.12.cloned.1.call-start = ((), (), s32[]{:S(2)}) async-start(), calls=%async_computation.11 | async-start | bytes 1945600 | tf_op jit(solution)/shard_map/reduce_scatter | solution.py:1330
  418.3 62.7 %collective-permute-start.6 = (bf16[256,2048]{1,0:T(8,128)(2,1)}, bf16[256,2048]{1,0:T(8,128)(2,1)}, u32[]{:S(2)}, u32[]{:S(2)}) collective-permute-start(bf16[256,2048]{1,0:T(8,128)(2,1)} %get-tuple-element.125), channel_id=1, source_target_pairs={{0,6},{2,4},{4,2},{6,0},{1,7},{3,5},{5,3},{7,1},{8,14},{10,12},{12... | collective-permute-start | bytes 3145736 | tf_op jit(solution)/shard_map/ppermute | solution.py:39
  420.1 60.9 %collective-permute-start.5 = (bf16[256,2048]{1,0:T(8,128)(2,1)}, bf16[256,2048]{1,0:T(8,128)(2,1)}, u32[]{:S(2)}, u32[]{:S(2)}) collective-permute-start(bf16[256,2048]{1,0:T(8,128)(2,1)} %get-tuple-element.124), channel_id=1, source_target_pairs={{0,4},{2,6},{4,0},{6,2},{1,5},{3,7},{5,1},{7,3},{8,12},{10,14},{12... | collective-permute-start | bytes 3145736 | tf_op jit(solution)/shard_map/ppermute | solution.py:39
  421.0 60.0 %collective-permute-start.4 = (bf16[256,2048]{1,0:T(8,128)(2,1)}, bf16[256,2048]{1,0:T(8,128)(2,1)}, u32[]{:S(2)}, u32[]{:S(2)}) collective-permute-start(bf16[256,2048]{1,0:T(8,128)(2,1)} %get-tuple-element.123), channel_id=1, source_target_pairs={{0,2},{2,0},{4,6},{6,4},{1,3},{3,1},{5,7},{7,5},{8,10},{10,8},{12,... | collective-permute-start | bytes 3145736 | tf_op jit(solution)/shard_map/ppermute | solution.py:39
  473.7 7.3 %copy-start.1 = (f32[256,2048]{1,0:T(8,128)S(1)}, f32[256,2048]{1,0:T(8,128)}, u32[]{:S(2)}) copy-start(f32[256,2048]{1,0:T(8,128)} %get-tuple-element.115.refs_4_) | copy-start | bytes 6291460
  473.7 7.3 %copy-start.6 = (bf16[256,2048]{1,0:T(8,128)(2,1)S(1)}, bf16[256,2048]{1,0:T(8,128)(2,1)}, u32[]{:S(2)}) copy-start(bf16[256,2048]{1,0:T(8,128)(2,1)} %get-tuple-element.122) | copy-start | bytes 3145732
  480.9 97.0 %reduce-scatter.14.cloned.1.call-start = ((), (), s32[]{:S(2)}) async-start(), calls=%async_computation.12 | async-start | bytes 3276800 | tf_op jit(solution)/shard_map/reduce_scatter | solution.py:1330
  493.6 11.2 %copy-start.11 = (bf16[64]{0:T(256)(128)(2,1)S(1)}, bf16[64]{0:T(256)(128)(2,1)}, u32[]{:S(2)}) copy-start(bf16[64]{0:T(256)(128)(2,1)} %param.40) | copy-start | bytes 388
  493.6 11.7 %copy-start.12 = (bf16[64]{0:T(256)(128)(2,1)S(1)}, bf16[64]{0:T(256)(128)(2,1)}, u32[]{:S(2)}) copy-start(bf16[64]{0:T(256)(128)(2,1)} %param.31) | copy-start | bytes 388
  493.6 12.3 %copy-start.3 = (bf16[192,1024]{1,0:T(8,128)(2,1)S(1)}, bf16[192,1024]{1,0:T(8,128)(2,1)}, u32[]{:S(2)}) copy-start(bf16[192,1024]{1,0:T(8,128)(2,1)} %reduce-scatter.6.cloned.1.call-done.refs_7_) | copy-start | bytes 1179652
  493.6 12.3 %copy-start.4 = (bf16[192,1024]{1,0:T(8,128)(2,1)S(1)}, bf16[192,1024]{1,0:T(8,128)(2,1)}, u32[]{:S(2)}) copy-start(bf16[192,1024]{1,0:T(8,128)(2,1)} %reduce-scatter.8.cloned.1.call-done.refs_0_) | copy-start | bytes 1179652
  576.2 16.8 %copy-start.7 = (bf16[256,2048]{1,0:T(8,128)(2,1)S(1)}, bf16[256,2048]{1,0:T(8,128)(2,1)}, u32[]{:S(2)}) copy-start(bf16[256,2048]{1,0:T(8,128)(2,1)} %get-tuple-element.143) | copy-start | bytes 3145732
Sparse Core Ops, SparseCore 0:
  9.6 42.8 all-gather.3
  99.7 117.0 all-gather.7
  218.4 63.1 all-gather.5
  288.3 36.2 reduce-scatter.5
  326.7 34.2 reduce-scatter.7
  363.2 110.5 reduce-scatter.9
  481.0 35.1 reduce-scatter.11
  518.5 57.3 reduce-scatter.13
